TPU v7x, 32 devices: a whole 2x2x4 slice. The times are simulated.
32 devices in a mesh: groups: 2 (over x), inst: 4 (over z), tp: 4 (over y, core).
Axes of the slice: x: 2, y: 2, z: 4, core: 2. Of those that a mesh axis runs over, the one named last changes fastest.
Arguments:
- res_pool: bfloat16 [8, 8, 64, 16, 256], P(('groups', 'inst'), 'tp'), parts along dimension 0, may hold values from -6 to 6
- res_table: int32 [8, 125, 8], P(('groups', 'inst')), parts along dimension 0, may hold values from 0 to 63
- res_len: int32 [8, 125], P(('groups', 'inst')), parts along dimension 0, may hold values from 1 to 128
- out_pool: bfloat16 [8, 8, 64, 16, 256], P(('groups', 'inst'), 'tp'), parts along dimension 0, may hold values from -6 to 6, as said below
- src_table: int32 [8, 2, 32], P(('groups', 'inst')), parts along dimension 0, may hold values from 0 to 63, as said below
- mig_len: int32 [16], P('groups'), parts along dimension 0, may hold values from 1 to 512
- mig_dest: int32 [16], P('groups'), parts along dimension 0, may hold values from 0 to 3, as said below
- queries: bfloat16 [1024, 4, 64, 128], P(('groups', 'inst'), None, 'tp'), parts along dimension 0, may hold values from -480 to 480
- new_kv: bfloat16 [1024, 4, 8, 256], P(('groups', 'inst'), None, 'tp'), parts along dimension 0, may hold values from -6 to 6
- out_weight: bfloat16 [8192, 8192], P('tp'), may hold values from -0.75 to 0.75
Outputs:
- arrived: bfloat16 [8, 3, 8, 512, 256], P(('groups', 'inst'), None, 'tp'), parts along dimension 0
- hidden: bfloat16 [8192, 4096], P('tp', ('groups', 'inst')), parts along dimension 1
There are 2 independent parts, one for each index of `groups`. A program takes and returns all parts, laid end to end along the dimension named above; an argument that names none is the same for every part. Nothing has to cross between parts.
Inputs may be any that keep to these rules, and one draw needn't show every extreme that they name: `mig_dest`: no request stays on its source instance; the 2 requests of one instance go to different instances; half of the instances receive exactly 3 requests and the other half one. `src_table`: the entries of one instance are all different. `out_pool`: head slots s and s2 hold equal entries where s * 1 equals s2 * 1.
All inputs are finite; a program needn't handle non-finite values.
Results may differ from a plain program's by a relative error of at most 0.0053.
Values may be sent and summed in bfloat16 or wider, within the bound.
No kernel may reach another device: no remote copies, remote signals or barrier semaphores. Data moves between devices by JAX's collectives and lax.ppermute only.
A program may use at most 192 MiB of HBM per device.

v0:
```python
import math

import jax
import jax.numpy as jnp
from jax import lax
from jax.sharding import PartitionSpec as P


def attend(query_in, context, lengths, newest, layout):
    head_width = query_in.shape[-1]
    step_count = query_in.shape[1]
    inv_root = 1.0 / math.sqrt(head_width)
    key_part = context[..., :head_width]
    value_part = context[..., head_width:]
    fresh_keys = newest[..., :head_width]
    fresh_values = newest[..., head_width:]
    cached_scores = (
        jnp.einsum(
            "rsngd," + layout + "->rsngc", query_in, key_part, preferred_element_type=jnp.float32
        )
        * inv_root
    )
    fresh_scores = (
        jnp.einsum("rsngd,rtnd->rsngt", query_in, fresh_keys, preferred_element_type=jnp.float32)
        * inv_root
    )
    extent = context.shape[2]
    in_range = (jnp.arange(extent, dtype=jnp.int32)[None, :] < lengths[:, None])[
        :, None, None, None, :
    ]
    causal = (
        jnp.arange(step_count, dtype=jnp.int32)[None, :]
        <= jnp.arange(step_count, dtype=jnp.int32)[:, None]
    )[None, :, None, None, :]
    largest = jnp.maximum(
        jnp.max(jnp.where(in_range, cached_scores, -jnp.inf), axis=-1),
        jnp.max(jnp.where(causal, fresh_scores, -jnp.inf), axis=-1),
    )
    cached_weights = jnp.where(in_range, jnp.exp(cached_scores - largest[..., None]), 0.0)
    fresh_weights = jnp.where(causal, jnp.exp(fresh_scores - largest[..., None]), 0.0)
    totals = jnp.sum(cached_weights, axis=-1) + jnp.sum(fresh_weights, axis=-1)
    blended = jnp.einsum(
        "rsngc," + layout + "->rsngd",
        cached_weights.astype(jnp.bfloat16),
        value_part,
        preferred_element_type=jnp.float32,
    )
    blended = blended + jnp.einsum(
        "rsngt,rtnd->rsngd",
        fresh_weights.astype(jnp.bfloat16),
        fresh_values,
        preferred_element_type=jnp.float32,
    )
    return (blended / totals[..., None]).astype(jnp.bfloat16)


def projector(out_weight, attention):
    return lax.dot_general(
        out_weight, attention, (((0,), (1,)), ((), ())), preferred_element_type=jnp.float32
    )


def shards(
    res_pool,
    res_table,
    res_len,
    out_pool,
    src_table,
    mig_len,
    mig_dest,
    queries,
    new_kv,
    out_weight,
):
    row_count = queries.shape[0]
    step_count = queries.shape[1]
    head_width = queries.shape[3]
    slot_count = res_pool.shape[1]
    per_slot = queries.shape[2] // slot_count
    resident = res_table.shape[1]
    inst_count = lax.axis_size("inst")
    inst_here = lax.axis_index("inst")
    mig_per = src_table.shape[1]
    arrive_cap = inst_count - 1
    request_count = mig_dest.shape[0]
    request_ids = jnp.arange(request_count, dtype=jnp.int32)
    same_dest = mig_dest[:, None] == mig_dest[None, :]
    standing = jnp.sum(same_dest & (request_ids[None, :] < request_ids[:, None]), axis=1)
    matches = (mig_dest[None, :] == inst_here) & (
        standing[None, :] == jnp.arange(arrive_cap, dtype=jnp.int32)[:, None]
    )
    arrival_req = jnp.sum(jnp.where(matches, request_ids[None, :], 0), axis=1)
    arrival_len = jnp.sum(jnp.where(matches, mig_len[None, :], 0), axis=1)
    outgoing = lax.dynamic_slice_in_dim(mig_dest, inst_here * mig_per, mig_per, 0)
    tables = src_table[0]
    blocks = out_pool[0][:, tables]
    targets = jnp.arange(inst_count, dtype=jnp.int32)
    outbox = jnp.zeros((inst_count,) + blocks[:, 0].shape, jnp.bfloat16)
    for slot_index in range(mig_per):
        chosen = (outgoing[slot_index] == targets)[:, None, None, None, None]
        outbox = jnp.where(chosen, blocks[:, slot_index][None], outbox)
    inbox = lax.all_to_all(outbox, "inst", split_axis=0, concat_axis=0, tiled=True)
    pieces = jnp.take(inbox, arrival_req // mig_per, axis=0)
    extent = pieces.shape[2] * pieces.shape[3]
    flattened = pieces.reshape(arrive_cap, slot_count, extent, 2 * head_width)
    inside = (jnp.arange(extent, dtype=jnp.int32)[None, :] < arrival_len[:, None])[:, None, :, None]
    arrived = jnp.where(inside, flattened, jnp.zeros_like(flattened))
    row_queries = queries.reshape(row_count, step_count, slot_count, per_slot, head_width)
    context = res_pool[0][:, res_table[0]]
    context = context.reshape(
        slot_count, resident, context.shape[2] * context.shape[3], 2 * head_width
    )
    resident_out = attend(row_queries[:resident], context, res_len[0], new_kv[:resident], "nrcd")
    arrival_out = attend(row_queries[resident:], arrived, arrival_len, new_kv[resident:], "rncd")
    resident_flat = resident_out.reshape(resident * step_count, -1)
    arrival_flat = arrival_out.reshape((row_count - resident) * step_count, -1)
    attention = jnp.concatenate([resident_flat, arrival_flat], axis=0)
    hidden = lax.psum_scatter(
        projector(out_weight, attention), "tp", scatter_dimension=0, tiled=True
    )
    return (arrived[None], hidden.astype(jnp.bfloat16))


def solution(mesh):
    placed = (
        P(("groups", "inst"), "tp", None, None, None),
        P(("groups", "inst"), None, None),
        P(("groups", "inst"), None),
        P(("groups", "inst"), "tp", None, None, None),
        P(("groups", "inst"), None, None),
        P("groups"),
        P("groups"),
        P(("groups", "inst"), None, "tp", None),
        P(("groups", "inst"), None, "tp", None),
        P("tp", None),
    )
    return jax.shard_map(
        shards,
        mesh=mesh,
        in_specs=placed,
        out_specs=(P(("groups", "inst"), None, "tp", None, None), P("tp", ("groups", "inst"))),
        check_vma=False,
    )
```

profile of v0, /device:TPU:0, one launch (start us, length us, event | category | flops | bytes accessed | tf_op | source)
XLA Modules:
  0.0 255.1 jit_solution(16442618863349721219)
XLA Ops:
  7.2 0.8 dynamic_slice.3
  8.0 0.6 fusion.63
  8.6 0.7 compare_select_fusion.1
  9.4 1.8 gather_fusion
  11.3 1.3 iota_compare_fusion.5
  12.6 1.8 select_select_fusion
  14.4 6.4 %all-to-all-start = ((bf16[4,2,32,16,256]{4,3,2,1,0:T(8,128)(2,1)}), bf16[4,2,32,16,256]{4,3,2,1,0:T(8,128)(2,1)}, u32[]{:S(2)}, u32[]{:S(2)}) async-start(bf16[4,2,32,16,256]{4,3,2,1,0:T(8,128)(2,1)} %select_select_fusion), calls=%async_computation | async-start | bytes 4194304 | tf_op jit(solution)/shard_map/all_to_all | solution.py:102
  21.3 0.4 fusion.61
  21.6 12.3 %gather_fusion.2 = bf16[1000,2,16,256]{3,2,1,0:T(8,128)(2,1)} fusion(bf16[2,64,16,256]{3,2,1,0:T(8,128)(2,1)S(1)} %bitcast.160, s32[1024]{0:T(1024)S(1)} %pad_clamp_fusion), kind=kCustom, calls=%fused_computation.2 | custom fusion | bytes 32772000 | tf_op jit(solution)/shard_map/gather | solution.py:109
  33.9 13.9 %copy.38 = bf16[125,8,2,16,256]{4,3,1,2,0:T(8,128)(2,1)} copy(bf16[125,8,2,16,256]{4,3,2,1,0:T(8,128)(2,1)} %bitcast.161) | data formatting | bytes 32768000 | tf_op jit(solution)/shard_map/gather | solution.py:109
  47.9 9.1 %fusion.13 = (f32[125,4,2,8]{3,1,2,0:T(4,128)S(1)}, f32[125,2,4,4,8]{4,2,3,1,0:T(4,128)S(1)}) fusion(pred[4,4]{1,0:T(4,128)(4,1)S(1)} %iota_compare_fusion.3, bf16[125,4,2,128]{3,2,1,0:T(2,128)(2,1)S(1)} %get-tuple-element.13, bf16[128,4,16,128]{3,2,1,0:T(8,128)(2,1)S(1)} %copy-done.6), kind=kOutput, calls=%fused_computation.24 | convolution fusion | flops 8280000 | bytes 2464512 | tf_op jit(solution)/shard_map/rsngd,rtnd->rsngt/dot_general | solution.py:24
  57.0 8.5 %fusion.4 = (f32[125,4,2,8]{3,1,2,0:T(4,128)S(1)}, f32[125,2,128,4,8]{2,4,3,1,0:T(8,128)S(1)}) fusion(pred[125,128]{1,0:T(8,128)(4,1)S(1)} %iota_compare_fusion, bf16[2,125,128,256]{3,2,0,1:T(8,128)(2,1)} %bitcast.162, bf16[128,4,16,128]{3,2,1,0:T(8,128)(2,1)} %param.17), kind=kOutput, calls=%fused_computation.13 | convolution fusion | flops 265208000 | bytes 14384000 | tf_op jit(solution)/shard_map/rsngd,nrcd->rsngc/dot_general | solution.py:18
  65.6 2.1 fusion.29
  67.7 3.1 %fusion.7 = f32[125,4,2,8]{3,1,2,0:T(4,128)S(1)} fusion(f32[125,2,128,4,8]{2,4,3,1,0:T(8,128)S(1)} %get-tuple-element.23, f32[125,4,2,8]{3,1,2,0:T(4,128)S(1)} %max.14, pred[125,128]{1,0:T(8,128)(4,1)S(1)} %iota_compare_fusion), kind=kLoop, calls=%fused_computation.16 | loop fusion | flops 4088000 | bytes 4176000 | tf_op jit(solution)/shard_map/reduce_sum | solution.py:41
  70.8 1.3 fusion.31
  72.3 5.7 %fusion.3 = bf16[125,4,2,8,128]{4,3,1,2,0:T(8,128)(2,1)S(1)} fusion(f32[125,2,4,8,128]{4,3,2,1,0:T(8,128)S(1)} %fusion.31, bf16[2,125,128,256]{3,2,0,1:T(8,128)(2,1)} %bitcast.163, f32[125,2,128,4,8]{2,4,3,1,0:T(8,128)S(1)} %get-tuple-element.23, f32[125,4,2,8]{3,1,2,0:T(4,128)S(1)} %add.84, f32[125,4,2,8]{3,1,2,0:T(4,128)S(1)} %max.14, ...), kind=kOutput, calls=%fused_computation.10 | convolution fusion | flops 269312000 | bytes 18512000 | tf_op jit(solution)/shard_map/rsngc,nrcd->rsngd/dot_general | solution.py:42
  78.0 0.4 copy.43
  78.4 2.2 reshape.254
  80.6 0.2 convert_reduce_fusion
  81.1 0.7 fusion.62
  81.8 1.1 select_reduce_fusion.1
  83.0 2.2 gather_fusion.1
  85.2 0.4 fusion.23
  85.6 1.2 select_reduce_fusion
  86.8 0.3 convolution_bitcast_fusion.2
  87.2 0.2 fusion.37
  87.5 0.3 fusion.27
  87.9 27.4 %convolution_bitcast_fusion = f32[8192,512]{0,1:T(8,128)} fusion(bf16[2048,8192]{1,0:T(8,128)(2,1)} %param.19, bf16[12,2048]{1,0:T(8,128)(2,1)S(1)} %reshape.255, bf16[500,2048]{1,0:T(8,128)(2,1)} %reshape.254), kind=kOutput, calls=%fused_computation.3 | convolution fusion | flops 17184063488 | bytes 52428800 | tf_op jit(solution)/shard_map/dot_general | solution.py:58
  115.3 1.4 select_select_fusion.1
  116.8 126.4 %reduce-scatter.2.cloned.1.call-done = f32[2048,512]{0,1:T(8,128)} async-done(((f32[8192,512]{0,1:T(8,128)}), f32[2048,512]{0,1:T(8,128)}) %reduce-scatter.2.cloned.1.call-update) | async-done | bytes 4194320 | tf_op jit(solution)/shard_map/reduce_scatter | solution.py:118
  243.1 2.6 %convert_element_type.31 = bf16[2048,512]{0,1:T(8,128)(2,1)S(1)} convert(f32[2048,512]{0,1:T(8,128)} %reduce-scatter.2.cloned.1.call-done) | non-fusion elementwise | flops 1048576 | bytes 6291456 | tf_op jit(solution)/shard_map/convert_element_type | solution.py:121
  245.7 2.5 copy.49
  (41 shorter events, 1.3 us)
Async XLA Ops:
  7.2 14.5 %copy-start = (bf16[1,2,64,16,256]{4,3,2,1,0:T(8,128)(2,1)S(1)}, bf16[1,2,64,16,256]{4,3,2,1,0:T(8,128)(2,1)}, u32[]{:S(2)}) copy-start(bf16[1,2,64,16,256]{4,3,2,1,0:T(8,128)(2,1)} %param.10) | copy-start | bytes 3145732
  14.4 6.5 %copy-start.3 = (s32[1,125,8]{1,2,0:T(8,128)S(1)}, s32[1,125,8]{1,2,0:T(8,128)}, u32[]{:S(2)}) copy-start(s32[1,125,8]{1,2,0:T(8,128)} %param.11) | copy-start | bytes 12004
  14.4 6.5 %copy-start.4 = (s32[1,125]{1,0:T(1,128)S(1)}, s32[1,125]{1,0:T(1,128)}, u32[]{:S(2)}) copy-start(s32[1,125]{1,0:T(1,128)} %param.12) | copy-start | bytes 1504
  14.4 6.8 %copy-start.2 = (bf16[128,4,2,256]{3,2,1,0:T(2,128)(2,1)S(1)}, bf16[128,4,2,256]{3,2,1,0:T(2,128)(2,1)}, u32[]{:S(2)}) copy-start(bf16[128,4,2,256]{3,2,1,0:T(2,128)(2,1)} %param.18) | copy-start | bytes 1572868
  14.4 68.5 %all-to-all-start = ((bf16[4,2,32,16,256]{4,3,2,1,0:T(8,128)(2,1)}), bf16[4,2,32,16,256]{4,3,2,1,0:T(8,128)(2,1)}, u32[]{:S(2)}, u32[]{:S(2)}) async-start(bf16[4,2,32,16,256]{4,3,2,1,0:T(8,128)(2,1)} %select_select_fusion), calls=%async_computation | async-start | bytes 4194304 | tf_op jit(solution)/shard_map/all_to_all | solution.py:102
  20.9 222.2 %reduce-scatter.2.cloned.1.call-start = ((), (), s32[]{:S(2)}) async-start(), calls=%async_computation.2 | async-start | bytes 20971520 | tf_op jit(solution)/shard_map/reduce_scatter | solution.py:118
  33.9 13.9 %copy-start.6 = (bf16[128,4,16,128]{3,2,1,0:T(8,128)(2,1)S(1)}, bf16[128,4,16,128]{3,2,1,0:T(8,128)(2,1)}, u32[]{:S(2)}) copy-start(bf16[128,4,16,128]{3,2,1,0:T(8,128)(2,1)} %param.17) | copy-start | bytes 6291460
  78.4 2.2 copy-start.7
  78.4 2.4 copy-start.5
  243.1 5.1 %copy-start.1 = (bf16[1,2,64,16,256]{4,3,2,1,0:T(8,128)(2,1)S(1)}, bf16[1,2,64,16,256]{4,3,2,1,0:T(8,128)(2,1)}, u32[]{:S(2)}) copy-start(bf16[1,2,64,16,256]{4,3,2,1,0:T(8,128)(2,1)} %param.10) | copy-start | bytes 3145732
Sparse Core Ops, SparseCore 0:
  115.5 127.6 reduce-scatter.1
where the time goes:
time: 256 us; the launch traced here: 255 us
  waiting for transfers between devices  126 us (49%)
  matrix products  55 us (21%)
  local copies, waits for them, and re-layouts  38.4 us (15%)
  other arithmetic  14.6 us (6%)
  between operations  14.3 us (6%)
  starting transfers between devices  6.45 us (3%)
    reduce_scatter x1, waiting for transfers between devices, shards(): lax.psum_scatter(projector(out_weight, attention), 'tp', scatter_dimensio...  126 us
    dot_general x1, matrix products, projector(): lax.dot_general(out_weight, attention, (((0,), (1,)), ((), ())), preferre...  27.4 us
    gather x2, local copies, waits for them, and re-layouts, shards(): context = res_pool[0][:, res_table[0]]  26.2 us
    dot_general x2, matrix products, attend(): jnp.einsum('rsngd,rtnd->rsngt', query_in, fresh_keys, preferred_element_t...  10.2 us
    dot_general x2, matrix products, attend(): jnp.einsum('rsngd,' + layout + '->rsngc', query_in, key_part, preferred_e...  9.73 us
    all_to_all x1, starting transfers between devices, shards(): lax.all_to_all(outbox, 'inst', split_axis=0, concat_axis=0, tiled=True)  6.45 us
    dot_general x2, matrix products, attend(): jnp.einsum('rsngc,' + layout + '->rsngd', cached_weights.astype(jnp.bfloa...  5.99 us
    reduce_sum x4, other arithmetic, attend(): totals = jnp.sum(cached_weights, axis=-1) + jnp.sum(fresh_weights, axis=-1)  5.55 us
  transfers between devices with their start and end apart: 2, of which 1 were waited for; matrix products, arithmetic and copies ran while one was open for 25% of the time, Pallas kernels for 0%

commit v1 on v0

v1 whole, which is shorter than its diff:
```python
import functools
import math

import jax
import jax.numpy as jnp
from jax import lax
from jax.experimental import pallas as pl
from jax.experimental.pallas import tpu as pltpu
from jax.sharding import PartitionSpec as P

CORES = 2
LOW = -1e30
MIB = 1 << 20
LANES = 128


def params(limit):
    return pltpu.CompilerParams(vmem_limit_bytes=limit * MIB)


def dot_t(left, right):
    return lax.dot_general(
        left, right, (((1,), (1,)), ((), ())), preferred_element_type=jnp.float32
    )


def row_plan(dest_ref, inst, cap):
    requests = [jnp.int32(-1)] * cap
    seen = jnp.int32(0)
    for g in range(dest_ref.shape[0]):
        here = dest_ref[g] == inst
        requests = [jnp.where(here & (seen == a), g, requests[a]) for a in range(cap)]
        seen = seen + here.astype(jnp.int32)
    return requests


def standing_of(dest_ref, request):
    dest = dest_ref[request]
    count = jnp.int32(0)
    for g in range(dest_ref.shape[0]):
        count = count + ((dest_ref[g] == dest) & (g < request)).astype(jnp.int32)
    return dest, count


def pick(choices, index):
    chosen = choices[0]
    for k in range(1, len(choices)):
        chosen = jnp.where(index == k, choices[k], chosen)
    return chosen


def pack_kernel(table_ref, dest_ref, pool_ref, *send_refs, insts, mig_per):
    inst = lax.axis_index("inst")
    slots, blocks = send_refs[0].shape[0], send_refs[0].shape[1]
    shifts = [lax.rem(dest_ref[inst * mig_per + m] - inst + insts, insts) for m in range(mig_per)]
    for k in range(1, insts):
        m = jnp.int32(0)
        for other in range(1, mig_per):
            m = jnp.where(shifts[other] == k, other, m)

        def copy_block(b, carry, m=m, k=k):
            block = table_ref[0, m, b]
            for s in range(slots):
                send_refs[k - 1][s, b] = pool_ref[0, s, block]
            return carry

        lax.fori_loop(0, blocks, copy_block, 0, unroll=8)


def pack(src_table, mig_dest, out_pool, insts):
    _, slots, _, block, width = out_pool.shape
    mig_per, blocks = src_table.shape[1:]
    shape = jax.ShapeDtypeStruct((slots, blocks, block, width), out_pool.dtype)
    smem = pl.BlockSpec(memory_space=pltpu.SMEM)
    vmem = pl.BlockSpec(memory_space=pltpu.VMEM)
    return pl.pallas_call(
        functools.partial(pack_kernel, insts=insts, mig_per=mig_per),
        out_shape=[shape] * (insts - 1),
        in_specs=[smem, smem, vmem],
        out_specs=[vmem] * (insts - 1),
        compiler_params=params(24),
        name="pack",
    )(src_table, mig_dest, out_pool)


def arrived_kernel(dest_ref, len_ref, *refs, insts, mig_per, cap):
    got, out_ref = refs[:-1], refs[-1]
    inst = lax.axis_index("inst")
    slots, blocks, block, width = got[0].shape
    requests = row_plan(dest_ref, inst, cap)
    place = lax.broadcasted_iota(jnp.int32, (block, width), 0)
    for a in range(cap):
        request = requests[a]
        known = jnp.maximum(request, 0)
        length = jnp.where(request >= 0, len_ref[known], 0)
        shift = lax.rem(known // mig_per - inst + insts, insts)

        for k in range(1, insts):

            @pl.when((shift == k) | ((request < 0) & (k == 1)))
            def _(a=a, k=k, length=length):
                def one(b, carry):
                    inside = place + b * block < length
                    for s in range(slots):
                        value = got[k - 1][s, b].astype(jnp.float32)
                        value = jnp.where(inside, value, 0.0).astype(jnp.bfloat16)
                        out_ref[0, a, s, pl.ds(pl.multiple_of(b * block, block), block), :] = value
                    return carry

                lax.fori_loop(0, blocks, one, 0, unroll=4)


def assemble(mig_dest, mig_len, got, insts, mig_per):
    slots, blocks, block, width = got[0].shape
    cap = insts - 1
    smem = pl.BlockSpec(memory_space=pltpu.SMEM)
    vmem = pl.BlockSpec(memory_space=pltpu.VMEM)
    return pl.pallas_call(
        functools.partial(arrived_kernel, insts=insts, mig_per=mig_per, cap=cap),
        out_shape=jax.ShapeDtypeStruct((1, cap, slots, blocks * block, width), jnp.bfloat16),
        in_specs=[smem, smem] + [vmem] * len(got),
        out_specs=vmem,
        compiler_params=params(32),
        name="assemble",
    )(mig_dest, mig_len, *got)


def fresh_code(rows, keys, steps, heads, slots):
    index = lax.broadcasted_iota(jnp.int32, (rows, keys), 0)
    key = lax.broadcasted_iota(jnp.int32, (rows, keys), 1)
    step = index // heads
    slot = lax.rem(index, heads) // (heads // slots)
    per_row = steps * slots
    in_row = lax.rem(key, per_row)
    seen = (in_row // slots <= step) & (lax.rem(in_row, slots) == slot)
    return jnp.where(seen, key // per_row, -1)


def blend(query, keys, values, length, fresh, fresh_seen, slot_of, slots):
    extent = keys.shape[0] // slots
    scale = math.log2(math.e) / math.sqrt(query.shape[1])
    scores = dot_t(query, keys)
    own = scores[:, :extent]
    for s in range(1, slots):
        own = jnp.where(slot_of == s, scores[:, s * extent : (s + 1) * extent], own)
    place = lax.broadcasted_iota(jnp.int32, own.shape, 1)
    own = jnp.where(place < length, own, LOW)
    fresh = jnp.where(fresh_seen, fresh, LOW)
    if own.shape == fresh.shape:
        largest = jnp.max(jnp.maximum(own, fresh), axis=1, keepdims=True)
    else:
        largest = jnp.maximum(
            jnp.max(own, axis=1, keepdims=True), jnp.max(fresh, axis=1, keepdims=True)
        )
    own = jnp.exp2((own - largest) * scale)
    fresh = jnp.exp2((fresh - largest) * scale)
    if own.shape == fresh.shape:
        total = jnp.sum(own + fresh, axis=1, keepdims=True)
    else:
        total = jnp.sum(own, axis=1, keepdims=True) + jnp.sum(fresh, axis=1, keepdims=True)
    spread = own
    if slots > 1:
        spread = jnp.concatenate([jnp.where(slot_of == s, own, 0.0) for s in range(slots)], axis=1)
    context = jnp.dot(spread.astype(jnp.bfloat16), values, preferred_element_type=jnp.float32)
    return context, fresh.astype(jnp.bfloat16), total


def gather_blocks(pool_ref, slots, ids):
    tiles = [pool_ref[0, s, block] for s in range(slots) for block in ids]
    return jnp.concatenate(tiles, axis=0)


def slot_index(rows, extent, heads, slots):
    index = lax.broadcasted_iota(jnp.int32, (rows, extent), 0)
    return lax.rem(index, heads) // (heads // slots)


def attend_kernel(
    table_ref, len_ref, dest_ref, query_ref, kv_ref, pool_ref, *refs,
    first_row, batch, steps, heads, slots, insts, mig_per, back_count,
):
    back = refs[:back_count]
    out_ref, fresh_ref, pf_ref, blend_ref, inv_ref = refs[back_count:]
    width = query_ref.shape[1]
    per = steps * heads
    rows = query_ref.shape[0] // per
    resident = len_ref.shape[1]
    blocks = table_ref.shape[0]
    extent = blocks * pool_ref.shape[3]
    start = first_row + pl.program_id(0) * rows

    fresh_ref[...] = dot_t(query_ref[...], kv_ref[:, :width])
    code = fresh_code(per, kv_ref.shape[0], steps, heads, slots)
    slot_of = slot_index(per, extent, heads, slots)
    for r in range(rows):
        row = start + r
        known = jnp.minimum(row, resident - 1)
        length = jnp.where(row < resident, len_ref[0, known], 0)
        ids = [table_ref[j, known] for j in range(blocks)]
        both = gather_blocks(pool_ref, slots, ids)
        at = slice(r * per, (r + 1) * per)
        context, weights, total = blend(
            query_ref[at, :], both[:, :width], both[:, width:], length,
            fresh_ref[at, :], code == r, slot_of, slots,
        )
        blend_ref[at, :] = context
        pf_ref[at, :] = weights
        inv_ref[at, :] = jnp.broadcast_to(1.0 / total, (per, width))

    done = blend_ref[...] + jnp.dot(
        pf_ref[...], kv_ref[:, width:], preferred_element_type=jnp.float32
    )
    blend_ref[...] = done * inv_ref[...]

    if back_count:
        cap = insts - 1
        inst = lax.axis_index("inst")
        requests = row_plan(dest_ref, inst, cap)

        @pl.when(pl.program_id(0) == pl.num_programs(0) - 1)
        def _():
            for a in range(cap):
                request = requests[a]
                known = jnp.maximum(request, 0)
                shift = lax.rem(known // mig_per - inst + insts, insts)
                begin = pl.multiple_of(lax.rem(known, mig_per) * per, per)
                choices = [ref[pl.ds(begin, per), :].astype(jnp.float32) for ref in back]
                at = slice((rows - cap + a) * per, (rows - cap + a + 1) * per)
                blend_ref[at, :] = jnp.where(
                    request >= 0, pick(choices, shift - 1), blend_ref[at, :]
                )

    for h in range(heads):
        column = blend_ref[pl.ds(h, rows * steps, stride=heads), :]
        out_ref[:, h * width : (h + 1) * width] = column.astype(jnp.bfloat16)


def attend(table, lengths, dest, queries, new_kv, pool, back, first_row, rows, dims):
    steps, heads, slots, insts, mig_per = dims
    width = queries.shape[1]
    per = steps * heads
    per_kv = steps * slots
    group = min(rows, LANES // per_kv)
    first = first_row // group
    smem = pl.BlockSpec(memory_space=pltpu.SMEM)
    vmem = pl.BlockSpec(memory_space=pltpu.VMEM)
    kernel = functools.partial(
        attend_kernel, first_row=first_row, batch=None, steps=steps, heads=heads, slots=slots,
        insts=insts, mig_per=mig_per, back_count=len(back),
    )
    tokens = rows * steps
    return pl.pallas_call(
        kernel,
        grid=(rows // group,),
        out_shape=jax.ShapeDtypeStruct((tokens, heads * width), jnp.bfloat16),
        in_specs=[
            smem, smem, smem,
            pl.BlockSpec((group * per, width), lambda i: (first + i, 0)),
            pl.BlockSpec((group * per_kv, 2 * width), lambda i: (first + i, 0)),
            vmem,
        ] + [vmem] * len(back),
        out_specs=pl.BlockSpec((group * steps, heads * width), lambda i: (i, 0)),
        scratch_shapes=[
            pltpu.VMEM((group * per, group * per_kv), jnp.float32),
            pltpu.VMEM((group * per, group * per_kv), jnp.bfloat16),
            pltpu.VMEM((group * per, width), jnp.float32),
            pltpu.VMEM((group * per, width), jnp.float32),
        ],
        compiler_params=params(24),
        cost_estimate=pl.CostEstimate(
            flops=rows * per * 1100 * width, bytes_accessed=4 * MIB, transcendentals=rows * per * 256
        ),
        name="attend",
    )(table, lengths, dest, queries, new_kv, pool, *back)


def serve_kernel(
    table_ref, len_ref, dest_ref, pool_ref, *refs, steps, heads, slots, insts, mig_per, query_rows
):
    tails, out_ref = refs[:-1], refs[-1]
    inst = lax.axis_index("inst")
    per = steps * heads
    width = out_ref.shape[1]
    blocks = table_ref.shape[2]
    extent = blocks * pool_ref.shape[3]
    fresh_keys = (tails[0].shape[0] - query_rows) // 2
    code = fresh_code(per, fresh_keys, steps, heads, slots)
    slot_of = slot_index(per, extent, heads, slots)
    for m in range(mig_per):
        request = inst * mig_per + m
        dest, place = standing_of(dest_ref, request)
        shift = lax.rem(dest - inst + insts, insts)
        begin = pl.multiple_of((place + 1) * per, per)
        query = pick([ref[pl.ds(begin, per), :] for ref in tails], shift - 1)
        keys = pick([ref[query_rows : query_rows + fresh_keys, :] for ref in tails], shift - 1)
        values = pick([ref[query_rows + fresh_keys :, :] for ref in tails], shift - 1)
        both = gather_blocks(pool_ref, slots, [table_ref[0, m, b] for b in range(blocks)])
        context, weights, total = blend(
            query, both[:, :width], both[:, width:], len_ref[request],
            dot_t(query, keys), code == place + 1, slot_of, slots,
        )
        context = context + jnp.dot(weights, values, preferred_element_type=jnp.float32)
        out_ref[m * per : (m + 1) * per, :] = (context / total).astype(jnp.bfloat16)


def serve(src_table, mig_len, mig_dest, out_pool, tails, query_rows, dims):
    steps, heads, slots, insts, mig_per = dims
    width = tails[0].shape[1]
    smem = pl.BlockSpec(memory_space=pltpu.SMEM)
    vmem = pl.BlockSpec(memory_space=pltpu.VMEM)
    return pl.pallas_call(
        functools.partial(
            serve_kernel, steps=steps, heads=heads, slots=slots, insts=insts, mig_per=mig_per,
            query_rows=query_rows,
        ),
        out_shape=jax.ShapeDtypeStruct((mig_per * steps * heads, width), jnp.bfloat16),
        in_specs=[smem, smem, smem] + [vmem] * (1 + len(tails)),
        out_specs=vmem,
        compiler_params=params(24),
        cost_estimate=pl.CostEstimate(flops=200_000_000, bytes_accessed=MIB, transcendentals=0),
        name="serve",
    )(src_table, mig_len, mig_dest, out_pool, *tails)


def project_kernel(pos_ref, weight_ref, *refs, parts, added, turned):
    attention = refs[:parts]
    extra = refs[parts : parts + added]
    out_ref = refs[-1]
    begin = 0
    for part in attention:
        tokens = part.shape[0]
        result = jnp.dot(part[...], weight_ref[...], preferred_element_type=jnp.float32)
        if extra:
            result = result + extra[0][begin : begin + tokens, :].astype(jnp.float32)
        if turned:
            out_ref[:, begin : begin + tokens] = result.T.astype(out_ref.dtype)
        else:
            out_ref[begin : begin + tokens, :] = result.astype(out_ref.dtype)
        begin += tokens


def project(pos, which, out_weight, attention, extra, turned, columns, tile, dtype, name):
    depth = out_weight.shape[0]
    tokens = sum(part.shape[0] for part in attention)
    tiles = columns // tile
    out_spec = (
        pl.BlockSpec((tile, tokens), lambda j, pos: (j, 0))
        if turned
        else pl.BlockSpec((tokens, tile), lambda j, pos: (0, j))
    )
    out_shape = (columns, tokens) if turned else (tokens, columns)
    return pl.pallas_call(
        functools.partial(project_kernel, parts=len(attention), added=len(extra), turned=turned),
        grid_spec=pltpu.PrefetchScalarGridSpec(
            num_scalar_prefetch=1,
            grid=(tiles,),
            in_specs=[pl.BlockSpec((depth, tile), lambda j, pos: (0, pos[which] * tiles + j))]
            + [pl.BlockSpec(part.shape, lambda j, pos: (0, 0)) for part in attention]
            + [pl.BlockSpec((tokens, tile), lambda j, pos: (0, j)) for _ in extra],
            out_specs=out_spec,
        ),
        out_shape=jax.ShapeDtypeStruct(out_shape, dtype),
        compiler_params=params(32),
        cost_estimate=pl.CostEstimate(
            flops=2 * tokens * depth * columns, bytes_accessed=2 * depth * columns, transcendentals=0
        ),
        name=name,
    )(pos, out_weight, *attention, *extra)


def finish_kernel(part_ref, *refs):
    got, out_ref = refs[:-1], refs[-1]
    begin = 0
    sums = part_ref[...]
    count = len(got)
    for ref in got:
        sums = sums + ref[...].astype(jnp.float32)
    out_ref[...] = sums.astype(jnp.bfloat16)


def shards(
    res_pool,
    res_table,
    res_len,
    out_pool,
    src_table,
    mig_len,
    mig_dest,
    queries,
    new_kv,
    out_weight,
):
    batch, steps, heads, width = queries.shape
    slots = res_pool.shape[1]
    insts = lax.axis_size("inst")
    tps = lax.axis_size("tp")
    chips = tps // CORES
    mig_per = src_table.shape[1]
    dims = (steps, heads, slots, insts, mig_per)
    features = out_weight.shape[1] // tps

    tp = lax.axis_index("tp")
    chip, core = tp // CORES, lax.rem(tp, CORES)
    order = [lax.rem(chip + k, chips) * CORES for k in list(range(1, chips)) + [0]]
    pos = jnp.stack([base + core for base in order] + [base + 1 - core for base in order])

    query_rows = queries.reshape(batch * steps * heads, width)
    kv_rows = new_kv.reshape(batch * steps * slots, 2 * width)
    table = res_table[0].T

    from_inst = [
        [((i + k) % insts, i) for i in range(insts)] for k in range(1, insts)
    ]
    to_inst = [[(i, (i + k) % insts) for i in range(insts)] for k in range(1, insts)]
    to_mate = [(i, i + 1 - 2 * (i % CORES)) for i in range(tps)]

    tail_q = query_rows[-insts * steps * heads :]
    tail_kv = kv_rows[-insts * steps * slots :]
    tail = jnp.concatenate([tail_q, tail_kv[:, :width], tail_kv[:, width:]], axis=0)
    tails = [lax.ppermute(tail, "inst", perm) for perm in from_inst]

    counts = (batch // 4, batch // 4, batch // 2)
    starts = (0, batch // 4, batch // 2)

    def remote(attention):
        got = []
        for k in range(chips - 1):
            give = project(
                pos, chips + k, out_weight, [attention], [], False, features, min(features, 256),
                jnp.bfloat16, "give",
            )
            mate = lax.ppermute(give, "tp", to_mate)
            keep = project(
                pos, k, out_weight, [attention], [mate], True, features, min(features, 256),
                jnp.bfloat16, "keep",
            )
            shift = (k + 1) * CORES
            got.append(lax.ppermute(keep, "tp", [(i, (i + shift) % tps) for i in range(tps)]))
        return got

    attention = []
    received = []
    sends = None
    for index, (start, rows) in enumerate(zip(starts, counts)):
        last = index == len(counts) - 1
        back = []
        if last:
            served = serve(
                src_table, mig_len, mig_dest, out_pool, tails, insts * steps * heads, dims
            )
            back = [lax.ppermute(served, "inst", perm) for perm in from_inst]
        piece = attend(
            table, res_len, mig_dest, query_rows, kv_rows, res_pool, back, start, rows, dims
        )
        attention.append(piece)
        received.append(remote(piece))
        if index == 0:
            sends = pack(src_table, mig_dest, out_pool, insts)
            arriving = [
                lax.ppermute(sends[insts - 1 - k], "inst", from_inst[k - 1])
                for k in range(1, insts)
            ]

    give = project(
        pos, 2 * chips - 1, out_weight, attention, [], False, features, min(features, 512),
        jnp.bfloat16, "give_own",
    )
    mate = lax.ppermute(give, "tp", to_mate)
    own = project(
        pos, chips - 1, out_weight, attention, [mate], True, features, min(features, 512),
        jnp.float32, "keep_own",
    )
    arrived = assemble(mig_dest, mig_len, arriving, insts, mig_per)

    hidden = finish(own, received, [rows * steps for rows in counts])
    return (arrived, hidden)


def finish(own, received, counts):
    features, tokens = own.shape
    tile = min(features, 512)
    hidden = None
    begin = 0
    for got, count in zip(received, counts):
        block = begin // count
        spec = pl.BlockSpec((tile, count), lambda j, block=block: (j, block))
        pieces = pl.BlockSpec((tile, count), lambda j: (j, 0))
        operands = [own] + list(got)
        in_specs = [spec] + [pieces] * len(got)
        aliases = {}
        kernel = finish_kernel
        if hidden is not None:
            operands = [hidden] + operands
            in_specs = [pl.BlockSpec(memory_space=pl.ANY)] + in_specs
            aliases = {0: 0}
            kernel = lambda _, *refs: finish_kernel(*refs)
        hidden = pl.pallas_call(
            kernel,
            grid=(features // tile,),
            out_shape=jax.ShapeDtypeStruct((features, tokens), jnp.bfloat16),
            in_specs=in_specs,
            out_specs=spec,
            input_output_aliases=aliases,
            compiler_params=params(24),
            name="finish",
        )(*operands)
        begin += count
    return hidden


def solution(mesh):
    placed = (
        P(("groups", "inst"), "tp", None, None, None),
        P(("groups", "inst"), None, None),
        P(("groups", "inst"), None),
        P(("groups", "inst"), "tp", None, None, None),
        P(("groups", "inst"), None, None),
        P("groups"),
        P("groups"),
        P(("groups", "inst"), None, "tp", None),
        P(("groups", "inst"), None, "tp", None),
        P("tp", None),
    )
    return jax.shard_map(
        shards,
        mesh=mesh,
        in_specs=placed,
        out_specs=(P(("groups", "inst"), None, "tp", None, None), P("tp", ("groups", "inst"))),
        check_vma=False,
    )
```

time: 256 us -> 159 us (0.62)
  Pallas kernels: 0 us -> 105 us
  waiting for transfers between devices: 126 us -> 24.8 us
  matrix products: 55 us -> 0 us
  local copies, waits for them, and re-layouts: 38.4 us -> 9.45 us
  other arithmetic: 14.6 us -> 0.09 us
  between operations: 14.3 us -> 0.88 us
  starting transfers between devices: 6.45 us -> 18.2 us
    reduce_scatter x1 -> x0, waiting for transfers between devices: 126 us -> none  [shards(): lax.psum_scatter(projector(out_weight, attention), 'tp', scatter_dimensio...]
    pallas_call x0 -> x17, Pallas kernels: none -> 105 us  [the longest x8 62.6 us: project(): pl.pallas_call(functools.partial(project_kernel, parts=len(attention), ad...]
    dot_general x9 -> x0, matrix products: 55 us -> none  [the longest x1 27.4 us: projector(): lax.dot_general(out_weight, attention, (((0,), (1,)), ((), ())), preferre...]
    gather x4 -> x0, local copies, waits for them, and re-layouts: 30.3 us -> none  [the longest x2 26.2 us: shards(): context = res_pool[0][:, res_table[0]]]
    ppermute x0 -> x16, waiting for transfers between devices: none -> 24.8 us  [the longest x3 19.6 us: shards(): lax.ppermute(sends[insts - 1 - k], 'inst', from_inst[k - 1])]
    ppermute x0 -> x16, starting transfers between devices: none -> 18.2 us  [the longest x3 6.11 us: shards(): tails = [lax.ppermute(tail, 'inst', perm) for perm in from_inst]]
    all_to_all x1 -> x0, starting transfers between devices: 6.45 us -> none  [shards(): lax.all_to_all(outbox, 'inst', split_axis=0, concat_axis=0, tiled=True)]
    reduce_sum x6 -> x0, other arithmetic: 5.87 us -> none  [the longest x4 5.55 us: attend(): totals = jnp.sum(cached_weights, axis=-1) + jnp.sum(fresh_weights, axis=-1)]
  transfers between devices with their start and end apart: 2 -> 16, of which waited for: 1 -> 3; matrix products, arithmetic and copies ran while one was open for 25% -> 1% of each run, Pallas kernels for 0% -> 49%
where the time goes in v1:
time: 159 us; the launch traced here: 158 us
  Pallas kernels  105 us (66%)
  waiting for transfers between devices  24.8 us (16%)
  starting transfers between devices  18.2 us (11%)
  local copies, waits for them, and re-layouts  9.45 us (6%)
    pallas_call x8, Pallas kernels, project(): pl.pallas_call(functools.partial(project_kernel, parts=len(attention), ad...  62.6 us
    pallas_call x3, Pallas kernels, attend(): pl.pallas_call(kernel, grid=(rows // group,), out_shape=jax.ShapeDtypeStr...  32.8 us
    ppermute x3, waiting for transfers between devices, shards(): lax.ppermute(sends[insts - 1 - k], 'inst', from_inst[k - 1])  19.6 us
    unnamed x26, local copies, waits for them, and re-layouts  6.47 us
    ppermute x3, starting transfers between devices, shards(): tails = [lax.ppermute(tail, 'inst', perm) for perm in from_inst]  6.11 us
    ppermute x3, waiting for transfers between devices, shards(): tails = [lax.ppermute(tail, 'inst', perm) for perm in from_inst]  5.18 us
    pallas_call x3, Pallas kernels, finish(): pl.pallas_call(kernel, grid=(features // tile,), out_shape=jax.ShapeDtype...  4.82 us
    ppermute x3, starting transfers between devices, shards(): back = [lax.ppermute(served, 'inst', perm) for perm in from_inst]  4.17 us
  transfers between devices with their start and end apart: 16, of which 3 were waited for; matrix products, arithmetic and copies ran while one was open for 1% of the time, Pallas kernels for 49%

profile of v1, /device:TPU:0, one launch (start us, length us, event | category | flops | bytes accessed | tf_op | source)
XLA Modules:
  0.0 158.2 jit_solution(17404900200457456637)
XLA Ops:
  0.6 0.9 slice.20
  1.6 0.8 slice.18
  2.4 5.1 %collective-permute-start.3 = (bf16[320,128]{1,0:T(8,128)(2,1)S(1)}, bf16[320,128]{1,0:T(8,128)(2,1)S(1)}, u32[]{:S(2)}, u32[]{:S(2)}) collective-permute-start(bf16[320,128]{1,0:T(8,128)(2,1)S(1)} %pad_maximum_fusion), channel_id=1, source_target_pairs={{4,0},{8,4},{12,8},{0,12},{5,1},{9,5},{13,9},{1,13},{6,2},{10,6},{... | collective-permute-start | bytes 245768 | tf_op jit(solution)/shard_map/ppermute | solution.py:420
  7.5 1.0 collective-permute-start.5
  8.5 1.2 reshape.13.kv_ref
  10.4 4.7 %collective-permute-done.4.refs_1_ = bf16[320,128]{1,0:T(8,128)(2,1)S(1)} collective-permute-done((bf16[320,128]{1,0:T(8,128)(2,1)S(1)}, bf16[320,128]{1,0:T(8,128)(2,1)S(1)}, u32[]{:S(2)}, u32[]{:S(2)}) %collective-permute-start.4) | collective-permute-done | bytes 81952 | tf_op jit(solution)/shard_map/ppermute | solution.py:420
  15.0 1.2 copy-done.2
  18.3 1.4 serve.1
  19.7 2.2 %collective-permute-start.6 = (bf16[128,128]{1,0:T(8,128)(2,1)S(1)}, bf16[128,128]{1,0:T(8,128)(2,1)S(1)}, u32[]{:S(2)}, u32[]{:S(2)}) collective-permute-start(bf16[128,128]{1,0:T(8,128)(2,1)S(1)} %serve.1), channel_id=1, source_target_pairs={{4,0},{8,4},{12,8},{0,12},{5,1},{9,5},{13,9},{1,13},{6,2},{10,6},{... | collective-permute-start | bytes 98312 | tf_op jit(solution)/shard_map/ppermute | solution.py:451
  21.9 1.9 %collective-permute-start.8 = (bf16[128,128]{1,0:T(8,128)(2,1)S(1)}, bf16[128,128]{1,0:T(8,128)(2,1)S(1)}, u32[]{:S(2)}, u32[]{:S(2)}) collective-permute-start(bf16[128,128]{1,0:T(8,128)(2,1)S(1)} %serve.1), channel_id=1, source_target_pairs={{12,0},{0,4},{4,8},{8,12},{13,1},{1,5},{5,9},{9,13},{14,2},{2,6},{... | collective-permute-start | bytes 98312 | tf_op jit(solution)/shard_map/ppermute | solution.py:451
  23.9 1.2 copy-done.1
  27.1 8.2 %attend.3.refs_0_ = bf16[128,2048]{1,0:T(8,128)(2,1)S(1)} custom-call(s32[8,125]{1,0:T(8,128)S(1)} %bitcast.12, s32[1,125]{1,0:T(1,128)S(1)} %copy-done.8, s32[8]{0:T(128)S(1)} %copy-done.6, bf16[8192,128]{1,0:T(8,128)(2,1)S(1)} %bitcast.9, bf16[1024,256]{1,0:T(8,128)(2,1)S(1)} %reshape.13.kv_ref, bf16[1,2,64,16,256]{4,3,2,1,0:T(8,128)(2,1)S(1)} %copy-done.1), custom_call_target="tpu_custom_call" | custom-call | flops 288358400 | bytes 4194304 | tf_op jit(solution)/shard_map/attend/pallas_call | solution.py:252
  35.3 8.3 %attend.4.refs_1_.refs_0_ = bf16[128,2048]{1,0:T(8,128)(2,1)S(1)} custom-call(s32[8,125]{1,0:T(8,128)S(1)} %bitcast.13, s32[1,125]{1,0:T(1,128)S(1)} %copy-done.8, s32[8]{0:T(128)S(1)} %copy-done.6, bf16[8192,128]{1,0:T(8,128)(2,1)S(1)} %bitcast.10, bf16[1024,256]{1,0:T(8,128)(2,1)S(1)} %reshape.13.kv_ref, bf16[1,2,64,16,256]{4,3,2,1,0:T(8,128)(2,1)S(1)} %copy-done.1), custom_call_target="tpu_custom_call" | custom-call | flops 288358400 | bytes 4194304 | tf_op jit(solution)/shard_map/attend/pallas_call | solution.py:252
  43.7 16.2 %attend.5.refs_2_.refs_0_ = bf16[256,2048]{1,0:T(8,128)(2,1)S(1)} custom-call(s32[8,125]{1,0:T(8,128)S(1)} %bitcast.14, s32[1,125]{1,0:T(1,128)S(1)} %copy-done.8, s32[8]{0:T(128)S(1)} %copy-done.6, bf16[8192,128]{1,0:T(8,128)(2,1)S(1)} %bitcast.11, bf16[1024,256]{1,0:T(8,128)(2,1)S(1)} %reshape.13.kv_ref, bf16[1,2,64,16,256]{4,3,2,1,0:T(8,128)(2,1)S(1)} %copy-done.1, ...), custom_call_target="tpu_custom_call" | custom-call | flops 576716800 | bytes 4194304 | tf_op jit(solution)/shard_map/attend/pallas_call | solution.py:252
  59.9 7.9 %give_own.1 = bf16[512,2048]{1,0:T(8,128)(2,1)S(1)} custom-call(s32[4]{0:T(128)S(1)} %pad_add_fusion.pos_ref, bf16[2048,8192]{1,0:T(8,128)(2,1)} %weight_ref.15, bf16[128,2048]{1,0:T(8,128)(2,1)S(1)} %attend.3.refs_0_, bf16[128,2048]{1,0:T(8,128)(2,1)S(1)} %attend.4.refs_1_.refs_0_, bf16[256,2048]{1,0:T(8,128)(2,1)S(1)} %attend.5.refs_2_.refs_0_), custom_call_target="tpu_custom_call" | custom-call | flops 4294967296 | bytes 8388608 | tf_op jit(solution)/shard_map/give_own/pallas_call | solution.py:352
  67.9 8.0 %give.5 = bf16[256,2048]{1,0:T(8,128)(2,1)S(1)} custom-call(s32[4]{0:T(128)S(1)} %pad_add_fusion.pos_ref, bf16[2048,8192]{1,0:T(8,128)(2,1)} %weight_ref.15, bf16[256,2048]{1,0:T(8,128)(2,1)S(1)} %attend.5.refs_2_.refs_0_), custom_call_target="tpu_custom_call" | custom-call | flops 2147483648 | bytes 8388608 | tf_op jit(solution)/shard_map/give/pallas_call | solution.py:352
  76.5 7.4 %give.3 = bf16[128,2048]{1,0:T(8,128)(2,1)S(1)} custom-call(s32[4]{0:T(128)S(1)} %pad_add_fusion.pos_ref, bf16[2048,8192]{1,0:T(8,128)(2,1)} %weight_ref.15, bf16[128,2048]{1,0:T(8,128)(2,1)S(1)} %attend.3.refs_0_), custom_call_target="tpu_custom_call" | custom-call | flops 1073741824 | bytes 8388608 | tf_op jit(solution)/shard_map/give/pallas_call | solution.py:352
  84.0 7.4 %give.4 = bf16[128,2048]{1,0:T(8,128)(2,1)S(1)} custom-call(s32[4]{0:T(128)S(1)} %pad_add_fusion.pos_ref, bf16[2048,8192]{1,0:T(8,128)(2,1)} %weight_ref.15, bf16[128,2048]{1,0:T(8,128)(2,1)S(1)} %attend.4.refs_1_.refs_0_), custom_call_target="tpu_custom_call" | custom-call | flops 1073741824 | bytes 8388608 | tf_op jit(solution)/shard_map/give/pallas_call | solution.py:352
  91.9 0.9 pack.1
  92.8 1.9 %collective-permute-start = (bf16[2,32,16,256]{3,2,1,0:T(8,128)(2,1)S(1)}, bf16[2,32,16,256]{3,2,1,0:T(8,128)(2,1)S(1)}, u32[]{:S(2)}, u32[]{:S(2)}) collective-permute-start(bf16[2,32,16,256]{3,2,1,0:T(8,128)(2,1)S(1)} %get-tuple-element.5), channel_id=1, source_target_pairs={{4,0},{8,4},{12,8},{0,12},{5,1},{9,5},{13,9},{1,13},{6,2},{10,6},{... | collective-permute-start | bytes 1572872 | tf_op jit(solution)/shard_map/ppermute | solution.py:460
  94.7 1.1 collective-permute-start.1
  95.8 8.4 %keep.5 = bf16[2048,256]{1,0:T(8,128)(2,1)S(1)} custom-call(s32[4]{0:T(128)S(1)} %pad_add_fusion.pos_ref, bf16[2048,8192]{1,0:T(8,128)(2,1)} %weight_ref.15, bf16[256,2048]{1,0:T(8,128)(2,1)S(1)} %attend.5.refs_2_.refs_0_, bf16[256,2048]{1,0:T(8,128)(2,1)S(1)} %collective-permute-done.14.refs_1_), custom_call_target="tpu_custom_call" | custom-call | flops 2147483648 | bytes 8388608 | tf_op jit(solution)/shard_map/keep/pallas_call | solution.py:352
  104.2 1.6 %collective-permute-start.15 = (bf16[2048,256]{1,0:T(8,128)(2,1)S(1)}, bf16[2048,256]{1,0:T(8,128)(2,1)S(1)}, u32[]{:S(2)}, u32[]{:S(2)}) collective-permute-start(bf16[2048,256]{1,0:T(8,128)(2,1)S(1)} %keep.5), channel_id=1, source_target_pairs={{0,2},{1,3},{2,0},{3,1},{4,6},{5,7},{6,4},{7,5},{8,10},{9,11},{10,... | collective-permute-start | bytes 3145736 | tf_op jit(solution)/shard_map/ppermute | solution.py:438
  105.8 7.7 %keep.3 = bf16[2048,128]{1,0:T(8,128)(2,1)S(1)} custom-call(s32[4]{0:T(128)S(1)} %pad_add_fusion.pos_ref, bf16[2048,8192]{1,0:T(8,128)(2,1)} %weight_ref.15, bf16[128,2048]{1,0:T(8,128)(2,1)S(1)} %attend.3.refs_0_, bf16[128,2048]{1,0:T(8,128)(2,1)S(1)} %collective-permute-done.10.refs_1_), custom_call_target="tpu_custom_call" | custom-call | flops 1073741824 | bytes 8388608 | tf_op jit(solution)/shard_map/keep/pallas_call | solution.py:352
  113.5 7.7 %keep.4 = bf16[2048,128]{1,0:T(8,128)(2,1)S(1)} custom-call(s32[4]{0:T(128)S(1)} %pad_add_fusion.pos_ref, bf16[2048,8192]{1,0:T(8,128)(2,1)} %weight_ref.15, bf16[128,2048]{1,0:T(8,128)(2,1)S(1)} %attend.4.refs_1_.refs_0_, bf16[128,2048]{1,0:T(8,128)(2,1)S(1)} %collective-permute-done.12.refs_1_), custom_call_target="tpu_custom_call" | custom-call | flops 1073741824 | bytes 8388608 | tf_op jit(solution)/shard_map/keep/pallas_call | solution.py:352
  121.7 19.6 %collective-permute-done.1.refs_1_ = bf16[2,32,16,256]{3,2,1,0:T(8,128)(2,1)S(1)} collective-permute-done((bf16[2,32,16,256]{3,2,1,0:T(8,128)(2,1)S(1)}, bf16[2,32,16,256]{3,2,1,0:T(8,128)(2,1)S(1)}, u32[]{:S(2)}, u32[]{:S(2)}) %collective-permute-start.1) | collective-permute-done | bytes 524320 | tf_op jit(solution)/shard_map/ppermute | solution.py:460
  141.3 1.5 collective-permute-start.13
  142.8 2.2 %assemble.1 = bf16[1,3,2,512,256]{4,3,2,1,0:T(8,128)(2,1)} custom-call(s32[8]{0:T(128)S(1)} %copy-done.7, s32[8]{0:T(128)S(1)} %copy-done.12, bf16[2,32,16,256]{3,2,1,0:T(8,128)(2,1)S(1)} %collective-permute-done.refs_0_, bf16[2,32,16,256]{3,2,1,0:T(8,128)(2,1)S(1)} %collective-permute-done.1.refs_1_, bf16[2,32,16,256]{3,2,1,0:T(8,128)(2,1)S(1)} %collective-permute-done.2.refs_2_), custom_call_target="tpu_custom_call" | custom-call | tf_op jit(solution)/shard_map/assemble/pallas_call | solution.py:118
  145.1 8.3 %keep_own.1.part_ref.refs_0_ = f32[2048,512]{1,0:T(8,128)S(1)} custom-call(s32[4]{0:T(128)S(1)} %pad_add_fusion.pos_ref, bf16[2048,8192]{1,0:T(8,128)(2,1)} %weight_ref.15, bf16[128,2048]{1,0:T(8,128)(2,1)S(1)} %attend.3.refs_0_, bf16[128,2048]{1,0:T(8,128)(2,1)S(1)} %attend.4.refs_1_.refs_0_, bf16[256,2048]{1,0:T(8,128)(2,1)S(1)} %attend.5.refs_2_.refs_0_, ...), custom_call_target="tpu_custom_call" | custom-call | flops 4294967296 | bytes 8388608 | tf_op jit(solution)/shard_map/keep_own/pallas_call | solution.py:352
  153.4 1.6 finish.3._
  154.9 1.5 finish.4._
  156.5 1.7 %finish.5 = bf16[2048,512]{1,0:T(8,128)(2,1)} custom-call(bf16[2048,512]{1,0:T(8,128)(2,1)} %finish.4._, f32[2048,512]{1,0:T(8,128)S(1)} %keep_own.1.part_ref.refs_0_, bf16[2048,256]{1,0:T(8,128)(2,1)S(1)} %collective-permute-done.15.refs_1_), custom_call_target="tpu_custom_call", output_to_operand_aliasing={{}: (0, {})} | custom-call | tf_op jit(solution)/shard_map/finish/pallas_call | solution.py:497
  (50 shorter events, 6.6 us)
Async XLA Ops:
  0.6 23.2 %copy-start = (bf16[128,4,16,128]{3,2,1,0:T(8,128)(2,1)S(1)}, bf16[128,4,16,128]{3,2,1,0:T(8,128)(2,1)}, u32[]{:S(2)}) copy-start(bf16[128,4,16,128]{3,2,1,0:T(8,128)(2,1)} %param.17) | copy-start | bytes 6291460
  2.4 8.0 %collective-permute-start.3 = (bf16[320,128]{1,0:T(8,128)(2,1)S(1)}, bf16[320,128]{1,0:T(8,128)(2,1)S(1)}, u32[]{:S(2)}, u32[]{:S(2)}) collective-permute-start(bf16[320,128]{1,0:T(8,128)(2,1)S(1)} %pad_maximum_fusion), channel_id=1, source_target_pairs={{4,0},{8,4},{12,8},{0,12},{5,1},{9,5},{13,9},{1,13},{6,2},{10,6},{... | collective-permute-start | bytes 245768 | tf_op jit(solution)/shard_map/ppermute | solution.py:420
  7.5 7.5 %collective-permute-start.4 = (bf16[320,128]{1,0:T(8,128)(2,1)S(1)}, bf16[320,128]{1,0:T(8,128)(2,1)S(1)}, u32[]{:S(2)}, u32[]{:S(2)}) collective-permute-start(bf16[320,128]{1,0:T(8,128)(2,1)S(1)} %pad_maximum_fusion), channel_id=1, source_target_pairs={{8,0},{12,4},{0,8},{4,12},{9,1},{13,5},{1,9},{5,13},{10,2},{14,6},... | collective-permute-start | bytes 245768 | tf_op jit(solution)/shard_map/ppermute | solution.py:420
  7.5 7.5 %collective-permute-start.5 = (bf16[320,128]{1,0:T(8,128)(2,1)S(1)}, bf16[320,128]{1,0:T(8,128)(2,1)S(1)}, u32[]{:S(2)}, u32[]{:S(2)}) collective-permute-start(bf16[320,128]{1,0:T(8,128)(2,1)S(1)} %pad_maximum_fusion), channel_id=1, source_target_pairs={{12,0},{0,4},{4,8},{8,12},{13,1},{1,5},{5,9},{9,13},{14,2},{2,6},{... | collective-permute-start | bytes 245768 | tf_op jit(solution)/shard_map/ppermute | solution.py:420
  15.0 1.2 copy-start.2
  16.3 0.7 copy-start.5
  16.9 0.7 copy-start.9
  17.6 0.7 copy-start.11
  19.7 23.9 %collective-permute-start.6 = (bf16[128,128]{1,0:T(8,128)(2,1)S(1)}, bf16[128,128]{1,0:T(8,128)(2,1)S(1)}, u32[]{:S(2)}, u32[]{:S(2)}) collective-permute-start(bf16[128,128]{1,0:T(8,128)(2,1)S(1)} %serve.1), channel_id=1, source_target_pairs={{4,0},{8,4},{12,8},{0,12},{5,1},{9,5},{13,9},{1,13},{6,2},{10,6},{... | collective-permute-start | bytes 98312 | tf_op jit(solution)/shard_map/ppermute | solution.py:451
  21.9 21.8 %collective-permute-start.7 = (bf16[128,128]{1,0:T(8,128)(2,1)S(1)}, bf16[128,128]{1,0:T(8,128)(2,1)S(1)}, u32[]{:S(2)}, u32[]{:S(2)}) collective-permute-start(bf16[128,128]{1,0:T(8,128)(2,1)S(1)} %serve.1), channel_id=1, source_target_pairs={{8,0},{12,4},{0,8},{4,12},{9,1},{13,5},{1,9},{5,13},{10,2},{14,6},... | collective-permute-start | bytes 98312 | tf_op jit(solution)/shard_map/ppermute | solution.py:451
  21.9 21.7 %collective-permute-start.8 = (bf16[128,128]{1,0:T(8,128)(2,1)S(1)}, bf16[128,128]{1,0:T(8,128)(2,1)S(1)}, u32[]{:S(2)}, u32[]{:S(2)}) collective-permute-start(bf16[128,128]{1,0:T(8,128)(2,1)S(1)} %serve.1), channel_id=1, source_target_pairs={{12,0},{0,4},{4,8},{8,12},{13,1},{1,5},{5,9},{9,13},{14,2},{2,6},{... | collective-permute-start | bytes 98312 | tf_op jit(solution)/shard_map/ppermute | solution.py:451
  23.9 1.2 copy-start.1
  25.1 0.7 copy-start.4
  25.8 0.7 copy-start.6
  26.4 0.7 copy-start.8
  67.8 77.3 %collective-permute-start.9 = (bf16[512,2048]{1,0:T(8,128)(2,1)S(1)}, bf16[512,2048]{1,0:T(8,128)(2,1)S(1)}, u32[]{:S(2)}, u32[]{:S(2)}) collective-permute-start(bf16[512,2048]{1,0:T(8,128)(2,1)S(1)} %give_own.1), channel_id=1, source_target_pairs={{0,1},{1,0},{2,3},{3,2},{4,5},{5,4},{6,7},{7,6},{8,9},{9,8},{10,11... | collective-permute-start | bytes 6291464 | tf_op jit(solution)/shard_map/ppermute | solution.py:468
  75.9 18.8 %collective-permute-start.14 = (bf16[256,2048]{1,0:T(8,128)(2,1)S(1)}, bf16[256,2048]{1,0:T(8,128)(2,1)S(1)}, u32[]{:S(2)}, u32[]{:S(2)}) collective-permute-start(bf16[256,2048]{1,0:T(8,128)(2,1)S(1)} %give.5), channel_id=1, source_target_pairs={{0,1},{1,0},{2,3},{3,2},{4,5},{5,4},{6,7},{7,6},{8,9},{9,8},{10,11... | collective-permute-start | bytes 3145736 | tf_op jit(solution)/shard_map/ppermute | solution.py:432
  83.8 8.0 %copy-start.3 = (bf16[1,2,64,16,256]{4,3,2,1,0:T(8,128)(2,1)S(1)}, bf16[1,2,64,16,256]{4,3,2,1,0:T(8,128)(2,1)}, u32[]{:S(2)}) copy-start(bf16[1,2,64,16,256]{4,3,2,1,0:T(8,128)(2,1)} %pool_ref.8) | copy-start | bytes 3145732
  83.9 8.0 %copy-start.7 = (s32[8]{0:T(128)S(1)}, s32[8]{0:T(128)}, u32[]{:S(2)}) copy-start(s32[8]{0:T(128)} %dest_ref.11) | copy-start | bytes 100
  83.9 8.0 %copy-start.10 = (s32[1,2,32]{2,1,0:T(2,128)S(1)}, s32[1,2,32]{2,1,0:T(2,128)}, u32[]{:S(2)}) copy-start(s32[1,2,32]{2,1,0:T(2,128)} %table_ref.3) | copy-start | bytes 772
  83.9 20.3 %collective-permute-start.10 = (bf16[128,2048]{1,0:T(8,128)(2,1)S(1)}, bf16[128,2048]{1,0:T(8,128)(2,1)S(1)}, u32[]{:S(2)}, u32[]{:S(2)}) collective-permute-start(bf16[128,2048]{1,0:T(8,128)(2,1)S(1)} %give.3), channel_id=1, source_target_pairs={{0,1},{1,0},{2,3},{3,2},{4,5},{5,4},{6,7},{7,6},{8,9},{9,8},{10,11... | collective-permute-start | bytes 1572872 | tf_op jit(solution)/shard_map/ppermute | solution.py:432
  91.3 14.4 %collective-permute-start.12 = (bf16[128,2048]{1,0:T(8,128)(2,1)S(1)}, bf16[128,2048]{1,0:T(8,128)(2,1)S(1)}, u32[]{:S(2)}, u32[]{:S(2)}) collective-permute-start(bf16[128,2048]{1,0:T(8,128)(2,1)S(1)} %give.4), channel_id=1, source_target_pairs={{0,1},{1,0},{2,3},{3,2},{4,5},{5,4},{6,7},{7,6},{8,9},{9,8},{10,11... | collective-permute-start | bytes 1572872 | tf_op jit(solution)/shard_map/ppermute | solution.py:432
  92.8 28.4 %collective-permute-start = (bf16[2,32,16,256]{3,2,1,0:T(8,128)(2,1)S(1)}, bf16[2,32,16,256]{3,2,1,0:T(8,128)(2,1)S(1)}, u32[]{:S(2)}, u32[]{:S(2)}) collective-permute-start(bf16[2,32,16,256]{3,2,1,0:T(8,128)(2,1)S(1)} %get-tuple-element.5), channel_id=1, source_target_pairs={{4,0},{8,4},{12,8},{0,12},{5,1},{9,5},{13,9},{1,13},{6,2},{10,6},{... | collective-permute-start | bytes 1572872 | tf_op jit(solution)/shard_map/ppermute | solution.py:460
  94.7 46.6 %collective-permute-start.1 = (bf16[2,32,16,256]{3,2,1,0:T(8,128)(2,1)S(1)}, bf16[2,32,16,256]{3,2,1,0:T(8,128)(2,1)S(1)}, u32[]{:S(2)}, u32[]{:S(2)}) collective-permute-start(bf16[2,32,16,256]{3,2,1,0:T(8,128)(2,1)S(1)} %get-tuple-element.6), channel_id=1, source_target_pairs={{8,0},{12,4},{0,8},{4,12},{9,1},{13,5},{1,9},{5,13},{10,2},{14,6},... | collective-permute-start | bytes 1572872 | tf_op jit(solution)/shard_map/ppermute | solution.py:460
  104.2 52.3 %collective-permute-start.15 = (bf16[2048,256]{1,0:T(8,128)(2,1)S(1)}, bf16[2048,256]{1,0:T(8,128)(2,1)S(1)}, u32[]{:S(2)}, u32[]{:S(2)}) collective-permute-start(bf16[2048,256]{1,0:T(8,128)(2,1)S(1)} %keep.5), channel_id=1, source_target_pairs={{0,2},{1,3},{2,0},{3,1},{4,6},{5,7},{6,4},{7,5},{8,10},{9,11},{10,... | collective-permute-start | bytes 3145736 | tf_op jit(solution)/shard_map/ppermute | solution.py:438
  105.8 37.1 %collective-permute-start.2 = (bf16[2,32,16,256]{3,2,1,0:T(8,128)(2,1)S(1)}, bf16[2,32,16,256]{3,2,1,0:T(8,128)(2,1)S(1)}, u32[]{:S(2)}, u32[]{:S(2)}) collective-permute-start(bf16[2,32,16,256]{3,2,1,0:T(8,128)(2,1)S(1)} %get-tuple-element.7), channel_id=1, source_target_pairs={{12,0},{0,4},{4,8},{8,12},{13,1},{1,5},{5,9},{9,13},{14,2},{2,6},{... | collective-permute-start | bytes 1572872 | tf_op jit(solution)/shard_map/ppermute | solution.py:460
  113.4 29.4 %copy-start.12 = (s32[8]{0:T(128)S(1)}, s32[8]{0:T(128)}, u32[]{:S(2)}) copy-start(s32[8]{0:T(128)} %len_ref.8) | copy-start | bytes 100
  121.1 32.2 %collective-permute-start.11 = (bf16[2048,128]{1,0:T(8,128)(2,1)S(1)}, bf16[2048,128]{1,0:T(8,128)(2,1)S(1)}, u32[]{:S(2)}, u32[]{:S(2)}) collective-permute-start(bf16[2048,128]{1,0:T(8,128)(2,1)S(1)} %keep.3), channel_id=1, source_target_pairs={{0,2},{1,3},{2,0},{3,1},{4,6},{5,7},{6,4},{7,5},{8,10},{9,11},{10,... | collective-permute-start | bytes 1572872 | tf_op jit(solution)/shard_map/ppermute | solution.py:438
  141.3 13.6 %collective-permute-start.13 = (bf16[2048,128]{1,0:T(8,128)(2,1)S(1)}, bf16[2048,128]{1,0:T(8,128)(2,1)S(1)}, u32[]{:S(2)}, u32[]{:S(2)}) collective-permute-start(bf16[2048,128]{1,0:T(8,128)(2,1)S(1)} %keep.4), channel_id=1, source_target_pairs={{0,2},{1,3},{2,0},{3,1},{4,6},{5,7},{6,4},{7,5},{8,10},{9,11},{10,... | collective-permute-start | bytes 1572872 | tf_op jit(solution)/shard_map/ppermute | solution.py:438

commit v2 on v1

v2 whole, which is shorter than its diff:
```python
import functools
import math

import jax
import jax.numpy as jnp
from jax import lax
from jax.experimental import pallas as pl
from jax.experimental.pallas import tpu as pltpu
from jax.sharding import PartitionSpec as P

CORES = 2
LOW = -1e30
MIB = 1 << 20
LANES = 128


def dot_t(left, right):
    return lax.dot_general(
        left, right, (((1,), (1,)), ((), ())), preferred_element_type=jnp.float32
    )


def row_plan(dest_ref, inst, cap):
    requests = [jnp.int32(-1)] * cap
    seen = jnp.int32(0)
    for g in range(dest_ref.shape[0]):
        here = dest_ref[g] == inst
        requests = [jnp.where(here & (seen == a), g, requests[a]) for a in range(cap)]
        seen = seen + here.astype(jnp.int32)
    return requests


def standing_of(dest_ref, request):
    dest = dest_ref[request]
    count = jnp.int32(0)
    for g in range(dest_ref.shape[0]):
        count = count + ((dest_ref[g] == dest) & (g < request)).astype(jnp.int32)
    return dest, count


SMEM = pl.BlockSpec(memory_space=pltpu.SMEM)
VMEM = pl.BlockSpec(memory_space=pltpu.VMEM)
ANY = pl.BlockSpec(memory_space=pl.ANY)


def run(kernel, operands, in_specs, deps, out_shape, out_specs, name, limit=56, grid=(),
        scratch=(), prefetch=0, aliases=None, flops=0):
    inputs = len(operands)
    count = len(deps)

    def call(*refs):
        return kernel(*refs[:inputs], *refs[inputs + count :])

    return pl.pallas_call(
        call,
        grid_spec=pltpu.PrefetchScalarGridSpec(
            num_scalar_prefetch=prefetch,
            grid=grid,
            in_specs=list(in_specs) + [ANY] * count,
            out_specs=out_specs,
            scratch_shapes=list(scratch),
        ),
        out_shape=out_shape,
        input_output_aliases=aliases or {},
        compiler_params=pltpu.CompilerParams(vmem_limit_bytes=limit * MIB),
        cost_estimate=pl.CostEstimate(flops=flops, bytes_accessed=1024, transcendentals=0),
        name=name,
    )(*operands, *deps)


def pack_kernel(
    table_ref, dest_ref, pool_ref, query_ref, kv_ref, send_ref, tail_ref, *, mig_per, rows, steps
):
    inst = lax.axis_index("inst")
    insts, slots, blocks = send_ref.shape[:3]
    width = query_ref.shape[1]
    tail_q = query_ref[...]
    tail_kv = kv_ref[...]
    queries, keys = tail_q.shape[0], tail_kv.shape[0]
    for i in range(insts):
        tail_ref[i, :queries, :] = tail_q
        tail_ref[i, queries : queries + keys, :] = tail_kv[:, :width]
        tail_ref[i, queries + keys :, :] = tail_kv[:, width:]
    for m in range(mig_per):
        dest = dest_ref[inst * mig_per + m]

        def copy_block(b, carry, m=m, dest=dest):
            block = table_ref[0, m, b]
            for s in range(slots):
                send_ref[dest, s, b] = pool_ref[0, s, block]
            return carry

        lax.fori_loop(0, blocks, copy_block, 0, unroll=8)


def pack(src_table, mig_dest, out_pool, query_rows, kv_rows, dims, deps):
    steps, heads, slots, insts, mig_per = dims
    _, _, _, block, width = out_pool.shape
    blocks = src_table.shape[2]
    tail_q, tail_kv = insts * steps * heads, insts * steps * slots
    shapes = (
        jax.ShapeDtypeStruct((insts, slots, blocks, block, width), out_pool.dtype),
        jax.ShapeDtypeStruct((insts, tail_q + 2 * tail_kv, width // 2), out_pool.dtype),
    )
    last_q = query_rows.shape[0] // tail_q - 1
    last_kv = kv_rows.shape[0] // tail_kv - 1
    return run(
        functools.partial(pack_kernel, mig_per=mig_per, rows=insts, steps=steps),
        [src_table, mig_dest, out_pool, query_rows, kv_rows],
        [
            SMEM, SMEM, pl.BlockSpec(out_pool.shape, lambda i: (0, 0, 0, 0, 0)),
            pl.BlockSpec((tail_q, width // 2), lambda i: (last_q, 0)),
            pl.BlockSpec((tail_kv, width), lambda i: (last_kv, 0)),
        ],
        deps,
        shapes,
        [
            pl.BlockSpec(shapes[0].shape, lambda i: (0, 0, 0, 0, 0)),
            pl.BlockSpec(shapes[1].shape, lambda i: (0, 0, 0)),
        ],
        "pack",
        grid=(1,),
    )


def arrived_kernel(dest_ref, len_ref, got_ref, out_ref, *, mig_per, cap):
    inst = lax.axis_index("inst")
    insts, slots, blocks, block, width = got_ref.shape
    requests = row_plan(dest_ref, inst, cap)
    place = lax.broadcasted_iota(jnp.int32, (block, width), 0)
    for a in range(cap):
        request = requests[a]
        known = jnp.maximum(request, 0)
        length = jnp.where(request >= 0, len_ref[known], 0)
        source = known // mig_per

        def one(b, carry, a=a, source=source, length=length):
            inside = place + b * block < length
            at = pl.ds(pl.multiple_of(b * block, block), block)
            for s in range(slots):
                value = got_ref[source, s, b].astype(jnp.float32)
                out_ref[0, a, s, at, :] = jnp.where(inside, value, 0.0).astype(jnp.bfloat16)
            return carry

        lax.fori_loop(0, blocks, one, 0, unroll=4)


def assemble(mig_dest, mig_len, got, mig_per, deps):
    insts, slots, blocks, block, width = got.shape
    cap = insts - 1
    return run(
        functools.partial(arrived_kernel, mig_per=mig_per, cap=cap),
        [mig_dest, mig_len, got],
        [SMEM, SMEM, VMEM],
        deps,
        jax.ShapeDtypeStruct((1, cap, slots, blocks * block, width), jnp.bfloat16),
        VMEM,
        "assemble",
    )


def fresh_code(rows, keys, steps, heads, slots):
    index = lax.broadcasted_iota(jnp.int32, (rows, keys), 0)
    key = lax.broadcasted_iota(jnp.int32, (rows, keys), 1)
    step = index // heads
    slot = lax.rem(index, heads) // (heads // slots)
    per_row = steps * slots
    in_row = lax.rem(key, per_row)
    seen = (in_row // slots <= step) & (lax.rem(in_row, slots) == slot)
    return jnp.where(seen, key // per_row, -1)


def own_scores(scores, slot_of, slots):
    extent = scores.shape[1] // slots
    own = scores[:, :extent]
    for s in range(1, slots):
        own = jnp.where(slot_of == s, scores[:, s * extent : (s + 1) * extent], own)
    return own


def weigh(own, length, fresh, fresh_seen, scale):
    place = lax.broadcasted_iota(jnp.int32, own.shape, 1)
    own = jnp.where(place < length, own, LOW)
    fresh = jnp.where(fresh_seen, fresh, LOW)
    same = own.shape == fresh.shape
    if same:
        largest = jnp.max(jnp.maximum(own, fresh), axis=1, keepdims=True)
    else:
        largest = jnp.maximum(
            jnp.max(own, axis=1, keepdims=True), jnp.max(fresh, axis=1, keepdims=True)
        )
    own = jnp.exp2((own - largest) * scale)
    fresh = jnp.exp2((fresh - largest) * scale)
    if same:
        total = jnp.sum(own + fresh, axis=1, keepdims=True)
    else:
        total = jnp.sum(own, axis=1, keepdims=True) + jnp.sum(fresh, axis=1, keepdims=True)
    return own, fresh, total


def spread(own, slot_of, slots):
    if slots == 1:
        return own.astype(jnp.bfloat16)
    parts = [jnp.where(slot_of == s, own, 0.0) for s in range(slots)]
    return jnp.concatenate(parts, axis=1).astype(jnp.bfloat16)


def gather_blocks(pool_ref, slots, ids):
    tiles = [pool_ref[0, s, block] for s in range(slots) for block in ids]
    return jnp.concatenate(tiles, axis=0)


def slot_index(rows, extent, heads, slots):
    index = lax.broadcasted_iota(jnp.int32, (rows, extent), 0)
    return lax.rem(index, heads) // (heads // slots)


def attend_kernel(
    table_ref, len_ref, dest_ref, query_ref, kv_ref, pool_ref, *refs,
    first_row, steps, heads, slots, insts, mig_per, with_back,
):
    back_ref = refs[0] if with_back else None
    out_ref, fresh_ref, pf_ref, blend_ref, inv_ref = refs[with_back:]
    width = query_ref.shape[1]
    per = steps * heads
    rows = query_ref.shape[0] // per
    resident = len_ref.shape[1]
    blocks = table_ref.shape[0]
    extent = blocks * pool_ref.shape[3]
    start = first_row + pl.program_id(0) * rows
    scale = math.log2(math.e) / math.sqrt(width)

    fresh_ref[...] = dot_t(query_ref[...], kv_ref[:, :width])
    code = fresh_code(per, kv_ref.shape[0], steps, heads, slots)
    slot_of = slot_index(per, extent, heads, slots)
    together = min(4, rows)
    for begin in range(0, rows, together):
        group = range(begin, begin + together)
        at = [slice(r * per, (r + 1) * per) for r in group]
        known = [jnp.minimum(start + r, resident - 1) for r in group]
        length = [
            jnp.where(start + r < resident, len_ref[0, k], 0) for r, k in zip(group, known)
        ]
        both = [
            gather_blocks(pool_ref, slots, [table_ref[j, k] for j in range(blocks)]) for k in known
        ]
        fresh = [fresh_ref[a, :] for a in at]
        scores = [dot_t(query_ref[a, :], b[:, :width]) for a, b in zip(at, both)]
        weights = [
            weigh(own_scores(s, slot_of, slots), n, f, code == r, scale)
            for s, n, f, r in zip(scores, length, fresh, group)
        ]
        context = [
            jnp.dot(spread(w[0], slot_of, slots), b[:, width:], preferred_element_type=jnp.float32)
            for w, b in zip(weights, both)
        ]
        for a, c, w in zip(at, context, weights):
            blend_ref[a, :] = c
            pf_ref[a, :] = w[1].astype(jnp.bfloat16)
            inv_ref[a, :] = jnp.broadcast_to(1.0 / w[2], (per, width))

    done = blend_ref[...] + jnp.dot(
        pf_ref[...], kv_ref[:, width:], preferred_element_type=jnp.float32
    )
    blend_ref[...] = done * inv_ref[...]

    if with_back:
        cap = insts - 1
        inst = lax.axis_index("inst")
        requests = row_plan(dest_ref, inst, cap)

        @pl.when(pl.program_id(0) == pl.num_programs(0) - 1)
        def _():
            for a in range(cap):
                request = requests[a]
                known = jnp.maximum(request, 0)
                begin = pl.multiple_of(lax.rem(known, mig_per) * per, per)
                served = back_ref[known // mig_per, pl.ds(begin, per), :].astype(jnp.float32)
                at = slice((rows - cap + a) * per, (rows - cap + a + 1) * per)
                blend_ref[at, :] = jnp.where(request >= 0, served, blend_ref[at, :])

    for h in range(heads):
        column = blend_ref[pl.ds(h, rows * steps, stride=heads), :]
        out_ref[:, h * width : (h + 1) * width] = column.astype(jnp.bfloat16)


def attend(table, lengths, dest, queries, new_kv, pool, back, first_row, rows, dims, deps):
    steps, heads, slots, insts, mig_per = dims
    width = queries.shape[1]
    per = steps * heads
    per_kv = steps * slots
    group = min(rows, LANES // per_kv)
    first = first_row // group
    kernel = functools.partial(
        attend_kernel, first_row=first_row, steps=steps, heads=heads, slots=slots,
        insts=insts, mig_per=mig_per, with_back=len(back),
    )
    return run(
        kernel,
        [table, lengths, dest, queries, new_kv, pool] + back,
        [
            SMEM, SMEM, SMEM,
            pl.BlockSpec((group * per, width), lambda i: (first + i, 0)),
            pl.BlockSpec((group * per_kv, 2 * width), lambda i: (first + i, 0)),
            VMEM,
        ] + [VMEM] * len(back),
        deps,
        jax.ShapeDtypeStruct((rows * steps, heads * width), jnp.bfloat16),
        pl.BlockSpec((group * steps, heads * width), lambda i: (i, 0)),
        "attend",
        grid=(rows // group,),
        scratch=[
            pltpu.VMEM((group * per, group * per_kv), jnp.float32),
            pltpu.VMEM((group * per, group * per_kv), jnp.bfloat16),
            pltpu.VMEM((group * per, width), jnp.float32),
            pltpu.VMEM((group * per, width), jnp.float32),
        ],
    )


def serve_kernel(
    table_ref, len_ref, dest_ref, pool_ref, tail_ref, out_ref, *, steps, heads, slots, insts, mig_per
):
    inst = lax.axis_index("inst")
    per = steps * heads
    width = out_ref.shape[2]
    blocks = table_ref.shape[2]
    extent = blocks * pool_ref.shape[3]
    queries = insts * per
    keys = insts * steps * slots
    code = fresh_code(per, keys, steps, heads, slots)
    slot_of = slot_index(per, extent, heads, slots)
    scale = math.log2(math.e) / math.sqrt(width)
    for m in range(mig_per):
        request = inst * mig_per + m
        dest, place = standing_of(dest_ref, request)
        begin = pl.multiple_of((place + 1) * per, per)
        query = tail_ref[dest, pl.ds(begin, per), :]
        new_keys = tail_ref[dest, queries : queries + keys, :]
        new_values = tail_ref[dest, queries + keys :, :]
        both = gather_blocks(pool_ref, slots, [table_ref[0, m, b] for b in range(blocks)])
        scores = dot_t(query, both[:, :width])
        own, fresh, total = weigh(
            own_scores(scores, slot_of, slots), len_ref[request],
            dot_t(query, new_keys), code == place + 1, scale,
        )
        context = jnp.dot(
            spread(own, slot_of, slots), both[:, width:], preferred_element_type=jnp.float32
        )
        context = context + jnp.dot(
            fresh.astype(jnp.bfloat16), new_values, preferred_element_type=jnp.float32
        )
        result = (context / total).astype(jnp.bfloat16)
        for i in range(insts):
            out_ref[i, m * per : (m + 1) * per, :] = result


def serve(src_table, mig_len, mig_dest, out_pool, tails, dims, deps):
    steps, heads, slots, insts, mig_per = dims
    return run(
        functools.partial(
            serve_kernel, steps=steps, heads=heads, slots=slots, insts=insts, mig_per=mig_per
        ),
        [src_table, mig_len, mig_dest, out_pool, tails],
        [SMEM, SMEM, SMEM, VMEM, VMEM],
        deps,
        jax.ShapeDtypeStruct((insts, mig_per * steps * heads, tails.shape[2]), jnp.bfloat16),
        VMEM,
        "serve",
    )


def project_kernel(pos_ref, *refs, cuts, parts, added, turned):
    weights = refs[:cuts]
    attention = refs[cuts : cuts + parts]
    extra = refs[cuts + parts : cuts + parts + added]
    out_ref = refs[-1]
    depth = weights[0].shape[0]
    begin = 0
    for part in attention:
        tokens = part.shape[0]
        result = None
        for c in range(cuts):
            term = jnp.dot(
                part[:, c * depth : (c + 1) * depth], weights[c][...],
                preferred_element_type=jnp.float32,
            )
            result = term if result is None else result + term
        if extra:
            result = result + extra[0][begin : begin + tokens, :].astype(jnp.float32)
        if turned:
            out_ref[:, begin : begin + tokens] = result.T.astype(out_ref.dtype)
        else:
            out_ref[begin : begin + tokens, :] = result.astype(out_ref.dtype)
        begin += tokens


def project(pos, which, begin, columns, out_weight, attention, extra, turned, features, tile, dtype,
            name, deps):
    cuts = 4
    depth = out_weight.shape[0] // cuts
    tokens = sum(part.shape[0] for part in attention)
    per_device = features // tile
    first = begin // tile
    out_spec = (
        pl.BlockSpec((tile, tokens), lambda j, pos: (j, 0))
        if turned
        else pl.BlockSpec((tokens, tile), lambda j, pos: (0, j))
    )
    return run(
        functools.partial(
            project_kernel, cuts=cuts, parts=len(attention), added=len(extra), turned=turned
        ),
        [pos] + [out_weight] * cuts + attention + extra,
        [
            pl.BlockSpec((depth, tile), lambda j, pos, c=c: (c, pos[which] * per_device + first + j))
            for c in range(cuts)
        ]
        + [pl.BlockSpec(part.shape, lambda j, pos: (0, 0)) for part in attention]
        + [pl.BlockSpec((tokens, tile), lambda j, pos: (0, j)) for _ in extra],
        deps,
        jax.ShapeDtypeStruct((columns, tokens) if turned else (tokens, columns), dtype),
        out_spec,
        name,
        grid=(columns // tile,),
        prefetch=1,
    )


def finish_kernel(part_ref, *refs):
    got, out_ref = refs[:-1], refs[-1]
    sums = part_ref[...]
    for ref in got:
        sums = sums + ref[...].astype(jnp.float32)
    out_ref[...] = sums.astype(jnp.bfloat16)


def finish(hidden, own, got, row, column, deps):
    height, count = got[0].shape
    tile = min(height, 512)
    first = row // tile
    block = column // count
    spec = pl.BlockSpec((tile, count), lambda j: (first + j, block))
    operands = [own] + got
    in_specs = [spec] + [pl.BlockSpec((tile, count), lambda j: (j, 0))] * len(got)
    kernel = finish_kernel
    aliases = None
    if hidden is not None:
        aliases = {len(operands): 0}
        deps = [hidden] + deps
    return run(
        kernel, operands, in_specs, deps,
        jax.ShapeDtypeStruct(own.shape, jnp.bfloat16), spec, "finish",
        grid=(height // tile,), aliases=aliases,
    )


def shards(
    res_pool,
    res_table,
    res_len,
    out_pool,
    src_table,
    mig_len,
    mig_dest,
    queries,
    new_kv,
    out_weight,
):
    batch, steps, heads, width = queries.shape
    slots = res_pool.shape[1]
    insts = lax.axis_size("inst")
    tps = lax.axis_size("tp")
    chips = tps // CORES
    mig_per = src_table.shape[1]
    dims = (steps, heads, slots, insts, mig_per)
    features = out_weight.shape[1] // tps

    tp = lax.axis_index("tp")
    chip, core = tp // CORES, lax.rem(tp, CORES)
    order = [lax.rem(chip + k, chips) * CORES for k in list(range(1, chips)) + [0]]
    pos = jnp.stack([base + core for base in order] + [base + 1 - core for base in order])

    query_rows = queries.reshape(batch * steps * heads, width)
    kv_rows = new_kv.reshape(batch * steps * slots, 2 * width)
    table = res_table[0].T

    to_mate = [(i, i + 1 - 2 * (i % CORES)) for i in range(tps)]
    half = features // 2
    tile = min(half, 512)
    rows = batch // 2

    def exchange(x):
        return lax.all_to_all(x, "inst", split_axis=0, concat_axis=0, tiled=True)

    def give(attention, k, part, deps):
        result = project(
            pos, chips + k, part * half, half, out_weight, [attention], [], False, features, tile,
            jnp.bfloat16, "give", deps,
        )
        return result, lax.ppermute(result, "tp", to_mate)

    def keep(attention, k, part, mate, deps):
        result = project(
            pos, k, part * half, half, out_weight, [attention], [mate], True, features, tile,
            jnp.bfloat16, "keep", deps,
        )
        shift = (k + 1) * CORES
        return result, lax.ppermute(result, "tp", [(i, (i + shift) % tps) for i in range(tps)])

    def remote(attention, between):
        got = [[], []]
        last = []
        extra = None
        for k in range(chips - 1):
            mates = []
            for part in range(2):
                result, mate = give(attention, k, part, last)
                mates.append(mate)
                last = [result]
            if between is not None and k == 0:
                extra, last = between(last)
            for part in range(2):
                result, sent = keep(attention, k, part, mates[part], last)
                last = [result]
                got[part].append(sent)
        return got, last, extra

    def ship(deps):
        sends, tail = pack(src_table, mig_dest, out_pool, query_rows, kv_rows, dims, deps)
        return (exchange(tail), exchange(sends)), [sends]

    first = attend(
        table, res_len, mig_dest, query_rows, kv_rows, res_pool, [], 0, rows, dims, []
    )
    got_first, last, (tails, arriving) = remote(first, ship)
    served = serve(src_table, mig_len, mig_dest, out_pool, tails, dims, last)
    second = attend(
        table, res_len, mig_dest, query_rows, kv_rows, res_pool, [exchange(served)], rows, rows,
        dims, [],
    )
    got_second, last, _ = remote(second, None)

    attention = [first, second]
    tile = min(features, 512)
    given = project(
        pos, 2 * chips - 1, 0, features, out_weight, attention, [], False, features, tile,
        jnp.bfloat16, "give_own", last,
    )
    mate = lax.ppermute(given, "tp", to_mate)
    own = project(
        pos, chips - 1, 0, features, out_weight, attention, [mate], True, features, tile,
        jnp.float32, "keep_own", [],
    )
    arrived = assemble(mig_dest, mig_len, arriving, mig_per, [own])
    hidden = None
    for column, got in ((0, got_first), (rows * steps, got_second)):
        for part in range(2):
            hidden = finish(hidden, own, got[part], part * half, column, [])
    return (arrived, hidden)


def solution(mesh):
    placed = (
        P(("groups", "inst"), "tp", None, None, None),
        P(("groups", "inst"), None, None),
        P(("groups", "inst"), None),
        P(("groups", "inst"), "tp", None, None, None),
        P(("groups", "inst"), None, None),
        P("groups"),
        P("groups"),
        P(("groups", "inst"), None, "tp", None),
        P(("groups", "inst"), None, "tp", None),
        P("tp", None),
    )
    return jax.shard_map(
        shards,
        mesh=mesh,
        in_specs=placed,
        out_specs=(P(("groups", "inst"), None, "tp", None, None), P("tp", ("groups", "inst"))),
        check_vma=False,
    )
```

time: 159 us -> 156 us (0.981)
  blocking collectives: 0 us -> 11.1 us
  Pallas kernels: 105 us -> 96 us
  waiting for transfers between devices: 24.8 us -> 21.4 us
  starting transfers between devices: 18.2 us -> 15.9 us
    ppermute x16 -> x9, starting transfers between devices: 18.2 us -> 5.14 us  [the longest x4 4.12 us: keep(): lax.ppermute(result, 'tp', [(i, (i + shift) % tps) for i in range(tps)])]
    all_to_all x0 -> x1, blocking collectives: none -> 11.1 us  [exchange(): return lax.all_to_all(x, 'inst', split_axis=0, concat_axis=0, tiled=True)]
    all_to_all x0 -> x2, starting transfers between devices: none -> 10.8 us  [exchange(): return lax.all_to_all(x, 'inst', split_axis=0, concat_axis=0, tiled=True)]
    pallas_call x17 -> x19, Pallas kernels: 105 us -> 96 us  [run(): pl.pallas_call(call, grid_spec=pltpu.PrefetchScalarGridSpec(num_scalar_pr...]
    ppermute x16 -> x9, waiting for transfers between devices: 24.8 us -> 21.4 us  [the longest x4 21.2 us: keep(): lax.ppermute(result, 'tp', [(i, (i + shift) % tps) for i in range(tps)])]
    slice x4 -> x0, local copies, waits for them, and re-layouts: 1.75 us -> none  [the longest x2 0.9 us: shards(): tail_kv = kv_rows[-insts * steps * slots:]]
    unnamed x26 -> x24, local copies, waits for them, and re-layouts: 6.47 us -> 6.93 us
  transfers between devices with their start and end apart: 16 -> 11, of which waited for: 3 -> 4; matrix products, arithmetic and copies ran while one was open for 1% -> 0% of each run, Pallas kernels for 49% -> 50%
where the time goes in v2:
time: 156 us; the launch traced here: 155 us
  Pallas kernels  96 us (62%)
  waiting for transfers between devices  21.4 us (14%)
  starting transfers between devices  15.9 us (10%)
  blocking collectives  11.1 us (7%)
  local copies, waits for them, and re-layouts  8.95 us (6%)
    pallas_call x19, Pallas kernels, run(): pl.pallas_call(call, grid_spec=pltpu.PrefetchScalarGridSpec(num_scalar_pr...  96 us
    ppermute x4, waiting for transfers between devices, keep(): lax.ppermute(result, 'tp', [(i, (i + shift) % tps) for i in range(tps)])  21.2 us
    all_to_all x1, blocking collectives, exchange(): return lax.all_to_all(x, 'inst', split_axis=0, concat_axis=0, tiled=True)  11.1 us
    all_to_all x2, starting transfers between devices, exchange(): return lax.all_to_all(x, 'inst', split_axis=0, concat_axis=0, tiled=True)  10.8 us
    unnamed x24, local copies, waits for them, and re-layouts  6.93 us
    ppermute x4, starting transfers between devices, keep(): lax.ppermute(result, 'tp', [(i, (i + shift) % tps) for i in range(tps)])  4.12 us
  transfers between devices with their start and end apart: 11, of which 4 were waited for; matrix products, arithmetic and copies ran while one was open for 0% of the time, Pallas kernels for 50%

profile of v2, /device:TPU:0, one launch (start us, length us, event | category | flops | bytes accessed | tf_op | source)
XLA Modules:
  0.0 154.8 jit_solution(1993998532037653432)
XLA Ops:
  0.7 2.0 %reshape.11.refs_4_ = bf16[1024,256]{1,0:T(8,128)(2,1)} reshape(bf16[128,4,2,256]{3,2,1,0:T(2,128)(2,1)} %param.18) | data formatting | bytes 1048576 | tf_op jit(solution)/shard_map/reshape | solution.py:485
  3.4 8.5 %attend.2.refs_5_ = bf16[256,2048]{1,0:T(8,128)(2,1)} custom-call(s32[8,125]{1,0:T(8,128)} %bitcast.11, s32[1,125]{1,0:T(1,128)} %refs_1_.22, s32[8]{0:T(128)} %refs_0_.5, bf16[8192,128]{1,0:T(8,128)(2,1)} %bitcast.8, bf16[1024,256]{1,0:T(8,128)(2,1)} %reshape.11.refs_4_, bf16[1,2,64,16,256]{4,3,2,1,0:T(8,128)(2,1)} %refs_5_.3), custom_call_target="tpu_custom_call" | custom-call | bytes 1024 | tf_op jit(solution)/shard_map/attend/pallas_call | solution.py:54
  11.9 4.9 %give.4.refs_6_ = bf16[256,1024]{1,0:T(8,128)(2,1)} custom-call(s32[4]{0:T(128)} %pad_add_fusion.refs_0_, bf16[2048,8192]{1,0:T(8,128)(2,1)} %refs_4_.19, bf16[2048,8192]{1,0:T(8,128)(2,1)} %refs_4_.19, bf16[2048,8192]{1,0:T(8,128)(2,1)} %refs_4_.19, bf16[2048,8192]{1,0:T(8,128)(2,1)} %refs_4_.19, bf16[256,2048]{1,0:T(8,128)(2,1)} %attend.2.refs_5_), custom_call_target="tpu_custom_call" | custom-call | bytes 1024 | tf_op jit(solution)/shard_map/give/pallas_call | solution.py:54
  17.3 4.9 %give.5.refs_5_ = bf16[256,1024]{1,0:T(8,128)(2,1)} custom-call(s32[4]{0:T(128)} %pad_add_fusion.refs_0_, bf16[2048,8192]{1,0:T(8,128)(2,1)} %refs_4_.19, bf16[2048,8192]{1,0:T(8,128)(2,1)} %refs_4_.19, bf16[2048,8192]{1,0:T(8,128)(2,1)} %refs_4_.19, bf16[2048,8192]{1,0:T(8,128)(2,1)} %refs_4_.19, bf16[256,2048]{1,0:T(8,128)(2,1)} %attend.2.refs_5_, ...), custom_call_target="tpu_custom_call" | custom-call | bytes 1024 | tf_op jit(solution)/shard_map/give/pallas_call | solution.py:54
  22.2 2.9 %pack.1 = (bf16[4,2,32,16,256]{4,3,2,1,0:T(8,128)(2,1)}, bf16[4,320,128]{2,1,0:T(8,128)(2,1)}) custom-call(s32[1,2,32]{2,1,0:T(2,128)} %refs_0_.4, s32[8]{0:T(128)} %refs_0_.5, bf16[1,2,64,16,256]{4,3,2,1,0:T(8,128)(2,1)} %refs_3_.15, bf16[8192,128]{1,0:T(8,128)(2,1)} %bitcast.9, bf16[1024,256]{1,0:T(8,128)(2,1)} %reshape.11.refs_4_, ...), custom_call_target="tpu_custom_call" | custom-call | bytes 1024 | tf_op jit(solution)/shard_map/pack/pallas_call | solution.py:54
  25.1 6.3 %all-to-all-start.1 = ((bf16[4,320,128]{2,1,0:T(8,128)(2,1)}), bf16[4,320,128]{2,1,0:T(8,128)(2,1)S(1)}, u32[]{:S(2)}, u32[]{:S(2)}) async-start(bf16[4,320,128]{2,1,0:T(8,128)(2,1)} %get-tuple-element.5), calls=%async_computation.1 | async-start | bytes 655360 | tf_op jit(solution)/shard_map/all_to_all | solution.py:494
  31.5 0.8 copy-done.7
  32.3 5.3 %keep.4.refs_7_ = bf16[1024,256]{1,0:T(8,128)(2,1)} custom-call(s32[4]{0:T(128)} %pad_add_fusion.refs_0_, bf16[2048,8192]{1,0:T(8,128)(2,1)} %refs_4_.19, bf16[2048,8192]{1,0:T(8,128)(2,1)} %refs_4_.19, bf16[2048,8192]{1,0:T(8,128)(2,1)} %refs_4_.19, bf16[2048,8192]{1,0:T(8,128)(2,1)} %refs_4_.19, bf16[256,2048]{1,0:T(8,128)(2,1)} %attend.2.refs_5_, ...), custom_call_target="tpu_custom_call" | custom-call | bytes 1024 | tf_op jit(solution)/shard_map/keep/pallas_call | solution.py:54
  37.6 0.8 copy-done.6
  38.4 5.3 %keep.5.refs_5_ = bf16[1024,256]{1,0:T(8,128)(2,1)} custom-call(s32[4]{0:T(128)} %pad_add_fusion.refs_0_, bf16[2048,8192]{1,0:T(8,128)(2,1)} %refs_4_.19, bf16[2048,8192]{1,0:T(8,128)(2,1)} %refs_4_.19, bf16[2048,8192]{1,0:T(8,128)(2,1)} %refs_4_.19, bf16[2048,8192]{1,0:T(8,128)(2,1)} %refs_4_.19, bf16[256,2048]{1,0:T(8,128)(2,1)} %attend.2.refs_5_, ...), custom_call_target="tpu_custom_call" | custom-call | bytes 1024 | tf_op jit(solution)/shard_map/keep/pallas_call | solution.py:54
  44.4 2.8 %serve.1 = bf16[4,128,128]{2,1,0:T(8,128)(2,1)} custom-call(s32[1,2,32]{2,1,0:T(2,128)} %refs_0_.4, s32[8]{0:T(128)} %refs_1_.29, s32[8]{0:T(128)} %refs_0_.5, bf16[1,2,64,16,256]{4,3,2,1,0:T(8,128)(2,1)} %refs_3_.15, bf16[4,320,128]{2,1,0:T(8,128)(2,1)} %copy-done.5, bf16[1024,256]{1,0:T(8,128)(2,1)} %keep.5.refs_5_), custom_call_target="tpu_custom_call" | custom-call | bytes 1024 | tf_op jit(solution)/shard_map/serve/pallas_call | solution.py:54
  47.2 11.1 %all_to_all.15.refs_6_ = bf16[4,128,128]{2,1,0:T(8,128)(2,1)} all-to-all(bf16[4,128,128]{2,1,0:T(8,128)(2,1)} %serve.1), channel_id=1, replica_groups=mesh['groups'=2,'inst'=4,'tp'=4] {'inst'}, dimensions={0} | all-to-all | bytes 262144 | tf_op jit(solution)/shard_map/all_to_all | solution.py:494
  58.3 4.5 %all-to-all-start = ((bf16[4,2,32,16,256]{4,3,2,1,0:T(8,128)(2,1)}), bf16[4,2,32,16,256]{4,3,2,1,0:T(8,128)(2,1)}, u32[]{:S(2)}, u32[]{:S(2)}) async-start(bf16[4,2,32,16,256]{4,3,2,1,0:T(8,128)(2,1)} %get-tuple-element.4.refs_7_), calls=%async_computation | async-start | bytes 4194304 | tf_op jit(solution)/shard_map/all_to_all | solution.py:494
  62.8 8.7 %attend.3.refs_5_.refs_6_ = bf16[256,2048]{1,0:T(8,128)(2,1)} custom-call(s32[8,125]{1,0:T(8,128)} %bitcast.12, s32[1,125]{1,0:T(1,128)} %refs_1_.22, s32[8]{0:T(128)} %refs_0_.5, bf16[8192,128]{1,0:T(8,128)(2,1)} %bitcast.10, bf16[1024,256]{1,0:T(8,128)(2,1)} %reshape.11.refs_4_, bf16[1,2,64,16,256]{4,3,2,1,0:T(8,128)(2,1)} %refs_5_.3, ...), custom_call_target="tpu_custom_call" | custom-call | bytes 1024 | tf_op jit(solution)/shard_map/attend/pallas_call | solution.py:54
  71.5 4.9 %give.6.refs_6_ = bf16[256,1024]{1,0:T(8,128)(2,1)} custom-call(s32[4]{0:T(128)} %pad_add_fusion.refs_0_, bf16[2048,8192]{1,0:T(8,128)(2,1)} %refs_4_.19, bf16[2048,8192]{1,0:T(8,128)(2,1)} %refs_4_.19, bf16[2048,8192]{1,0:T(8,128)(2,1)} %refs_4_.19, bf16[2048,8192]{1,0:T(8,128)(2,1)} %refs_4_.19, bf16[256,2048]{1,0:T(8,128)(2,1)} %attend.3.refs_5_.refs_6_), custom_call_target="tpu_custom_call" | custom-call | bytes 1024 | tf_op jit(solution)/shard_map/give/pallas_call | solution.py:54
  76.4 4.9 %give.7.refs_7_ = bf16[256,1024]{1,0:T(8,128)(2,1)} custom-call(s32[4]{0:T(128)} %pad_add_fusion.refs_0_, bf16[2048,8192]{1,0:T(8,128)(2,1)} %refs_4_.19, bf16[2048,8192]{1,0:T(8,128)(2,1)} %refs_4_.19, bf16[2048,8192]{1,0:T(8,128)(2,1)} %refs_4_.19, bf16[2048,8192]{1,0:T(8,128)(2,1)} %refs_4_.19, bf16[256,2048]{1,0:T(8,128)(2,1)} %attend.3.refs_5_.refs_6_, ...), custom_call_target="tpu_custom_call" | custom-call | bytes 1024 | tf_op jit(solution)/shard_map/give/pallas_call | solution.py:54
  81.9 0.8 copy-done.9
  82.7 5.3 %keep.6.refs_7_ = bf16[1024,256]{1,0:T(8,128)(2,1)} custom-call(s32[4]{0:T(128)} %pad_add_fusion.refs_0_, bf16[2048,8192]{1,0:T(8,128)(2,1)} %refs_4_.19, bf16[2048,8192]{1,0:T(8,128)(2,1)} %refs_4_.19, bf16[2048,8192]{1,0:T(8,128)(2,1)} %refs_4_.19, bf16[2048,8192]{1,0:T(8,128)(2,1)} %refs_4_.19, bf16[256,2048]{1,0:T(8,128)(2,1)} %attend.3.refs_5_.refs_6_, ...), custom_call_target="tpu_custom_call" | custom-call | bytes 1024 | tf_op jit(solution)/shard_map/keep/pallas_call | solution.py:54
  88.8 5.3 %keep.7.refs_7_ = bf16[1024,256]{1,0:T(8,128)(2,1)} custom-call(s32[4]{0:T(128)} %pad_add_fusion.refs_0_, bf16[2048,8192]{1,0:T(8,128)(2,1)} %refs_4_.19, bf16[2048,8192]{1,0:T(8,128)(2,1)} %refs_4_.19, bf16[2048,8192]{1,0:T(8,128)(2,1)} %refs_4_.19, bf16[2048,8192]{1,0:T(8,128)(2,1)} %refs_4_.19, bf16[256,2048]{1,0:T(8,128)(2,1)} %attend.3.refs_5_.refs_6_, ...), custom_call_target="tpu_custom_call" | custom-call | bytes 1024 | tf_op jit(solution)/shard_map/keep/pallas_call | solution.py:54
  94.1 9.7 %give_own.1 = bf16[512,2048]{1,0:T(8,128)(2,1)} custom-call(s32[4]{0:T(128)} %pad_add_fusion.refs_0_, bf16[2048,8192]{1,0:T(8,128)(2,1)} %refs_4_.19, bf16[2048,8192]{1,0:T(8,128)(2,1)} %refs_4_.19, bf16[2048,8192]{1,0:T(8,128)(2,1)} %refs_4_.19, bf16[2048,8192]{1,0:T(8,128)(2,1)} %refs_4_.19, bf16[256,2048]{1,0:T(8,128)(2,1)} %attend.2.refs_5_, ...), custom_call_target="tpu_custom_call" | custom-call | bytes 1024 | tf_op jit(solution)/shard_map/give_own/pallas_call | solution.py:54
  103.8 1.6 %collective-permute-start.8 = (bf16[1024,256]{1,0:T(8,128)(2,1)S(1)}, bf16[1024,256]{1,0:T(8,128)(2,1)}, u32[]{:S(2)}, u32[]{:S(2)}) collective-permute-start(bf16[1024,256]{1,0:T(8,128)(2,1)S(1)} %copy-done.1), channel_id=1, source_target_pairs={{0,2},{1,3},{2,0},{3,1},{4,6},{5,7},{6,4},{7,5},{8,10},{9,11},{10,... | collective-permute-start | bytes 1572872 | tf_op jit(solution)/shard_map/ppermute | solution.py:509
  105.9 1.5 collective-permute-start.6
  108.2 1.4 copy-done
  109.6 10.8 %keep_own.1.refs_3_.refs_0_ = f32[2048,512]{1,0:T(8,128)} custom-call(s32[4]{0:T(128)} %pad_add_fusion.refs_0_, bf16[2048,8192]{1,0:T(8,128)(2,1)} %refs_4_.19, bf16[2048,8192]{1,0:T(8,128)(2,1)} %refs_4_.19, bf16[2048,8192]{1,0:T(8,128)(2,1)} %refs_4_.19, bf16[2048,8192]{1,0:T(8,128)(2,1)} %refs_4_.19, bf16[256,2048]{1,0:T(8,128)(2,1)} %attend.2.refs_5_, ...), custom_call_target="tpu_custom_call" | custom-call | bytes 1024 | tf_op jit(solution)/shard_map/keep_own/pallas_call | solution.py:54
  120.4 3.2 %assemble.1 = bf16[1,3,2,512,256]{4,3,2,1,0:T(8,128)(2,1)} custom-call(s32[8]{0:T(128)} %refs_0_.5, s32[8]{0:T(128)} %refs_1_.29, bf16[4,2,32,16,256]{4,3,2,1,0:T(8,128)(2,1)} %all-to-all-done.refs_2_, f32[2048,512]{1,0:T(8,128)} %keep_own.1.refs_3_.refs_0_), custom_call_target="tpu_custom_call" | custom-call | bytes 1024 | tf_op jit(solution)/shard_map/assemble/pallas_call | solution.py:54
  123.6 2.1 %finish.4.refs_2_ = bf16[2048,512]{1,0:T(8,128)(2,1)} custom-call(f32[2048,512]{1,0:T(8,128)} %keep_own.1.refs_3_.refs_0_, bf16[1024,256]{1,0:T(8,128)(2,1)} %collective-permute-done.8.refs_1_), custom_call_target="tpu_custom_call" | custom-call | bytes 1024 | tf_op jit(solution)/shard_map/finish/pallas_call | solution.py:54
  125.7 4.3 %collective-permute-done.7.refs_1_ = bf16[1024,256]{1,0:T(8,128)(2,1)} collective-permute-done((bf16[1024,256]{1,0:T(8,128)(2,1)S(1)}, bf16[1024,256]{1,0:T(8,128)(2,1)}, u32[]{:S(2)}, u32[]{:S(2)}) %collective-permute-start.7) | collective-permute-done | bytes 524320 | tf_op jit(solution)/shard_map/ppermute | solution.py:509
  130.0 2.1 %finish.5.refs_2_ = bf16[2048,512]{1,0:T(8,128)(2,1)} custom-call(f32[2048,512]{1,0:T(8,128)} %keep_own.1.refs_3_.refs_0_, bf16[1024,256]{1,0:T(8,128)(2,1)} %collective-permute-done.7.refs_1_, bf16[2048,512]{1,0:T(8,128)(2,1)} %finish.4.refs_2_), custom_call_target="tpu_custom_call", output_to_operand_aliasing={{}: (2, {})} | custom-call | bytes 1024 | tf_op jit(solution)/shard_map/finish/pallas_call | solution.py:54
  132.1 9.0 %collective-permute-done.6.refs_1_ = bf16[1024,256]{1,0:T(8,128)(2,1)S(1)} collective-permute-done((bf16[1024,256]{1,0:T(8,128)(2,1)S(1)}, bf16[1024,256]{1,0:T(8,128)(2,1)S(1)}, u32[]{:S(2)}, u32[]{:S(2)}) %collective-permute-start.6) | collective-permute-done | bytes 524320 | tf_op jit(solution)/shard_map/ppermute | solution.py:509
  141.9 2.1 %finish.6.refs_2_ = bf16[2048,512]{1,0:T(8,128)(2,1)} custom-call(f32[2048,512]{1,0:T(8,128)} %keep_own.1.refs_3_.refs_0_, bf16[1024,256]{1,0:T(8,128)(2,1)} %copy-done.11, bf16[2048,512]{1,0:T(8,128)(2,1)} %finish.5.refs_2_), custom_call_target="tpu_custom_call", output_to_operand_aliasing={{}: (2, {})} | custom-call | bytes 1024 | tf_op jit(solution)/shard_map/finish/pallas_call | solution.py:54
  144.0 7.9 %collective-permute-done.5.refs_1_ = bf16[1024,256]{1,0:T(8,128)(2,1)S(1)} collective-permute-done((bf16[1024,256]{1,0:T(8,128)(2,1)S(1)}, bf16[1024,256]{1,0:T(8,128)(2,1)S(1)}, u32[]{:S(2)}, u32[]{:S(2)}) %collective-permute-start.5) | collective-permute-done | bytes 524320 | tf_op jit(solution)/shard_map/ppermute | solution.py:509
  152.7 2.1 %finish.7 = bf16[2048,512]{1,0:T(8,128)(2,1)} custom-call(f32[2048,512]{1,0:T(8,128)} %keep_own.1.refs_3_.refs_0_, bf16[1024,256]{1,0:T(8,128)(2,1)} %copy-done.10, bf16[2048,512]{1,0:T(8,128)(2,1)} %finish.6.refs_2_), custom_call_target="tpu_custom_call", output_to_operand_aliasing={{}: (2, {})} | custom-call | bytes 1024 | tf_op jit(solution)/shard_map/finish/pallas_call | solution.py:54
  (36 shorter events, 6.1 us)
Async XLA Ops:
  16.8 14.6 %collective-permute-start.1 = (bf16[256,1024]{1,0:T(8,128)(2,1)}, bf16[256,1024]{1,0:T(8,128)(2,1)S(1)}, u32[]{:S(2)}, u32[]{:S(2)}) collective-permute-start(bf16[256,1024]{1,0:T(8,128)(2,1)} %give.4.refs_6_), channel_id=1, source_target_pairs={{0,1},{1,0},{2,3},{3,2},{4,5},{5,4},{6,7},{7,6},{8,9},{9,8},{10,11... | collective-permute-start | bytes 1572872 | tf_op jit(solution)/shard_map/ppermute | solution.py:501
  22.2 15.4 %collective-permute-start = (bf16[256,1024]{1,0:T(8,128)(2,1)}, bf16[256,1024]{1,0:T(8,128)(2,1)S(1)}, u32[]{:S(2)}, u32[]{:S(2)}) collective-permute-start(bf16[256,1024]{1,0:T(8,128)(2,1)} %give.5.refs_5_), channel_id=1, source_target_pairs={{0,1},{1,0},{2,3},{3,2},{4,5},{5,4},{6,7},{7,6},{8,9},{9,8},{10,11... | collective-permute-start | bytes 1572872 | tf_op jit(solution)/shard_map/ppermute | solution.py:501
  25.1 18.6 %all-to-all-start.1 = ((bf16[4,320,128]{2,1,0:T(8,128)(2,1)}), bf16[4,320,128]{2,1,0:T(8,128)(2,1)S(1)}, u32[]{:S(2)}, u32[]{:S(2)}) async-start(bf16[4,320,128]{2,1,0:T(8,128)(2,1)} %get-tuple-element.5), calls=%async_computation.1 | async-start | bytes 655360 | tf_op jit(solution)/shard_map/all_to_all | solution.py:494
  31.5 0.8 copy-start.7
  37.6 0.8 copy-start.6
  43.7 0.7 copy-start.5
  58.3 62.0 %all-to-all-start = ((bf16[4,2,32,16,256]{4,3,2,1,0:T(8,128)(2,1)}), bf16[4,2,32,16,256]{4,3,2,1,0:T(8,128)(2,1)}, u32[]{:S(2)}, u32[]{:S(2)}) async-start(bf16[4,2,32,16,256]{4,3,2,1,0:T(8,128)(2,1)} %get-tuple-element.4.refs_7_), calls=%async_computation | async-start | bytes 4194304 | tf_op jit(solution)/shard_map/all_to_all | solution.py:494
  76.4 5.4 %collective-permute-start.3 = (bf16[256,1024]{1,0:T(8,128)(2,1)}, bf16[256,1024]{1,0:T(8,128)(2,1)S(1)}, u32[]{:S(2)}, u32[]{:S(2)}) collective-permute-start(bf16[256,1024]{1,0:T(8,128)(2,1)} %give.6.refs_6_), channel_id=1, source_target_pairs={{0,1},{1,0},{2,3},{3,2},{4,5},{5,4},{6,7},{7,6},{8,9},{9,8},{10,11... | collective-permute-start | bytes 1572872 | tf_op jit(solution)/shard_map/ppermute | solution.py:501
  81.4 6.6 %collective-permute-start.2 = (bf16[256,1024]{1,0:T(8,128)(2,1)}, bf16[256,1024]{1,0:T(8,128)(2,1)S(1)}, u32[]{:S(2)}, u32[]{:S(2)}) collective-permute-start(bf16[256,1024]{1,0:T(8,128)(2,1)} %give.7.refs_7_), channel_id=1, source_target_pairs={{0,1},{1,0},{2,3},{3,2},{4,5},{5,4},{6,7},{7,6},{8,9},{9,8},{10,11... | collective-permute-start | bytes 1572872 | tf_op jit(solution)/shard_map/ppermute | solution.py:501
  81.9 0.8 copy-start.9
  88.0 0.8 copy-start.8
  94.1 9.7 %copy-start.1 = (bf16[1024,256]{1,0:T(8,128)(2,1)S(1)}, bf16[1024,256]{1,0:T(8,128)(2,1)}, u32[]{:S(2)}) copy-start(bf16[1024,256]{1,0:T(8,128)(2,1)} %keep.4.refs_7_) | copy-start | bytes 1572868
  94.1 11.3 %copy-start.4 = (bf16[1024,256]{1,0:T(8,128)(2,1)S(1)}, bf16[1024,256]{1,0:T(8,128)(2,1)}, u32[]{:S(2)}) copy-start(bf16[1024,256]{1,0:T(8,128)(2,1)} %keep.5.refs_5_) | copy-start | bytes 1572868
  94.1 11.8 %copy-start.3 = (bf16[1024,256]{1,0:T(8,128)(2,1)S(1)}, bf16[1024,256]{1,0:T(8,128)(2,1)}, u32[]{:S(2)}) copy-start(bf16[1024,256]{1,0:T(8,128)(2,1)} %keep.6.refs_7_) | copy-start | bytes 1572868
  94.1 13.4 %copy-start.2 = (bf16[1024,256]{1,0:T(8,128)(2,1)S(1)}, bf16[1024,256]{1,0:T(8,128)(2,1)}, u32[]{:S(2)}) copy-start(bf16[1024,256]{1,0:T(8,128)(2,1)} %keep.7.refs_7_) | copy-start | bytes 1572868
  103.8 4.4 %collective-permute-start.4 = (bf16[512,2048]{1,0:T(8,128)(2,1)}, bf16[512,2048]{1,0:T(8,128)(2,1)S(1)}, u32[]{:S(2)}, u32[]{:S(2)}) collective-permute-start(bf16[512,2048]{1,0:T(8,128)(2,1)} %give_own.1), channel_id=1, source_target_pairs={{0,1},{1,0},{2,3},{3,2},{4,5},{5,4},{6,7},{7,6},{8,9},{9,8},{10,11... | collective-permute-start | bytes 6291464 | tf_op jit(solution)/shard_map/ppermute | solution.py:550
  103.8 19.8 %collective-permute-start.8 = (bf16[1024,256]{1,0:T(8,128)(2,1)S(1)}, bf16[1024,256]{1,0:T(8,128)(2,1)}, u32[]{:S(2)}, u32[]{:S(2)}) collective-permute-start(bf16[1024,256]{1,0:T(8,128)(2,1)S(1)} %copy-done.1), channel_id=1, source_target_pairs={{0,2},{1,3},{2,0},{3,1},{4,6},{5,7},{6,4},{7,5},{8,10},{9,11},{10,... | collective-permute-start | bytes 1572872 | tf_op jit(solution)/shard_map/ppermute | solution.py:509
  105.4 24.5 %collective-permute-start.7 = (bf16[1024,256]{1,0:T(8,128)(2,1)S(1)}, bf16[1024,256]{1,0:T(8,128)(2,1)}, u32[]{:S(2)}, u32[]{:S(2)}) collective-permute-start(bf16[1024,256]{1,0:T(8,128)(2,1)S(1)} %copy-done.4), channel_id=1, source_target_pairs={{0,2},{1,3},{2,0},{3,1},{4,6},{5,7},{6,4},{7,5},{8,10},{9,11},{10,... | collective-permute-start | bytes 1572872 | tf_op jit(solution)/shard_map/ppermute | solution.py:509
  105.9 35.2 %collective-permute-start.6 = (bf16[1024,256]{1,0:T(8,128)(2,1)S(1)}, bf16[1024,256]{1,0:T(8,128)(2,1)S(1)}, u32[]{:S(2)}, u32[]{:S(2)}) collective-permute-start(bf16[1024,256]{1,0:T(8,128)(2,1)S(1)} %copy-done.3), channel_id=1, source_target_pairs={{0,2},{1,3},{2,0},{3,1},{4,6},{5,7},{6,4},{7,5},{8,10},{9,11},{10,... | collective-permute-start | bytes 1572872 | tf_op jit(solution)/shard_map/ppermute | solution.py:509
  107.5 44.4 %collective-permute-start.5 = (bf16[1024,256]{1,0:T(8,128)(2,1)S(1)}, bf16[1024,256]{1,0:T(8,128)(2,1)S(1)}, u32[]{:S(2)}, u32[]{:S(2)}) collective-permute-start(bf16[1024,256]{1,0:T(8,128)(2,1)S(1)} %copy-done.2), channel_id=1, source_target_pairs={{0,2},{1,3},{2,0},{3,1},{4,6},{5,7},{6,4},{7,5},{8,10},{9,11},{10,... | collective-permute-start | bytes 1572872 | tf_op jit(solution)/shard_map/ppermute | solution.py:509
  108.2 1.4 copy-start
  141.1 0.8 copy-start.11
  151.9 0.8 copy-start.10

commit v3 on v0

v3 whole, which is shorter than its diff:
```python
import functools
import math

import jax
import jax.numpy as jnp
from jax import lax
from jax.experimental import pallas as pl
from jax.experimental.pallas import tpu as pltpu
from jax.sharding import PartitionSpec as P

CORES = 2
LOW = -1e30
MIB = 1 << 20
LANES = 128
GROUP = 16
TOGETHER = 8


def dot_t(left, right):
    return lax.dot_general(
        left, right, (((1,), (1,)), ((), ())), preferred_element_type=jnp.float32
    )


def row_plan(dest_ref, inst, cap):
    requests = [jnp.int32(-1)] * cap
    seen = jnp.int32(0)
    for g in range(dest_ref.shape[0]):
        here = dest_ref[g] == inst
        requests = [jnp.where(here & (seen == a), g, requests[a]) for a in range(cap)]
        seen = seen + here.astype(jnp.int32)
    return requests


def standing_of(dest_ref, request):
    dest = dest_ref[request]
    standing = jnp.int32(0)
    for g in range(dest_ref.shape[0]):
        standing = standing + ((dest_ref[g] == dest) & (g < request)).astype(jnp.int32)
    return dest, standing


VMEM = pl.BlockSpec(memory_space=pltpu.VMEM)
ANY = pl.BlockSpec(memory_space=pl.ANY)
HBM = pl.BlockSpec(memory_space=pltpu.HBM)


class Sizes:
    def __init__(self, queries, res_pool, res_table, src_table, mig_dest, out_weight):
        self.batch, self.steps, self.heads, self.width = queries.shape
        self.slots = res_pool.shape[1]
        self.block = res_pool.shape[3]
        self.resident, self.blocks = res_table.shape[1:]
        self.mig_per, self.mig_blocks = src_table.shape[1:]
        self.requests = mig_dest.shape[0]
        self.insts = lax.axis_size("inst")
        self.tps = lax.axis_size("tp")
        self.chips = self.tps // CORES
        self.cap = self.insts - 1
        self.per = self.steps * self.heads
        self.per_kv = self.steps * self.slots
        self.depth = out_weight.shape[0]
        self.features = out_weight.shape[1] // self.tps
        self.quarter = self.features // 4
        self.tail_q = self.insts * self.per
        self.tail_kv = self.insts * self.per_kv


def piece_columns(piece, sizes):
    ahead, mine, part = piece
    tp = lax.axis_index("tp")
    core = lax.rem(tp, CORES)
    chip = lax.rem(tp // CORES + ahead, sizes.chips)
    owner = chip * CORES + (core if mine else 1 - core)
    return owner * sizes.features + part * sizes.quarter


def run(kernel, tables, operands, in_specs, deps, out_shapes, out_specs, name, sizes,
        pieces=(), weight=None, limit=16, grid=(), scratch=(), aliases=None):
    inputs, outputs, many = len(operands), len(out_shapes), len(tables)
    count = len(deps)
    fetches = len(pieces)
    extra_in = [weight] if fetches else []
    limit = max(limit, 36) if fetches else limit

    def call(*refs):
        table_in, refs = refs[:many], refs[many:]
        own_in = refs[:inputs]
        position = inputs + len(extra_in) + count
        own_out = refs[position : position + outputs]
        fetched = refs[position + outputs : position + outputs + fetches]
        rest = list(refs[position + outputs + fetches :])
        copies, reads = [], []
        if fetches:
            source, sems = refs[inputs], rest.pop()
            for n, piece in enumerate(pieces):
                first = pl.multiple_of(piece_columns(piece, sizes), LANES)
                copies.append(
                    pltpu.make_async_copy(
                        source.at[:, pl.ds(first, sizes.quarter)], fetched[n], sems.at[n]
                    )
                )
        table_refs = []
        if many:
            sems = rest.pop()
            table_refs = rest[len(rest) - many :]
            rest = rest[: len(rest) - many]
            reads = [
                pltpu.make_async_copy(source, target, sems.at[n])
                for n, (source, target) in enumerate(zip(table_in, table_refs))
            ]

        def ready():
            for read in reads:
                read.wait()

        def launch():
            for copy in copies:
                copy.start()

        def each(step, action):
            if not grid:
                action()
            else:
                pl.when(pl.program_id(0) == step)(action)

        def begin():
            for read in reads:
                read.start()

        def end():
            for copy in copies:
                copy.wait()

        if reads:
            each(0, begin)
        kernel(ready, launch, *table_refs, *own_in, *own_out, *rest)
        if copies:
            each(grid[0] - 1 if grid else 0, end)

    result = pl.pallas_call(
        call,
        grid_spec=pltpu.PrefetchScalarGridSpec(
            num_scalar_prefetch=0,
            grid=grid,
            in_specs=[HBM] * many + list(in_specs) + [HBM] * len(extra_in) + [ANY] * count,
            out_specs=list(out_specs) + [ANY] * fetches,
            scratch_shapes=list(scratch)
            + [pltpu.SMEM(t.shape, t.dtype) for t in tables]
            + ([pltpu.SemaphoreType.DMA((many,))] if many else [])
            + ([pltpu.SemaphoreType.DMA((fetches,))] if fetches else []),
        ),
        out_shape=list(out_shapes)
        + [jax.ShapeDtypeStruct((sizes.depth, sizes.quarter), jnp.bfloat16)] * fetches,
        input_output_aliases=aliases or {},
        compiler_params=pltpu.CompilerParams(vmem_limit_bytes=limit * MIB),
        cost_estimate=pl.CostEstimate(flops=0, bytes_accessed=1024, transcendentals=0),
        name=name,
    )(*tables, *operands, *extra_in, *deps)
    return result[:outputs], result[outputs:]


def pack_kernel(
    ready, launch, table_ref, dest_ref, pool_ref, query_ref, kv_ref, send_ref, tail_ref, *, sizes
):
    inst = lax.axis_index("inst")
    queries, keys, width = sizes.tail_q, sizes.tail_kv, sizes.width
    launch()
    tail_kv = kv_ref[...].reshape(keys, 2 * width)
    tail_ref[:queries, :] = query_ref[...]
    tail_ref[queries : queries + keys, :] = tail_kv[:, :width]
    tail_ref[queries + keys :, :] = tail_kv[:, width:]
    ready()
    for m in range(sizes.mig_per):
        dest = dest_ref[inst * sizes.mig_per + m]

        def copy_block(b, carry, m=m, dest=dest):
            block = table_ref[0, m, b]
            for s in range(sizes.slots):
                send_ref[dest, s, b] = pool_ref[0, s, block]
            return carry

        lax.fori_loop(0, sizes.mig_blocks, copy_block, 0, unroll=8)


def pack(src_table, mig_dest, out_pool, query_rows, new_kv, sizes, deps, **fetch):
    z = sizes
    shapes = (
        jax.ShapeDtypeStruct(
            (z.insts, z.slots, z.mig_blocks, z.block, 2 * z.width), out_pool.dtype
        ),
        jax.ShapeDtypeStruct((z.tail_q + 2 * z.tail_kv, z.width), out_pool.dtype),
    )
    last_q = query_rows.shape[0] // z.tail_q - 1
    last_kv = z.batch // z.insts - 1
    return run(
        functools.partial(pack_kernel, sizes=z),
        [src_table, mig_dest],
        [out_pool, query_rows, new_kv],
        [
            pl.BlockSpec(out_pool.shape, lambda i: (0, 0, 0, 0, 0)),
            pl.BlockSpec((z.tail_q, z.width), lambda i: (last_q, 0)),
            pl.BlockSpec((z.insts,) + new_kv.shape[1:], lambda i: (last_kv, 0, 0, 0)),
        ],
        deps,
        shapes,
        [VMEM, VMEM],
        "pack", z, grid=(1,), **fetch,
    )


def arrived_kernel(ready, launch, dest_ref, len_ref, got_ref, out_ref, *, sizes):
    ready()
    inst = lax.axis_index("inst")
    block = sizes.block
    requests = row_plan(dest_ref, inst, sizes.cap)
    place = lax.broadcasted_iota(jnp.int32, (block, 2 * sizes.width), 0)
    for a in range(sizes.cap):
        request = requests[a]
        known = jnp.maximum(request, 0)
        length = jnp.where(request >= 0, len_ref[known], 0)
        source = known // sizes.mig_per

        def one(b, carry, a=a, source=source, length=length):
            inside = place + b * block < length
            at = pl.ds(pl.multiple_of(b * block, block), block)
            for s in range(sizes.slots):
                value = got_ref[source, s, b].astype(jnp.float32)
                out_ref[0, a, s, at, :] = jnp.where(inside, value, 0.0).astype(jnp.bfloat16)
            return carry

        lax.fori_loop(0, sizes.mig_blocks, one, 0, unroll=4)


def assemble(mig_dest, mig_len, got, sizes, deps):
    z = sizes
    shape = (1, z.cap, z.slots, z.mig_blocks * z.block, 2 * z.width)
    result, _ = run(
        functools.partial(arrived_kernel, sizes=z),
        [mig_dest, mig_len], [got], [VMEM], deps,
        [jax.ShapeDtypeStruct(shape, jnp.bfloat16)], [VMEM], "assemble", z,
    )
    return result[0]


def fresh_code(rows, keys, sizes):
    index = lax.broadcasted_iota(jnp.int32, (rows, keys), 0)
    key = lax.broadcasted_iota(jnp.int32, (rows, keys), 1)
    step = index // sizes.heads
    slot = lax.rem(index, sizes.heads) // (sizes.heads // sizes.slots)
    in_row = lax.rem(key, sizes.per_kv)
    seen = (in_row // sizes.slots <= step) & (lax.rem(in_row, sizes.slots) == slot)
    return jnp.where(seen, key // sizes.per_kv, -1)


def slot_index(extent, sizes):
    index = lax.broadcasted_iota(jnp.int32, (sizes.per, extent), 0)
    return lax.rem(index, sizes.heads) // (sizes.heads // sizes.slots)


def own_scores(scores, slot_of, slots):
    extent = scores.shape[1] // slots
    own = scores[:, :extent]
    for s in range(1, slots):
        own = jnp.where(slot_of == s, scores[:, s * extent : (s + 1) * extent], own)
    return own


def weigh(own, length, fresh, fresh_seen, scale):
    place = lax.broadcasted_iota(jnp.int32, own.shape, 1)
    own = jnp.where(place < length, own, LOW)
    fresh = jnp.where(fresh_seen, fresh, LOW)
    if own.shape == fresh.shape:
        largest = jnp.max(jnp.maximum(own, fresh), axis=1, keepdims=True)
    else:
        largest = jnp.maximum(
            jnp.max(own, axis=1, keepdims=True), jnp.max(fresh, axis=1, keepdims=True)
        )
    return jnp.exp2((own - largest) * scale), jnp.exp2((fresh - largest) * scale)


def spread(own, slot_of, slots):
    if slots == 1:
        return own.astype(jnp.bfloat16)
    parts = [jnp.where(slot_of == s, own, 0.0) for s in range(slots)]
    return jnp.concatenate(parts, axis=1).astype(jnp.bfloat16)


def gather_blocks(pool_ref, slots, ids):
    tiles = [pool_ref[0, s, block] for s in range(slots) for block in ids]
    return jnp.concatenate(tiles, axis=0)


def with_ones(values):
    return jnp.concatenate([values, jnp.ones_like(values)], axis=1)


def dot(left, right):
    return jnp.dot(left, right, preferred_element_type=jnp.float32)


def attend_kernel(
    ready, launch, table_ref, len_ref, query_hbm, kv_hbm, pool_in, out_ref, *refs,
    first_row, steps_in_all, brings, sizes,
):
    z = sizes
    pool_ref, refs = (refs[0], refs[1:]) if brings else (pool_in, refs)
    query_all, kv_all, fresh_ref, pf_ref, blend_ref, done_ref, sems = refs
    width, per = z.width, z.per
    rows = GROUP
    step = pl.program_id(0)
    extent = z.blocks * z.block
    start = first_row + step * rows
    scale = math.log2(math.e) / math.sqrt(width)

    def copies(n):
        begin = first_row + n * rows
        return (
            pltpu.make_async_copy(
                query_hbm.at[pl.ds(pl.multiple_of(begin * per, rows * per), rows * per)],
                query_all.at[n], sems.at[0, n],
            ),
            pltpu.make_async_copy(kv_hbm.at[pl.ds(begin, rows)], kv_all.at[n], sems.at[1, n]),
        )

    @pl.when(step == 0)
    def _():
        if brings:
            pool_copy = pltpu.make_async_copy(pool_in, pool_ref, sems.at[2, 0])
            pool_copy.start()
        for n in range(steps_in_all):
            for copy in copies(n):
                copy.start()
        launch()
        ready()
        if brings:
            pool_copy.wait()

    for copy in copies(step):
        copy.wait()

    query_ref = query_all.at[step]
    new_kv = kv_all[step].reshape(rows * z.per_kv, 2 * width)
    fresh_ref[...] = dot_t(query_ref[...], new_kv[:, :width])
    code = fresh_code(per, rows * z.per_kv, z)
    slot_of = slot_index(extent, z)
    together = min(TOGETHER, rows)
    for begin in range(0, rows, together):
        group = range(begin, begin + together)
        at = [slice(r * per, (r + 1) * per) for r in group]
        known = [jnp.minimum(start + r, z.resident - 1) for r in group]
        length = [
            jnp.where(start + r < z.resident, len_ref[0, k], 0) for r, k in zip(group, known)
        ]
        both = [
            gather_blocks(pool_ref, z.slots, [table_ref[j, k] for j in range(z.blocks)])
            for k in known
        ]
        fresh = [fresh_ref[a, :] for a in at]
        scores = [dot_t(query_ref[a, :], b[:, :width]) for a, b in zip(at, both)]
        weights = [
            weigh(own_scores(s, slot_of, z.slots), n, f, code == r, scale)
            for s, n, f, r in zip(scores, length, fresh, group)
        ]
        context = [
            dot(spread(w[0], slot_of, z.slots), with_ones(b[:, width:]))
            for w, b in zip(weights, both)
        ]
        for a, c, w in zip(at, context, weights):
            blend_ref[a, :] = c
            pf_ref[a, :] = w[1].astype(jnp.bfloat16)

    done = blend_ref[...] + dot(pf_ref[...], with_ones(new_kv[:, width:]))
    done_ref[...] = done[:, :width] / done[:, width:]
    for h in range(z.heads):
        column = done_ref[pl.ds(h, rows * z.steps, stride=z.heads), :]
        out_ref[:, h * width : (h + 1) * width] = column.astype(jnp.bfloat16)


def attend(table, lengths, queries, new_kv, pool, brings, first_row, rows, sizes, deps, **fetch):
    z = sizes
    groups = rows // GROUP
    tokens = rows * z.steps
    shapes = [jax.ShapeDtypeStruct((tokens, z.heads * z.width), jnp.bfloat16)]
    specs = [pl.BlockSpec((GROUP * z.steps, z.heads * z.width), lambda i: (i, 0))]
    if brings:
        shapes.append(jax.ShapeDtypeStruct(pool.shape, pool.dtype))
        specs.append(VMEM)
    return run(
        functools.partial(
            attend_kernel, first_row=first_row, steps_in_all=groups, brings=brings, sizes=z
        ),
        [table, lengths],
        [queries, new_kv, pool],
        [HBM, HBM, HBM if brings else VMEM],
        deps, shapes, specs, "attend", z, limit=46 if brings else 36,
        grid=(groups,),
        scratch=[
            pltpu.VMEM((groups, GROUP * z.per, z.width), jnp.bfloat16),
            pltpu.VMEM((groups, GROUP) + new_kv.shape[1:], jnp.bfloat16),
            pltpu.VMEM((GROUP * z.per, GROUP * z.per_kv), jnp.float32),
            pltpu.VMEM((GROUP * z.per, GROUP * z.per_kv), jnp.bfloat16),
            pltpu.VMEM((GROUP * z.per, 2 * z.width), jnp.float32),
            pltpu.VMEM((GROUP * z.per, z.width), jnp.float32),
            pltpu.SemaphoreType.DMA((3, groups)),
        ],
        **fetch,
    )


def serve_kernel(ready, launch, table_ref, len_ref, dest_ref, pool_ref, *refs, sizes):
    z = sizes
    launch()
    ready()
    tails, out_ref = refs[:-1], refs[-1]
    inst = lax.axis_index("inst")
    queries, keys = z.tail_q, z.tail_kv
    extent = z.mig_blocks * z.block
    code = fresh_code(z.per, keys, z)
    slot_of = slot_index(extent, z)
    scale = math.log2(math.e) / math.sqrt(z.width)
    for m in range(z.mig_per):
        request = inst * z.mig_per + m
        dest, place = standing_of(dest_ref, request)
        ahead = lax.rem(dest - inst + z.insts, z.insts)
        begin = pl.multiple_of((place + 1) * z.per, z.per)
        query = pick([ref[pl.ds(begin, z.per), :] for ref in tails], ahead - 1)
        new_keys = pick([ref[queries : queries + keys, :] for ref in tails], ahead - 1)
        new_values = pick([ref[queries + keys :, :] for ref in tails], ahead - 1)
        ids = [table_ref[0, m, b] for b in range(z.mig_blocks)]
        both = gather_blocks(pool_ref, z.slots, ids)
        scores = dot_t(query, both[:, : z.width])
        own, fresh = weigh(
            own_scores(scores, slot_of, z.slots), len_ref[request],
            dot_t(query, new_keys), code == place + 1, scale,
        )
        done = dot(spread(own, slot_of, z.slots), with_ones(both[:, z.width :]))
        done = done + dot(fresh.astype(jnp.bfloat16), with_ones(new_values))
        result = done[:, : z.width] / done[:, z.width :]
        out_ref[m * z.per : (m + 1) * z.per, :] = result.astype(jnp.bfloat16)


def pick(choices, index):
    chosen = choices[0]
    for k in range(1, len(choices)):
        chosen = jnp.where(index == k, choices[k], chosen)
    return chosen


def serve(src_table, mig_len, mig_dest, out_pool, tails, sizes, deps, **fetch):
    z = sizes
    result, pieces = run(
        functools.partial(serve_kernel, sizes=z),
        [src_table, mig_len, mig_dest],
        [out_pool] + tails,
        [VMEM] * (1 + len(tails)),
        deps,
        [jax.ShapeDtypeStruct((z.mig_per * z.per, z.width), jnp.bfloat16)],
        [VMEM], "serve", z, **fetch,
    )
    return result[0], pieces


def merge_kernel(ready, launch, dest_ref, *refs, sizes):
    z = sizes
    launch()
    ready()
    back, old_ref, out_ref, rows_ref = refs[:-3], refs[-3], refs[-2], refs[-1]
    inst = lax.axis_index("inst")
    requests = row_plan(dest_ref, inst, z.cap)
    for a in range(z.cap):
        known = jnp.maximum(requests[a], 0)
        ahead = lax.rem(known // z.mig_per - inst + z.insts, z.insts)
        begin = pl.multiple_of(lax.rem(known, z.mig_per) * z.per, z.per)
        served = pick([ref[pl.ds(begin, z.per), :].astype(jnp.float32) for ref in back], ahead - 1)
        rows_ref[(a + 1) * z.per : (a + 2) * z.per, :] = served
    rows_ref[: z.per, :] = jnp.zeros((z.per, z.width), jnp.float32)
    tokens = z.insts * z.steps
    row = lax.broadcasted_iota(jnp.int32, (tokens, z.width), 0) // z.steps
    filled = row < 0
    for a in range(z.cap):
        filled = filled | ((row == a + 1) & (requests[a] >= 0))
    for h in range(z.heads):
        at = slice(h * z.width, (h + 1) * z.width)
        column = rows_ref[pl.ds(h, tokens, stride=z.heads), :]
        old = old_ref[:, at].astype(jnp.float32)
        out_ref[:, at] = jnp.where(filled, column, old).astype(jnp.bfloat16)


def merge(mig_dest, attention, back, sizes, deps, **fetch):
    z = sizes
    tokens = z.insts * z.steps
    last = attention.shape[0] // tokens - 1
    spec = pl.BlockSpec((tokens, attention.shape[1]), lambda i: (last, 0))
    result, pieces = run(
        functools.partial(merge_kernel, sizes=z),
        [mig_dest],
        back + [attention],
        [pl.BlockSpec(b.shape, lambda i: (0, 0)) for b in back] + [spec],
        deps,
        [jax.ShapeDtypeStruct(attention.shape, jnp.bfloat16)],
        [spec], "merge", z, grid=(1,),
        scratch=[pltpu.VMEM((z.insts * z.per, z.width), jnp.float32)],
        aliases={1 + len(back): 0}, **fetch,
    )
    return result[0], pieces


def project_kernel(
    ready, launch, *refs, parts, count, streamed, added, turned, sizes
):
    launch()
    attention, weights = refs[:parts], list(refs[parts : parts + count])
    extra = refs[parts + count : parts + count + added]
    position = parts + count + added
    copies = [None] * count
    if streamed:
        source = refs[position]
        buffers, sems = refs[position + 2], refs[position + 3]
        for n, piece in enumerate(streamed):
            first = pl.multiple_of(piece_columns(piece, sizes), LANES)
            copy = pltpu.make_async_copy(
                source.at[:, pl.ds(first, sizes.quarter)], buffers.at[n], sems.at[n]
            )
            copy.start()
            copies.append(copy)
            weights.append(buffers.at[n])
        position += 1
    out_ref = refs[position]
    width = sizes.quarter
    tile = min(width, 256)
    for n, (weight, copy) in enumerate(zip(weights, copies)):
        if copy is not None:
            copy.wait()

        def one(j, carry, n=n, weight=weight):
            at = pl.ds(pl.multiple_of(j * tile, tile), tile)
            to = pl.ds(pl.multiple_of(n * width + j * tile, tile), tile)
            begin = 0
            for part in attention:
                tokens = part.shape[0]
                result = dot(part[...], weight[:, at])
                if extra:
                    mate = extra[0][begin : begin + tokens, to]
                    result = result + mate.astype(jnp.float32)
                if turned:
                    out_ref[to, begin : begin + tokens] = result.T.astype(out_ref.dtype)
                else:
                    out_ref[begin : begin + tokens, to] = result.astype(out_ref.dtype)
                begin += tokens
            return carry

        lax.fori_loop(0, width // tile, one, 0)


def project(attention, weights, streamed, out_weight, mate, sizes, name, deps, pieces=()):
    tokens = sum(a.shape[0] for a in attention)
    columns = (len(weights) + len(streamed)) * sizes.quarter
    turned = mate is not None
    extra = [mate] if turned else []
    shape = (columns, tokens) if turned else (tokens, columns)
    operands = attention + weights + extra
    specs = [VMEM] * len(operands)
    scratch = []
    if streamed:
        operands = operands + [out_weight]
        specs = specs + [HBM]
        scratch = [
            pltpu.VMEM((len(streamed), sizes.depth, sizes.quarter), jnp.bfloat16),
            pltpu.SemaphoreType.DMA((len(streamed),)),
        ]
    result, new = run(
        functools.partial(
            project_kernel, parts=len(attention), count=len(weights), streamed=streamed,
            added=len(extra), turned=turned, sizes=sizes,
        ),
        [], operands, specs, deps,
        [jax.ShapeDtypeStruct(shape, jnp.bfloat16)], [VMEM], name, sizes,
        limit=36 if streamed or pieces else 16, scratch=scratch,
        pieces=pieces, weight=out_weight,
    )
    return result[0], new


def finish_kernel(ready, launch, part_ref, *refs):
    got, out_ref = refs[:-1], refs[-1]
    sums = part_ref[...].astype(jnp.float32)
    for ref in got:
        sums = sums + ref[...].astype(jnp.float32)
    out_ref[...] = sums.astype(jnp.bfloat16)


def finish(hidden, own, got, row, column, sizes, deps):
    height, count = got[0].shape
    tile = min(height, 512)
    first = row // tile
    block = column // count
    spec = pl.BlockSpec((tile, count), lambda j: (first + j, block))
    operands = [own] + got
    in_specs = [spec] + [pl.BlockSpec((tile, count), lambda j: (j, 0))] * len(got)
    aliases = None
    if hidden is not None:
        aliases = {len(operands): 0}
        deps = [hidden] + deps
    result, _ = run(
        finish_kernel, [], operands, in_specs, deps,
        [jax.ShapeDtypeStruct(own.shape, jnp.bfloat16)], [spec], "finish", sizes,
        grid=(height // tile,), aliases=aliases,
    )
    return result[0]


def shards(
    res_pool,
    res_table,
    res_len,
    out_pool,
    src_table,
    mig_len,
    mig_dest,
    queries,
    new_kv,
    out_weight,
):
    z = Sizes(queries, res_pool, res_table, src_table, mig_dest, out_weight)
    tps, insts, chips = z.tps, z.insts, z.chips
    table = res_table[0].T
    query_rows = queries.reshape(z.batch * z.per, z.width)

    from_inst = [[((i + k) % insts, i) for i in range(insts)] for k in range(1, insts)]
    to_mate = [(i, i + 1 - 2 * (i % CORES)) for i in range(tps)]
    far = range(1, chips)
    held = {}

    def mate_of(x):
        return lax.ppermute(x, "tp", to_mate)

    def across(x, ahead):
        shift = ahead * CORES
        return lax.ppermute(x, "tp", [(i, (i + shift) % tps) for i in range(tps)])

    def bringing(pieces):
        return dict(pieces=pieces, weight=out_weight)

    def gives(ks, parts):
        return [(k, False, part) for k in ks for part in parts]

    def keeps(ks, parts):
        return [(k, True, part) for k in ks for part in parts]

    def at_hand(pieces):
        here = [held[piece] for piece in pieces if piece in held]
        return here, [piece for piece in pieces if piece not in held]

    def hold(pieces, arrays):
        held.update(zip(pieces, arrays))

    def give(attention, ks, parts, name, deps, pieces=()):
        weights, streamed = at_hand(gives(ks, parts))
        result, new = project(
            attention, weights, streamed, out_weight, None, z, name, deps, pieces
        )
        hold(pieces, new)
        return result, mate_of(result)

    def keep(attention, ks, parts, mate, name, deps, pieces=()):
        results = []
        width = mate.shape[1] // len(ks)
        for n, k in enumerate(ks):
            weights, streamed = at_hand(keeps([k], parts))
            given = mate if len(ks) == 1 else mate[:, n * width : (n + 1) * width]
            now = pieces if n == 0 else ()
            result, new = project(
                attention, weights, streamed, out_weight, given, z, name, deps, now
            )
            hold(now, new)
            deps = [result]
            results.append(result)
        return results

    def sent(results):
        return [across(result, k) for k, result in zip(far, results)]

    def rows_of(n, first, rows, pool, deps, pieces):
        (piece, *pool_out), new = attend(
            table, res_len, query_rows, new_kv, pool, n == 0, first, rows, z, deps,
            **bringing(pieces),
        )
        hold(pieces, new)
        return piece, pool_out[0] if n == 0 else pool

    counts = (z.batch // 2, z.batch // 4, z.batch // 4)
    low, high, every = (0, 1), (2, 3), (0, 1, 2, 3)

    a, pool = rows_of(0, 0, counts[0], res_pool, [], gives(far, low) + keeps(far, low))
    given, mate = give([a], far, low, "give", [])
    (sends, tail), new = pack(
        src_table, mig_dest, out_pool, query_rows, new_kv, z, [given], **bringing(gives(far, (2,)))
    )
    hold(gives(far, (2,)), new)
    arriving = lax.all_to_all(sends, "inst", split_axis=0, concat_axis=0, tiled=True)
    kept = keep([a], far, low, mate, "keep", [tail], gives(far, (3,)))
    got_low = sent(kept)
    tails = [lax.ppermute(tail, "inst", perm) for perm in from_inst]
    given, mate = give([a], far, high, "give", [kept[-1]])
    b, _ = rows_of(1, counts[0], counts[1], pool, [given], keeps(far, high))
    kept = keep([a], far, high, mate, "keep", [b])
    got_high = sent(kept)
    served, _ = serve(src_table, mig_len, mig_dest, out_pool, tails, z, [kept[-1]])
    back = [lax.ppermute(served, "inst", perm) for perm in from_inst]
    given, mate = give([b], far, every, "give", [served] + got_low)
    c, _ = rows_of(2, counts[0] + counts[1], counts[2], pool, [given], [])
    kept = keep([b], far, every, mate, "keep", [c])
    got_b = sent(kept)
    c, _ = merge(mig_dest, c, back, z, [kept[-1]])
    given, mate = give([c], far, every, "give", got_high)
    own_given, own_mate = give([a, b, c], [0], every, "give_own", [given])
    kept = keep([c], far, every, mate, "keep", [own_given])
    got_c = sent(kept)
    own = keep([a, b, c], [0], every, own_mate, "keep_own", [kept[-1]])[0]
    arrived = assemble(mig_dest, mig_len, arriving, z, [own])

    hidden = finish(None, own, got_low, 0, 0, z, [])
    hidden = finish(hidden, own, got_high, z.features // 2, 0, z, [])
    hidden = finish(hidden, own, got_b, 0, counts[0] * z.steps, z, [])
    hidden = finish(hidden, own, got_c, 0, (counts[0] + counts[1]) * z.steps, z, [])
    return (arrived, hidden)


def solution(mesh):
    placed = (
        P(("groups", "inst"), "tp", None, None, None),
        P(("groups", "inst"), None, None),
        P(("groups", "inst"), None),
        P(("groups", "inst"), "tp", None, None, None),
        P(("groups", "inst"), None, None),
        P("groups"),
        P("groups"),
        P(("groups", "inst"), None, "tp", None),
        P(("groups", "inst"), None, "tp", None),
        P("tp", None),
    )
    return jax.shard_map(
        shards,
        mesh=mesh,
        in_specs=placed,
        out_specs=(P(("groups", "inst"), None, "tp", None, None), P("tp", ("groups", "inst"))),
        check_vma=False,
    )
```

time: 256 us -> 270 us (1.055)
  Pallas kernels: 0 us -> 193 us
  waiting for transfers between devices: 126 us -> 45.5 us
  matrix products: 55 us -> 0 us
  local copies, waits for them, and re-layouts: 38.4 us -> 9.43 us
  other arithmetic: 14.6 us -> 0 us
  starting transfers between devices: 6.45 us -> 20.3 us
  between operations: 14.3 us -> 1.02 us
    pallas_call x0 -> x21, Pallas kernels: none -> 193 us  [run(): pl.pallas_call(call, grid_spec=pltpu.PrefetchScalarGridSpec(num_scalar_pr...]
    reduce_scatter x1 -> x0, waiting for transfers between devices: 126 us -> none  [shards(): lax.psum_scatter(projector(out_weight, attention), 'tp', scatter_dimensio...]
    dot_general x9 -> x0, matrix products: 55 us -> none  [the longest x1 27.4 us: projector(): lax.dot_general(out_weight, attention, (((0,), (1,)), ((), ())), preferre...]
    ppermute x0 -> x15, waiting for transfers between devices: none -> 45.5 us  [the longest x3 39.8 us: shards(): tails = [lax.ppermute(tail, 'inst', perm) for perm in from_inst]]
    gather x4 -> x0, local copies, waits for them, and re-layouts: 30.3 us -> none  [the longest x2 26.2 us: shards(): context = res_pool[0][:, res_table[0]]]
    ppermute x0 -> x15, starting transfers between devices: none -> 15.3 us  [the longest x3 5.85 us: shards(): tails = [lax.ppermute(tail, 'inst', perm) for perm in from_inst]]
    unnamed x17 -> x62, local copies, waits for them, and re-layouts: 2.55 us -> 9.43 us
    reduce_sum x6 -> x0, other arithmetic: 5.87 us -> none  [the longest x4 5.55 us: attend(): totals = jnp.sum(cached_weights, axis=-1) + jnp.sum(fresh_weights, axis=-1)]
  transfers between devices with their start and end apart: 2 -> 16, of which waited for: 1 -> 4; matrix products, arithmetic and copies ran while one was open for 25% -> 0% of each run, Pallas kernels for 0% -> 20%
where the time goes in v3:
time: 270 us; the launch traced here: 269 us
  Pallas kernels  193 us (71%)
  waiting for transfers between devices  45.5 us (17%)
  starting transfers between devices  20.3 us (8%)
  local copies, waits for them, and re-layouts  9.43 us (3%)
    pallas_call x21, Pallas kernels, run(): pl.pallas_call(call, grid_spec=pltpu.PrefetchScalarGridSpec(num_scalar_pr...  193 us
    ppermute x3, waiting for transfers between devices, shards(): tails = [lax.ppermute(tail, 'inst', perm) for perm in from_inst]  39.8 us
    unnamed x62, local copies, waits for them, and re-layouts  9.43 us
    ppermute x3, starting transfers between devices, shards(): tails = [lax.ppermute(tail, 'inst', perm) for perm in from_inst]  5.85 us
  transfers between devices with their start and end apart: 16, of which 4 were waited for; matrix products, arithmetic and copies ran while one was open for 0% of the time, Pallas kernels for 20%

profile of v3, /device:TPU:0, one launch (start us, length us, event | category | flops | bytes accessed | tf_op | source)
XLA Modules:
  0.0 269.0 jit_solution(17366788001273076650)
XLA Ops:
  1.7 1.2 copy-done.23
  4.2 128.8 %attend.3 = (bf16[256,2048]{1,0:T(8,128)(2,1)S(1)}, bf16[1,2,64,16,256]{4,3,2,1,0:T(8,128)(2,1)S(1)}, bf16[2048,512]{1,0:T(8,128)(2,1)S(1)}, bf16[2048,512]{1,0:...) custom-call(s32[8,125]{1,0:T(8,128)S(1)} %bitcast.8, s32[1,125]{1,0:T(1,128)S(1)} %copy-done.27, ...), custom_call_target="tpu_custom_call" | custom-call | bytes 1024 | tf_op jit(solution)/shard_map/attend/pallas_call | solution.py:141
  134.1 1.8 give.4.refs_6_
  137.6 1.9 pack.1
  139.6 1.3 copy-done.20
  140.9 2.9 %keep.4 = (bf16[1024,256]{1,0:T(8,128)(2,1)}, bf16[2048,512]{1,0:T(8,128)(2,1)S(1)}) custom-call(bf16[256,2048]{1,0:T(8,128)(2,1)S(1)} %get-tuple-element.16.refs_0_, bf16[2048,512]{1,0:T(8,128)(2,1)S(1)} %copy-done.5, bf16[2048,512]{1,0:T(8,128)(2,1)S(1)} %copy-done.7, bf16[256,1024]{1,0:T(8,128)(2,1)S(1)} %collective-permute-done.refs_3_, ...), custom_call_target="tpu_custom_call" | custom-call | bytes 1024 | tf_op jit(solution)/shard_map/keep/pallas_call | solution.py:141
  143.8 2.6 give.5.refs_6_
  146.9 2.5 collective-permute-start.8
  149.4 5.0 %all-to-all-start = ((bf16[4,2,32,16,256]{4,3,2,1,0:T(8,128)(2,1)}), bf16[4,2,32,16,256]{4,3,2,1,0:T(8,128)(2,1)}, u32[]{:S(2)}, u32[]{:S(2)}) async-start(bf16[4,2,32,16,256]{4,3,2,1,0:T(8,128)(2,1)} %copy-done.20), calls=%async_computation | async-start | bytes 4194304 | tf_op jit(solution)/shard_map/all_to_all | solution.py:701
  154.4 2.0 collective-permute-start.3
  156.4 2.4 collective-permute-start.2
  158.8 1.5 collective-permute-start.1
  162.5 3.5 %attend.4 = (bf16[128,2048]{1,0:T(8,128)(2,1)S(1)}, bf16[2048,512]{1,0:T(8,128)(2,1)S(1)}, bf16[2048,512]{1,0:T(8,128)(2,1)S(1)}) custom-call(s32[8,125]{1,0:T(8,128)S(1)} %bitcast.9, s32[1,125]{1,0:T(1,128)S(1)} %copy-done.28, bf16[8192,128]{1,0:T(8,128)(2,1)S(1)} %bitcast.6, bf16[128,4,2,256]{3,2,1,0:T(2,128)(2,1)S(1)} %copy-done.15, ...), custom_call_target="tpu_custom_call" | custom-call | bytes 1024 | tf_op jit(solution)/shard_map/attend/pallas_call | solution.py:141
  166.0 3.3 %keep.5.refs_7_ = bf16[1024,256]{1,0:T(8,128)(2,1)S(1)} custom-call(bf16[256,2048]{1,0:T(8,128)(2,1)S(1)} %get-tuple-element.16.refs_0_, bf16[2048,512]{1,0:T(8,128)(2,1)S(1)} %get-tuple-element.28.refs_1_.refs_3_, bf16[2048,512]{1,0:T(8,128)(2,1)S(1)} %get-tuple-element.29.refs_2_.refs_4_, bf16[256,1024]{1,0:T(8,128)(2,1)} %collective-permute-done.4.refs_3_, ...), custom_call_target="tpu_custom_call" | custom-call | bytes 1024 | tf_op jit(solution)/shard_map/keep/pallas_call | solution.py:141
  169.3 26.1 %collective-permute-done.3.refs_6_ = bf16[320,128]{1,0:T(8,128)(2,1)S(1)} collective-permute-done((bf16[320,128]{1,0:T(8,128)(2,1)S(1)}, bf16[320,128]{1,0:T(8,128)(2,1)S(1)}, u32[]{:S(2)}, u32[]{:S(2)}) %collective-permute-start.3) | collective-permute-done | bytes 81952 | tf_op jit(solution)/shard_map/ppermute | solution.py:704
  195.5 13.7 %collective-permute-done.2.refs_5_ = bf16[320,128]{1,0:T(8,128)(2,1)S(1)} collective-permute-done((bf16[320,128]{1,0:T(8,128)(2,1)S(1)}, bf16[320,128]{1,0:T(8,128)(2,1)S(1)}, u32[]{:S(2)}, u32[]{:S(2)}) %collective-permute-start.2) | collective-permute-done | bytes 81952 | tf_op jit(solution)/shard_map/ppermute | solution.py:704
  209.2 1.4 serve.1.refs_5_
  210.6 2.6 give.6.refs_5_
  214.0 1.4 collective-permute-start.7
  215.4 1.5 collective-permute-start.6
  217.8 3.4 %attend.5.refs_6_.refs_4_ = bf16[128,2048]{1,0:T(8,128)(2,1)S(1)} custom-call(s32[8,125]{1,0:T(8,128)S(1)} %bitcast.10, s32[1,125]{1,0:T(1,128)S(1)} %copy-done.28, bf16[8192,128]{1,0:T(8,128)(2,1)S(1)} %bitcast.7, bf16[128,4,2,256]{3,2,1,0:T(2,128)(2,1)S(1)} %copy-done.15, bf16[1,2,64,16,256]{4,3,2,1,0:T(8,128)(2,1)S(1)} %copy-done.19, ...), custom_call_target="tpu_custom_call" | custom-call | bytes 1024 | tf_op jit(solution)/shard_map/attend/pallas_call | solution.py:141
  221.2 4.0 %keep.6.refs_5_ = bf16[2048,128]{1,0:T(8,128)(2,1)} custom-call(bf16[128,2048]{1,0:T(8,128)(2,1)S(1)} %get-tuple-element.27.refs_4_.refs_0_.refs_1_, bf16[2048,512]{1,0:T(8,128)(2,1)S(1)} %copy-done.6, bf16[2048,512]{1,0:T(8,128)(2,1)S(1)} %copy-done.8, bf16[2048,512]{1,0:T(8,128)(2,1)S(1)} %get-tuple-element.28.refs_1_.refs_3_, ...), custom_call_target="tpu_custom_call" | custom-call | bytes 1024 | tf_op jit(solution)/shard_map/keep/pallas_call | solution.py:141
  225.9 1.8 collective-permute-done.10.refs_5_.refs_1_
  227.7 2.6 give.7.refs_4_
  230.4 7.6 %give_own.1.refs_6_ = bf16[512,2048]{1,0:T(8,128)(2,1)S(1)} custom-call(bf16[256,2048]{1,0:T(8,128)(2,1)S(1)} %get-tuple-element.16.refs_0_, bf16[128,2048]{1,0:T(8,128)(2,1)S(1)} %get-tuple-element.27.refs_4_.refs_0_.refs_1_, bf16[128,2048]{1,0:T(8,128)(2,1)S(1)} %merge.1.refs_0_.refs_2_, bf16[2048,8192]{1,0:T(8,128)(2,1)} %refs_4_.7, ...), custom_call_target="tpu_custom_call" | custom-call | bytes 1024 | tf_op jit(solution)/shard_map/give_own/pallas_call | solution.py:141
  239.1 3.9 %collective-permute-done.12.refs_5_ = bf16[128,2048]{1,0:T(8,128)(2,1)S(1)} collective-permute-done((bf16[128,2048]{1,0:T(8,128)(2,1)S(1)}, bf16[128,2048]{1,0:T(8,128)(2,1)S(1)}, u32[]{:S(2)}, u32[]{:S(2)}) %collective-permute-start.12) | collective-permute-done | bytes 524320 | tf_op jit(solution)/shard_map/ppermute | solution.py:636
  243.0 4.0 %keep.7.refs_5_ = bf16[2048,128]{1,0:T(8,128)(2,1)} custom-call(bf16[128,2048]{1,0:T(8,128)(2,1)S(1)} %merge.1.refs_0_.refs_2_, bf16[2048,512]{1,0:T(8,128)(2,1)S(1)} %copy-done.6, bf16[2048,512]{1,0:T(8,128)(2,1)S(1)} %copy-done.8, bf16[2048,512]{1,0:T(8,128)(2,1)S(1)} %get-tuple-element.28.refs_1_.refs_3_, ...), custom_call_target="tpu_custom_call" | custom-call | bytes 1024 | tf_op jit(solution)/shard_map/keep/pallas_call | solution.py:141
  247.5 8.4 %keep_own.1.refs_3_.refs_0_ = bf16[2048,512]{1,0:T(8,128)(2,1)S(1)} custom-call(bf16[256,2048]{1,0:T(8,128)(2,1)S(1)} %get-tuple-element.16.refs_0_, bf16[128,2048]{1,0:T(8,128)(2,1)S(1)} %get-tuple-element.27.refs_4_.refs_0_.refs_1_, bf16[128,2048]{1,0:T(8,128)(2,1)S(1)} %merge.1.refs_0_.refs_2_, bf16[512,2048]{1,0:T(8,128)(2,1)S(1)} %collective-permute-done.11.refs_3_, ...), custom_call_target="tpu_custom_call" | custom-call | bytes 1024 | tf_op jit(solution)/shard_map/keep_own/pallas_call | solution.py:141
  255.9 1.8 finish.4.refs_2_
  257.8 3.8 %assemble.1 = bf16[1,3,2,512,256]{4,3,2,1,0:T(8,128)(2,1)} custom-call(s32[8]{0:T(128)S(1)} %copy-done.26, s32[8]{0:T(128)S(1)} %copy-done.30, bf16[4,2,32,16,256]{4,3,2,1,0:T(8,128)(2,1)} %all-to-all-done.refs_2_, bf16[2048,512]{1,0:T(8,128)(2,1)S(1)} %keep_own.1.refs_3_.refs_0_), custom_call_target="tpu_custom_call" | custom-call | bytes 1024 | tf_op jit(solution)/shard_map/assemble/pallas_call | solution.py:141
  262.5 3.2 %finish.6.refs_2_ = bf16[2048,512]{1,0:T(8,128)(2,1)} custom-call(bf16[2048,512]{1,0:T(8,128)(2,1)S(1)} %keep_own.1.refs_3_.refs_0_, bf16[2048,128]{1,0:T(8,128)(2,1)} %collective-permute-done.14.refs_1_, bf16[2048,512]{1,0:T(8,128)(2,1)} %finish.5.refs_2_), custom_call_target="tpu_custom_call", output_to_operand_aliasing={{}: (2, {})} | custom-call | bytes 1024 | tf_op jit(solution)/shard_map/finish/pallas_call | solution.py:141
  265.8 3.2 %finish.7 = bf16[2048,512]{1,0:T(8,128)(2,1)} custom-call(bf16[2048,512]{1,0:T(8,128)(2,1)S(1)} %keep_own.1.refs_3_.refs_0_, bf16[2048,128]{1,0:T(8,128)(2,1)} %collective-permute-done.13.refs_1_, bf16[2048,512]{1,0:T(8,128)(2,1)} %finish.6.refs_2_), custom_call_target="tpu_custom_call", output_to_operand_aliasing={{}: (2, {})} | custom-call | bytes 1024 | tf_op jit(solution)/shard_map/finish/pallas_call | solution.py:141
  (83 shorter events, 12.6 us)
Async XLA Ops:
  134.1 3.5 %copy-start.16 = (bf16[1,2,64,16,256]{4,3,2,1,0:T(8,128)(2,1)S(1)}, bf16[1,2,64,16,256]{4,3,2,1,0:T(8,128)(2,1)}, u32[]{:S(2)}) copy-start(bf16[1,2,64,16,256]{4,3,2,1,0:T(8,128)(2,1)} %refs_3_.7) | copy-start | bytes 3145732
  134.1 3.5 %copy-start.26 = (s32[8]{0:T(128)S(1)}, s32[8]{0:T(128)}, u32[]{:S(2)}) copy-start(s32[8]{0:T(128)} %refs_0_.7) | copy-start | bytes 100
  136.2 4.7 %copy-start.5 = (bf16[2048,512]{1,0:T(8,128)(2,1)S(1)}, bf16[2048,512]{1,0:T(8,128)(2,1)}, u32[]{:S(2)}) copy-start(bf16[2048,512]{1,0:T(8,128)(2,1)} %get-tuple-element.22.refs_1_) | copy-start | bytes 6291460
  136.2 4.7 %copy-start.7 = (bf16[2048,512]{1,0:T(8,128)(2,1)S(1)}, bf16[2048,512]{1,0:T(8,128)(2,1)}, u32[]{:S(2)}) copy-start(bf16[2048,512]{1,0:T(8,128)(2,1)} %get-tuple-element.23.refs_2_) | copy-start | bytes 6291460
  136.2 3.4 %collective-permute-start = (bf16[256,1024]{1,0:T(8,128)(2,1)S(1)}, bf16[256,1024]{1,0:T(8,128)(2,1)S(1)}, u32[]{:S(2)}, u32[]{:S(2)}) collective-permute-start(bf16[256,1024]{1,0:T(8,128)(2,1)S(1)} %give.4.refs_6_), channel_id=1, source_target_pairs={{0,1},{1,0},{2,3},{3,2},{4,5},{5,4},{6,7},{7,6},{8,9},{9,8},{10,11... | collective-permute-start | bytes 1572872 | tf_op jit(solution)/shard_map/ppermute | solution.py:636
  139.5 4.3 %copy-start.1 = (bf16[2048,512]{1,0:T(8,128)(2,1)}, bf16[2048,512]{1,0:T(8,128)(2,1)S(1)}, u32[]{:S(2)}) copy-start(bf16[2048,512]{1,0:T(8,128)(2,1)S(1)} %get-tuple-element.21.refs_1_.refs_3_) | copy-start | bytes 6291460
  146.4 19.6 %collective-permute-start.4 = (bf16[256,1024]{1,0:T(8,128)(2,1)}, bf16[256,1024]{1,0:T(8,128)(2,1)}, u32[]{:S(2)}, u32[]{:S(2)}) collective-permute-start(bf16[256,1024]{1,0:T(8,128)(2,1)} %give.5.refs_6_), channel_id=1, source_target_pairs={{0,1},{1,0},{2,3},{3,2},{4,5},{5,4},{6,7},{7,6},{8,9},{9,8},{10,11... | collective-permute-start | bytes 1572872 | tf_op jit(solution)/shard_map/ppermute | solution.py:636
  146.9 63.7 %collective-permute-start.8 = (bf16[1024,256]{1,0:T(8,128)(2,1)}, bf16[1024,256]{1,0:T(8,128)(2,1)}, u32[]{:S(2)}, u32[]{:S(2)}) collective-permute-start(bf16[1024,256]{1,0:T(8,128)(2,1)} %get-tuple-element.26.refs_3_), channel_id=1, source_target_pairs={{0,2},{1,3},{2,0},{3,1},{4,6},{5,7},{6,4},{7,5},{8,10},{9,11},{10,... | collective-permute-start | bytes 1572872 | tf_op jit(solution)/shard_map/ppermute | solution.py:640
  149.4 10.9 %copy-start.25 = (s32[1,125,8]{1,2,0:T(8,128)S(1)}, s32[1,125,8]{1,2,0:T(8,128)}, u32[]{:S(2)}) copy-start(s32[1,125,8]{1,2,0:T(8,128)} %param.11) | copy-start | bytes 12004
  149.4 10.9 %copy-start.28 = (s32[1,125]{1,0:T(1,128)S(1)}, s32[1,125]{1,0:T(1,128)}, u32[]{:S(2)}) copy-start(s32[1,125]{1,0:T(1,128)} %refs_1_.10) | copy-start | bytes 1504
  149.4 108.3 %all-to-all-start = ((bf16[4,2,32,16,256]{4,3,2,1,0:T(8,128)(2,1)}), bf16[4,2,32,16,256]{4,3,2,1,0:T(8,128)(2,1)}, u32[]{:S(2)}, u32[]{:S(2)}) async-start(bf16[4,2,32,16,256]{4,3,2,1,0:T(8,128)(2,1)} %copy-done.20), calls=%async_computation | async-start | bytes 4194304 | tf_op jit(solution)/shard_map/all_to_all | solution.py:701
  154.4 41.1 %collective-permute-start.3 = (bf16[320,128]{1,0:T(8,128)(2,1)S(1)}, bf16[320,128]{1,0:T(8,128)(2,1)S(1)}, u32[]{:S(2)}, u32[]{:S(2)}) collective-permute-start(bf16[320,128]{1,0:T(8,128)(2,1)S(1)} %get-tuple-element.24.refs_5_), channel_id=1, source_target_pairs={{12,0},{0,4},{4,8},{8,12},{13,1},{1,5},{5,9},{9,13},{14,2},{2,6},{... | collective-permute-start | bytes 245768 | tf_op jit(solution)/shard_map/ppermute | solution.py:704
  156.4 52.7 %collective-permute-start.2 = (bf16[320,128]{1,0:T(8,128)(2,1)S(1)}, bf16[320,128]{1,0:T(8,128)(2,1)S(1)}, u32[]{:S(2)}, u32[]{:S(2)}) collective-permute-start(bf16[320,128]{1,0:T(8,128)(2,1)S(1)} %get-tuple-element.24.refs_5_), channel_id=1, source_target_pairs={{8,0},{12,4},{0,8},{4,12},{9,1},{13,5},{1,9},{5,13},{10,2},{14,6},... | collective-permute-start | bytes 245768 | tf_op jit(solution)/shard_map/ppermute | solution.py:704
  158.8 50.3 %collective-permute-start.1 = (bf16[320,128]{1,0:T(8,128)(2,1)S(1)}, bf16[320,128]{1,0:T(8,128)(2,1)S(1)}, u32[]{:S(2)}, u32[]{:S(2)}) collective-permute-start(bf16[320,128]{1,0:T(8,128)(2,1)S(1)} %get-tuple-element.24.refs_5_), channel_id=1, source_target_pairs={{4,0},{8,4},{12,8},{0,12},{5,1},{9,5},{13,9},{1,13},{6,2},{10,6},{... | collective-permute-start | bytes 245768 | tf_op jit(solution)/shard_map/ppermute | solution.py:704
  162.5 46.6 %copy-start.17 = (bf16[1,2,64,16,256]{4,3,2,1,0:T(8,128)(2,1)S(1)}, bf16[1,2,64,16,256]{4,3,2,1,0:T(8,128)(2,1)}, u32[]{:S(2)}) copy-start(bf16[1,2,64,16,256]{4,3,2,1,0:T(8,128)(2,1)} %refs_3_.7) | copy-start | bytes 3145732
  162.5 46.6 %copy-start.30 = (s32[8]{0:T(128)S(1)}, s32[8]{0:T(128)}, u32[]{:S(2)}) copy-start(s32[8]{0:T(128)} %refs_1_.11) | copy-start | bytes 100
  166.0 44.6 %copy-start.2 = (bf16[2048,512]{1,0:T(8,128)(2,1)S(1)}, bf16[2048,512]{1,0:T(8,128)(2,1)}, u32[]{:S(2)}) copy-start(bf16[2048,512]{1,0:T(8,128)(2,1)} %copy-done.1) | copy-start | bytes 6291460
  166.0 44.6 %copy-start.4 = (bf16[2048,512]{1,0:T(8,128)(2,1)S(1)}, bf16[2048,512]{1,0:T(8,128)(2,1)}, u32[]{:S(2)}) copy-start(bf16[2048,512]{1,0:T(8,128)(2,1)} %copy-done.3) | copy-start | bytes 6291460
  166.0 44.6 %copy-start.10 = (bf16[2048,512]{1,0:T(8,128)(2,1)S(1)}, bf16[2048,512]{1,0:T(8,128)(2,1)}, u32[]{:S(2)}) copy-start(bf16[2048,512]{1,0:T(8,128)(2,1)} %copy-done.9) | copy-start | bytes 6291460
  166.0 44.6 %copy-start.12 = (bf16[2048,512]{1,0:T(8,128)(2,1)S(1)}, bf16[2048,512]{1,0:T(8,128)(2,1)}, u32[]{:S(2)}) copy-start(bf16[2048,512]{1,0:T(8,128)(2,1)} %copy-done.11) | copy-start | bytes 6291460
  213.3 7.9 %copy-start.6 = (bf16[2048,512]{1,0:T(8,128)(2,1)S(1)}, bf16[2048,512]{1,0:T(8,128)(2,1)}, u32[]{:S(2)}) copy-start(bf16[2048,512]{1,0:T(8,128)(2,1)} %get-tuple-element.22.refs_1_) | copy-start | bytes 6291460
  213.3 7.9 %copy-start.8 = (bf16[2048,512]{1,0:T(8,128)(2,1)S(1)}, bf16[2048,512]{1,0:T(8,128)(2,1)}, u32[]{:S(2)}) copy-start(bf16[2048,512]{1,0:T(8,128)(2,1)} %get-tuple-element.23.refs_2_) | copy-start | bytes 6291460
  213.3 7.9 %collective-permute-start.9 = (bf16[128,2048]{1,0:T(8,128)(2,1)S(1)}, bf16[128,2048]{1,0:T(8,128)(2,1)S(1)}, u32[]{:S(2)}, u32[]{:S(2)}) collective-permute-start(bf16[128,2048]{1,0:T(8,128)(2,1)S(1)} %give.6.refs_5_), channel_id=1, source_target_pairs={{0,1},{1,0},{2,3},{3,2},{4,5},{5,4},{6,7},{7,6},{8,9},{9,8},{10,11... | collective-permute-start | bytes 1572872 | tf_op jit(solution)/shard_map/ppermute | solution.py:636
  213.4 14.3 %collective-permute-start.10 = (bf16[1024,256]{1,0:T(8,128)(2,1)S(1)}, bf16[1024,256]{1,0:T(8,128)(2,1)S(1)}, u32[]{:S(2)}, u32[]{:S(2)}) collective-permute-start(bf16[1024,256]{1,0:T(8,128)(2,1)S(1)} %keep.5.refs_7_), channel_id=1, source_target_pairs={{0,2},{1,3},{2,0},{3,1},{4,6},{5,7},{6,4},{7,5},{8,10},{9,11},{10,... | collective-permute-start | bytes 1572872 | tf_op jit(solution)/shard_map/ppermute | solution.py:640
  214.0 11.3 %collective-permute-start.7 = (bf16[128,128]{1,0:T(8,128)(2,1)S(1)}, bf16[128,128]{1,0:T(8,128)(2,1)S(1)}, u32[]{:S(2)}, u32[]{:S(2)}) collective-permute-start(bf16[128,128]{1,0:T(8,128)(2,1)S(1)} %serve.1.refs_5_), channel_id=1, source_target_pairs={{12,0},{0,4},{4,8},{8,12},{13,1},{1,5},{5,9},{9,13},{14,2},{2,6},{... | collective-permute-start | bytes 98312 | tf_op jit(solution)/shard_map/ppermute | solution.py:710
  215.4 9.8 %collective-permute-start.6 = (bf16[128,128]{1,0:T(8,128)(2,1)S(1)}, bf16[128,128]{1,0:T(8,128)(2,1)S(1)}, u32[]{:S(2)}, u32[]{:S(2)}) collective-permute-start(bf16[128,128]{1,0:T(8,128)(2,1)S(1)} %serve.1.refs_5_), channel_id=1, source_target_pairs={{8,0},{12,4},{0,8},{4,12},{9,1},{13,5},{1,9},{5,13},{10,2},{14,6},... | collective-permute-start | bytes 98312 | tf_op jit(solution)/shard_map/ppermute | solution.py:710
  216.9 8.4 %collective-permute-start.5 = (bf16[128,128]{1,0:T(8,128)(2,1)S(1)}, bf16[128,128]{1,0:T(8,128)(2,1)S(1)}, u32[]{:S(2)}, u32[]{:S(2)}) collective-permute-start(bf16[128,128]{1,0:T(8,128)(2,1)S(1)} %serve.1.refs_5_), channel_id=1, source_target_pairs={{4,0},{8,4},{12,8},{0,12},{5,1},{9,5},{13,9},{1,13},{6,2},{10,6},{... | collective-permute-start | bytes 98312 | tf_op jit(solution)/shard_map/ppermute | solution.py:710
  238.0 9.5 %collective-permute-start.11 = (bf16[512,2048]{1,0:T(8,128)(2,1)S(1)}, bf16[512,2048]{1,0:T(8,128)(2,1)S(1)}, u32[]{:S(2)}, u32[]{:S(2)}) collective-permute-start(bf16[512,2048]{1,0:T(8,128)(2,1)S(1)} %give_own.1.refs_6_), channel_id=1, source_target_pairs={{0,1},{1,0},{2,3},{3,2},{4,5},{5,4},{6,7},{7,6},{8,9},{9,8},{10,11... | collective-permute-start | bytes 6291464 | tf_op jit(solution)/shard_map/ppermute | solution.py:636
  238.1 4.9 %collective-permute-start.12 = (bf16[128,2048]{1,0:T(8,128)(2,1)S(1)}, bf16[128,2048]{1,0:T(8,128)(2,1)S(1)}, u32[]{:S(2)}, u32[]{:S(2)}) collective-permute-start(bf16[128,2048]{1,0:T(8,128)(2,1)S(1)} %give.7.refs_4_), channel_id=1, source_target_pairs={{0,1},{1,0},{2,3},{3,2},{4,5},{5,4},{6,7},{7,6},{8,9},{9,8},{10,11... | collective-permute-start | bytes 1572872 | tf_op jit(solution)/shard_map/ppermute | solution.py:636
  238.6 24.0 %collective-permute-start.14 = (bf16[2048,128]{1,0:T(8,128)(2,1)}, bf16[2048,128]{1,0:T(8,128)(2,1)}, u32[]{:S(2)}, u32[]{:S(2)}) collective-permute-start(bf16[2048,128]{1,0:T(8,128)(2,1)} %keep.6.refs_5_), channel_id=1, source_target_pairs={{0,2},{1,3},{2,0},{3,1},{4,6},{5,7},{6,4},{7,5},{8,10},{9,11},{10,... | collective-permute-start | bytes 1572872 | tf_op jit(solution)/shard_map/ppermute | solution.py:640
  247.0 18.8 %collective-permute-start.13 = (bf16[2048,128]{1,0:T(8,128)(2,1)}, bf16[2048,128]{1,0:T(8,128)(2,1)}, u32[]{:S(2)}, u32[]{:S(2)}) collective-permute-start(bf16[2048,128]{1,0:T(8,128)(2,1)} %keep.7.refs_5_), channel_id=1, source_target_pairs={{0,2},{1,3},{2,0},{3,1},{4,6},{5,7},{6,4},{7,5},{8,10},{9,11},{10,... | collective-permute-start | bytes 1572872 | tf_op jit(solution)/shard_map/ppermute | solution.py:640
  257.7 3.9 %copy-start.22 = (bf16[1024,256]{1,0:T(8,128)(2,1)S(1)}, bf16[1024,256]{1,0:T(8,128)(2,1)}, u32[]{:S(2)}) copy-start(bf16[1024,256]{1,0:T(8,128)(2,1)} %copy-done.21) | copy-start | bytes 1572868
  (15 other events, 27.2 us)

commit v4 on v3

--- a/solution.py
+++ b/solution.py
@@ -30,14 +30,6 @@
         requests = [jnp.where(here & (seen == a), g, requests[a]) for a in range(cap)]
         seen = seen + here.astype(jnp.int32)
     return requests
-
-
-def standing_of(dest_ref, request):
-    dest = dest_ref[request]
-    standing = jnp.int32(0)
-    for g in range(dest_ref.shape[0]):
-        standing = standing + ((dest_ref[g] == dest) & (g < request)).astype(jnp.int32)
-    return dest, standing
 
 
 VMEM = pl.BlockSpec(memory_space=pltpu.VMEM)
@@ -160,16 +152,8 @@
     return result[:outputs], result[outputs:]
 
 
-def pack_kernel(
-    ready, launch, table_ref, dest_ref, pool_ref, query_ref, kv_ref, send_ref, tail_ref, *, sizes
-):
+def pack_kernel(ready, launch, table_ref, dest_ref, pool_ref, send_ref, *, sizes):
     inst = lax.axis_index("inst")
-    queries, keys, width = sizes.tail_q, sizes.tail_kv, sizes.width
-    launch()
-    tail_kv = kv_ref[...].reshape(keys, 2 * width)
-    tail_ref[:queries, :] = query_ref[...]
-    tail_ref[queries : queries + keys, :] = tail_kv[:, :width]
-    tail_ref[queries + keys :, :] = tail_kv[:, width:]
     ready()
     for m in range(sizes.mig_per):
         dest = dest_ref[inst * sizes.mig_per + m]
@@ -183,30 +167,15 @@
         lax.fori_loop(0, sizes.mig_blocks, copy_block, 0, unroll=8)
 
 
-def pack(src_table, mig_dest, out_pool, query_rows, new_kv, sizes, deps, **fetch):
+def pack(src_table, mig_dest, out_pool, sizes):
     z = sizes
-    shapes = (
-        jax.ShapeDtypeStruct(
-            (z.insts, z.slots, z.mig_blocks, z.block, 2 * z.width), out_pool.dtype
-        ),
-        jax.ShapeDtypeStruct((z.tail_q + 2 * z.tail_kv, z.width), out_pool.dtype),
-    )
-    last_q = query_rows.shape[0] // z.tail_q - 1
-    last_kv = z.batch // z.insts - 1
-    return run(
+    shape = (z.insts, z.slots, z.mig_blocks, z.block, 2 * z.width)
+    result, _ = run(
         functools.partial(pack_kernel, sizes=z),
-        [src_table, mig_dest],
-        [out_pool, query_rows, new_kv],
-        [
-            pl.BlockSpec(out_pool.shape, lambda i: (0, 0, 0, 0, 0)),
-            pl.BlockSpec((z.tail_q, z.width), lambda i: (last_q, 0)),
-            pl.BlockSpec((z.insts,) + new_kv.shape[1:], lambda i: (last_kv, 0, 0, 0)),
-        ],
-        deps,
-        shapes,
-        [VMEM, VMEM],
-        "pack", z, grid=(1,), **fetch,
-    )
+        [src_table, mig_dest], [out_pool], [VMEM], [],
+        [jax.ShapeDtypeStruct(shape, out_pool.dtype)], [VMEM], "pack", z,
+    )
+    return result[0]
 
 
 def arrived_kernel(ready, launch, dest_ref, len_ref, got_ref, out_ref, *, sizes):
@@ -216,9 +185,8 @@
     requests = row_plan(dest_ref, inst, sizes.cap)
     place = lax.broadcasted_iota(jnp.int32, (block, 2 * sizes.width), 0)
     for a in range(sizes.cap):
-        request = requests[a]
-        known = jnp.maximum(request, 0)
-        length = jnp.where(request >= 0, len_ref[known], 0)
+        known = jnp.maximum(requests[a], 0)
+        length = jnp.where(requests[a] >= 0, len_ref[known], 0)
         source = known // sizes.mig_per
 
         def one(b, carry, a=a, source=source, length=length):
@@ -300,12 +268,10 @@
 
 
 def attend_kernel(
-    ready, launch, table_ref, len_ref, query_hbm, kv_hbm, pool_in, out_ref, *refs,
-    first_row, steps_in_all, brings, sizes,
+    ready, launch, table_ref, len_ref, query_hbm, kv_hbm, pool_ref, out_ref, query_all, kv_all,
+    fresh_ref, pf_ref, blend_ref, done_ref, sems, *, first_row, steps_in_all, sizes,
 ):
     z = sizes
-    pool_ref, refs = (refs[0], refs[1:]) if brings else (pool_in, refs)
-    query_all, kv_all, fresh_ref, pf_ref, blend_ref, done_ref, sems = refs
     width, per = z.width, z.per
     rows = GROUP
     step = pl.program_id(0)
@@ -325,16 +291,11 @@
 
     @pl.when(step == 0)
     def _():
-        if brings:
-            pool_copy = pltpu.make_async_copy(pool_in, pool_ref, sems.at[2, 0])
-            pool_copy.start()
         for n in range(steps_in_all):
             for copy in copies(n):
                 copy.start()
         launch()
         ready()
-        if brings:
-            pool_copy.wait()
 
     for copy in copies(step):
         copy.wait()
@@ -377,23 +338,21 @@
         out_ref[:, h * width : (h + 1) * width] = column.astype(jnp.bfloat16)
 
 
-def attend(table, lengths, queries, new_kv, pool, brings, first_row, rows, sizes, deps, **fetch):
+def attend(table, lengths, queries, new_kv, pool, first_row, rows, sizes, deps, **fetch):
     z = sizes
     groups = rows // GROUP
     tokens = rows * z.steps
-    shapes = [jax.ShapeDtypeStruct((tokens, z.heads * z.width), jnp.bfloat16)]
-    specs = [pl.BlockSpec((GROUP * z.steps, z.heads * z.width), lambda i: (i, 0))]
-    if brings:
-        shapes.append(jax.ShapeDtypeStruct(pool.shape, pool.dtype))
-        specs.append(VMEM)
-    return run(
+    result, pieces = run(
         functools.partial(
-            attend_kernel, first_row=first_row, steps_in_all=groups, brings=brings, sizes=z
+            attend_kernel, first_row=first_row, steps_in_all=groups, sizes=z
         ),
         [table, lengths],
         [queries, new_kv, pool],
-        [HBM, HBM, HBM if brings else VMEM],
-        deps, shapes, specs, "attend", z, limit=46 if brings else 36,
+        [HBM, HBM, VMEM],
+        deps,
+        [jax.ShapeDtypeStruct((tokens, z.heads * z.width), jnp.bfloat16)],
+        [pl.BlockSpec((GROUP * z.steps, z.heads * z.width), lambda i: (i, 0))],
+        "attend", z, limit=36,
         grid=(groups,),
         scratch=[
             pltpu.VMEM((groups, GROUP * z.per, z.width), jnp.bfloat16),
@@ -402,131 +361,107 @@
             pltpu.VMEM((GROUP * z.per, GROUP * z.per_kv), jnp.bfloat16),
             pltpu.VMEM((GROUP * z.per, 2 * z.width), jnp.float32),
             pltpu.VMEM((GROUP * z.per, z.width), jnp.float32),
-            pltpu.SemaphoreType.DMA((3, groups)),
+            pltpu.SemaphoreType.DMA((2, groups)),
         ],
         **fetch,
     )
-
-
-def serve_kernel(ready, launch, table_ref, len_ref, dest_ref, pool_ref, *refs, sizes):
+    return result[0], pieces
+
+
+def settle_kernel(
+    ready, launch, dest_ref, len_ref, got_ref, query_ref, kv_ref, old_ref, out_ref, last_ref,
+    rows_ref, *, sizes
+):
     z = sizes
-    launch()
     ready()
-    tails, out_ref = refs[:-1], refs[-1]
     inst = lax.axis_index("inst")
-    queries, keys = z.tail_q, z.tail_kv
+    requests = row_plan(dest_ref, inst, z.cap)
     extent = z.mig_blocks * z.block
-    code = fresh_code(z.per, keys, z)
+    new_kv = kv_ref[...].reshape(z.tail_kv, 2 * z.width)
+    code = fresh_code(z.per, z.tail_kv, z)
     slot_of = slot_index(extent, z)
     scale = math.log2(math.e) / math.sqrt(z.width)
-    for m in range(z.mig_per):
-        request = inst * z.mig_per + m
-        dest, place = standing_of(dest_ref, request)
-        ahead = lax.rem(dest - inst + z.insts, z.insts)
-        begin = pl.multiple_of((place + 1) * z.per, z.per)
-        query = pick([ref[pl.ds(begin, z.per), :] for ref in tails], ahead - 1)
-        new_keys = pick([ref[queries : queries + keys, :] for ref in tails], ahead - 1)
-        new_values = pick([ref[queries + keys :, :] for ref in tails], ahead - 1)
-        ids = [table_ref[0, m, b] for b in range(z.mig_blocks)]
-        both = gather_blocks(pool_ref, z.slots, ids)
-        scores = dot_t(query, both[:, : z.width])
-        own, fresh = weigh(
-            own_scores(scores, slot_of, z.slots), len_ref[request],
-            dot_t(query, new_keys), code == place + 1, scale,
-        )
-        done = dot(spread(own, slot_of, z.slots), with_ones(both[:, z.width :]))
-        done = done + dot(fresh.astype(jnp.bfloat16), with_ones(new_values))
-        result = done[:, : z.width] / done[:, z.width :]
-        out_ref[m * z.per : (m + 1) * z.per, :] = result.astype(jnp.bfloat16)
-
-
-def pick(choices, index):
-    chosen = choices[0]
-    for k in range(1, len(choices)):
-        chosen = jnp.where(index == k, choices[k], chosen)
-    return chosen
-
-
-def serve(src_table, mig_len, mig_dest, out_pool, tails, sizes, deps, **fetch):
-    z = sizes
-    result, pieces = run(
-        functools.partial(serve_kernel, sizes=z),
-        [src_table, mig_len, mig_dest],
-        [out_pool] + tails,
-        [VMEM] * (1 + len(tails)),
-        deps,
-        [jax.ShapeDtypeStruct((z.mig_per * z.per, z.width), jnp.bfloat16)],
-        [VMEM], "serve", z, **fetch,
-    )
-    return result[0], pieces
-
-
-def merge_kernel(ready, launch, dest_ref, *refs, sizes):
-    z = sizes
-    launch()
-    ready()
-    back, old_ref, out_ref, rows_ref = refs[:-3], refs[-3], refs[-2], refs[-1]
-    inst = lax.axis_index("inst")
-    requests = row_plan(dest_ref, inst, z.cap)
-    for a in range(z.cap):
-        known = jnp.maximum(requests[a], 0)
-        ahead = lax.rem(known // z.mig_per - inst + z.insts, z.insts)
-        begin = pl.multiple_of(lax.rem(known, z.mig_per) * z.per, z.per)
-        served = pick([ref[pl.ds(begin, z.per), :].astype(jnp.float32) for ref in back], ahead - 1)
-        rows_ref[(a + 1) * z.per : (a + 2) * z.per, :] = served
-    rows_ref[: z.per, :] = jnp.zeros((z.per, z.width), jnp.float32)
     tokens = z.insts * z.steps
     row = lax.broadcasted_iota(jnp.int32, (tokens, z.width), 0) // z.steps
     filled = row < 0
+    rows_ref[: z.per, :] = jnp.zeros((z.per, z.width), jnp.float32)
     for a in range(z.cap):
+        at = slice((a + 1) * z.per, (a + 2) * z.per)
+        known = jnp.maximum(requests[a], 0)
+        source = known // z.mig_per
+        both = jnp.concatenate(
+            [got_ref[source, s].reshape(extent, 2 * z.width) for s in range(z.slots)], axis=0
+        )
+        own = own_scores(dot_t(query_ref[at, :], both[:, : z.width]), slot_of, z.slots)
+        fresh = dot_t(query_ref[at, :], new_kv[:, : z.width])
+        own, fresh = weigh(own, len_ref[known], fresh, code == a + 1, scale)
+        done = dot(spread(own, slot_of, z.slots), with_ones(both[:, z.width :]))
+        done = done + dot(fresh.astype(jnp.bfloat16), with_ones(new_kv[:, z.width :]))
+        rows_ref[at, :] = done[:, : z.width] / done[:, z.width :]
         filled = filled | ((row == a + 1) & (requests[a] >= 0))
     for h in range(z.heads):
         at = slice(h * z.width, (h + 1) * z.width)
         column = rows_ref[pl.ds(h, tokens, stride=z.heads), :]
         old = old_ref[:, at].astype(jnp.float32)
-        out_ref[:, at] = jnp.where(filled, column, old).astype(jnp.bfloat16)
-
-
-def merge(mig_dest, attention, back, sizes, deps, **fetch):
+        value = jnp.where(filled, column, old).astype(jnp.bfloat16)
+        out_ref[:, at] = value
+        last_ref[:, at] = value
+
+
+def settle(mig_dest, mig_len, got, query_rows, new_kv, attention, sizes, deps):
     z = sizes
     tokens = z.insts * z.steps
     last = attention.shape[0] // tokens - 1
+    last_q = query_rows.shape[0] // z.tail_q - 1
+    last_kv = z.batch // z.insts - 1
     spec = pl.BlockSpec((tokens, attention.shape[1]), lambda i: (last, 0))
-    result, pieces = run(
-        functools.partial(merge_kernel, sizes=z),
-        [mig_dest],
-        back + [attention],
-        [pl.BlockSpec(b.shape, lambda i: (0, 0)) for b in back] + [spec],
+    result, _ = run(
+        functools.partial(settle_kernel, sizes=z),
+        [mig_dest, mig_len], [got, query_rows, new_kv, attention],
+        [
+            VMEM,
+            pl.BlockSpec((z.tail_q, z.width), lambda i: (last_q, 0)),
+            pl.BlockSpec((z.insts,) + new_kv.shape[1:], lambda i: (last_kv, 0, 0, 0)),
+            spec,
+        ],
         deps,
-        [jax.ShapeDtypeStruct(attention.shape, jnp.bfloat16)],
-        [spec], "merge", z, grid=(1,),
+        [
+            jax.ShapeDtypeStruct(attention.shape, jnp.bfloat16),
+            jax.ShapeDtypeStruct((tokens, attention.shape[1]), jnp.bfloat16),
+        ],
+        [spec, VMEM], "settle", z, grid=(1,),
         scratch=[pltpu.VMEM((z.insts * z.per, z.width), jnp.float32)],
-        aliases={1 + len(back): 0}, **fetch,
-    )
-    return result[0], pieces
+        aliases={5: 0},
+    )
+    return result
 
 
 def project_kernel(
-    ready, launch, *refs, parts, count, streamed, added, turned, sizes
+    ready, launch, *refs, parts, count, streamed, added, joined, kept, sizes
 ):
     launch()
     attention, weights = refs[:parts], list(refs[parts : parts + count])
-    extra = refs[parts + count : parts + count + added]
-    position = parts + count + added
+    position = parts + count
+    extra = refs[position : position + added]
+    position += added
+    source = refs[position]
+    position += bool(streamed)
+    outs = 1 if joined else count + len(streamed)
+    out_refs = refs[position : position + outs]
     copies = [None] * count
     if streamed:
-        source = refs[position]
-        buffers, sems = refs[position + 2], refs[position + 3]
+        if kept:
+            buffers = refs[position + outs : position + outs + len(streamed)]
+        else:
+            buffers = [refs[-2].at[n] for n in range(len(streamed))]
         for n, piece in enumerate(streamed):
             first = pl.multiple_of(piece_columns(piece, sizes), LANES)
             copy = pltpu.make_async_copy(
-                source.at[:, pl.ds(first, sizes.quarter)], buffers.at[n], sems.at[n]
+                source.at[:, pl.ds(first, sizes.quarter)], buffers[n], refs[-1].at[n]
             )
             copy.start()
             copies.append(copy)
-            weights.append(buffers.at[n])
-        position += 1
-    out_ref = refs[position]
+            weights.append(buffers[n])
     width = sizes.quarter
     tile = min(width, 256)
     for n, (weight, copy) in enumerate(zip(weights, copies)):
@@ -535,76 +470,88 @@
 
         def one(j, carry, n=n, weight=weight):
             at = pl.ds(pl.multiple_of(j * tile, tile), tile)
-            to = pl.ds(pl.multiple_of(n * width + j * tile, tile), tile)
             begin = 0
             for part in attention:
                 tokens = part.shape[0]
+                rows = slice(begin, begin + tokens)
                 result = dot(part[...], weight[:, at])
-                if extra:
-                    mate = extra[0][begin : begin + tokens, to]
-                    result = result + mate.astype(jnp.float32)
-                if turned:
-                    out_ref[to, begin : begin + tokens] = result.T.astype(out_ref.dtype)
+                to = pl.ds(pl.multiple_of(n * width + j * tile, tile), tile)
+                if added == 1:
+                    result = result + extra[0][rows, to].astype(jnp.float32)
+                elif added:
+                    result = result + extra[n][rows, at].astype(jnp.float32)
+                if joined:
+                    out_refs[0][rows, to] = result.astype(jnp.bfloat16)
                 else:
-                    out_ref[begin : begin + tokens, to] = result.astype(out_ref.dtype)
+                    out_refs[n][rows, at] = result.astype(jnp.bfloat16)
                 begin += tokens
             return carry
 
         lax.fori_loop(0, width // tile, one, 0)
 
 
-def project(attention, weights, streamed, out_weight, mate, sizes, name, deps, pieces=()):
+def project(attention, weights, streamed, out_weight, mates, joined, kept, sizes, name, deps,
+            pieces=()):
     tokens = sum(a.shape[0] for a in attention)
-    columns = (len(weights) + len(streamed)) * sizes.quarter
-    turned = mate is not None
-    extra = [mate] if turned else []
-    shape = (columns, tokens) if turned else (tokens, columns)
-    operands = attention + weights + extra
+    count = len(weights) + len(streamed)
+    if joined:
+        shapes = [jax.ShapeDtypeStruct((tokens, count * sizes.quarter), jnp.bfloat16)]
+    else:
+        shapes = [jax.ShapeDtypeStruct((tokens, sizes.quarter), jnp.bfloat16)] * count
+    results = len(shapes)
+    operands = attention + weights + mates
     specs = [VMEM] * len(operands)
     scratch = []
+    piece = (sizes.depth, sizes.quarter)
     if streamed:
         operands = operands + [out_weight]
         specs = specs + [HBM]
-        scratch = [
-            pltpu.VMEM((len(streamed), sizes.depth, sizes.quarter), jnp.bfloat16),
-            pltpu.SemaphoreType.DMA((len(streamed),)),
-        ]
+        if kept:
+            shapes = shapes + [jax.ShapeDtypeStruct(piece, jnp.bfloat16)] * len(streamed)
+        else:
+            scratch.append(pltpu.VMEM((len(streamed),) + piece, jnp.bfloat16))
+        scratch.append(pltpu.SemaphoreType.DMA((len(streamed),)))
     result, new = run(
         functools.partial(
             project_kernel, parts=len(attention), count=len(weights), streamed=streamed,
-            added=len(extra), turned=turned, sizes=sizes,
+            added=len(mates), joined=joined, kept=kept, sizes=sizes,
         ),
-        [], operands, specs, deps,
-        [jax.ShapeDtypeStruct(shape, jnp.bfloat16)], [VMEM], name, sizes,
+        [], operands, specs, deps, shapes, [VMEM] * len(shapes), name, sizes,
         limit=36 if streamed or pieces else 16, scratch=scratch,
         pieces=pieces, weight=out_weight,
     )
-    return result[0], new
-
-
-def finish_kernel(ready, launch, part_ref, *refs):
-    got, out_ref = refs[:-1], refs[-1]
+    return result[:results], result[results:], new
+
+
+def finish_kernel(ready, launch, part_ref, *refs, count):
+    got, late, out_ref = refs[:count], refs[count:-1], refs[-1]
     sums = part_ref[...].astype(jnp.float32)
-    for ref in got:
-        sums = sums + ref[...].astype(jnp.float32)
-    out_ref[...] = sums.astype(jnp.bfloat16)
-
-
-def finish(hidden, own, got, row, column, sizes, deps):
-    height, count = got[0].shape
+    for n, ref in enumerate(got):
+        arrived = ref[...]
+        if late:
+            rows = late[n].shape[0]
+            arrived = jnp.concatenate([arrived[:-rows], late[n][...]], axis=0)
+        sums = sums + arrived.astype(jnp.float32)
+    out_ref[...] = sums.T.astype(jnp.bfloat16)
+
+
+def finish(hidden, own, got, late, row, column, sizes, deps):
+    count, height = got[0].shape
     tile = min(height, 512)
     first = row // tile
     block = column // count
     spec = pl.BlockSpec((tile, count), lambda j: (first + j, block))
-    operands = [own] + got
-    in_specs = [spec] + [pl.BlockSpec((tile, count), lambda j: (j, 0))] * len(got)
+    operands = [own] + got + late
+    in_specs = [pl.BlockSpec((count, tile), lambda j: (block, first + j))]
+    in_specs += [pl.BlockSpec((count, tile), lambda j: (0, j))] * len(got)
+    in_specs += [pl.BlockSpec((x.shape[0], tile), lambda j: (0, first + j)) for x in late]
     aliases = None
     if hidden is not None:
         aliases = {len(operands): 0}
         deps = [hidden] + deps
     result, _ = run(
-        finish_kernel, [], operands, in_specs, deps,
-        [jax.ShapeDtypeStruct(own.shape, jnp.bfloat16)], [spec], "finish", sizes,
+        functools.partial(finish_kernel, count=len(got)), [], operands, in_specs, deps,
+        [jax.ShapeDtypeStruct(own.shape[::-1], jnp.bfloat16)], [spec], "finish", sizes,
         grid=(height // tile,), aliases=aliases,
     )
     return result[0]
@@ -623,11 +570,10 @@
     out_weight,
 ):
     z = Sizes(queries, res_pool, res_table, src_table, mig_dest, out_weight)
-    tps, insts, chips = z.tps, z.insts, z.chips
+    tps, chips = z.tps, z.chips
     table = res_table[0].T
     query_rows = queries.reshape(z.batch * z.per, z.width)
 
-    from_inst = [[((i + k) % insts, i) for i in range(insts)] for k in range(1, insts)]
     to_mate = [(i, i + 1 - 2 * (i % CORES)) for i in range(tps)]
     far = range(1, chips)
     held = {}
@@ -655,75 +601,72 @@
     def hold(pieces, arrays):
         held.update(zip(pieces, arrays))
 
-    def give(attention, ks, parts, name, deps, pieces=()):
+    def give(attention, ks, parts, name, deps, pieces=(), kept=True, joined=False):
         weights, streamed = at_hand(gives(ks, parts))
-        result, new = project(
-            attention, weights, streamed, out_weight, None, z, name, deps, pieces
+        results, mine, new = project(
+            attention, weights, streamed, out_weight, [], joined, kept, z, name, deps, pieces
         )
+        if kept:
+            hold(streamed, mine)
         hold(pieces, new)
-        return result, mate_of(result)
-
-    def keep(attention, ks, parts, mate, name, deps, pieces=()):
+        return results[0], [mate_of(result) for result in results]
+
+    def keep(attention, ks, parts, mates, name, deps, kept=True):
         results = []
-        width = mate.shape[1] // len(ks)
         for n, k in enumerate(ks):
             weights, streamed = at_hand(keeps([k], parts))
-            given = mate if len(ks) == 1 else mate[:, n * width : (n + 1) * width]
-            now = pieces if n == 0 else ()
-            result, new = project(
-                attention, weights, streamed, out_weight, given, z, name, deps, now
+            if len(mates) == 1:
+                width = mates[0].shape[1] // len(ks)
+                now = [mates[0][:, n * width : (n + 1) * width] if len(ks) > 1 else mates[0]]
+            else:
+                now = mates[n * len(parts) : (n + 1) * len(parts)]
+            result, mine, _ = project(
+                attention, weights, streamed, out_weight, now, True, kept, z, name, deps
             )
-            hold(now, new)
-            deps = [result]
-            results.append(result)
+            if kept:
+                hold(streamed, mine)
+            deps = [result[0]]
+            results.append(result[0])
         return results
 
     def sent(results):
         return [across(result, k) for k, result in zip(far, results)]
 
-    def rows_of(n, first, rows, pool, deps, pieces):
-        (piece, *pool_out), new = attend(
-            table, res_len, query_rows, new_kv, pool, n == 0, first, rows, z, deps,
-            **bringing(pieces),
-        )
-        hold(pieces, new)
-        return piece, pool_out[0] if n == 0 else pool
-
-    counts = (z.batch // 2, z.batch // 4, z.batch // 4)
+    half = z.batch // 2
     low, high, every = (0, 1), (2, 3), (0, 1, 2, 3)
 
-    a, pool = rows_of(0, 0, counts[0], res_pool, [], gives(far, low) + keeps(far, low))
-    given, mate = give([a], far, low, "give", [])
-    (sends, tail), new = pack(
-        src_table, mig_dest, out_pool, query_rows, new_kv, z, [given], **bringing(gives(far, (2,)))
-    )
-    hold(gives(far, (2,)), new)
+    sends = pack(src_table, mig_dest, out_pool, z)
     arriving = lax.all_to_all(sends, "inst", split_axis=0, concat_axis=0, tiled=True)
-    kept = keep([a], far, low, mate, "keep", [tail], gives(far, (3,)))
-    got_low = sent(kept)
-    tails = [lax.ppermute(tail, "inst", perm) for perm in from_inst]
-    given, mate = give([a], far, high, "give", [kept[-1]])
-    b, _ = rows_of(1, counts[0], counts[1], pool, [given], keeps(far, high))
-    kept = keep([a], far, high, mate, "keep", [b])
-    got_high = sent(kept)
-    served, _ = serve(src_table, mig_len, mig_dest, out_pool, tails, z, [kept[-1]])
-    back = [lax.ppermute(served, "inst", perm) for perm in from_inst]
-    given, mate = give([b], far, every, "give", [served] + got_low)
-    c, _ = rows_of(2, counts[0] + counts[1], counts[2], pool, [given], [])
-    kept = keep([b], far, every, mate, "keep", [c])
+
+    a, new = attend(
+        table, res_len, query_rows, new_kv, res_pool, 0, half, z, [sends],
+        **bringing(gives(far, low) + keeps(far, low)),
+    )
+    hold(gives(far, low) + keeps(far, low), new)
+    given, mates = give([a], far, low, "give", [])
+    kept = keep([a], far, low, mates, "keep", [given])
+    got_a_low = sent(kept)
+    given, mates = give([a], far, high, "give", kept[-1:])
+    kept = keep([a], far, high, mates, "keep", [given])
+    got_a_high = sent(kept)
+    b, _ = attend(
+        table, res_len, query_rows, new_kv, res_pool, half, half, z, kept[-1:],
+    )
+    given, mates = give([b], far, every, "give", got_a_low)
+    kept = keep([b], far, every, mates, "keep", [given])
     got_b = sent(kept)
-    c, _ = merge(mig_dest, c, back, z, [kept[-1]])
-    given, mate = give([c], far, every, "give", got_high)
-    own_given, own_mate = give([a, b, c], [0], every, "give_own", [given])
-    kept = keep([c], far, every, mate, "keep", [own_given])
-    got_c = sent(kept)
-    own = keep([a, b, c], [0], every, own_mate, "keep_own", [kept[-1]])[0]
+    b, d = settle(mig_dest, mig_len, arriving, query_rows, new_kv, b, z, kept[-1:])
+    given, mates = give([d], far, every, "give_last", got_a_high, joined=True)
+    given, own_mates = give([a, b], [0], every, "give_own", [given], kept=False)
+    kept = keep([d], far, every, mates, "keep_last", [given])
+    got_d = sent(kept)
+    own = keep([a, b], [0], every, own_mates, "keep_own", kept[-1:], kept=False)[0]
+
     arrived = assemble(mig_dest, mig_len, arriving, z, [own])
-
-    hidden = finish(None, own, got_low, 0, 0, z, [])
-    hidden = finish(hidden, own, got_high, z.features // 2, 0, z, [])
-    hidden = finish(hidden, own, got_b, 0, counts[0] * z.steps, z, [])
-    hidden = finish(hidden, own, got_c, 0, (counts[0] + counts[1]) * z.steps, z, [])
+    tokens = half * z.steps
+    hidden = finish(None, own, got_a_low, [], 0, 0, z, [])
+    hidden = finish(hidden, own, got_a_high, [], z.features // 2, 0, z, [])
+    hidden = finish(hidden, own, got_b, got_d, 0, tokens, z, [])
     return (arrived, hidden)
 
 

time: 270 us -> 99.8 us (0.37)
  Pallas kernels: 193 us -> 65.9 us
  waiting for transfers between devices: 45.5 us -> 7.31 us
  starting transfers between devices: 20.3 us -> 13.9 us
    pallas_call x21 -> x18, Pallas kernels: 193 us -> 65.9 us  [run(): pl.pallas_call(call, grid_spec=pltpu.PrefetchScalarGridSpec(num_scalar_pr...]
    ppermute x6 -> x0, waiting for transfers between devices: 39.8 us -> none  [the longest x3 39.8 us: shards(): tails = [lax.ppermute(tail, 'inst', perm) for perm in from_inst]]
    ppermute x6 -> x0, starting transfers between devices: 9.67 us -> none  [the longest x3 5.85 us: shards(): tails = [lax.ppermute(tail, 'inst', perm) for perm in from_inst]]
    all_to_all x1, waiting for transfers between devices: 0.01 us -> 3.34 us  [shards(): lax.all_to_all(sends, 'inst', split_axis=0, concat_axis=0, tiled=True)]
  transfers between devices with their start and end apart: 16 -> 18, of which waited for: 4 -> 8; matrix products, arithmetic and copies ran while one was open for 0% -> 0% of each run, Pallas kernels for 20% -> 62%
where the time goes in v4:
time: 99.8 us; the launch traced here: 99.2 us
  Pallas kernels  65.9 us (66%)
  starting transfers between devices  13.9 us (14%)
  local copies, waits for them, and re-layouts  11.1 us (11%)
  waiting for transfers between devices  7.31 us (7%)
  between operations  1.02 us (1%)
    pallas_call x18, Pallas kernels, run(): pl.pallas_call(call, grid_spec=pltpu.PrefetchScalarGridSpec(num_scalar_pr...  65.9 us
    unnamed x62, local copies, waits for them, and re-layouts  11.1 us
    all_to_all x1, starting transfers between devices, shards(): lax.all_to_all(sends, 'inst', split_axis=0, concat_axis=0, tiled=True)  6.45 us
    ppermute x4, starting transfers between devices, across(): return lax.ppermute(x, 'tp', [(i, (i + shift) % tps) for i in range(tps)])  4.12 us
    ppermute x13, waiting for transfers between devices, mate_of(): return lax.ppermute(x, 'tp', to_mate)  3.95 us
    all_to_all x1, waiting for transfers between devices, shards(): lax.all_to_all(sends, 'inst', split_axis=0, concat_axis=0, tiled=True)  3.34 us
    ppermute x13, starting transfers between devices, mate_of(): return lax.ppermute(x, 'tp', to_mate)  3.34 us
  transfers between devices with their start and end apart: 18, of which 8 were waited for; matrix products, arithmetic and copies ran while one was open for 0% of the time, Pallas kernels for 62%

profile of v4, /device:TPU:0, one launch (start us, length us, event | category | flops | bytes accessed | tf_op | source)
XLA Modules:
  0.0 99.2 jit_solution(3848353391796545015)
XLA Ops:
  0.6 1.2 %copy-done.24 = bf16[1,2,64,16,256]{4,3,2,1,0:T(8,128)(2,1)S(1)} copy-done((bf16[1,2,64,16,256]{4,3,2,1,0:T(8,128)(2,1)S(1)}, bf16[1,2,64,16,256]{4,3,2,1,0:T(8,128)(2,1)}, u32[]{:S(2)}) %copy-start.24) | copy-done | bytes 1048600
  2.5 0.7 copy-done.30
  3.2 0.7 pack.1.refs_6_
  3.9 1.3 %copy-done.11 = bf16[4,2,32,16,256]{4,3,2,1,0:T(8,128)(2,1)} copy-done((bf16[4,2,32,16,256]{4,3,2,1,0:T(8,128)(2,1)}, bf16[4,2,32,16,256]{4,3,2,1,0:T(8,128)(2,1)S(1)}, u32[]{:S(2)}) %copy-start.11) | copy-done | bytes 2097176
  5.3 6.4 %all-to-all-start = ((bf16[4,2,32,16,256]{4,3,2,1,0:T(8,128)(2,1)}), bf16[4,2,32,16,256]{4,3,2,1,0:T(8,128)(2,1)}, u32[]{:S(2)}, u32[]{:S(2)}) async-start(bf16[4,2,32,16,256]{4,3,2,1,0:T(8,128)(2,1)} %copy-done.11), calls=%async_computation | async-start | bytes 4194304 | tf_op jit(solution)/shard_map/all_to_all | solution.py:639
  11.7 1.6 %copy-done.12 = bf16[4,2,32,16,256]{4,3,2,1,0:T(8,128)(2,1)S(1)} copy-done((bf16[4,2,32,16,256]{4,3,2,1,0:T(8,128)(2,1)S(1)}, bf16[4,2,32,16,256]{4,3,2,1,0:T(8,128)(2,1)}, u32[]{:S(2)}) %copy-start.12) | copy-done | bytes 2097176
  13.3 1.0 %copy-done.21 = bf16[128,4,2,256]{3,2,1,0:T(2,128)(2,1)S(1)} copy-done((bf16[128,4,2,256]{3,2,1,0:T(2,128)(2,1)S(1)}, bf16[128,4,2,256]{3,2,1,0:T(2,128)(2,1)}, u32[]{:S(2)}) %copy-start.21) | copy-done | bytes 524312
  14.4 1.2 %copy-done.23 = bf16[1,2,64,16,256]{4,3,2,1,0:T(8,128)(2,1)S(1)} copy-done((bf16[1,2,64,16,256]{4,3,2,1,0:T(8,128)(2,1)S(1)}, bf16[1,2,64,16,256]{4,3,2,1,0:T(8,128)(2,1)}, u32[]{:S(2)}) %copy-start.23) | copy-done | bytes 1048600
  15.6 6.3 %attend.2 = (bf16[256,2048]{1,0:T(8,128)(2,1)S(1)}, bf16[2048,512]{1,0:T(8,128)(2,1)S(1)}, bf16[2048,512]{1,0:T(8,128)(2,1)S(1)}, bf16[2048,512]{1,0:T(8,128)(2,1)S(1)}, bf16[2048,512]{1,0:T(8,128)(2,1)S(1)}) custom-call(s32[8,125]{1,0:T(8,128)S(1)} %bitcast.7, s32[1,125]{1,0:T(1,128)S(1)} %copy-done.29, bf16[8192,128]{1,0:T(8,128)(2,1)S(1)} %bitcast.4, ...), custom_call_target="tpu_custom_call" | custom-call | bytes 1024 | tf_op jit(solution)/shard_map/attend/pallas_call | solution.py:133
  21.9 1.8 %give.3 = (bf16[256,512]{1,0:T(8,128)(2,1)S(1)}, bf16[256,512]{1,0:T(8,128)(2,1)S(1)}) custom-call(bf16[256,2048]{1,0:T(8,128)(2,1)S(1)} %get-tuple-element.26.refs_0_, bf16[2048,512]{1,0:T(8,128)(2,1)S(1)} %get-tuple-element.29.refs_1_, bf16[2048,512]{1,0:T(8,128)(2,1)S(1)} %get-tuple-element.30.refs_2_), custom_call_target="tpu_custom_call" | custom-call | bytes 1024 | tf_op jit(solution)/shard_map/give/pallas_call | solution.py:133
  24.3 1.0 %collective-permute-done.1.refs_4_ = bf16[256,512]{1,0:T(8,128)(2,1)S(1)} collective-permute-done((bf16[256,512]{1,0:T(8,128)(2,1)S(1)}, bf16[256,512]{1,0:T(8,128)(2,1)S(1)}, u32[]{:S(2)}, u32[]{:S(2)}) %collective-permute-start.1) | collective-permute-done | bytes 262176 | tf_op jit(solution)/shard_map/ppermute | solution.py:582
  25.7 1.8 %keep.3.refs_2_ = bf16[256,1024]{1,0:T(8,128)(2,1)S(1)} custom-call(bf16[256,2048]{1,0:T(8,128)(2,1)S(1)} %get-tuple-element.26.refs_0_, bf16[2048,512]{1,0:T(8,128)(2,1)S(1)} %get-tuple-element.27.refs_1_, bf16[2048,512]{1,0:T(8,128)(2,1)S(1)} %get-tuple-element.28.refs_2_, bf16[256,512]{1,0:T(8,128)(2,1)S(1)} %collective-permute-done.refs_3_, ...), custom_call_target="tpu_custom_call" | custom-call | bytes 1024 | tf_op jit(solution)/shard_map/keep/pallas_call | solution.py:133
  27.5 1.6 %collective-permute-start.4 = (bf16[256,1024]{1,0:T(8,128)(2,1)S(1)}, bf16[256,1024]{1,0:T(8,128)(2,1)S(1)}, u32[]{:S(2)}, u32[]{:S(2)}) collective-permute-start(bf16[256,1024]{1,0:T(8,128)(2,1)S(1)} %keep.3.refs_2_), channel_id=1, source_target_pairs={{0,2},{1,3},{2,0},{3,1},{4,6},{5,7},{6,4},{7,5},{8,10},{9,11},{10,... | collective-permute-start | bytes 1572872 | tf_op jit(solution)/shard_map/ppermute | solution.py:586
  29.1 3.4 %give.4 = (bf16[256,512]{1,0:T(8,128)(2,1)S(1)}, bf16[256,512]{1,0:T(8,128)(2,1)S(1)}, bf16[2048,512]{1,0:T(8,128)(2,1)S(1)}, bf16[2048,512]{1,0:T(8,128)(2,1)S(1)}) custom-call(bf16[256,2048]{1,0:T(8,128)(2,1)S(1)} %get-tuple-element.26.refs_0_, bf16[2048,8192]{1,0:T(8,128)(2,1)} %refs_6_.1, bf16[256,1024]{1,0:T(8,128)(2,1)S(1)} %keep.3.refs_2_), custom_call_target="tpu_custom_call" | custom-call | bytes 1024 | tf_op jit(solution)/shard_map/give/pallas_call | solution.py:133
  33.1 1.0 %collective-permute-done.3.refs_2_ = bf16[256,512]{1,0:T(8,128)(2,1)S(1)} collective-permute-done((bf16[256,512]{1,0:T(8,128)(2,1)S(1)}, bf16[256,512]{1,0:T(8,128)(2,1)S(1)}, u32[]{:S(2)}, u32[]{:S(2)}) %collective-permute-start.3) | collective-permute-done | bytes 262176 | tf_op jit(solution)/shard_map/ppermute | solution.py:582
  34.5 4.4 %keep.4 = (bf16[256,1024]{1,0:T(8,128)(2,1)}, bf16[2048,512]{1,0:T(8,128)(2,1)S(1)}, bf16[2048,512]{1,0:T(8,128)(2,1)S(1)}) custom-call(bf16[256,2048]{1,0:T(8,128)(2,1)S(1)} %get-tuple-element.26.refs_0_, bf16[256,512]{1,0:T(8,128)(2,1)S(1)} %collective-permute-done.2.refs_1_, bf16[256,512]{1,0:T(8,128)(2,1)S(1)} %collective-permute-done.3.refs_2_, ...), custom_call_target="tpu_custom_call" | custom-call | bytes 1024 | tf_op jit(solution)/shard_map/keep/pallas_call | solution.py:133
  38.9 6.2 %attend.3.refs_0_.refs_5_ = bf16[256,2048]{1,0:T(8,128)(2,1)S(1)} custom-call(s32[8,125]{1,0:T(8,128)S(1)} %bitcast.8, s32[1,125]{1,0:T(1,128)S(1)} %copy-done.29, bf16[8192,128]{1,0:T(8,128)(2,1)S(1)} %bitcast.5, bf16[128,4,2,256]{3,2,1,0:T(2,128)(2,1)S(1)} %copy-done.21, bf16[1,2,64,16,256]{4,3,2,1,0:T(8,128)(2,1)S(1)} %copy-done.23, ...), custom_call_target="tpu_custom_call" | custom-call | bytes 1024 | tf_op jit(solution)/shard_map/attend/pallas_call | solution.py:133
  45.2 3.6 %give.5 = (bf16[256,512]{1,0:T(8,128)(2,1)S(1)}, bf16[256,512]{1,0:T(8,128)(2,1)S(1)}, bf16[256,512]{1,0:T(8,128)(2,1)S(1)}, bf16[256,512]{1,0:T(8,128)(2,1)S(1)}) custom-call(bf16[256,2048]{1,0:T(8,128)(2,1)S(1)} %attend.3.refs_0_.refs_5_, bf16[2048,512]{1,0:T(8,128)(2,1)S(1)} %get-tuple-element.29.refs_1_, ...), custom_call_target="tpu_custom_call" | custom-call | bytes 1024 | tf_op jit(solution)/shard_map/give/pallas_call | solution.py:133
  51.6 4.6 %keep.5.refs_6_ = bf16[256,2048]{1,0:T(8,128)(2,1)} custom-call(bf16[256,2048]{1,0:T(8,128)(2,1)S(1)} %attend.3.refs_0_.refs_5_, bf16[2048,512]{1,0:T(8,128)(2,1)S(1)} %get-tuple-element.27.refs_1_, bf16[2048,512]{1,0:T(8,128)(2,1)S(1)} %get-tuple-element.28.refs_2_, bf16[2048,512]{1,0:T(8,128)(2,1)S(1)} %get-tuple-element.36.refs_3_, ...), custom_call_target="tpu_custom_call" | custom-call | bytes 1024 | tf_op jit(solution)/shard_map/keep/pallas_call | solution.py:133
  56.7 3.3 %all-to-all-done.refs_2_ = bf16[4,2,32,16,256]{4,3,2,1,0:T(8,128)(2,1)} async-done(((bf16[4,2,32,16,256]{4,3,2,1,0:T(8,128)(2,1)}), bf16[4,2,32,16,256]{4,3,2,1,0:T(8,128)(2,1)}, u32[]{:S(2)}, u32[]{:S(2)}) %all-to-all-start) | async-done | bytes 2097184 | tf_op jit(solution)/shard_map/all_to_all | solution.py:639
  60.0 1.6 %copy-done.6 = bf16[128,4,16,128]{3,2,1,0:T(8,128)(2,1)S(1)} copy-done((bf16[128,4,16,128]{3,2,1,0:T(8,128)(2,1)S(1)}, bf16[128,4,16,128]{3,2,1,0:T(8,128)(2,1)}, u32[]{:S(2)}) %copy-start.6) | copy-done | bytes 2097176
  61.6 3.3 %settle.1 = (bf16[256,2048]{1,0:T(8,128)(2,1)S(1)}, bf16[16,2048]{1,0:T(8,128)(2,1)S(1)}) custom-call(s32[8]{0:T(128)S(1)} %copy-done.27, s32[8]{0:T(128)S(1)} %copy-done.28, bf16[4,2,32,16,256]{4,3,2,1,0:T(8,128)(2,1)} %all-to-all-done.refs_2_, bf16[8192,128]{1,0:T(8,128)(2,1)S(1)} %bitcast.6, ...), custom_call_target="tpu_custom_call", output_to_operand_aliasing={{0}: (5, {})} | custom-call | bytes 1024 | tf_op jit(solution)/shard_map/settle/pallas_call | solution.py:133
  65.1 1.6 %copy-done.16 = bf16[2048,512]{1,0:T(8,128)(2,1)S(1)} copy-done((bf16[2048,512]{1,0:T(8,128)(2,1)S(1)}, bf16[2048,512]{1,0:T(8,128)(2,1)}, u32[]{:S(2)}) %copy-start.16) | copy-done | bytes 2097176
  66.7 2.0 %give_last.1.refs_3_ = bf16[16,2048]{1,0:T(8,128)(2,1)S(1)} custom-call(bf16[16,2048]{1,0:T(8,128)(2,1)S(1)} %get-tuple-element.45.refs_0_, bf16[2048,512]{1,0:T(8,128)(2,1)S(1)} %copy-done.1, bf16[2048,512]{1,0:T(8,128)(2,1)S(1)} %copy-done.3, bf16[2048,512]{1,0:T(8,128)(2,1)S(1)} %copy-done.14, bf16[2048,512]{1,0:T(8,128)(2,1)S(1)} %copy-done.16, ...), custom_call_target="tpu_custom_call" | custom-call | bytes 1024 | tf_op jit(solution)/shard_map/give_last/pallas_call | solution.py:133
  68.8 7.7 %give_own.1 = (bf16[512,512]{1,0:T(8,128)(2,1)S(1)}, bf16[512,512]{1,0:T(8,128)(2,1)S(1)}, bf16[512,512]{1,0:T(8,128)(2,1)S(1)}, bf16[512,512]{1,0:T(8,128)(2,1)S(1)}) custom-call(bf16[256,2048]{1,0:T(8,128)(2,1)S(1)} %get-tuple-element.26.refs_0_, bf16[256,2048]{1,0:T(8,128)(2,1)S(1)} %get-tuple-element.44.refs_1_, bf16[2048,8192]{1,0:T(8,128)(2,1)} %refs_6_.1, ...), custom_call_target="tpu_custom_call" | custom-call | bytes 1024 | tf_op jit(solution)/shard_map/give_own/pallas_call | solution.py:133
  77.7 2.0 %keep_last.1.refs_7_ = bf16[16,2048]{1,0:T(8,128)(2,1)S(1)} custom-call(bf16[16,2048]{1,0:T(8,128)(2,1)S(1)} %get-tuple-element.45.refs_0_, bf16[2048,512]{1,0:T(8,128)(2,1)S(1)} %copy-done.8, bf16[2048,512]{1,0:T(8,128)(2,1)S(1)} %copy-done.10, bf16[2048,512]{1,0:T(8,128)(2,1)S(1)} %copy-done.18, bf16[2048,512]{1,0:T(8,128)(2,1)S(1)} %copy-done.20, ...), custom_call_target="tpu_custom_call" | custom-call | bytes 1024 | tf_op jit(solution)/shard_map/keep_last/pallas_call | solution.py:133
  79.7 1.6 %collective-permute-start.16 = (bf16[16,2048]{1,0:T(8,128)(2,1)S(1)}, bf16[16,2048]{1,0:T(8,128)(2,1)S(1)}, u32[]{:S(2)}, u32[]{:S(2)}) collective-permute-start(bf16[16,2048]{1,0:T(8,128)(2,1)S(1)} %keep_last.1.refs_7_), channel_id=1, source_target_pairs={{0,2},{1,3},{2,0},{3,1},{4,6},{5,7},{6,4},{7,5},{8,10},{9,11},{10,... | collective-permute-start | bytes 196616 | tf_op jit(solution)/shard_map/ppermute | solution.py:586
  81.3 7.4 %keep_own.1.refs_3_.refs_0_ = bf16[512,2048]{1,0:T(8,128)(2,1)S(1)} custom-call(bf16[256,2048]{1,0:T(8,128)(2,1)S(1)} %get-tuple-element.26.refs_0_, bf16[256,2048]{1,0:T(8,128)(2,1)S(1)} %get-tuple-element.44.refs_1_, bf16[512,512]{1,0:T(8,128)(2,1)S(1)} %collective-permute-done.10.refs_2_, bf16[512,512]{1,0:T(8,128)(2,1)S(1)} %collective-permute-done.11.refs_3_, ...), custom_call_target="tpu_custom_call" | custom-call | bytes 1024 | tf_op jit(solution)/shard_map/keep_own/pallas_call | solution.py:133
  88.7 3.8 %assemble.1 = bf16[1,3,2,512,256]{4,3,2,1,0:T(8,128)(2,1)} custom-call(s32[8]{0:T(128)S(1)} %copy-done.27, s32[8]{0:T(128)S(1)} %copy-done.28, bf16[4,2,32,16,256]{4,3,2,1,0:T(8,128)(2,1)} %all-to-all-done.refs_2_, bf16[512,2048]{1,0:T(8,128)(2,1)S(1)} %keep_own.1.refs_3_.refs_0_), custom_call_target="tpu_custom_call" | custom-call | bytes 1024 | tf_op jit(solution)/shard_map/assemble/pallas_call | solution.py:133
  92.5 1.1 %finish.3.refs_2_ = bf16[2048,512]{1,0:T(8,128)(2,1)} custom-call(bf16[512,2048]{1,0:T(8,128)(2,1)S(1)} %keep_own.1.refs_3_.refs_0_, bf16[256,1024]{1,0:T(8,128)(2,1)S(1)} %collective-permute-done.4.refs_5_.refs_1_), custom_call_target="tpu_custom_call" | custom-call | bytes 1024 | tf_op jit(solution)/shard_map/finish/pallas_call | solution.py:133
  93.6 2.0 %finish.4.refs_3_ = bf16[2048,512]{1,0:T(8,128)(2,1)} custom-call(bf16[512,2048]{1,0:T(8,128)(2,1)S(1)} %keep_own.1.refs_3_.refs_0_, bf16[256,1024]{1,0:T(8,128)(2,1)} %collective-permute-done.9.refs_5_.refs_1_, bf16[2048,512]{1,0:T(8,128)(2,1)} %finish.3.refs_2_), custom_call_target="tpu_custom_call", output_to_operand_aliasing={{}: (2, {})} | custom-call | bytes 1024 | tf_op jit(solution)/shard_map/finish/pallas_call | solution.py:133
  95.6 3.6 %finish.5 = bf16[2048,512]{1,0:T(8,128)(2,1)} custom-call(bf16[512,2048]{1,0:T(8,128)(2,1)S(1)} %keep_own.1.refs_3_.refs_0_, bf16[256,2048]{1,0:T(8,128)(2,1)} %collective-permute-done.15.refs_1_, bf16[16,2048]{1,0:T(8,128)(2,1)S(1)} %collective-permute-done.16.refs_2_, bf16[2048,512]{1,0:T(8,128)(2,1)} %finish.4.refs_3_), custom_call_target="tpu_custom_call", output_to_operand_aliasing={{}: (3, {})} | custom-call | bytes 1024 | tf_op jit(solution)/shard_map/finish/pallas_call | solution.py:133
  (84 shorter events, 7.1 us)
Async XLA Ops:
  5.3 54.8 %all-to-all-start = ((bf16[4,2,32,16,256]{4,3,2,1,0:T(8,128)(2,1)}), bf16[4,2,32,16,256]{4,3,2,1,0:T(8,128)(2,1)}, u32[]{:S(2)}, u32[]{:S(2)}) async-start(bf16[4,2,32,16,256]{4,3,2,1,0:T(8,128)(2,1)} %copy-done.11), calls=%async_computation | async-start | bytes 4194304 | tf_op jit(solution)/shard_map/all_to_all | solution.py:639
  21.9 23.3 %copy-start = (bf16[2048,512]{1,0:T(8,128)(2,1)}, bf16[2048,512]{1,0:T(8,128)(2,1)S(1)}, u32[]{:S(2)}) copy-start(bf16[2048,512]{1,0:T(8,128)(2,1)S(1)} %get-tuple-element.29.refs_1_) | copy-start | bytes 6291460
  21.9 23.3 %copy-start.2 = (bf16[2048,512]{1,0:T(8,128)(2,1)}, bf16[2048,512]{1,0:T(8,128)(2,1)S(1)}, u32[]{:S(2)}) copy-start(bf16[2048,512]{1,0:T(8,128)(2,1)S(1)} %get-tuple-element.30.refs_2_) | copy-start | bytes 6291460
  21.9 29.6 %copy-start.7 = (bf16[2048,512]{1,0:T(8,128)(2,1)}, bf16[2048,512]{1,0:T(8,128)(2,1)S(1)}, u32[]{:S(2)}) copy-start(bf16[2048,512]{1,0:T(8,128)(2,1)S(1)} %get-tuple-element.27.refs_1_) | copy-start | bytes 6291460
  21.9 29.6 %copy-start.9 = (bf16[2048,512]{1,0:T(8,128)(2,1)}, bf16[2048,512]{1,0:T(8,128)(2,1)S(1)}, u32[]{:S(2)}) copy-start(bf16[2048,512]{1,0:T(8,128)(2,1)S(1)} %get-tuple-element.28.refs_2_) | copy-start | bytes 6291460
  23.7 1.6 %collective-permute-start.1 = (bf16[256,512]{1,0:T(8,128)(2,1)S(1)}, bf16[256,512]{1,0:T(8,128)(2,1)S(1)}, u32[]{:S(2)}, u32[]{:S(2)}) collective-permute-start(bf16[256,512]{1,0:T(8,128)(2,1)S(1)} %get-tuple-element.32), channel_id=1, source_target_pairs={{0,1},{1,0},{2,3},{3,2},{4,5},{5,4},{6,7},{7,6},{8,9},{9,8},{10,11... | collective-permute-start | bytes 786440 | tf_op jit(solution)/shard_map/ppermute | solution.py:582
  23.8 1.9 %collective-permute-start = (bf16[256,512]{1,0:T(8,128)(2,1)S(1)}, bf16[256,512]{1,0:T(8,128)(2,1)S(1)}, u32[]{:S(2)}, u32[]{:S(2)}) collective-permute-start(bf16[256,512]{1,0:T(8,128)(2,1)S(1)} %get-tuple-element.31.refs_5_), channel_id=1, source_target_pairs={{0,1},{1,0},{2,3},{3,2},{4,5},{5,4},{6,7},{7,6},{8,9},{9,8},{10,11... | collective-permute-start | bytes 786440 | tf_op jit(solution)/shard_map/ppermute | solution.py:582
  27.5 17.6 %collective-permute-start.4 = (bf16[256,1024]{1,0:T(8,128)(2,1)S(1)}, bf16[256,1024]{1,0:T(8,128)(2,1)S(1)}, u32[]{:S(2)}, u32[]{:S(2)}) collective-permute-start(bf16[256,1024]{1,0:T(8,128)(2,1)S(1)} %keep.3.refs_2_), channel_id=1, source_target_pairs={{0,2},{1,3},{2,0},{3,1},{4,6},{5,7},{6,4},{7,5},{8,10},{9,11},{10,... | collective-permute-start | bytes 1572872 | tf_op jit(solution)/shard_map/ppermute | solution.py:586
  32.5 12.6 %copy-start.13 = (bf16[2048,512]{1,0:T(8,128)(2,1)}, bf16[2048,512]{1,0:T(8,128)(2,1)S(1)}, u32[]{:S(2)}) copy-start(bf16[2048,512]{1,0:T(8,128)(2,1)S(1)} %get-tuple-element.38.refs_3_) | copy-start | bytes 6291460
  32.5 12.6 %copy-start.15 = (bf16[2048,512]{1,0:T(8,128)(2,1)}, bf16[2048,512]{1,0:T(8,128)(2,1)S(1)}, u32[]{:S(2)}) copy-start(bf16[2048,512]{1,0:T(8,128)(2,1)S(1)} %get-tuple-element.39.refs_4_) | copy-start | bytes 6291460
  32.6 1.6 %collective-permute-start.3 = (bf16[256,512]{1,0:T(8,128)(2,1)S(1)}, bf16[256,512]{1,0:T(8,128)(2,1)S(1)}, u32[]{:S(2)}, u32[]{:S(2)}) collective-permute-start(bf16[256,512]{1,0:T(8,128)(2,1)S(1)} %get-tuple-element.34), channel_id=1, source_target_pairs={{0,1},{1,0},{2,3},{3,2},{4,5},{5,4},{6,7},{7,6},{8,9},{9,8},{10,11... | collective-permute-start | bytes 786440 | tf_op jit(solution)/shard_map/ppermute | solution.py:582
  32.6 1.9 %collective-permute-start.2 = (bf16[256,512]{1,0:T(8,128)(2,1)S(1)}, bf16[256,512]{1,0:T(8,128)(2,1)S(1)}, u32[]{:S(2)}, u32[]{:S(2)}) collective-permute-start(bf16[256,512]{1,0:T(8,128)(2,1)S(1)} %get-tuple-element.33.refs_4_), channel_id=1, source_target_pairs={{0,1},{1,0},{2,3},{3,2},{4,5},{5,4},{6,7},{7,6},{8,9},{9,8},{10,11... | collective-permute-start | bytes 786440 | tf_op jit(solution)/shard_map/ppermute | solution.py:582
  38.9 12.6 %copy-start.17 = (bf16[2048,512]{1,0:T(8,128)(2,1)}, bf16[2048,512]{1,0:T(8,128)(2,1)S(1)}, u32[]{:S(2)}) copy-start(bf16[2048,512]{1,0:T(8,128)(2,1)S(1)} %get-tuple-element.36.refs_3_) | copy-start | bytes 6291460
  38.9 12.6 %copy-start.19 = (bf16[2048,512]{1,0:T(8,128)(2,1)}, bf16[2048,512]{1,0:T(8,128)(2,1)S(1)}, u32[]{:S(2)}) copy-start(bf16[2048,512]{1,0:T(8,128)(2,1)S(1)} %get-tuple-element.37.refs_4_) | copy-start | bytes 6291460
  48.8 1.6 %collective-permute-start.6 = (bf16[256,512]{1,0:T(8,128)(2,1)S(1)}, bf16[256,512]{1,0:T(8,128)(2,1)S(1)}, u32[]{:S(2)}, u32[]{:S(2)}) collective-permute-start(bf16[256,512]{1,0:T(8,128)(2,1)S(1)} %get-tuple-element.41), channel_id=1, source_target_pairs={{0,1},{1,0},{2,3},{3,2},{4,5},{5,4},{6,7},{7,6},{8,9},{9,8},{10,11... | collective-permute-start | bytes 786440 | tf_op jit(solution)/shard_map/ppermute | solution.py:582
  48.9 1.9 %collective-permute-start.7 = (bf16[256,512]{1,0:T(8,128)(2,1)S(1)}, bf16[256,512]{1,0:T(8,128)(2,1)S(1)}, u32[]{:S(2)}, u32[]{:S(2)}) collective-permute-start(bf16[256,512]{1,0:T(8,128)(2,1)S(1)} %get-tuple-element.42), channel_id=1, source_target_pairs={{0,1},{1,0},{2,3},{3,2},{4,5},{5,4},{6,7},{7,6},{8,9},{9,8},{10,11... | collective-permute-start | bytes 786440 | tf_op jit(solution)/shard_map/ppermute | solution.py:582
  49.4 1.8 %collective-permute-start.8 = (bf16[256,512]{1,0:T(8,128)(2,1)S(1)}, bf16[256,512]{1,0:T(8,128)(2,1)S(1)}, u32[]{:S(2)}, u32[]{:S(2)}) collective-permute-start(bf16[256,512]{1,0:T(8,128)(2,1)S(1)} %get-tuple-element.43), channel_id=1, source_target_pairs={{0,1},{1,0},{2,3},{3,2},{4,5},{5,4},{6,7},{7,6},{8,9},{9,8},{10,11... | collective-permute-start | bytes 786440 | tf_op jit(solution)/shard_map/ppermute | solution.py:582
  49.4 2.1 %collective-permute-start.5 = (bf16[256,512]{1,0:T(8,128)(2,1)S(1)}, bf16[256,512]{1,0:T(8,128)(2,1)S(1)}, u32[]{:S(2)}, u32[]{:S(2)}) collective-permute-start(bf16[256,512]{1,0:T(8,128)(2,1)S(1)} %get-tuple-element.40.refs_9_), channel_id=1, source_target_pairs={{0,1},{1,0},{2,3},{3,2},{4,5},{5,4},{6,7},{7,6},{8,9},{9,8},{10,11... | collective-permute-start | bytes 786440 | tf_op jit(solution)/shard_map/ppermute | solution.py:582
  49.9 15.1 %collective-permute-start.9 = (bf16[256,1024]{1,0:T(8,128)(2,1)}, bf16[256,1024]{1,0:T(8,128)(2,1)}, u32[]{:S(2)}, u32[]{:S(2)}) collective-permute-start(bf16[256,1024]{1,0:T(8,128)(2,1)} %get-tuple-element.35.refs_5_), channel_id=1, source_target_pairs={{0,2},{1,3},{2,0},{3,1},{4,6},{5,7},{6,4},{7,5},{8,10},{9,11},{10,... | collective-permute-start | bytes 1572872 | tf_op jit(solution)/shard_map/ppermute | solution.py:586
  51.5 8.5 %copy-start.22 = (bf16[128,4,2,256]{3,2,1,0:T(2,128)(2,1)S(1)}, bf16[128,4,2,256]{3,2,1,0:T(2,128)(2,1)}, u32[]{:S(2)}) copy-start(bf16[128,4,2,256]{3,2,1,0:T(2,128)(2,1)} %refs_4_.5) | copy-start | bytes 1572868
  51.6 8.5 %copy-start.27 = (s32[8]{0:T(128)S(1)}, s32[8]{0:T(128)}, u32[]{:S(2)}) copy-start(s32[8]{0:T(128)} %refs_0_.5) | copy-start | bytes 100
  56.2 39.4 %collective-permute-start.15 = (bf16[256,2048]{1,0:T(8,128)(2,1)}, bf16[256,2048]{1,0:T(8,128)(2,1)}, u32[]{:S(2)}, u32[]{:S(2)}) collective-permute-start(bf16[256,2048]{1,0:T(8,128)(2,1)} %keep.5.refs_6_), channel_id=1, source_target_pairs={{0,2},{1,3},{2,0},{3,1},{4,6},{5,7},{6,4},{7,5},{8,10},{9,11},{10,... | collective-permute-start | bytes 3145736 | tf_op jit(solution)/shard_map/ppermute | solution.py:586
  68.7 8.8 %collective-permute-start.14 = (bf16[16,2048]{1,0:T(8,128)(2,1)S(1)}, bf16[16,2048]{1,0:T(8,128)(2,1)S(1)}, u32[]{:S(2)}, u32[]{:S(2)}) collective-permute-start(bf16[16,2048]{1,0:T(8,128)(2,1)S(1)} %give_last.1.refs_3_), channel_id=1, source_target_pairs={{0,1},{1,0},{2,3},{3,2},{4,5},{5,4},{6,7},{7,6},{8,9},{9,8},{10,11... | collective-permute-start | bytes 196616 | tf_op jit(solution)/shard_map/ppermute | solution.py:582
  68.7 8.9 %copy-start.8 = (bf16[2048,512]{1,0:T(8,128)(2,1)S(1)}, bf16[2048,512]{1,0:T(8,128)(2,1)}, u32[]{:S(2)}) copy-start(bf16[2048,512]{1,0:T(8,128)(2,1)} %copy-done.7) | copy-start | bytes 6291460
  68.7 8.9 %copy-start.10 = (bf16[2048,512]{1,0:T(8,128)(2,1)S(1)}, bf16[2048,512]{1,0:T(8,128)(2,1)}, u32[]{:S(2)}) copy-start(bf16[2048,512]{1,0:T(8,128)(2,1)} %copy-done.9) | copy-start | bytes 6291460
  68.8 8.9 %copy-start.18 = (bf16[2048,512]{1,0:T(8,128)(2,1)S(1)}, bf16[2048,512]{1,0:T(8,128)(2,1)}, u32[]{:S(2)}) copy-start(bf16[2048,512]{1,0:T(8,128)(2,1)} %copy-done.17) | copy-start | bytes 6291460
  68.8 8.9 %copy-start.20 = (bf16[2048,512]{1,0:T(8,128)(2,1)S(1)}, bf16[2048,512]{1,0:T(8,128)(2,1)}, u32[]{:S(2)}) copy-start(bf16[2048,512]{1,0:T(8,128)(2,1)} %copy-done.19) | copy-start | bytes 6291460
  76.5 3.2 %collective-permute-start.11 = (bf16[512,512]{1,0:T(8,128)(2,1)S(1)}, bf16[512,512]{1,0:T(8,128)(2,1)S(1)}, u32[]{:S(2)}, u32[]{:S(2)}) collective-permute-start(bf16[512,512]{1,0:T(8,128)(2,1)S(1)} %get-tuple-element.47), channel_id=1, source_target_pairs={{0,1},{1,0},{2,3},{3,2},{4,5},{5,4},{6,7},{7,6},{8,9},{9,8},{10,11... | collective-permute-start | bytes 1572872 | tf_op jit(solution)/shard_map/ppermute | solution.py:582
  77.1 4.2 %collective-permute-start.12 = (bf16[512,512]{1,0:T(8,128)(2,1)S(1)}, bf16[512,512]{1,0:T(8,128)(2,1)S(1)}, u32[]{:S(2)}, u32[]{:S(2)}) collective-permute-start(bf16[512,512]{1,0:T(8,128)(2,1)S(1)} %get-tuple-element.48), channel_id=1, source_target_pairs={{0,1},{1,0},{2,3},{3,2},{4,5},{5,4},{6,7},{7,6},{8,9},{9,8},{10,11... | collective-permute-start | bytes 1572872 | tf_op jit(solution)/shard_map/ppermute | solution.py:582
  77.1 4.1 %collective-permute-start.13 = (bf16[512,512]{1,0:T(8,128)(2,1)S(1)}, bf16[512,512]{1,0:T(8,128)(2,1)S(1)}, u32[]{:S(2)}, u32[]{:S(2)}) collective-permute-start(bf16[512,512]{1,0:T(8,128)(2,1)S(1)} %get-tuple-element.49), channel_id=1, source_target_pairs={{0,1},{1,0},{2,3},{3,2},{4,5},{5,4},{6,7},{7,6},{8,9},{9,8},{10,11... | collective-permute-start | bytes 1572872 | tf_op jit(solution)/shard_map/ppermute | solution.py:582
  77.6 3.7 %collective-permute-start.10 = (bf16[512,512]{1,0:T(8,128)(2,1)S(1)}, bf16[512,512]{1,0:T(8,128)(2,1)S(1)}, u32[]{:S(2)}, u32[]{:S(2)}) collective-permute-start(bf16[512,512]{1,0:T(8,128)(2,1)S(1)} %get-tuple-element.46.refs_6_), channel_id=1, source_target_pairs={{0,1},{1,0},{2,3},{3,2},{4,5},{5,4},{6,7},{7,6},{8,9},{9,8},{10,11... | collective-permute-start | bytes 1572872 | tf_op jit(solution)/shard_map/ppermute | solution.py:582
  79.7 15.9 %collective-permute-start.16 = (bf16[16,2048]{1,0:T(8,128)(2,1)S(1)}, bf16[16,2048]{1,0:T(8,128)(2,1)S(1)}, u32[]{:S(2)}, u32[]{:S(2)}) collective-permute-start(bf16[16,2048]{1,0:T(8,128)(2,1)S(1)} %keep_last.1.refs_7_), channel_id=1, source_target_pairs={{0,2},{1,3},{2,0},{3,1},{4,6},{5,7},{6,4},{7,5},{8,10},{9,11},{10,... | collective-permute-start | bytes 196616 | tf_op jit(solution)/shard_map/ppermute | solution.py:586
  (17 other events, 55.3 us)

commit v5 on v4

--- a/solution.py
+++ b/solution.py
@@ -14,6 +14,7 @@
 LANES = 128
 GROUP = 16
 TOGETHER = 8
+LARGE_FIRST = 40
 
 
 def dot_t(left, right):
@@ -173,40 +174,7 @@
     result, _ = run(
         functools.partial(pack_kernel, sizes=z),
         [src_table, mig_dest], [out_pool], [VMEM], [],
-        [jax.ShapeDtypeStruct(shape, out_pool.dtype)], [VMEM], "pack", z,
-    )
-    return result[0]
-
-
-def arrived_kernel(ready, launch, dest_ref, len_ref, got_ref, out_ref, *, sizes):
-    ready()
-    inst = lax.axis_index("inst")
-    block = sizes.block
-    requests = row_plan(dest_ref, inst, sizes.cap)
-    place = lax.broadcasted_iota(jnp.int32, (block, 2 * sizes.width), 0)
-    for a in range(sizes.cap):
-        known = jnp.maximum(requests[a], 0)
-        length = jnp.where(requests[a] >= 0, len_ref[known], 0)
-        source = known // sizes.mig_per
-
-        def one(b, carry, a=a, source=source, length=length):
-            inside = place + b * block < length
-            at = pl.ds(pl.multiple_of(b * block, block), block)
-            for s in range(sizes.slots):
-                value = got_ref[source, s, b].astype(jnp.float32)
-                out_ref[0, a, s, at, :] = jnp.where(inside, value, 0.0).astype(jnp.bfloat16)
-            return carry
-
-        lax.fori_loop(0, sizes.mig_blocks, one, 0, unroll=4)
-
-
-def assemble(mig_dest, mig_len, got, sizes, deps):
-    z = sizes
-    shape = (1, z.cap, z.slots, z.mig_blocks * z.block, 2 * z.width)
-    result, _ = run(
-        functools.partial(arrived_kernel, sizes=z),
-        [mig_dest, mig_len], [got], [VMEM], deps,
-        [jax.ShapeDtypeStruct(shape, jnp.bfloat16)], [VMEM], "assemble", z,
+        [jax.ShapeDtypeStruct(shape, out_pool.dtype)], [VMEM], "pack", z, limit=60,
     )
     return result[0]
 
@@ -338,7 +306,7 @@
         out_ref[:, h * width : (h + 1) * width] = column.astype(jnp.bfloat16)
 
 
-def attend(table, lengths, queries, new_kv, pool, first_row, rows, sizes, deps, **fetch):
+def attend(table, lengths, queries, new_kv, pool, first_row, rows, sizes, deps, limit=12, **fetch):
     z = sizes
     groups = rows // GROUP
     tokens = rows * z.steps
@@ -352,7 +320,7 @@
         deps,
         [jax.ShapeDtypeStruct((tokens, z.heads * z.width), jnp.bfloat16)],
         [pl.BlockSpec((GROUP * z.steps, z.heads * z.width), lambda i: (i, 0))],
-        "attend", z, limit=36,
+        "attend", z, limit=limit,
         grid=(groups,),
         scratch=[
             pltpu.VMEM((groups, GROUP * z.per, z.width), jnp.bfloat16),
@@ -369,32 +337,54 @@
 
 
 def settle_kernel(
-    ready, launch, dest_ref, len_ref, got_ref, query_ref, kv_ref, old_ref, out_ref, last_ref,
-    rows_ref, *, sizes
+    ready, launch, dest_ref, len_ref, got_hbm, query_ref, kv_ref, old_ref, out_ref, last_ref,
+    arrived_hbm, rows_ref, got_ref, keep_ref, sems, *, sizes
 ):
     z = sizes
+    launch()
     ready()
     inst = lax.axis_index("inst")
     requests = row_plan(dest_ref, inst, z.cap)
+    known = [jnp.maximum(request, 0) for request in requests]
     extent = z.mig_blocks * z.block
+    reads = [
+        pltpu.make_async_copy(got_hbm.at[known[a] // z.mig_per], got_ref.at[a], sems.at[0, a])
+        for a in range(z.cap)
+    ]
+    writes = [
+        pltpu.make_async_copy(keep_ref.at[a], arrived_hbm.at[0, a], sems.at[1, a])
+        for a in range(z.cap)
+    ]
+    for read in reads:
+        read.start()
     new_kv = kv_ref[...].reshape(z.tail_kv, 2 * z.width)
     code = fresh_code(z.per, z.tail_kv, z)
     slot_of = slot_index(extent, z)
     scale = math.log2(math.e) / math.sqrt(z.width)
     tokens = z.insts * z.steps
     row = lax.broadcasted_iota(jnp.int32, (tokens, z.width), 0) // z.steps
+    place = lax.broadcasted_iota(jnp.int32, (z.block, 2 * z.width), 0)
     filled = row < 0
     rows_ref[: z.per, :] = jnp.zeros((z.per, z.width), jnp.float32)
     for a in range(z.cap):
+        length = jnp.where(requests[a] >= 0, len_ref[known[a]], 0)
+        reads[a].wait()
+
+        def one(b, carry, a=a, length=length):
+            inside = place + b * z.block < length
+            at = pl.ds(pl.multiple_of(b * z.block, z.block), z.block)
+            for s in range(z.slots):
+                value = got_ref[a, s, b].astype(jnp.float32)
+                keep_ref[a, s, at, :] = jnp.where(inside, value, 0.0).astype(jnp.bfloat16)
+            return carry
+
+        lax.fori_loop(0, z.mig_blocks, one, 0, unroll=8)
+        writes[a].start()
         at = slice((a + 1) * z.per, (a + 2) * z.per)
-        known = jnp.maximum(requests[a], 0)
-        source = known // z.mig_per
-        both = jnp.concatenate(
-            [got_ref[source, s].reshape(extent, 2 * z.width) for s in range(z.slots)], axis=0
-        )
+        both = jnp.concatenate([keep_ref[a, s] for s in range(z.slots)], axis=0)
         own = own_scores(dot_t(query_ref[at, :], both[:, : z.width]), slot_of, z.slots)
         fresh = dot_t(query_ref[at, :], new_kv[:, : z.width])
-        own, fresh = weigh(own, len_ref[known], fresh, code == a + 1, scale)
+        own, fresh = weigh(own, length, fresh, code == a + 1, scale)
         done = dot(spread(own, slot_of, z.slots), with_ones(both[:, z.width :]))
         done = done + dot(fresh.astype(jnp.bfloat16), with_ones(new_kv[:, z.width :]))
         rows_ref[at, :] = done[:, : z.width] / done[:, z.width :]
@@ -406,20 +396,23 @@
         value = jnp.where(filled, column, old).astype(jnp.bfloat16)
         out_ref[:, at] = value
         last_ref[:, at] = value
-
-
-def settle(mig_dest, mig_len, got, query_rows, new_kv, attention, sizes, deps):
+    for write in writes:
+        write.wait()
+
+
+def settle(mig_dest, mig_len, got, query_rows, new_kv, attention, sizes, deps, **fetch):
     z = sizes
     tokens = z.insts * z.steps
     last = attention.shape[0] // tokens - 1
     last_q = query_rows.shape[0] // z.tail_q - 1
     last_kv = z.batch // z.insts - 1
     spec = pl.BlockSpec((tokens, attention.shape[1]), lambda i: (last, 0))
-    result, _ = run(
+    cache = (z.slots, z.mig_blocks * z.block, 2 * z.width)
+    return run(
         functools.partial(settle_kernel, sizes=z),
         [mig_dest, mig_len], [got, query_rows, new_kv, attention],
         [
-            VMEM,
+            HBM,
             pl.BlockSpec((z.tail_q, z.width), lambda i: (last_q, 0)),
             pl.BlockSpec((z.insts,) + new_kv.shape[1:], lambda i: (last_kv, 0, 0, 0)),
             spec,
@@ -428,12 +421,17 @@
         [
             jax.ShapeDtypeStruct(attention.shape, jnp.bfloat16),
             jax.ShapeDtypeStruct((tokens, attention.shape[1]), jnp.bfloat16),
+            jax.ShapeDtypeStruct((1, z.cap) + cache, jnp.bfloat16),
         ],
-        [spec, VMEM], "settle", z, grid=(1,),
-        scratch=[pltpu.VMEM((z.insts * z.per, z.width), jnp.float32)],
-        aliases={5: 0},
-    )
-    return result
+        [spec, VMEM, ANY], "settle", z, grid=(1,),
+        scratch=[
+            pltpu.VMEM((z.insts * z.per, z.width), jnp.float32),
+            pltpu.VMEM((z.cap,) + got.shape[1:], jnp.bfloat16),
+            pltpu.VMEM((z.cap,) + cache, jnp.bfloat16),
+            pltpu.SemaphoreType.DMA((2, z.cap)),
+        ],
+        aliases={5: 0}, **fetch,
+    )
 
 
 def project_kernel(
@@ -523,36 +521,91 @@
     return result[:results], result[results:], new
 
 
-def finish_kernel(ready, launch, part_ref, *refs, count):
-    got, late, out_ref = refs[:count], refs[count:-1], refs[-1]
-    sums = part_ref[...].astype(jnp.float32)
-    for n, ref in enumerate(got):
-        arrived = ref[...]
-        if late:
-            rows = late[n].shape[0]
-            arrived = jnp.concatenate([arrived[:-rows], late[n][...]], axis=0)
-        sums = sums + arrived.astype(jnp.float32)
-    out_ref[...] = sums.T.astype(jnp.bfloat16)
-
-
-def finish(hidden, own, got, late, row, column, sizes, deps):
-    count, height = got[0].shape
-    tile = min(height, 512)
-    first = row // tile
-    block = column // count
-    spec = pl.BlockSpec((tile, count), lambda j: (first + j, block))
-    operands = [own] + got + late
-    in_specs = [pl.BlockSpec((count, tile), lambda j: (block, first + j))]
-    in_specs += [pl.BlockSpec((count, tile), lambda j: (0, j))] * len(got)
-    in_specs += [pl.BlockSpec((x.shape[0], tile), lambda j: (0, first + j)) for x in late]
-    aliases = None
-    if hidden is not None:
-        aliases = {len(operands): 0}
-        deps = [hidden] + deps
+def final_kernel(ready, launch, *refs, parts, count, streamed, mates, fars, sizes):
+    z = sizes
+    refs = list(refs)
+
+    def take(n):
+        taken = refs[:n]
+        del refs[:n]
+        return taken
+
+    attention, weights, extra = take(parts), take(count), take(mates)
+    low, high, second, late = take(fars), take(fars), take(fars), take(fars)
+    source = take(bool(streamed))
+    (out_hbm,) = take(1)
+    block_ref, block_sems = take(2)
+    copies = [None] * count
+    for n, piece in enumerate(streamed):
+        first = pl.multiple_of(piece_columns(piece, z), LANES)
+        copy = pltpu.make_async_copy(
+            source[0].at[:, pl.ds(first, z.quarter)], refs[0].at[n], refs[1].at[n]
+        )
+        copy.start()
+        copies.append(copy)
+        weights.append(refs[0].at[n])
+    tile = min(z.quarter, 256)
+    writes = []
+    for n, (weight, copy) in enumerate(zip(weights, copies)):
+        if copy is not None:
+            copy.wait()
+
+        def one(j, carry, n=n, weight=weight):
+            start = pl.multiple_of(j * tile, tile)
+            at = pl.ds(start, tile)
+            whole = pl.ds(n * z.quarter + start, tile)
+            half = pl.ds((n % 2) * z.quarter + start, tile)
+            begin = 0
+            for p, part in enumerate(attention):
+                tokens = part.shape[0]
+                rows = slice(begin, begin + tokens)
+                sums = dot(part[...], weight[:, at]) + extra[n][rows, at].astype(jnp.float32)
+                for k in range(fars):
+                    if p == 0:
+                        arrived = (low if n < 2 else high)[k][:, half]
+                    else:
+                        count = late[k].shape[0]
+                        arrived = jnp.concatenate(
+                            [second[k][: tokens - count, whole], late[k][:, whole]], axis=0
+                        )
+                    sums = sums + arrived.astype(jnp.float32)
+                block_ref[n, at, rows] = sums.T.astype(jnp.bfloat16)
+                begin += tokens
+            return carry
+
+        lax.fori_loop(0, z.quarter // tile, one, 0)
+        write = pltpu.make_async_copy(
+            block_ref.at[n], out_hbm.at[pl.ds(n * z.quarter, z.quarter)], block_sems.at[n]
+        )
+        write.start()
+        writes.append(write)
+    for write in writes:
+        write.wait()
+
+
+def final(attention, weights, streamed, out_weight, mates, low, high, second, late, sizes, deps):
+    z = sizes
+    tokens = sum(a.shape[0] for a in attention)
+    operands = attention + weights + mates + low + high + second + late
+    specs = [VMEM] * len(operands)
+    scratch = [
+        pltpu.VMEM((4, z.quarter, tokens), jnp.bfloat16), pltpu.SemaphoreType.DMA((4,))
+    ]
+    if streamed:
+        operands = operands + [out_weight]
+        specs = specs + [HBM]
+        scratch += [
+            pltpu.VMEM((len(streamed), z.depth, z.quarter), jnp.bfloat16),
+            pltpu.SemaphoreType.DMA((len(streamed),)),
+        ]
     result, _ = run(
-        functools.partial(finish_kernel, count=len(got)), [], operands, in_specs, deps,
-        [jax.ShapeDtypeStruct(own.shape[::-1], jnp.bfloat16)], [spec], "finish", sizes,
-        grid=(height // tile,), aliases=aliases,
+        functools.partial(
+            final_kernel, parts=len(attention), count=len(weights), streamed=streamed,
+            mates=len(mates), fars=len(low), sizes=z,
+        ),
+        [], operands, specs, deps,
+        [jax.ShapeDtypeStruct((z.features, tokens), jnp.bfloat16)], [ANY], "final", z,
+        limit=36 if streamed else 24, scratch=scratch,
     )
     return result[0]
 
@@ -639,34 +692,36 @@
     arriving = lax.all_to_all(sends, "inst", split_axis=0, concat_axis=0, tiled=True)
 
     a, new = attend(
-        table, res_len, query_rows, new_kv, res_pool, 0, half, z, [sends],
+        table, res_len, query_rows, new_kv, res_pool, 0, half, z, [sends], limit=LARGE_FIRST,
         **bringing(gives(far, low) + keeps(far, low)),
     )
     hold(gives(far, low) + keeps(far, low), new)
     given, mates = give([a], far, low, "give", [])
     kept = keep([a], far, low, mates, "keep", [given])
-    got_a_low = sent(kept)
+    got_low = sent(kept)
     given, mates = give([a], far, high, "give", kept[-1:])
     kept = keep([a], far, high, mates, "keep", [given])
-    got_a_high = sent(kept)
-    b, _ = attend(
+    got_high = sent(kept)
+    b, new = attend(
         table, res_len, query_rows, new_kv, res_pool, half, half, z, kept[-1:],
-    )
-    given, mates = give([b], far, every, "give", got_a_low)
-    kept = keep([b], far, every, mates, "keep", [given])
-    got_b = sent(kept)
-    b, d = settle(mig_dest, mig_len, arriving, query_rows, new_kv, b, z, kept[-1:])
-    given, mates = give([d], far, every, "give_last", got_a_high, joined=True)
-    given, own_mates = give([a, b], [0], every, "give_own", [given], kept=False)
+        **bringing(gives([0], every)),
+    )
+    hold(gives([0], every), new)
+    given, mates = give([b], far, every, "give", got_low)
+    kept = keep([b], far, every, mates, "keep", [given] + got_high)
+    got_second = sent(kept)
+    (b, d, arrived), new = settle(
+        mig_dest, mig_len, arriving, query_rows, new_kv, b, z, kept[-1:]
+    )
+    given, mates = give([d], far, every, "give_last", [], joined=True)
+    given, own_mates = give([a, b], [0], every, "give_own", [given])
     kept = keep([d], far, every, mates, "keep_last", [given])
-    got_d = sent(kept)
-    own = keep([a, b], [0], every, own_mates, "keep_own", kept[-1:], kept=False)[0]
-
-    arrived = assemble(mig_dest, mig_len, arriving, z, [own])
-    tokens = half * z.steps
-    hidden = finish(None, own, got_a_low, [], 0, 0, z, [])
-    hidden = finish(hidden, own, got_a_high, [], z.features // 2, 0, z, [])
-    hidden = finish(hidden, own, got_b, got_d, 0, tokens, z, [])
+    got_late = sent(kept)
+    weights, streamed = at_hand(keeps([0], every))
+    hidden = final(
+        [a, b], weights, streamed, out_weight, own_mates, got_low, got_high, got_second, got_late,
+        z, kept[-1:],
+    )
     return (arrived, hidden)
 
 

time: 99.8 us -> 102 us (1.022)
  Pallas kernels: 65.9 us -> 59.5 us
  local copies, waits for them, and re-layouts: 11.1 us -> 15.5 us
  waiting for transfers between devices: 7.31 us -> 10.9 us
    ppermute x4, waiting for transfers between devices: 0.02 us -> 6.48 us  [across(): return lax.ppermute(x, 'tp', [(i, (i + shift) % tps) for i in range(tps)])]
    pallas_call x18 -> x14, Pallas kernels: 65.9 us -> 59.5 us  [run(): pl.pallas_call(call, grid_spec=pltpu.PrefetchScalarGridSpec(num_scalar_pr...]
    unnamed x62 -> x80, local copies, waits for them, and re-layouts: 11.1 us -> 15.5 us
    all_to_all x1, waiting for transfers between devices: 3.34 us -> 0.01 us  [shards(): lax.all_to_all(sends, 'inst', split_axis=0, concat_axis=0, tiled=True)]
  transfers between devices with their start and end apart: 18 -> 18, of which waited for: 8 -> 10; matrix products, arithmetic and copies ran while one was open for 0% -> 0% of each run, Pallas kernels for 62% -> 45%
where the time goes in v5:
time: 102 us
  Pallas kernels  59.5 us (58%)
  local copies, waits for them, and re-layouts  15.5 us (15%)
  starting transfers between devices  14.8 us (15%)
  waiting for transfers between devices  10.9 us (11%)
  between operations  1.24 us (1%)
    pallas_call x14, Pallas kernels, run(): pl.pallas_call(call, grid_spec=pltpu.PrefetchScalarGridSpec(num_scalar_pr...  59.5 us
    unnamed x80, local copies, waits for them, and re-layouts  15.5 us
    ppermute x4, waiting for transfers between devices, across(): return lax.ppermute(x, 'tp', [(i, (i + shift) % tps) for i in range(tps)])  6.48 us
    all_to_all x1, starting transfers between devices, shards(): lax.all_to_all(sends, 'inst', split_axis=0, concat_axis=0, tiled=True)  6.46 us
    ppermute x4, starting transfers between devices, across(): return lax.ppermute(x, 'tp', [(i, (i + shift) % tps) for i in range(tps)])  5.11 us
    ppermute x13, waiting for transfers between devices, mate_of(): return lax.ppermute(x, 'tp', to_mate)  4.44 us
    ppermute x13, starting transfers between devices, mate_of(): return lax.ppermute(x, 'tp', to_mate)  3.24 us
  transfers between devices with their start and end apart: 18, of which 10 were waited for; matrix products, arithmetic and copies ran while one was open for 0% of the time, Pallas kernels for 45%

profile of v5, /device:TPU:0, one launch (start us, length us, event | category | flops | bytes accessed | tf_op | source)
XLA Modules:
  0.0 101.9 jit_solution(9174997557944133786)
XLA Ops:
  0.6 3.4 %pack.1.refs_6_ = bf16[4,2,32,16,256]{4,3,2,1,0:T(8,128)(2,1)} custom-call(s32[1,2,32]{2,1,0:T(2,128)} %refs_0_.2, s32[8]{0:T(128)} %refs_0_.3, bf16[1,2,64,16,256]{4,3,2,1,0:T(8,128)(2,1)} %refs_2_.1), custom_call_target="tpu_custom_call" | custom-call | bytes 1024 | tf_op jit(solution)/shard_map/pack/pallas_call | solution.py:134
  4.1 6.5 %all-to-all-start = ((bf16[4,2,32,16,256]{4,3,2,1,0:T(8,128)(2,1)}), bf16[4,2,32,16,256]{4,3,2,1,0:T(8,128)(2,1)}, u32[]{:S(2)}, u32[]{:S(2)}) async-start(bf16[4,2,32,16,256]{4,3,2,1,0:T(8,128)(2,1)} %pack.1.refs_6_), calls=%async_computation | async-start | bytes 4194304 | tf_op jit(solution)/shard_map/all_to_all | solution.py:692
  10.6 1.0 %copy-done.23 = bf16[128,4,2,256]{3,2,1,0:T(2,128)(2,1)S(1)} copy-done((bf16[128,4,2,256]{3,2,1,0:T(2,128)(2,1)S(1)}, bf16[128,4,2,256]{3,2,1,0:T(2,128)(2,1)}, u32[]{:S(2)}) %copy-start.23) | copy-done | bytes 524312
  11.6 1.2 %copy-done.25 = bf16[1,2,64,16,256]{4,3,2,1,0:T(8,128)(2,1)S(1)} copy-done((bf16[1,2,64,16,256]{4,3,2,1,0:T(8,128)(2,1)S(1)}, bf16[1,2,64,16,256]{4,3,2,1,0:T(8,128)(2,1)}, u32[]{:S(2)}) %copy-start.25) | copy-done | bytes 1048600
  12.8 6.3 %attend.2 = (bf16[256,2048]{1,0:T(8,128)(2,1)S(1)}, bf16[2048,512]{1,0:T(8,128)(2,1)S(1)}, bf16[2048,512]{1,0:T(8,128)(2,1)S(1)}, bf16[2048,512]{1,0:T(8,128)(2,1)S(1)}, bf16[2048,512]{1,0:T(8,128)(2,1)S(1)}) custom-call(s32[8,125]{1,0:T(8,128)S(1)} %bitcast.7, s32[1,125]{1,0:T(1,128)S(1)} %copy-done.38, bf16[8192,128]{1,0:T(8,128)(2,1)S(1)} %bitcast.4, ...), custom_call_target="tpu_custom_call" | custom-call | bytes 1024 | tf_op jit(solution)/shard_map/attend/pallas_call | solution.py:134
  19.1 1.8 %give.3 = (bf16[256,512]{1,0:T(8,128)(2,1)S(1)}, bf16[256,512]{1,0:T(8,128)(2,1)S(1)}) custom-call(bf16[256,2048]{1,0:T(8,128)(2,1)S(1)} %get-tuple-element.32.refs_0_, bf16[2048,512]{1,0:T(8,128)(2,1)S(1)} %get-tuple-element.35.refs_1_, bf16[2048,512]{1,0:T(8,128)(2,1)S(1)} %get-tuple-element.36.refs_2_), custom_call_target="tpu_custom_call" | custom-call | bytes 1024 | tf_op jit(solution)/shard_map/give/pallas_call | solution.py:134
  21.5 1.0 %collective-permute-done.1.refs_4_ = bf16[256,512]{1,0:T(8,128)(2,1)S(1)} collective-permute-done((bf16[256,512]{1,0:T(8,128)(2,1)S(1)}, bf16[256,512]{1,0:T(8,128)(2,1)S(1)}, u32[]{:S(2)}, u32[]{:S(2)}) %collective-permute-start.1) | collective-permute-done | bytes 262176 | tf_op jit(solution)/shard_map/ppermute | solution.py:635
  22.9 1.8 %keep.3.refs_2_ = bf16[256,1024]{1,0:T(8,128)(2,1)S(1)} custom-call(bf16[256,2048]{1,0:T(8,128)(2,1)S(1)} %get-tuple-element.32.refs_0_, bf16[2048,512]{1,0:T(8,128)(2,1)S(1)} %get-tuple-element.33.refs_1_, bf16[2048,512]{1,0:T(8,128)(2,1)S(1)} %get-tuple-element.34.refs_2_, bf16[256,512]{1,0:T(8,128)(2,1)S(1)} %collective-permute-done.refs_3_, ...), custom_call_target="tpu_custom_call" | custom-call | bytes 1024 | tf_op jit(solution)/shard_map/keep/pallas_call | solution.py:134
  24.7 1.6 %collective-permute-start.4 = (bf16[256,1024]{1,0:T(8,128)(2,1)S(1)}, bf16[256,1024]{1,0:T(8,128)(2,1)S(1)}, u32[]{:S(2)}, u32[]{:S(2)}) collective-permute-start(bf16[256,1024]{1,0:T(8,128)(2,1)S(1)} %keep.3.refs_2_), channel_id=1, source_target_pairs={{0,2},{1,3},{2,0},{3,1},{4,6},{5,7},{6,4},{7,5},{8,10},{9,11},{10,... | collective-permute-start | bytes 1572872 | tf_op jit(solution)/shard_map/ppermute | solution.py:639
  26.3 3.4 %give.4 = (bf16[256,512]{1,0:T(8,128)(2,1)S(1)}, bf16[256,512]{1,0:T(8,128)(2,1)S(1)}, bf16[2048,512]{1,0:T(8,128)(2,1)S(1)}, bf16[2048,512]{1,0:T(8,128)(2,1)S(1)}) custom-call(bf16[256,2048]{1,0:T(8,128)(2,1)S(1)} %get-tuple-element.32.refs_0_, bf16[2048,8192]{1,0:T(8,128)(2,1)} %refs_10_.1, bf16[256,1024]{1,0:T(8,128)(2,1)S(1)} %keep.3.refs_2_), custom_call_target="tpu_custom_call" | custom-call | bytes 1024 | tf_op jit(solution)/shard_map/give/pallas_call | solution.py:134
  29.7 1.3 %copy-done.17 = bf16[2048,512]{1,0:T(8,128)(2,1)} copy-done((bf16[2048,512]{1,0:T(8,128)(2,1)}, bf16[2048,512]{1,0:T(8,128)(2,1)S(1)}, u32[]{:S(2)}) %copy-start.17) | copy-done | bytes 2097176
  31.0 1.3 %copy-done.20 = bf16[2048,512]{1,0:T(8,128)(2,1)} copy-done((bf16[2048,512]{1,0:T(8,128)(2,1)}, bf16[2048,512]{1,0:T(8,128)(2,1)S(1)}, u32[]{:S(2)}) %copy-start.20) | copy-done | bytes 2097176
  32.9 1.0 %collective-permute-done.3.refs_2_ = bf16[256,512]{1,0:T(8,128)(2,1)S(1)} collective-permute-done((bf16[256,512]{1,0:T(8,128)(2,1)S(1)}, bf16[256,512]{1,0:T(8,128)(2,1)S(1)}, u32[]{:S(2)}, u32[]{:S(2)}) %collective-permute-start.3) | collective-permute-done | bytes 262176 | tf_op jit(solution)/shard_map/ppermute | solution.py:635
  34.3 3.4 %keep.4 = (bf16[256,1024]{1,0:T(8,128)(2,1)S(1)}, bf16[2048,512]{1,0:T(8,128)(2,1)S(1)}, bf16[2048,512]{1,0:T(8,128)(2,1)S(1)}) custom-call(bf16[256,2048]{1,0:T(8,128)(2,1)S(1)} %get-tuple-element.32.refs_0_, bf16[256,512]{1,0:T(8,128)(2,1)S(1)} %collective-permute-done.2.refs_1_, bf16[256,512]{1,0:T(8,128)(2,1)S(1)} %collective-permute-done.3.refs_2_, ...), custom_call_target="tpu_custom_call" | custom-call | bytes 1024 | tf_op jit(solution)/shard_map/keep/pallas_call | solution.py:134
  37.7 1.4 %copy-done.11 = bf16[2048,512]{1,0:T(8,128)(2,1)} copy-done((bf16[2048,512]{1,0:T(8,128)(2,1)}, bf16[2048,512]{1,0:T(8,128)(2,1)S(1)}, u32[]{:S(2)}) %copy-start.11) | copy-done | bytes 2097176
  39.1 1.4 %copy-done.14 = bf16[2048,512]{1,0:T(8,128)(2,1)} copy-done((bf16[2048,512]{1,0:T(8,128)(2,1)}, bf16[2048,512]{1,0:T(8,128)(2,1)S(1)}, u32[]{:S(2)}) %copy-start.14) | copy-done | bytes 2097176
  41.0 6.2 %attend.3 = (bf16[256,2048]{1,0:T(8,128)(2,1)S(1)}, bf16[2048,512]{1,0:T(8,128)(2,1)S(1)}, bf16[2048,512]{1,0:T(8,128)(2,1)S(1)}, bf16[2048,512]{1,0:T(8,128)(2,1)S(1)}, bf16[2048,512]{1,0:T(8,128)(2,1)S(1)}) custom-call(s32[8,125]{1,0:T(8,128)S(1)} %bitcast.8, s32[1,125]{1,0:T(1,128)S(1)} %copy-done.38, bf16[8192,128]{1,0:T(8,128)(2,1)S(1)} %bitcast.5, ...), custom_call_target="tpu_custom_call" | custom-call | bytes 1024 | tf_op jit(solution)/shard_map/attend/pallas_call | solution.py:134
  47.3 3.1 %copy-done.21 = bf16[2048,512]{1,0:T(8,128)(2,1)S(1)} copy-done((bf16[2048,512]{1,0:T(8,128)(2,1)S(1)}, bf16[2048,512]{1,0:T(8,128)(2,1)}, u32[]{:S(2)}) %copy-start.21) | copy-done | bytes 2097176
  50.4 3.6 %give.5 = (bf16[256,512]{1,0:T(8,128)(2,1)S(1)}, bf16[256,512]{1,0:T(8,128)(2,1)S(1)}, bf16[256,512]{1,0:T(8,128)(2,1)S(1)}, bf16[256,512]{1,0:T(8,128)(2,1)S(1)}) custom-call(bf16[256,2048]{1,0:T(8,128)(2,1)S(1)} %get-tuple-element.42.refs_0_.refs_5_, bf16[2048,512]{1,0:T(8,128)(2,1)S(1)} %get-tuple-element.35.refs_1_, ...), custom_call_target="tpu_custom_call" | custom-call | bytes 1024 | tf_op jit(solution)/shard_map/give/pallas_call | solution.py:134
  56.9 4.7 %keep.5.refs_6_ = bf16[256,2048]{1,0:T(8,128)(2,1)} custom-call(bf16[256,2048]{1,0:T(8,128)(2,1)S(1)} %get-tuple-element.42.refs_0_.refs_5_, bf16[2048,512]{1,0:T(8,128)(2,1)S(1)} %get-tuple-element.33.refs_1_, bf16[2048,512]{1,0:T(8,128)(2,1)S(1)} %get-tuple-element.34.refs_2_, bf16[2048,512]{1,0:T(8,128)(2,1)S(1)} %copy-done.12, ...), custom_call_target="tpu_custom_call" | custom-call | bytes 1024 | tf_op jit(solution)/shard_map/keep/pallas_call | solution.py:134
  61.5 1.5 %collective-permute-start.14 = (bf16[256,2048]{1,0:T(8,128)(2,1)}, bf16[256,2048]{1,0:T(8,128)(2,1)}, u32[]{:S(2)}, u32[]{:S(2)}) collective-permute-start(bf16[256,2048]{1,0:T(8,128)(2,1)} %keep.5.refs_6_), channel_id=1, source_target_pairs={{0,2},{1,3},{2,0},{3,1},{4,6},{5,7},{6,4},{7,5},{8,10},{9,11},{10,... | collective-permute-start | bytes 3145736 | tf_op jit(solution)/shard_map/ppermute | solution.py:639
  63.1 1.6 %copy-done.10 = bf16[128,4,16,128]{3,2,1,0:T(8,128)(2,1)S(1)} copy-done((bf16[128,4,16,128]{3,2,1,0:T(8,128)(2,1)S(1)}, bf16[128,4,16,128]{3,2,1,0:T(8,128)(2,1)}, u32[]{:S(2)}) %copy-start.10) | copy-done | bytes 2097176
  64.7 4.5 %settle.1 = (bf16[256,2048]{1,0:T(8,128)(2,1)S(1)}, bf16[16,2048]{1,0:T(8,128)(2,1)S(1)}, bf16[1,3,2,512,256]{4,3,2,1,0:T(8,128)(2,1)}) custom-call(s32[8]{0:T(128)S(1)} %copy-done.37, s32[8]{0:T(128)S(1)} %copy-done.39, bf16[4,2,32,16,256]{4,3,2,1,0:T(8,128)(2,1)} %all-to-all-done.refs_2_, ...), custom_call_target="tpu_custom_call", output_to_operand_aliasing={{0}: (5, {})} | custom-call | bytes 1024 | tf_op jit(solution)/shard_map/settle/pallas_call | solution.py:134
  69.2 1.6 %copy-done.22 = bf16[2048,512]{1,0:T(8,128)(2,1)S(1)} copy-done((bf16[2048,512]{1,0:T(8,128)(2,1)S(1)}, bf16[2048,512]{1,0:T(8,128)(2,1)}, u32[]{:S(2)}) %copy-start.22) | copy-done | bytes 2097176
  70.8 2.0 %give_last.1.refs_6_ = bf16[16,2048]{1,0:T(8,128)(2,1)S(1)} custom-call(bf16[16,2048]{1,0:T(8,128)(2,1)S(1)} %get-tuple-element.57.refs_0_, bf16[2048,512]{1,0:T(8,128)(2,1)S(1)} %copy-done.5, bf16[2048,512]{1,0:T(8,128)(2,1)S(1)} %copy-done.7, bf16[2048,512]{1,0:T(8,128)(2,1)S(1)} %copy-done.19, bf16[2048,512]{1,0:T(8,128)(2,1)S(1)} %copy-done.22), custom_call_target="tpu_custom_call" | custom-call | bytes 1024 | tf_op jit(solution)/shard_map/give_last/pallas_call | solution.py:134
  73.0 0.6 copy-done.33
  74.2 5.9 %give_own.1 = (bf16[512,512]{1,0:T(8,128)(2,1)S(1)}, bf16[512,512]{1,0:T(8,128)(2,1)S(1)}, bf16[512,512]{1,0:T(8,128)(2,1)S(1)}, bf16[512,512]{1,0:T(8,128)(2,1)S(1)}) custom-call(bf16[256,2048]{1,0:T(8,128)(2,1)S(1)} %get-tuple-element.32.refs_0_, bf16[256,2048]{1,0:T(8,128)(2,1)S(1)} %get-tuple-element.52.refs_1_, bf16[2048,512]{1,0:T(8,128)(2,1)S(1)} %copy-done.29, ...), custom_call_target="tpu_custom_call" | custom-call | bytes 1024 | tf_op jit(solution)/shard_map/give_own/pallas_call | solution.py:134
  81.3 2.0 %keep_last.1.refs_11_ = bf16[16,2048]{1,0:T(8,128)(2,1)S(1)} custom-call(bf16[16,2048]{1,0:T(8,128)(2,1)S(1)} %get-tuple-element.57.refs_0_, bf16[2048,512]{1,0:T(8,128)(2,1)S(1)} %copy-done.1, bf16[2048,512]{1,0:T(8,128)(2,1)S(1)} %copy-done.3, bf16[2048,512]{1,0:T(8,128)(2,1)S(1)} %copy-done.13, bf16[2048,512]{1,0:T(8,128)(2,1)S(1)} %copy-done.16, ...), custom_call_target="tpu_custom_call" | custom-call | bytes 1024 | tf_op jit(solution)/shard_map/keep_last/pallas_call | solution.py:134
  83.3 3.7 %collective-permute-done.14.refs_8_ = bf16[256,2048]{1,0:T(8,128)(2,1)} collective-permute-done((bf16[256,2048]{1,0:T(8,128)(2,1)}, bf16[256,2048]{1,0:T(8,128)(2,1)}, u32[]{:S(2)}, u32[]{:S(2)}) %collective-permute-start.14) | collective-permute-done | bytes 1048608 | tf_op jit(solution)/shard_map/ppermute | solution.py:639
  87.1 1.5 %collective-permute-start.16 = (bf16[16,2048]{1,0:T(8,128)(2,1)S(1)}, bf16[16,2048]{1,0:T(8,128)(2,1)S(1)}, u32[]{:S(2)}, u32[]{:S(2)}) collective-permute-start(bf16[16,2048]{1,0:T(8,128)(2,1)S(1)} %keep_last.1.refs_11_), channel_id=1, source_target_pairs={{0,2},{1,3},{2,0},{3,1},{4,6},{5,7},{6,4},{7,5},{8,10},{9,11},{10,... | collective-permute-start | bytes 196616 | tf_op jit(solution)/shard_map/ppermute | solution.py:639
  88.6 2.8 %collective-permute-done.16.refs_9_ = bf16[16,2048]{1,0:T(8,128)(2,1)S(1)} collective-permute-done((bf16[16,2048]{1,0:T(8,128)(2,1)S(1)}, bf16[16,2048]{1,0:T(8,128)(2,1)S(1)}, u32[]{:S(2)}, u32[]{:S(2)}) %collective-permute-start.16) | collective-permute-done | bytes 65568 | tf_op jit(solution)/shard_map/ppermute | solution.py:639
  91.4 10.4 %final.1 = bf16[2048,512]{1,0:T(8,128)(2,1)} custom-call(bf16[256,2048]{1,0:T(8,128)(2,1)S(1)} %get-tuple-element.32.refs_0_, bf16[256,2048]{1,0:T(8,128)(2,1)S(1)} %get-tuple-element.52.refs_1_, bf16[512,512]{1,0:T(8,128)(2,1)S(1)} %collective-permute-done.10.refs_2_, bf16[512,512]{1,0:T(8,128)(2,1)S(1)} %collective-permute-done.11.refs_3_, ...), custom_call_target="tpu_custom_call" | custom-call | bytes 1024 | tf_op jit(solution)/shard_map/final/pallas_call | solution.py:134
  (98 shorter events, 7.1 us)
Async XLA Ops:
  4.1 59.0 %all-to-all-start = ((bf16[4,2,32,16,256]{4,3,2,1,0:T(8,128)(2,1)}), bf16[4,2,32,16,256]{4,3,2,1,0:T(8,128)(2,1)}, u32[]{:S(2)}, u32[]{:S(2)}) async-start(bf16[4,2,32,16,256]{4,3,2,1,0:T(8,128)(2,1)} %pack.1.refs_6_), calls=%async_computation | async-start | bytes 4194304 | tf_op jit(solution)/shard_map/all_to_all | solution.py:692
  19.1 28.2 %copy-start.4 = (bf16[2048,512]{1,0:T(8,128)(2,1)}, bf16[2048,512]{1,0:T(8,128)(2,1)S(1)}, u32[]{:S(2)}) copy-start(bf16[2048,512]{1,0:T(8,128)(2,1)S(1)} %get-tuple-element.35.refs_1_) | copy-start | bytes 6291460
  19.1 28.2 %copy-start.6 = (bf16[2048,512]{1,0:T(8,128)(2,1)}, bf16[2048,512]{1,0:T(8,128)(2,1)S(1)}, u32[]{:S(2)}) copy-start(bf16[2048,512]{1,0:T(8,128)(2,1)S(1)} %get-tuple-element.36.refs_2_) | copy-start | bytes 6291460
  19.1 37.7 %copy-start = (bf16[2048,512]{1,0:T(8,128)(2,1)}, bf16[2048,512]{1,0:T(8,128)(2,1)S(1)}, u32[]{:S(2)}) copy-start(bf16[2048,512]{1,0:T(8,128)(2,1)S(1)} %get-tuple-element.33.refs_1_) | copy-start | bytes 6291460
  19.1 37.7 %copy-start.2 = (bf16[2048,512]{1,0:T(8,128)(2,1)}, bf16[2048,512]{1,0:T(8,128)(2,1)S(1)}, u32[]{:S(2)}) copy-start(bf16[2048,512]{1,0:T(8,128)(2,1)S(1)} %get-tuple-element.34.refs_2_) | copy-start | bytes 6291460
  20.9 1.6 %collective-permute-start.1 = (bf16[256,512]{1,0:T(8,128)(2,1)S(1)}, bf16[256,512]{1,0:T(8,128)(2,1)S(1)}, u32[]{:S(2)}, u32[]{:S(2)}) collective-permute-start(bf16[256,512]{1,0:T(8,128)(2,1)S(1)} %get-tuple-element.38), channel_id=1, source_target_pairs={{0,1},{1,0},{2,3},{3,2},{4,5},{5,4},{6,7},{7,6},{8,9},{9,8},{10,11... | collective-permute-start | bytes 786440 | tf_op jit(solution)/shard_map/ppermute | solution.py:635
  21.0 1.9 %collective-permute-start = (bf16[256,512]{1,0:T(8,128)(2,1)S(1)}, bf16[256,512]{1,0:T(8,128)(2,1)S(1)}, u32[]{:S(2)}, u32[]{:S(2)}) collective-permute-start(bf16[256,512]{1,0:T(8,128)(2,1)S(1)} %get-tuple-element.37.refs_5_), channel_id=1, source_target_pairs={{0,1},{1,0},{2,3},{3,2},{4,5},{5,4},{6,7},{7,6},{8,9},{9,8},{10,11... | collective-permute-start | bytes 786440 | tf_op jit(solution)/shard_map/ppermute | solution.py:635
  24.7 22.5 %collective-permute-start.4 = (bf16[256,1024]{1,0:T(8,128)(2,1)S(1)}, bf16[256,1024]{1,0:T(8,128)(2,1)S(1)}, u32[]{:S(2)}, u32[]{:S(2)}) collective-permute-start(bf16[256,1024]{1,0:T(8,128)(2,1)S(1)} %keep.3.refs_2_), channel_id=1, source_target_pairs={{0,2},{1,3},{2,0},{3,1},{4,6},{5,7},{6,4},{7,5},{8,10},{9,11},{10,... | collective-permute-start | bytes 1572872 | tf_op jit(solution)/shard_map/ppermute | solution.py:639
  32.4 1.5 %collective-permute-start.3 = (bf16[256,512]{1,0:T(8,128)(2,1)S(1)}, bf16[256,512]{1,0:T(8,128)(2,1)S(1)}, u32[]{:S(2)}, u32[]{:S(2)}) collective-permute-start(bf16[256,512]{1,0:T(8,128)(2,1)S(1)} %get-tuple-element.40), channel_id=1, source_target_pairs={{0,1},{1,0},{2,3},{3,2},{4,5},{5,4},{6,7},{7,6},{8,9},{9,8},{10,11... | collective-permute-start | bytes 786440 | tf_op jit(solution)/shard_map/ppermute | solution.py:635
  32.4 8.6 %copy-start.9 = (bf16[128,4,16,128]{3,2,1,0:T(8,128)(2,1)S(1)}, bf16[128,4,16,128]{3,2,1,0:T(8,128)(2,1)}, u32[]{:S(2)}) copy-start(bf16[128,4,16,128]{3,2,1,0:T(8,128)(2,1)} %param.17) | copy-start | bytes 6291460
  32.4 1.9 %collective-permute-start.2 = (bf16[256,512]{1,0:T(8,128)(2,1)S(1)}, bf16[256,512]{1,0:T(8,128)(2,1)S(1)}, u32[]{:S(2)}, u32[]{:S(2)}) collective-permute-start(bf16[256,512]{1,0:T(8,128)(2,1)S(1)} %get-tuple-element.39.refs_4_), channel_id=1, source_target_pairs={{0,1},{1,0},{2,3},{3,2},{4,5},{5,4},{6,7},{7,6},{8,9},{9,8},{10,11... | collective-permute-start | bytes 786440 | tf_op jit(solution)/shard_map/ppermute | solution.py:635
  40.4 14.7 %collective-permute-start.9 = (bf16[256,1024]{1,0:T(8,128)(2,1)S(1)}, bf16[256,1024]{1,0:T(8,128)(2,1)S(1)}, u32[]{:S(2)}, u32[]{:S(2)}) collective-permute-start(bf16[256,1024]{1,0:T(8,128)(2,1)S(1)} %get-tuple-element.41.refs_6_), channel_id=1, source_target_pairs={{0,2},{1,3},{2,0},{3,1},{4,6},{5,7},{6,4},{7,5},{8,10},{9,11},{10,... | collective-permute-start | bytes 1572872 | tf_op jit(solution)/shard_map/ppermute | solution.py:639
  47.2 6.8 %copy-start.28 = (bf16[2048,512]{1,0:T(8,128)(2,1)}, bf16[2048,512]{1,0:T(8,128)(2,1)S(1)}, u32[]{:S(2)}) copy-start(bf16[2048,512]{1,0:T(8,128)(2,1)S(1)} %get-tuple-element.53.refs_2_) | copy-start | bytes 6291460
  47.2 6.8 %copy-start.30 = (bf16[2048,512]{1,0:T(8,128)(2,1)}, bf16[2048,512]{1,0:T(8,128)(2,1)S(1)}, u32[]{:S(2)}) copy-start(bf16[2048,512]{1,0:T(8,128)(2,1)S(1)} %get-tuple-element.54.refs_3_) | copy-start | bytes 6291460
  47.2 6.8 %copy-start.32 = (bf16[2048,512]{1,0:T(8,128)(2,1)}, bf16[2048,512]{1,0:T(8,128)(2,1)S(1)}, u32[]{:S(2)}) copy-start(bf16[2048,512]{1,0:T(8,128)(2,1)S(1)} %get-tuple-element.55.refs_4_) | copy-start | bytes 6291460
  47.2 6.8 %copy-start.34 = (bf16[2048,512]{1,0:T(8,128)(2,1)}, bf16[2048,512]{1,0:T(8,128)(2,1)S(1)}, u32[]{:S(2)}) copy-start(bf16[2048,512]{1,0:T(8,128)(2,1)S(1)} %get-tuple-element.56.refs_5_) | copy-start | bytes 6291460
  54.1 1.6 %collective-permute-start.6 = (bf16[256,512]{1,0:T(8,128)(2,1)S(1)}, bf16[256,512]{1,0:T(8,128)(2,1)S(1)}, u32[]{:S(2)}, u32[]{:S(2)}) collective-permute-start(bf16[256,512]{1,0:T(8,128)(2,1)S(1)} %get-tuple-element.48), channel_id=1, source_target_pairs={{0,1},{1,0},{2,3},{3,2},{4,5},{5,4},{6,7},{7,6},{8,9},{9,8},{10,11... | collective-permute-start | bytes 786440 | tf_op jit(solution)/shard_map/ppermute | solution.py:635
  54.2 1.9 %collective-permute-start.7 = (bf16[256,512]{1,0:T(8,128)(2,1)S(1)}, bf16[256,512]{1,0:T(8,128)(2,1)S(1)}, u32[]{:S(2)}, u32[]{:S(2)}) collective-permute-start(bf16[256,512]{1,0:T(8,128)(2,1)S(1)} %get-tuple-element.49), channel_id=1, source_target_pairs={{0,1},{1,0},{2,3},{3,2},{4,5},{5,4},{6,7},{7,6},{8,9},{9,8},{10,11... | collective-permute-start | bytes 786440 | tf_op jit(solution)/shard_map/ppermute | solution.py:635
  54.7 1.8 %collective-permute-start.8 = (bf16[256,512]{1,0:T(8,128)(2,1)S(1)}, bf16[256,512]{1,0:T(8,128)(2,1)S(1)}, u32[]{:S(2)}, u32[]{:S(2)}) collective-permute-start(bf16[256,512]{1,0:T(8,128)(2,1)S(1)} %get-tuple-element.50), channel_id=1, source_target_pairs={{0,1},{1,0},{2,3},{3,2},{4,5},{5,4},{6,7},{7,6},{8,9},{9,8},{10,11... | collective-permute-start | bytes 786440 | tf_op jit(solution)/shard_map/ppermute | solution.py:635
  54.8 2.1 %collective-permute-start.5 = (bf16[256,512]{1,0:T(8,128)(2,1)S(1)}, bf16[256,512]{1,0:T(8,128)(2,1)S(1)}, u32[]{:S(2)}, u32[]{:S(2)}) collective-permute-start(bf16[256,512]{1,0:T(8,128)(2,1)S(1)} %get-tuple-element.47.refs_9_), channel_id=1, source_target_pairs={{0,1},{1,0},{2,3},{3,2},{4,5},{5,4},{6,7},{7,6},{8,9},{9,8},{10,11... | collective-permute-start | bytes 786440 | tf_op jit(solution)/shard_map/ppermute | solution.py:635
  61.5 25.5 %collective-permute-start.14 = (bf16[256,2048]{1,0:T(8,128)(2,1)}, bf16[256,2048]{1,0:T(8,128)(2,1)}, u32[]{:S(2)}, u32[]{:S(2)}) collective-permute-start(bf16[256,2048]{1,0:T(8,128)(2,1)} %keep.5.refs_6_), channel_id=1, source_target_pairs={{0,2},{1,3},{2,0},{3,1},{4,6},{5,7},{6,4},{7,5},{8,10},{9,11},{10,... | collective-permute-start | bytes 3145736 | tf_op jit(solution)/shard_map/ppermute | solution.py:639
  72.8 8.0 %collective-permute-start.15 = (bf16[16,2048]{1,0:T(8,128)(2,1)S(1)}, bf16[16,2048]{1,0:T(8,128)(2,1)S(1)}, u32[]{:S(2)}, u32[]{:S(2)}) collective-permute-start(bf16[16,2048]{1,0:T(8,128)(2,1)S(1)} %give_last.1.refs_6_), channel_id=1, source_target_pairs={{0,1},{1,0},{2,3},{3,2},{4,5},{5,4},{6,7},{7,6},{8,9},{9,8},{10,11... | collective-permute-start | bytes 196616 | tf_op jit(solution)/shard_map/ppermute | solution.py:635
  74.2 7.1 %copy-start.1 = (bf16[2048,512]{1,0:T(8,128)(2,1)S(1)}, bf16[2048,512]{1,0:T(8,128)(2,1)}, u32[]{:S(2)}) copy-start(bf16[2048,512]{1,0:T(8,128)(2,1)} %copy-done) | copy-start | bytes 6291460
  74.2 7.1 %copy-start.3 = (bf16[2048,512]{1,0:T(8,128)(2,1)S(1)}, bf16[2048,512]{1,0:T(8,128)(2,1)}, u32[]{:S(2)}) copy-start(bf16[2048,512]{1,0:T(8,128)(2,1)} %copy-done.2) | copy-start | bytes 6291460
  74.2 7.1 %copy-start.13 = (bf16[2048,512]{1,0:T(8,128)(2,1)S(1)}, bf16[2048,512]{1,0:T(8,128)(2,1)}, u32[]{:S(2)}) copy-start(bf16[2048,512]{1,0:T(8,128)(2,1)} %copy-done.11) | copy-start | bytes 6291460
  74.2 7.1 %copy-start.16 = (bf16[2048,512]{1,0:T(8,128)(2,1)S(1)}, bf16[2048,512]{1,0:T(8,128)(2,1)}, u32[]{:S(2)}) copy-start(bf16[2048,512]{1,0:T(8,128)(2,1)} %copy-done.14) | copy-start | bytes 6291460
  80.2 11.1 %collective-permute-start.11 = (bf16[512,512]{1,0:T(8,128)(2,1)S(1)}, bf16[512,512]{1,0:T(8,128)(2,1)S(1)}, u32[]{:S(2)}, u32[]{:S(2)}) collective-permute-start(bf16[512,512]{1,0:T(8,128)(2,1)S(1)} %get-tuple-element.59), channel_id=1, source_target_pairs={{0,1},{1,0},{2,3},{3,2},{4,5},{5,4},{6,7},{7,6},{8,9},{9,8},{10,11... | collective-permute-start | bytes 1572872 | tf_op jit(solution)/shard_map/ppermute | solution.py:635
  80.3 11.1 %collective-permute-start.12 = (bf16[512,512]{1,0:T(8,128)(2,1)S(1)}, bf16[512,512]{1,0:T(8,128)(2,1)S(1)}, u32[]{:S(2)}, u32[]{:S(2)}) collective-permute-start(bf16[512,512]{1,0:T(8,128)(2,1)S(1)} %get-tuple-element.60), channel_id=1, source_target_pairs={{0,1},{1,0},{2,3},{3,2},{4,5},{5,4},{6,7},{7,6},{8,9},{9,8},{10,11... | collective-permute-start | bytes 1572872 | tf_op jit(solution)/shard_map/ppermute | solution.py:635
  80.8 10.6 %collective-permute-start.13 = (bf16[512,512]{1,0:T(8,128)(2,1)S(1)}, bf16[512,512]{1,0:T(8,128)(2,1)S(1)}, u32[]{:S(2)}, u32[]{:S(2)}) collective-permute-start(bf16[512,512]{1,0:T(8,128)(2,1)S(1)} %get-tuple-element.61), channel_id=1, source_target_pairs={{0,1},{1,0},{2,3},{3,2},{4,5},{5,4},{6,7},{7,6},{8,9},{9,8},{10,11... | collective-permute-start | bytes 1572872 | tf_op jit(solution)/shard_map/ppermute | solution.py:635
  80.9 10.5 %copy-start.27 = (bf16[256,1024]{1,0:T(8,128)(2,1)S(1)}, bf16[256,1024]{1,0:T(8,128)(2,1)}, u32[]{:S(2)}) copy-start(bf16[256,1024]{1,0:T(8,128)(2,1)} %copy-done.26) | copy-start | bytes 1572868
  80.9 10.5 %collective-permute-start.10 = (bf16[512,512]{1,0:T(8,128)(2,1)S(1)}, bf16[512,512]{1,0:T(8,128)(2,1)S(1)}, u32[]{:S(2)}, u32[]{:S(2)}) collective-permute-start(bf16[512,512]{1,0:T(8,128)(2,1)S(1)} %get-tuple-element.58.refs_6_), channel_id=1, source_target_pairs={{0,1},{1,0},{2,3},{3,2},{4,5},{5,4},{6,7},{7,6},{8,9},{9,8},{10,11... | collective-permute-start | bytes 1572872 | tf_op jit(solution)/shard_map/ppermute | solution.py:635
  87.1 4.3 %collective-permute-start.16 = (bf16[16,2048]{1,0:T(8,128)(2,1)S(1)}, bf16[16,2048]{1,0:T(8,128)(2,1)S(1)}, u32[]{:S(2)}, u32[]{:S(2)}) collective-permute-start(bf16[16,2048]{1,0:T(8,128)(2,1)S(1)} %keep_last.1.refs_11_), channel_id=1, source_target_pairs={{0,2},{1,3},{2,0},{3,1},{4,6},{5,7},{6,4},{7,5},{8,10},{9,11},{10,... | collective-permute-start | bytes 196616 | tf_op jit(solution)/shard_map/ppermute | solution.py:639
  (26 other events, 102.1 us)

commit v6 on v5

--- a/solution.py
+++ b/solution.py
@@ -15,6 +15,7 @@
 GROUP = 16
 TOGETHER = 8
 LARGE_FIRST = 40
+FETCHING = 33
 
 
 def dot_t(left, right):
@@ -74,7 +75,7 @@
     count = len(deps)
     fetches = len(pieces)
     extra_in = [weight] if fetches else []
-    limit = max(limit, 36) if fetches else limit
+    limit = max(limit, FETCHING) if fetches else limit
 
     def call(*refs):
         table_in, refs = refs[:many], refs[many:]
@@ -153,8 +154,14 @@
     return result[:outputs], result[outputs:]
 
 
-def pack_kernel(ready, launch, table_ref, dest_ref, pool_ref, send_ref, *, sizes):
+def pack_kernel(
+    ready, launch, table_ref, dest_ref, pool_ref, query_ref, kv_ref, send_ref, tail_q_ref,
+    tail_kv_ref, *, sizes
+):
     inst = lax.axis_index("inst")
+    launch()
+    tail_q_ref[...] = query_ref[...]
+    tail_kv_ref[...] = kv_ref[...].reshape(sizes.tail_kv, 2 * sizes.width)
     ready()
     for m in range(sizes.mig_per):
         dest = dest_ref[inst * sizes.mig_per + m]
@@ -168,15 +175,29 @@
         lax.fori_loop(0, sizes.mig_blocks, copy_block, 0, unroll=8)
 
 
-def pack(src_table, mig_dest, out_pool, sizes):
+def pack(src_table, mig_dest, out_pool, query_rows, new_kv, sizes):
     z = sizes
-    shape = (z.insts, z.slots, z.mig_blocks, z.block, 2 * z.width)
+    last_q = query_rows.shape[0] // z.tail_q - 1
+    last_kv = z.batch // z.insts - 1
     result, _ = run(
         functools.partial(pack_kernel, sizes=z),
-        [src_table, mig_dest], [out_pool], [VMEM], [],
-        [jax.ShapeDtypeStruct(shape, out_pool.dtype)], [VMEM], "pack", z, limit=60,
-    )
-    return result[0]
+        [src_table, mig_dest], [out_pool, query_rows, new_kv],
+        [
+            VMEM,
+            pl.BlockSpec((z.tail_q, z.width), lambda i: (last_q, 0)),
+            pl.BlockSpec((z.insts,) + new_kv.shape[1:], lambda i: (last_kv, 0, 0, 0)),
+        ],
+        [],
+        [
+            jax.ShapeDtypeStruct(
+                (z.insts, z.slots, z.mig_blocks, z.block, 2 * z.width), out_pool.dtype
+            ),
+            jax.ShapeDtypeStruct((z.tail_q, z.width), out_pool.dtype),
+            jax.ShapeDtypeStruct((z.tail_kv, 2 * z.width), out_pool.dtype),
+        ],
+        [VMEM] * 3, "pack", z, limit=60, grid=(1,),
+    )
+    return result
 
 
 def fresh_code(rows, keys, sizes):
@@ -236,10 +257,11 @@
 
 
 def attend_kernel(
-    ready, launch, table_ref, len_ref, query_hbm, kv_hbm, pool_ref, out_ref, query_all, kv_all,
-    fresh_ref, pf_ref, blend_ref, done_ref, sems, *, first_row, steps_in_all, sizes,
+    ready, launch, table_ref, len_ref, query_hbm, kv_hbm, pool_ref, *refs, first_row,
+    steps_in_all, sizes,
 ):
     z = sizes
+    out_ref, query_all, kv_all, fresh_ref, pf_ref, blend_ref, done_ref, sems = refs
     width, per = z.width, z.per
     rows = GROUP
     step = pl.program_id(0)
@@ -306,10 +328,16 @@
         out_ref[:, h * width : (h + 1) * width] = column.astype(jnp.bfloat16)
 
 
-def attend(table, lengths, queries, new_kv, pool, first_row, rows, sizes, deps, limit=12, **fetch):
+def attend(table, lengths, queries, new_kv, pool, into, first_row, rows, sizes, deps, limit=12,
+           **fetch):
     z = sizes
     groups = rows // GROUP
-    tokens = rows * z.steps
+    first = first_row // GROUP
+    tokens = z.batch * z.steps
+    aliases = {}
+    if into is not None:
+        deps = [into] + deps
+        aliases = {5 + (1 if fetch else 0): 0}
     result, pieces = run(
         functools.partial(
             attend_kernel, first_row=first_row, steps_in_all=groups, sizes=z
@@ -319,7 +347,7 @@
         [HBM, HBM, VMEM],
         deps,
         [jax.ShapeDtypeStruct((tokens, z.heads * z.width), jnp.bfloat16)],
-        [pl.BlockSpec((GROUP * z.steps, z.heads * z.width), lambda i: (i, 0))],
+        [pl.BlockSpec((GROUP * z.steps, z.heads * z.width), lambda i: (first + i, 0))],
         "attend", z, limit=limit,
         grid=(groups,),
         scratch=[
@@ -331,7 +359,7 @@
             pltpu.VMEM((GROUP * z.per, z.width), jnp.float32),
             pltpu.SemaphoreType.DMA((2, groups)),
         ],
-        **fetch,
+        aliases=aliases, **fetch,
     )
     return result[0], pieces
 
@@ -357,7 +385,7 @@
     ]
     for read in reads:
         read.start()
-    new_kv = kv_ref[...].reshape(z.tail_kv, 2 * z.width)
+    new_kv = kv_ref[...]
     code = fresh_code(z.per, z.tail_kv, z)
     slot_of = slot_index(extent, z)
     scale = math.log2(math.e) / math.sqrt(z.width)
@@ -400,23 +428,16 @@
         write.wait()
 
 
-def settle(mig_dest, mig_len, got, query_rows, new_kv, attention, sizes, deps, **fetch):
+def settle(mig_dest, mig_len, got, tail_q, tail_kv, attention, sizes, deps, **fetch):
     z = sizes
     tokens = z.insts * z.steps
     last = attention.shape[0] // tokens - 1
-    last_q = query_rows.shape[0] // z.tail_q - 1
-    last_kv = z.batch // z.insts - 1
     spec = pl.BlockSpec((tokens, attention.shape[1]), lambda i: (last, 0))
     cache = (z.slots, z.mig_blocks * z.block, 2 * z.width)
     return run(
         functools.partial(settle_kernel, sizes=z),
-        [mig_dest, mig_len], [got, query_rows, new_kv, attention],
-        [
-            HBM,
-            pl.BlockSpec((z.tail_q, z.width), lambda i: (last_q, 0)),
-            pl.BlockSpec((z.insts,) + new_kv.shape[1:], lambda i: (last_kv, 0, 0, 0)),
-            spec,
-        ],
+        [mig_dest, mig_len], [got, tail_q, tail_kv, attention],
+        [HBM, VMEM, VMEM, spec],
         deps,
         [
             jax.ShapeDtypeStruct(attention.shape, jnp.bfloat16),
@@ -435,11 +456,11 @@
 
 
 def project_kernel(
-    ready, launch, *refs, parts, count, streamed, added, joined, kept, sizes
+    ready, launch, attention, *refs, first, tokens, count, streamed, added, joined, kept, sizes
 ):
     launch()
-    attention, weights = refs[:parts], list(refs[parts : parts + count])
-    position = parts + count
+    weights = list(refs[:count])
+    position = count
     extra = refs[position : position + added]
     position += added
     source = refs[position]
@@ -468,21 +489,16 @@
 
         def one(j, carry, n=n, weight=weight):
             at = pl.ds(pl.multiple_of(j * tile, tile), tile)
-            begin = 0
-            for part in attention:
-                tokens = part.shape[0]
-                rows = slice(begin, begin + tokens)
-                result = dot(part[...], weight[:, at])
-                to = pl.ds(pl.multiple_of(n * width + j * tile, tile), tile)
-                if added == 1:
-                    result = result + extra[0][rows, to].astype(jnp.float32)
-                elif added:
-                    result = result + extra[n][rows, at].astype(jnp.float32)
-                if joined:
-                    out_refs[0][rows, to] = result.astype(jnp.bfloat16)
-                else:
-                    out_refs[n][rows, at] = result.astype(jnp.bfloat16)
-                begin += tokens
+            to = pl.ds(pl.multiple_of(n * width + j * tile, tile), tile)
+            result = dot(attention[first : first + tokens, :], weight[:, at])
+            if added == 1:
+                result = result + extra[0][:, to].astype(jnp.float32)
+            elif added:
+                result = result + extra[n][:, at].astype(jnp.float32)
+            if joined:
+                out_refs[0][:, to] = result.astype(jnp.bfloat16)
+            else:
+                out_refs[n][:, at] = result.astype(jnp.bfloat16)
             return carry
 
         lax.fori_loop(0, width // tile, one, 0)
@@ -490,14 +506,14 @@
 
 def project(attention, weights, streamed, out_weight, mates, joined, kept, sizes, name, deps,
             pieces=()):
-    tokens = sum(a.shape[0] for a in attention)
+    attention, first, tokens = attention
     count = len(weights) + len(streamed)
     if joined:
         shapes = [jax.ShapeDtypeStruct((tokens, count * sizes.quarter), jnp.bfloat16)]
     else:
         shapes = [jax.ShapeDtypeStruct((tokens, sizes.quarter), jnp.bfloat16)] * count
     results = len(shapes)
-    operands = attention + weights + mates
+    operands = [attention] + weights + mates
     specs = [VMEM] * len(operands)
     scratch = []
     piece = (sizes.depth, sizes.quarter)
@@ -511,17 +527,17 @@
         scratch.append(pltpu.SemaphoreType.DMA((len(streamed),)))
     result, new = run(
         functools.partial(
-            project_kernel, parts=len(attention), count=len(weights), streamed=streamed,
+            project_kernel, first=first, tokens=tokens, count=len(weights), streamed=streamed,
             added=len(mates), joined=joined, kept=kept, sizes=sizes,
         ),
         [], operands, specs, deps, shapes, [VMEM] * len(shapes), name, sizes,
-        limit=36 if streamed or pieces else 16, scratch=scratch,
+        limit=FETCHING if streamed or pieces else 16, scratch=scratch,
         pieces=pieces, weight=out_weight,
     )
     return result[:results], result[results:], new
 
 
-def final_kernel(ready, launch, *refs, parts, count, streamed, mates, fars, sizes):
+def final_kernel(ready, launch, attention, *refs, count, streamed, mates, fars, sizes):
     z = sizes
     refs = list(refs)
 
@@ -530,8 +546,8 @@
         del refs[:n]
         return taken
 
-    attention, weights, extra = take(parts), take(count), take(mates)
-    low, high, second, late = take(fars), take(fars), take(fars), take(fars)
+    weights, extra = take(count), take(mates)
+    low, second, high, late = take(fars), take(fars), take(fars), take(fars)
     source = take(bool(streamed))
     (out_hbm,) = take(1)
     block_ref, block_sems = take(2)
@@ -555,22 +571,16 @@
             at = pl.ds(start, tile)
             whole = pl.ds(n * z.quarter + start, tile)
             half = pl.ds((n % 2) * z.quarter + start, tile)
-            begin = 0
-            for p, part in enumerate(attention):
-                tokens = part.shape[0]
-                rows = slice(begin, begin + tokens)
-                sums = dot(part[...], weight[:, at]) + extra[n][rows, at].astype(jnp.float32)
-                for k in range(fars):
-                    if p == 0:
-                        arrived = (low if n < 2 else high)[k][:, half]
-                    else:
-                        count = late[k].shape[0]
-                        arrived = jnp.concatenate(
-                            [second[k][: tokens - count, whole], late[k][:, whole]], axis=0
-                        )
-                    sums = sums + arrived.astype(jnp.float32)
-                block_ref[n, at, rows] = sums.T.astype(jnp.bfloat16)
-                begin += tokens
+            sums = dot(attention[...], weight[:, at]) + extra[n][:, at].astype(jnp.float32)
+            for k in range(fars):
+                if n < 2:
+                    parts = [low[k][:, half], second[k][:, half]]
+                else:
+                    parts = [high[k][:, half]]
+                rows = late[k].shape[0]
+                parts = parts[:-1] + [parts[-1][:-rows], late[k][:, whole]]
+                sums = sums + jnp.concatenate(parts, axis=0).astype(jnp.float32)
+            block_ref[n, at, :] = sums.T.astype(jnp.bfloat16)
             return carry
 
         lax.fori_loop(0, z.quarter // tile, one, 0)
@@ -583,10 +593,10 @@
         write.wait()
 
 
-def final(attention, weights, streamed, out_weight, mates, low, high, second, late, sizes, deps):
+def final(attention, weights, streamed, out_weight, mates, low, second, high, late, sizes, deps):
     z = sizes
-    tokens = sum(a.shape[0] for a in attention)
-    operands = attention + weights + mates + low + high + second + late
+    tokens = attention.shape[0]
+    operands = [attention] + weights + mates + low + second + high + late
     specs = [VMEM] * len(operands)
     scratch = [
         pltpu.VMEM((4, z.quarter, tokens), jnp.bfloat16), pltpu.SemaphoreType.DMA((4,))
@@ -600,14 +610,27 @@
         ]
     result, _ = run(
         functools.partial(
-            final_kernel, parts=len(attention), count=len(weights), streamed=streamed,
-            mates=len(mates), fars=len(low), sizes=z,
+            final_kernel, count=len(weights), streamed=streamed, mates=len(mates),
+            fars=len(low), sizes=z,
         ),
         [], operands, specs, deps,
         [jax.ShapeDtypeStruct((z.features, tokens), jnp.bfloat16)], [ANY], "final", z,
-        limit=36 if streamed else 24, scratch=scratch,
+        limit=FETCHING if streamed else 24, scratch=scratch,
     )
     return result[0]
+
+
+def fetch_kernel(ready, launch, out_ref):
+    launch()
+    out_ref[...] = jnp.zeros_like(out_ref)
+
+
+def fetch_pieces(pieces, out_weight, sizes, deps):
+    _, new = run(
+        fetch_kernel, [], [], [], deps, [jax.ShapeDtypeStruct((8, LANES), jnp.float32)], [VMEM],
+        "fetch", sizes, pieces=pieces, weight=out_weight,
+    )
+    return new
 
 
 def shards(
@@ -688,39 +711,48 @@
     half = z.batch // 2
     low, high, every = (0, 1), (2, 3), (0, 1, 2, 3)
 
-    sends = pack(src_table, mig_dest, out_pool, z)
+    sends, tail_q, tail_kv = pack(src_table, mig_dest, out_pool, query_rows, new_kv, z)
     arriving = lax.all_to_all(sends, "inst", split_axis=0, concat_axis=0, tiled=True)
 
-    a, new = attend(
-        table, res_len, query_rows, new_kv, res_pool, 0, half, z, [sends], limit=LARGE_FIRST,
-        **bringing(gives(far, low) + keeps(far, low)),
-    )
-    hold(gives(far, low) + keeps(far, low), new)
-    given, mates = give([a], far, low, "give", [])
-    kept = keep([a], far, low, mates, "keep", [given])
+    tokens = half * z.steps
+    pieces = gives(far, low) + keeps(far, low)
+    rows, new = attend(
+        table, res_len, query_rows, new_kv, res_pool, None, 0, half, z, [sends],
+        limit=LARGE_FIRST, **bringing(pieces),
+    )
+    hold(pieces, new)
+    given, mates = give((rows, 0, tokens), far, low, "give", [])
+    kept = keep((rows, 0, tokens), far, low, mates, "keep", [given])
     got_low = sent(kept)
-    given, mates = give([a], far, high, "give", kept[-1:])
-    kept = keep([a], far, high, mates, "keep", [given])
+    pieces = gives(far, high) + keeps(far, high)
+    rows, new = attend(
+        table, res_len, query_rows, new_kv, res_pool, rows, half, half, z, kept[-1:],
+        **bringing(pieces),
+    )
+    hold(pieces, new)
+    given, mates_low = give((rows, tokens, tokens), far, low, "give", [])
+    given, mates = give((rows, 0, 2 * tokens), far, high, "give", [given])
+    kept = keep((rows, tokens, tokens), far, low, mates_low, "keep", [given] + got_low)
+    got_second = sent(kept)
+    kept = keep((rows, 0, 2 * tokens), far, high, mates, "keep", kept[-1:])
     got_high = sent(kept)
-    b, new = attend(
-        table, res_len, query_rows, new_kv, res_pool, half, half, z, kept[-1:],
-        **bringing(gives([0], every)),
-    )
-    hold(gives([0], every), new)
-    given, mates = give([b], far, every, "give", got_low)
-    kept = keep([b], far, every, mates, "keep", [given] + got_high)
-    got_second = sent(kept)
-    (b, d, arrived), new = settle(
-        mig_dest, mig_len, arriving, query_rows, new_kv, b, z, kept[-1:]
-    )
-    given, mates = give([d], far, every, "give_last", [], joined=True)
-    given, own_mates = give([a, b], [0], every, "give_own", [given])
-    kept = keep([d], far, every, mates, "keep_last", [given])
+    early = gives([0], every)
+    new = fetch_pieces(early, out_weight, z, kept[-1:])
+    hold(early, new)
+    (rows, last, arrived), _ = settle(
+        mig_dest, mig_len, arriving, tail_q, tail_kv, rows, z, new[:1]
+    )
+    late = (last, 0, last.shape[0])
+    given, mates = give(late, far, every, "give_last", [], joined=True)
+    kept = keep(late, far, every, mates, "keep_last", [given])
     got_late = sent(kept)
+    whole = (rows, 0, 2 * tokens)
+    given, own_low = give(whole, [0], low, "give_own", kept[-1:] + got_second)
+    given, own_high = give(whole, [0], high, "give_own", [given] + got_late)
     weights, streamed = at_hand(keeps([0], every))
     hidden = final(
-        [a, b], weights, streamed, out_weight, own_mates, got_low, got_high, got_second, got_late,
-        z, kept[-1:],
+        rows, weights, streamed, out_weight, own_low + own_high, got_low, got_second, got_high,
+        got_late, z, [given],
     )
     return (arrived, hidden)
 

time: 102 us -> 100 us (0.980)
  local copies, waits for them, and re-layouts: 15.5 us -> 13 us
  waiting for transfers between devices: 10.9 us -> 13.3 us
  starting transfers between devices: 14.8 us -> 13.4 us
    ppermute x13 -> x11, waiting for transfers between devices: 4.44 us -> 7.18 us  [mate_of(): return lax.ppermute(x, 'tp', to_mate)]
    unnamed x80 -> x76, local copies, waits for them, and re-layouts: 15.5 us -> 13 us
    pallas_call x14 -> x16, Pallas kernels: 59.5 us -> 58.6 us  [run(): pl.pallas_call(call, grid_spec=pltpu.PrefetchScalarGridSpec(num_scalar_pr...]
    ppermute x13 -> x11, starting transfers between devices: 3.24 us -> 2.74 us  [mate_of(): return lax.ppermute(x, 'tp', to_mate)]
  transfers between devices with their start and end apart: 18 -> 16, of which waited for: 10 -> 8; matrix products, arithmetic and copies ran while one was open for 0% -> 0% of each run, Pallas kernels for 45% -> 45%
where the time goes in v6:
time: 100 us; the launch traced here: 99.6 us
  Pallas kernels  58.6 us (59%)
  starting transfers between devices  13.4 us (13%)
  waiting for transfers between devices  13.3 us (13%)
  local copies, waits for them, and re-layouts  13 us (13%)
  between operations  1.22 us (1%)
    pallas_call x16, Pallas kernels, run(): pl.pallas_call(call, grid_spec=pltpu.PrefetchScalarGridSpec(num_scalar_pr...  58.6 us
    unnamed x76, local copies, waits for them, and re-layouts  13 us
    ppermute x11, waiting for transfers between devices, mate_of(): return lax.ppermute(x, 'tp', to_mate)  7.18 us
    all_to_all x1, starting transfers between devices, shards(): lax.all_to_all(sends, 'inst', split_axis=0, concat_axis=0, tiled=True)  6.46 us
    ppermute x4, waiting for transfers between devices, across(): return lax.ppermute(x, 'tp', [(i, (i + shift) % tps) for i in range(tps)])  6.15 us
    ppermute x4, starting transfers between devices, across(): return lax.ppermute(x, 'tp', [(i, (i + shift) % tps) for i in range(tps)])  4.22 us
    ppermute x11, starting transfers between devices, mate_of(): return lax.ppermute(x, 'tp', to_mate)  2.74 us
  transfers between devices with their start and end apart: 16, of which 8 were waited for; matrix products, arithmetic and copies ran while one was open for 0% of the time, Pallas kernels for 45%

profile of v6, /device:TPU:0, one launch (start us, length us, event | category | flops | bytes accessed | tf_op | source)
XLA Modules:
  0.0 99.6 jit_solution(16576444603742870977)
XLA Ops:
  0.6 3.5 %pack.1 = (bf16[4,2,32,16,256]{4,3,2,1,0:T(8,128)(2,1)}, bf16[256,128]{1,0:T(8,128)(2,1)}, bf16[32,256]{1,0:T(8,128)(2,1)}) custom-call(s32[1,2,32]{2,1,0:T(2,128)} %refs_0_.3, s32[8]{0:T(128)} %refs_0_.5, bf16[1,2,64,16,256]{4,3,2,1,0:T(8,128)(2,1)} %refs_2_.1, bf16[8192,128]{1,0:T(8,128)(2,1)} %bitcast.4, bf16[128,4,2,256]{3,2,1,0:T(2,128)(2,1)} %refs_3_.3), custom_call_target="tpu_custom_call" | custom-call | bytes 1024 | tf_op jit(solution)/shard_map/pack/pallas_call | solution.py:135
  4.2 6.5 %all-to-all-start = ((bf16[4,2,32,16,256]{4,3,2,1,0:T(8,128)(2,1)}), bf16[4,2,32,16,256]{4,3,2,1,0:T(8,128)(2,1)}, u32[]{:S(2)}, u32[]{:S(2)}) async-start(bf16[4,2,32,16,256]{4,3,2,1,0:T(8,128)(2,1)} %get-tuple-element.32.refs_6_), calls=%async_computation | async-start | bytes 4194304 | tf_op jit(solution)/shard_map/all_to_all | solution.py:715
  10.6 1.6 %copy-done = bf16[128,4,16,128]{3,2,1,0:T(8,128)(2,1)S(1)} copy-done((bf16[128,4,16,128]{3,2,1,0:T(8,128)(2,1)S(1)}, bf16[128,4,16,128]{3,2,1,0:T(8,128)(2,1)}, u32[]{:S(2)}) %copy-start) | copy-done | bytes 2097176
  12.2 1.2 %copy-done.22 = bf16[1,2,64,16,256]{4,3,2,1,0:T(8,128)(2,1)S(1)} copy-done((bf16[1,2,64,16,256]{4,3,2,1,0:T(8,128)(2,1)S(1)}, bf16[1,2,64,16,256]{4,3,2,1,0:T(8,128)(2,1)}, u32[]{:S(2)}) %copy-start.22) | copy-done | bytes 1048600
  13.4 6.3 %attend.2 = (bf16[512,2048]{1,0:T(8,128)(2,1)S(1)}, bf16[2048,512]{1,0:T(8,128)(2,1)S(1)}, bf16[2048,512]{1,0:T(8,128)(2,1)S(1)}, bf16[2048,512]{1,0:T(8,128)(2,1)S(1)}, bf16[2048,512]{1,0:T(8,128)(2,1)S(1)}) custom-call(s32[8,125]{1,0:T(8,128)S(1)} %bitcast.7, s32[1,125]{1,0:T(1,128)S(1)} %copy-done.36, bf16[8192,128]{1,0:T(8,128)(2,1)S(1)} %bitcast.5, ...), custom_call_target="tpu_custom_call" | custom-call | bytes 1024 | tf_op jit(solution)/shard_map/attend/pallas_call | solution.py:135
  19.7 1.8 %give.3 = (bf16[256,512]{1,0:T(8,128)(2,1)S(1)}, bf16[256,512]{1,0:T(8,128)(2,1)S(1)}) custom-call(bf16[512,2048]{1,0:T(8,128)(2,1)S(1)} %get-tuple-element.35.refs_0_.refs_6_, bf16[2048,512]{1,0:T(8,128)(2,1)S(1)} %get-tuple-element.38.refs_1_, bf16[2048,512]{1,0:T(8,128)(2,1)S(1)} %get-tuple-element.39.refs_2_), custom_call_target="tpu_custom_call" | custom-call | bytes 1024 | tf_op jit(solution)/shard_map/give/pallas_call | solution.py:135
  23.5 1.8 %keep.3.refs_7_ = bf16[256,1024]{1,0:T(8,128)(2,1)S(1)} custom-call(bf16[512,2048]{1,0:T(8,128)(2,1)S(1)} %get-tuple-element.35.refs_0_.refs_6_, bf16[2048,512]{1,0:T(8,128)(2,1)S(1)} %get-tuple-element.36.refs_1_, bf16[2048,512]{1,0:T(8,128)(2,1)S(1)} %get-tuple-element.37.refs_2_, bf16[256,512]{1,0:T(8,128)(2,1)S(1)} %collective-permute-done.refs_3_, ...), custom_call_target="tpu_custom_call" | custom-call | bytes 1024 | tf_op jit(solution)/shard_map/keep/pallas_call | solution.py:135
  25.3 1.6 %collective-permute-start.6 = (bf16[256,1024]{1,0:T(8,128)(2,1)S(1)}, bf16[256,1024]{1,0:T(8,128)(2,1)S(1)}, u32[]{:S(2)}, u32[]{:S(2)}) collective-permute-start(bf16[256,1024]{1,0:T(8,128)(2,1)S(1)} %keep.3.refs_7_), channel_id=1, source_target_pairs={{0,2},{1,3},{2,0},{3,1},{4,6},{5,7},{6,4},{7,5},{8,10},{9,11},{10,... | collective-permute-start | bytes 1572872 | tf_op jit(solution)/shard_map/ppermute | solution.py:662
  26.9 6.3 %attend.3 = (bf16[512,2048]{1,0:T(8,128)(2,1)S(1)}, bf16[2048,512]{1,0:T(8,128)(2,1)S(1)}, bf16[2048,512]{1,0:T(8,128)(2,1)S(1)}, bf16[2048,512]{1,0:T(8,128)(2,1)S(1)}, bf16[2048,512]{1,0:T(8,128)(2,1)S(1)}) custom-call(s32[8,125]{1,0:T(8,128)S(1)} %bitcast.8, s32[1,125]{1,0:T(1,128)S(1)} %copy-done.36, ...), custom_call_target="tpu_custom_call", output_to_operand_aliasing={{0}: (6, {})} | custom-call | bytes 1024 | tf_op jit(solution)/shard_map/attend/pallas_call | solution.py:135
  33.3 1.8 %give.4 = (bf16[256,512]{1,0:T(8,128)(2,1)S(1)}, bf16[256,512]{1,0:T(8,128)(2,1)S(1)}) custom-call(bf16[512,2048]{1,0:T(8,128)(2,1)S(1)} %get-tuple-element.42.refs_0_.refs_5_, bf16[2048,512]{1,0:T(8,128)(2,1)S(1)} %get-tuple-element.38.refs_1_, bf16[2048,512]{1,0:T(8,128)(2,1)S(1)} %get-tuple-element.39.refs_2_), custom_call_target="tpu_custom_call" | custom-call | bytes 1024 | tf_op jit(solution)/shard_map/give/pallas_call | solution.py:135
  35.1 2.9 %give.5 = (bf16[512,512]{1,0:T(8,128)(2,1)S(1)}, bf16[512,512]{1,0:T(8,128)(2,1)S(1)}) custom-call(bf16[512,2048]{1,0:T(8,128)(2,1)S(1)} %get-tuple-element.42.refs_0_.refs_5_, bf16[2048,512]{1,0:T(8,128)(2,1)S(1)} %get-tuple-element.45.refs_1_.refs_3_, bf16[2048,512]{1,0:T(8,128)(2,1)S(1)} %get-tuple-element.46.refs_2_.refs_4_, ...), custom_call_target="tpu_custom_call" | custom-call | bytes 1024 | tf_op jit(solution)/shard_map/give/pallas_call | solution.py:135
  38.0 1.3 %copy-done.16 = bf16[2048,512]{1,0:T(8,128)(2,1)} copy-done((bf16[2048,512]{1,0:T(8,128)(2,1)}, bf16[2048,512]{1,0:T(8,128)(2,1)S(1)}, u32[]{:S(2)}) %copy-start.16) | copy-done | bytes 2097176
  40.3 2.0 %collective-permute-done.5.refs_4_ = bf16[256,512]{1,0:T(8,128)(2,1)S(1)} collective-permute-done((bf16[256,512]{1,0:T(8,128)(2,1)S(1)}, bf16[256,512]{1,0:T(8,128)(2,1)S(1)}, u32[]{:S(2)}, u32[]{:S(2)}) %collective-permute-start.5) | collective-permute-done | bytes 262176 | tf_op jit(solution)/shard_map/ppermute | solution.py:658
  42.8 2.6 %keep.4.refs_5_ = bf16[256,1024]{1,0:T(8,128)(2,1)} custom-call(bf16[512,2048]{1,0:T(8,128)(2,1)S(1)} %get-tuple-element.42.refs_0_.refs_5_, bf16[2048,512]{1,0:T(8,128)(2,1)S(1)} %get-tuple-element.36.refs_1_, bf16[2048,512]{1,0:T(8,128)(2,1)S(1)} %get-tuple-element.37.refs_2_, bf16[256,512]{1,0:T(8,128)(2,1)S(1)} %collective-permute-done.4.refs_3_, ...), custom_call_target="tpu_custom_call" | custom-call | bytes 1024 | tf_op jit(solution)/shard_map/keep/pallas_call | solution.py:135
  45.9 2.9 %keep.5.refs_1_ = bf16[512,1024]{1,0:T(8,128)(2,1)S(1)} custom-call(bf16[512,2048]{1,0:T(8,128)(2,1)S(1)} %get-tuple-element.42.refs_0_.refs_5_, bf16[2048,512]{1,0:T(8,128)(2,1)S(1)} %get-tuple-element.43.refs_1_.refs_3_, bf16[2048,512]{1,0:T(8,128)(2,1)S(1)} %get-tuple-element.44.refs_2_.refs_4_, bf16[512,512]{1,0:T(8,128)(2,1)S(1)} %collective-permute-done.2.refs_3_, ...), custom_call_target="tpu_custom_call" | custom-call | bytes 1024 | tf_op jit(solution)/shard_map/keep/pallas_call | solution.py:135
  48.8 1.6 %collective-permute-start.14 = (bf16[512,1024]{1,0:T(8,128)(2,1)S(1)}, bf16[512,1024]{1,0:T(8,128)(2,1)}, u32[]{:S(2)}, u32[]{:S(2)}) collective-permute-start(bf16[512,1024]{1,0:T(8,128)(2,1)S(1)} %keep.5.refs_1_), channel_id=1, source_target_pairs={{0,2},{1,3},{2,0},{3,1},{4,6},{5,7},{6,4},{7,5},{8,10},{9,11},{10,... | collective-permute-start | bytes 3145736 | tf_op jit(solution)/shard_map/ppermute | solution.py:662
  50.4 4.1 %fetch.1 = (f32[8,128]{1,0:T(8,128)}, bf16[2048,512]{1,0:T(8,128)(2,1)S(1)}, bf16[2048,512]{1,0:T(8,128)(2,1)S(1)}, bf16[2048,512]{1,0:T(8,128)(2,1)S(1)}, bf16[2048,512]{1,0:T(8,128)(2,1)S(1)}) custom-call(bf16[2048,8192]{1,0:T(8,128)(2,1)} %refs_9_.1, bf16[512,1024]{1,0:T(8,128)(2,1)S(1)} %keep.5.refs_1_), custom_call_target="tpu_custom_call" | custom-call | bytes 1024 | tf_op jit(solution)/shard_map/fetch/pallas_call | solution.py:135
  54.6 1.4 %copy-done.18 = bf16[2048,512]{1,0:T(8,128)(2,1)} copy-done((bf16[2048,512]{1,0:T(8,128)(2,1)}, bf16[2048,512]{1,0:T(8,128)(2,1)S(1)}, u32[]{:S(2)}) %copy-start.18) | copy-done | bytes 2097176
  56.0 1.4 %copy-done.24 = bf16[2048,512]{1,0:T(8,128)(2,1)} copy-done((bf16[2048,512]{1,0:T(8,128)(2,1)}, bf16[2048,512]{1,0:T(8,128)(2,1)S(1)}, u32[]{:S(2)}) %copy-start.24) | copy-done | bytes 2097176
  57.3 1.4 %copy-done.26 = bf16[2048,512]{1,0:T(8,128)(2,1)} copy-done((bf16[2048,512]{1,0:T(8,128)(2,1)}, bf16[2048,512]{1,0:T(8,128)(2,1)S(1)}, u32[]{:S(2)}) %copy-start.26) | copy-done | bytes 2097176
  58.7 1.3 %copy-done.28 = bf16[2048,512]{1,0:T(8,128)(2,1)} copy-done((bf16[2048,512]{1,0:T(8,128)(2,1)}, bf16[2048,512]{1,0:T(8,128)(2,1)S(1)}, u32[]{:S(2)}) %copy-start.28) | copy-done | bytes 2097176
  60.1 1.6 %copy-done.19 = bf16[2048,512]{1,0:T(8,128)(2,1)S(1)} copy-done((bf16[2048,512]{1,0:T(8,128)(2,1)S(1)}, bf16[2048,512]{1,0:T(8,128)(2,1)}, u32[]{:S(2)}) %copy-start.19) | copy-done | bytes 2097176
  61.6 4.5 %settle.1 = (bf16[512,2048]{1,0:T(8,128)(2,1)S(1)}, bf16[16,2048]{1,0:T(8,128)(2,1)S(1)}, bf16[1,3,2,512,256]{4,3,2,1,0:T(8,128)(2,1)}) custom-call(s32[8]{0:T(128)S(1)} %copy-done.35, s32[8]{0:T(128)S(1)} %copy-done.37, bf16[4,2,32,16,256]{4,3,2,1,0:T(8,128)(2,1)} %all-to-all-done.refs_2_, ...), custom_call_target="tpu_custom_call", output_to_operand_aliasing={{0}: (5, {})} | custom-call | bytes 1024 | tf_op jit(solution)/shard_map/settle/pallas_call | solution.py:135
  66.1 1.6 %copy-done.17 = bf16[2048,512]{1,0:T(8,128)(2,1)S(1)} copy-done((bf16[2048,512]{1,0:T(8,128)(2,1)S(1)}, bf16[2048,512]{1,0:T(8,128)(2,1)}, u32[]{:S(2)}) %copy-start.17) | copy-done | bytes 2097176
  67.7 2.0 %give_last.1.refs_6_ = bf16[16,2048]{1,0:T(8,128)(2,1)S(1)} custom-call(bf16[16,2048]{1,0:T(8,128)(2,1)S(1)} %get-tuple-element.55.refs_0_, bf16[2048,512]{1,0:T(8,128)(2,1)S(1)} %copy-done.3, bf16[2048,512]{1,0:T(8,128)(2,1)S(1)} %copy-done.5, bf16[2048,512]{1,0:T(8,128)(2,1)S(1)} %copy-done.15, bf16[2048,512]{1,0:T(8,128)(2,1)S(1)} %copy-done.17), custom_call_target="tpu_custom_call" | custom-call | bytes 1024 | tf_op jit(solution)/shard_map/give_last/pallas_call | solution.py:135
  69.8 1.2 %collective-permute-done.7.refs_5_ = bf16[16,2048]{1,0:T(8,128)(2,1)S(1)} collective-permute-done((bf16[16,2048]{1,0:T(8,128)(2,1)S(1)}, bf16[16,2048]{1,0:T(8,128)(2,1)S(1)}, u32[]{:S(2)}, u32[]{:S(2)}) %collective-permute-start.7) | collective-permute-done | bytes 65568 | tf_op jit(solution)/shard_map/ppermute | solution.py:658
  71.2 2.0 %keep_last.1.refs_3_ = bf16[16,2048]{1,0:T(8,128)(2,1)S(1)} custom-call(bf16[16,2048]{1,0:T(8,128)(2,1)S(1)} %get-tuple-element.55.refs_0_, bf16[2048,512]{1,0:T(8,128)(2,1)S(1)} %copy-done.7, bf16[2048,512]{1,0:T(8,128)(2,1)S(1)} %copy-done.9, bf16[2048,512]{1,0:T(8,128)(2,1)S(1)} %copy-done.11, bf16[2048,512]{1,0:T(8,128)(2,1)S(1)} %copy-done.13, ...), custom_call_target="tpu_custom_call" | custom-call | bytes 1024 | tf_op jit(solution)/shard_map/keep_last/pallas_call | solution.py:135
  73.8 2.9 %give_own.2 = (bf16[512,512]{1,0:T(8,128)(2,1)S(1)}, bf16[512,512]{1,0:T(8,128)(2,1)S(1)}) custom-call(bf16[512,2048]{1,0:T(8,128)(2,1)S(1)} %get-tuple-element.53.refs_0_, bf16[2048,512]{1,0:T(8,128)(2,1)S(1)} %copy-done.20, bf16[2048,512]{1,0:T(8,128)(2,1)S(1)} %copy-done.29, bf16[16,2048]{1,0:T(8,128)(2,1)S(1)} %keep_last.1.refs_3_, ...), custom_call_target="tpu_custom_call" | custom-call | bytes 1024 | tf_op jit(solution)/shard_map/give_own/pallas_call | solution.py:135
  77.3 6.1 %collective-permute-done.11.refs_4_.refs_8_ = bf16[16,2048]{1,0:T(8,128)(2,1)S(1)} collective-permute-done((bf16[16,2048]{1,0:T(8,128)(2,1)S(1)}, bf16[16,2048]{1,0:T(8,128)(2,1)S(1)}, u32[]{:S(2)}, u32[]{:S(2)}) %collective-permute-start.11) | collective-permute-done | bytes 65568 | tf_op jit(solution)/shard_map/ppermute | solution.py:662
  83.4 3.1 %give_own.3 = (bf16[512,512]{1,0:T(8,128)(2,1)S(1)}, bf16[512,512]{1,0:T(8,128)(2,1)S(1)}) custom-call(bf16[512,2048]{1,0:T(8,128)(2,1)S(1)} %get-tuple-element.53.refs_0_, bf16[2048,512]{1,0:T(8,128)(2,1)S(1)} %copy-done.25, bf16[2048,512]{1,0:T(8,128)(2,1)S(1)} %copy-done.27, bf16[512,512]{1,0:T(8,128)(2,1)S(1)} %get-tuple-element.56.refs_3_, ...), custom_call_target="tpu_custom_call" | custom-call | bytes 1024 | tf_op jit(solution)/shard_map/give_own/pallas_call | solution.py:135
  87.1 1.4 %collective-permute-done.13.refs_4_ = bf16[512,512]{1,0:T(8,128)(2,1)S(1)} collective-permute-done((bf16[512,512]{1,0:T(8,128)(2,1)S(1)}, bf16[512,512]{1,0:T(8,128)(2,1)S(1)}, u32[]{:S(2)}, u32[]{:S(2)}) %collective-permute-start.13) | collective-permute-done | bytes 524320 | tf_op jit(solution)/shard_map/ppermute | solution.py:658
  89.2 10.2 %final.1 = bf16[2048,512]{1,0:T(8,128)(2,1)} custom-call(bf16[512,2048]{1,0:T(8,128)(2,1)S(1)} %get-tuple-element.53.refs_0_, bf16[512,512]{1,0:T(8,128)(2,1)S(1)} %collective-permute-done.9.refs_1_, bf16[512,512]{1,0:T(8,128)(2,1)S(1)} %collective-permute-done.10.refs_2_, bf16[512,512]{1,0:T(8,128)(2,1)S(1)} %collective-permute-done.12.refs_3_, ...), custom_call_target="tpu_custom_call" | custom-call | bytes 1024 | tf_op jit(solution)/shard_map/final/pallas_call | solution.py:135
  (92 shorter events, 6.6 us)
Async XLA Ops:
  4.1 6.5 %copy-start.21 = (bf16[128,4,2,256]{3,2,1,0:T(2,128)(2,1)S(1)}, bf16[128,4,2,256]{3,2,1,0:T(2,128)(2,1)}, u32[]{:S(2)}) copy-start(bf16[128,4,2,256]{3,2,1,0:T(2,128)(2,1)} %refs_3_.3) | copy-start | bytes 1572868
  4.1 6.5 %copy-start.34 = (s32[1,125,8]{1,2,0:T(8,128)S(1)}, s32[1,125,8]{1,2,0:T(8,128)}, u32[]{:S(2)}) copy-start(s32[1,125,8]{1,2,0:T(8,128)} %param.11) | copy-start | bytes 12004
  4.1 6.5 %copy-start.36 = (s32[1,125]{1,0:T(1,128)S(1)}, s32[1,125]{1,0:T(1,128)}, u32[]{:S(2)}) copy-start(s32[1,125]{1,0:T(1,128)} %refs_1_.6) | copy-start | bytes 1504
  4.2 55.9 %all-to-all-start = ((bf16[4,2,32,16,256]{4,3,2,1,0:T(8,128)(2,1)}), bf16[4,2,32,16,256]{4,3,2,1,0:T(8,128)(2,1)}, u32[]{:S(2)}, u32[]{:S(2)}) async-start(bf16[4,2,32,16,256]{4,3,2,1,0:T(8,128)(2,1)} %get-tuple-element.32.refs_6_), calls=%async_computation | async-start | bytes 4194304 | tf_op jit(solution)/shard_map/all_to_all | solution.py:715
  19.7 13.5 %copy-start.2 = (bf16[2048,512]{1,0:T(8,128)(2,1)}, bf16[2048,512]{1,0:T(8,128)(2,1)S(1)}, u32[]{:S(2)}) copy-start(bf16[2048,512]{1,0:T(8,128)(2,1)S(1)} %get-tuple-element.38.refs_1_) | copy-start | bytes 6291460
  19.7 13.5 %copy-start.4 = (bf16[2048,512]{1,0:T(8,128)(2,1)}, bf16[2048,512]{1,0:T(8,128)(2,1)S(1)}, u32[]{:S(2)}) copy-start(bf16[2048,512]{1,0:T(8,128)(2,1)S(1)} %get-tuple-element.39.refs_2_) | copy-start | bytes 6291460
  19.7 23.0 %copy-start.6 = (bf16[2048,512]{1,0:T(8,128)(2,1)}, bf16[2048,512]{1,0:T(8,128)(2,1)S(1)}, u32[]{:S(2)}) copy-start(bf16[2048,512]{1,0:T(8,128)(2,1)S(1)} %get-tuple-element.36.refs_1_) | copy-start | bytes 6291460
  19.7 23.0 %copy-start.8 = (bf16[2048,512]{1,0:T(8,128)(2,1)}, bf16[2048,512]{1,0:T(8,128)(2,1)S(1)}, u32[]{:S(2)}) copy-start(bf16[2048,512]{1,0:T(8,128)(2,1)S(1)} %get-tuple-element.37.refs_2_) | copy-start | bytes 6291460
  21.6 1.6 %collective-permute-start.1 = (bf16[256,512]{1,0:T(8,128)(2,1)S(1)}, bf16[256,512]{1,0:T(8,128)(2,1)S(1)}, u32[]{:S(2)}, u32[]{:S(2)}) collective-permute-start(bf16[256,512]{1,0:T(8,128)(2,1)S(1)} %get-tuple-element.41), channel_id=1, source_target_pairs={{0,1},{1,0},{2,3},{3,2},{4,5},{5,4},{6,7},{7,6},{8,9},{9,8},{10,11... | collective-permute-start | bytes 786440 | tf_op jit(solution)/shard_map/ppermute | solution.py:658
  21.6 1.9 %collective-permute-start = (bf16[256,512]{1,0:T(8,128)(2,1)S(1)}, bf16[256,512]{1,0:T(8,128)(2,1)S(1)}, u32[]{:S(2)}, u32[]{:S(2)}) collective-permute-start(bf16[256,512]{1,0:T(8,128)(2,1)S(1)} %get-tuple-element.40.refs_5_), channel_id=1, source_target_pairs={{0,1},{1,0},{2,3},{3,2},{4,5},{5,4},{6,7},{7,6},{8,9},{9,8},{10,11... | collective-permute-start | bytes 786440 | tf_op jit(solution)/shard_map/ppermute | solution.py:658
  25.3 17.4 %collective-permute-start.6 = (bf16[256,1024]{1,0:T(8,128)(2,1)S(1)}, bf16[256,1024]{1,0:T(8,128)(2,1)S(1)}, u32[]{:S(2)}, u32[]{:S(2)}) collective-permute-start(bf16[256,1024]{1,0:T(8,128)(2,1)S(1)} %keep.3.refs_7_), channel_id=1, source_target_pairs={{0,2},{1,3},{2,0},{3,1},{4,6},{5,7},{6,4},{7,5},{8,10},{9,11},{10,... | collective-permute-start | bytes 1572872 | tf_op jit(solution)/shard_map/ppermute | solution.py:662
  33.2 12.6 %copy-start.10 = (bf16[2048,512]{1,0:T(8,128)(2,1)}, bf16[2048,512]{1,0:T(8,128)(2,1)S(1)}, u32[]{:S(2)}) copy-start(bf16[2048,512]{1,0:T(8,128)(2,1)S(1)} %get-tuple-element.43.refs_1_.refs_3_) | copy-start | bytes 6291460
  33.2 12.6 %copy-start.12 = (bf16[2048,512]{1,0:T(8,128)(2,1)}, bf16[2048,512]{1,0:T(8,128)(2,1)S(1)}, u32[]{:S(2)}) copy-start(bf16[2048,512]{1,0:T(8,128)(2,1)S(1)} %get-tuple-element.44.refs_2_.refs_4_) | copy-start | bytes 6291460
  39.3 6.5 %collective-permute-start.3 = (bf16[512,512]{1,0:T(8,128)(2,1)S(1)}, bf16[512,512]{1,0:T(8,128)(2,1)S(1)}, u32[]{:S(2)}, u32[]{:S(2)}) collective-permute-start(bf16[512,512]{1,0:T(8,128)(2,1)S(1)} %get-tuple-element.49), channel_id=1, source_target_pairs={{0,1},{1,0},{2,3},{3,2},{4,5},{5,4},{6,7},{7,6},{8,9},{9,8},{10,11... | collective-permute-start | bytes 1572872 | tf_op jit(solution)/shard_map/ppermute | solution.py:658
  39.3 6.5 %collective-permute-start.2 = (bf16[512,512]{1,0:T(8,128)(2,1)S(1)}, bf16[512,512]{1,0:T(8,128)(2,1)S(1)}, u32[]{:S(2)}, u32[]{:S(2)}) collective-permute-start(bf16[512,512]{1,0:T(8,128)(2,1)S(1)} %get-tuple-element.48.refs_5_), channel_id=1, source_target_pairs={{0,1},{1,0},{2,3},{3,2},{4,5},{5,4},{6,7},{7,6},{8,9},{9,8},{10,11... | collective-permute-start | bytes 1572872 | tf_op jit(solution)/shard_map/ppermute | solution.py:658
  39.8 2.5 %collective-permute-start.5 = (bf16[256,512]{1,0:T(8,128)(2,1)S(1)}, bf16[256,512]{1,0:T(8,128)(2,1)S(1)}, u32[]{:S(2)}, u32[]{:S(2)}) collective-permute-start(bf16[256,512]{1,0:T(8,128)(2,1)S(1)} %get-tuple-element.50), channel_id=1, source_target_pairs={{0,1},{1,0},{2,3},{3,2},{4,5},{5,4},{6,7},{7,6},{8,9},{9,8},{10,11... | collective-permute-start | bytes 786440 | tf_op jit(solution)/shard_map/ppermute | solution.py:658
  39.8 2.9 %collective-permute-start.4 = (bf16[256,512]{1,0:T(8,128)(2,1)S(1)}, bf16[256,512]{1,0:T(8,128)(2,1)S(1)}, u32[]{:S(2)}, u32[]{:S(2)}) collective-permute-start(bf16[256,512]{1,0:T(8,128)(2,1)S(1)} %get-tuple-element.47.refs_3_), channel_id=1, source_target_pairs={{0,1},{1,0},{2,3},{3,2},{4,5},{5,4},{6,7},{7,6},{8,9},{9,8},{10,11... | collective-permute-start | bytes 786440 | tf_op jit(solution)/shard_map/ppermute | solution.py:658
  45.4 28.4 %collective-permute-start.8 = (bf16[256,1024]{1,0:T(8,128)(2,1)}, bf16[256,1024]{1,0:T(8,128)(2,1)}, u32[]{:S(2)}, u32[]{:S(2)}) collective-permute-start(bf16[256,1024]{1,0:T(8,128)(2,1)} %keep.4.refs_5_), channel_id=1, source_target_pairs={{0,2},{1,3},{2,0},{3,1},{4,6},{5,7},{6,4},{7,5},{8,10},{9,11},{10,... | collective-permute-start | bytes 1572872 | tf_op jit(solution)/shard_map/ppermute | solution.py:662
  48.8 11.2 %copy-start.32 = (bf16[256,128]{1,0:T(8,128)(2,1)S(1)}, bf16[256,128]{1,0:T(8,128)(2,1)}, u32[]{:S(2)}) copy-start(bf16[256,128]{1,0:T(8,128)(2,1)} %get-tuple-element.33.refs_3_) | copy-start | bytes 196612
  48.8 11.2 %copy-start.33 = (bf16[32,256]{1,0:T(8,128)(2,1)S(1)}, bf16[32,256]{1,0:T(8,128)(2,1)}, u32[]{:S(2)}) copy-start(bf16[32,256]{1,0:T(8,128)(2,1)} %get-tuple-element.34.refs_4_) | copy-start | bytes 49156
  48.8 11.2 %copy-start.35 = (s32[8]{0:T(128)S(1)}, s32[8]{0:T(128)}, u32[]{:S(2)}) copy-start(s32[8]{0:T(128)} %refs_0_.5) | copy-start | bytes 100
  48.8 11.2 %copy-start.37 = (s32[8]{0:T(128)S(1)}, s32[8]{0:T(128)}, u32[]{:S(2)}) copy-start(s32[8]{0:T(128)} %refs_1_.7) | copy-start | bytes 100
  48.8 38.2 %collective-permute-start.14 = (bf16[512,1024]{1,0:T(8,128)(2,1)S(1)}, bf16[512,1024]{1,0:T(8,128)(2,1)}, u32[]{:S(2)}, u32[]{:S(2)}) collective-permute-start(bf16[512,1024]{1,0:T(8,128)(2,1)S(1)} %keep.5.refs_1_), channel_id=1, source_target_pairs={{0,2},{1,3},{2,0},{3,1},{4,6},{5,7},{6,4},{7,5},{8,10},{9,11},{10,... | collective-permute-start | bytes 3145736 | tf_op jit(solution)/shard_map/ppermute | solution.py:662
  69.8 1.3 %collective-permute-start.7 = (bf16[16,2048]{1,0:T(8,128)(2,1)S(1)}, bf16[16,2048]{1,0:T(8,128)(2,1)S(1)}, u32[]{:S(2)}, u32[]{:S(2)}) collective-permute-start(bf16[16,2048]{1,0:T(8,128)(2,1)S(1)} %give_last.1.refs_6_), channel_id=1, source_target_pairs={{0,1},{1,0},{2,3},{3,2},{4,5},{5,4},{6,7},{7,6},{8,9},{9,8},{10,11... | collective-permute-start | bytes 196616 | tf_op jit(solution)/shard_map/ppermute | solution.py:658
  73.2 10.2 %collective-permute-start.11 = (bf16[16,2048]{1,0:T(8,128)(2,1)S(1)}, bf16[16,2048]{1,0:T(8,128)(2,1)S(1)}, u32[]{:S(2)}, u32[]{:S(2)}) collective-permute-start(bf16[16,2048]{1,0:T(8,128)(2,1)S(1)} %keep_last.1.refs_3_), channel_id=1, source_target_pairs={{0,2},{1,3},{2,0},{3,1},{4,6},{5,7},{6,4},{7,5},{8,10},{9,11},{10,... | collective-permute-start | bytes 196616 | tf_op jit(solution)/shard_map/ppermute | solution.py:662
  73.8 9.6 %copy-start.25 = (bf16[2048,512]{1,0:T(8,128)(2,1)S(1)}, bf16[2048,512]{1,0:T(8,128)(2,1)}, u32[]{:S(2)}) copy-start(bf16[2048,512]{1,0:T(8,128)(2,1)} %copy-done.24) | copy-start | bytes 6291460
  73.8 9.6 %copy-start.27 = (bf16[2048,512]{1,0:T(8,128)(2,1)S(1)}, bf16[2048,512]{1,0:T(8,128)(2,1)}, u32[]{:S(2)}) copy-start(bf16[2048,512]{1,0:T(8,128)(2,1)} %copy-done.26) | copy-start | bytes 6291460
  76.7 10.4 %collective-permute-start.10 = (bf16[512,512]{1,0:T(8,128)(2,1)S(1)}, bf16[512,512]{1,0:T(8,128)(2,1)S(1)}, u32[]{:S(2)}, u32[]{:S(2)}) collective-permute-start(bf16[512,512]{1,0:T(8,128)(2,1)S(1)} %get-tuple-element.57), channel_id=1, source_target_pairs={{0,1},{1,0},{2,3},{3,2},{4,5},{5,4},{6,7},{7,6},{8,9},{9,8},{10,11... | collective-permute-start | bytes 1572872 | tf_op jit(solution)/shard_map/ppermute | solution.py:658
  76.8 10.3 %collective-permute-start.9 = (bf16[512,512]{1,0:T(8,128)(2,1)S(1)}, bf16[512,512]{1,0:T(8,128)(2,1)S(1)}, u32[]{:S(2)}, u32[]{:S(2)}) collective-permute-start(bf16[512,512]{1,0:T(8,128)(2,1)S(1)} %get-tuple-element.56.refs_3_), channel_id=1, source_target_pairs={{0,1},{1,0},{2,3},{3,2},{4,5},{5,4},{6,7},{7,6},{8,9},{9,8},{10,11... | collective-permute-start | bytes 1572872 | tf_op jit(solution)/shard_map/ppermute | solution.py:658
  83.4 5.8 %copy-start.31 = (bf16[256,1024]{1,0:T(8,128)(2,1)S(1)}, bf16[256,1024]{1,0:T(8,128)(2,1)}, u32[]{:S(2)}) copy-start(bf16[256,1024]{1,0:T(8,128)(2,1)} %copy-done.30) | copy-start | bytes 1572868
  86.5 2.0 %collective-permute-start.13 = (bf16[512,512]{1,0:T(8,128)(2,1)S(1)}, bf16[512,512]{1,0:T(8,128)(2,1)S(1)}, u32[]{:S(2)}, u32[]{:S(2)}) collective-permute-start(bf16[512,512]{1,0:T(8,128)(2,1)S(1)} %get-tuple-element.61), channel_id=1, source_target_pairs={{0,1},{1,0},{2,3},{3,2},{4,5},{5,4},{6,7},{7,6},{8,9},{9,8},{10,11... | collective-permute-start | bytes 1572872 | tf_op jit(solution)/shard_map/ppermute | solution.py:658
  86.6 2.6 %collective-permute-start.12 = (bf16[512,512]{1,0:T(8,128)(2,1)S(1)}, bf16[512,512]{1,0:T(8,128)(2,1)S(1)}, u32[]{:S(2)}, u32[]{:S(2)}) collective-permute-start(bf16[512,512]{1,0:T(8,128)(2,1)S(1)} %get-tuple-element.60.refs_10_), channel_id=1, source_target_pairs={{0,1},{1,0},{2,3},{3,2},{4,5},{5,4},{6,7},{7,6},{8,9},{9,8},{10,11... | collective-permute-start | bytes 1572872 | tf_op jit(solution)/shard_map/ppermute | solution.py:658
  (22 other events, 59.0 us)

commit v7 on v6

--- a/solution.py
+++ b/solution.py
@@ -14,8 +14,8 @@
 LANES = 128
 GROUP = 16
 TOGETHER = 8
-LARGE_FIRST = 40
-FETCHING = 33
+LARGE_FIRST = 12
+FETCHING = 16
 
 
 def dot_t(left, right):
@@ -189,13 +189,11 @@
         ],
         [],
         [
-            jax.ShapeDtypeStruct(
-                (z.insts, z.slots, z.mig_blocks, z.block, 2 * z.width), out_pool.dtype
-            ),
+            pltpu.HBM((z.insts, z.slots, z.mig_blocks, z.block, 2 * z.width), out_pool.dtype),
             jax.ShapeDtypeStruct((z.tail_q, z.width), out_pool.dtype),
             jax.ShapeDtypeStruct((z.tail_kv, 2 * z.width), out_pool.dtype),
         ],
-        [VMEM] * 3, "pack", z, limit=60, grid=(1,),
+        [VMEM] * 3, "pack", z, limit=16, grid=(1,),
     )
     return result
 
@@ -365,8 +363,8 @@
 
 
 def settle_kernel(
-    ready, launch, dest_ref, len_ref, got_hbm, query_ref, kv_ref, old_ref, out_ref, last_ref,
-    arrived_hbm, rows_ref, got_ref, keep_ref, sems, *, sizes
+    ready, launch, dest_ref, len_ref, got_hbm, query_ref, kv_ref, old_ref, last_ref, arrived_hbm,
+    rows_ref, got_ref, keep_ref, sems, *, sizes
 ):
     z = sizes
     launch()
@@ -421,9 +419,7 @@
         at = slice(h * z.width, (h + 1) * z.width)
         column = rows_ref[pl.ds(h, tokens, stride=z.heads), :]
         old = old_ref[:, at].astype(jnp.float32)
-        value = jnp.where(filled, column, old).astype(jnp.bfloat16)
-        out_ref[:, at] = value
-        last_ref[:, at] = value
+        last_ref[:, at] = jnp.where(filled, column, old).astype(jnp.bfloat16)
     for write in writes:
         write.wait()
 
@@ -440,52 +436,26 @@
         [HBM, VMEM, VMEM, spec],
         deps,
         [
-            jax.ShapeDtypeStruct(attention.shape, jnp.bfloat16),
             jax.ShapeDtypeStruct((tokens, attention.shape[1]), jnp.bfloat16),
             jax.ShapeDtypeStruct((1, z.cap) + cache, jnp.bfloat16),
         ],
-        [spec, VMEM, ANY], "settle", z, grid=(1,),
+        [VMEM, ANY], "settle", z, grid=(1,),
         scratch=[
             pltpu.VMEM((z.insts * z.per, z.width), jnp.float32),
             pltpu.VMEM((z.cap,) + got.shape[1:], jnp.bfloat16),
             pltpu.VMEM((z.cap,) + cache, jnp.bfloat16),
             pltpu.SemaphoreType.DMA((2, z.cap)),
         ],
-        aliases={5: 0}, **fetch,
-    )
-
-
-def project_kernel(
-    ready, launch, attention, *refs, first, tokens, count, streamed, added, joined, kept, sizes
-):
+        **fetch,
+    )
+
+
+def project_kernel(ready, launch, attention, *refs, first, tokens, count, added, joined, sizes):
     launch()
-    weights = list(refs[:count])
-    position = count
-    extra = refs[position : position + added]
-    position += added
-    source = refs[position]
-    position += bool(streamed)
-    outs = 1 if joined else count + len(streamed)
-    out_refs = refs[position : position + outs]
-    copies = [None] * count
-    if streamed:
-        if kept:
-            buffers = refs[position + outs : position + outs + len(streamed)]
-        else:
-            buffers = [refs[-2].at[n] for n in range(len(streamed))]
-        for n, piece in enumerate(streamed):
-            first = pl.multiple_of(piece_columns(piece, sizes), LANES)
-            copy = pltpu.make_async_copy(
-                source.at[:, pl.ds(first, sizes.quarter)], buffers[n], refs[-1].at[n]
-            )
-            copy.start()
-            copies.append(copy)
-            weights.append(buffers[n])
+    weights, extra, out_refs = refs[:count], refs[count : count + added], refs[count + added :]
     width = sizes.quarter
     tile = min(width, 256)
-    for n, (weight, copy) in enumerate(zip(weights, copies)):
-        if copy is not None:
-            copy.wait()
+    for n, weight in enumerate(weights):
 
         def one(j, carry, n=n, weight=weight):
             at = pl.ds(pl.multiple_of(j * tile, tile), tile)
@@ -496,48 +466,33 @@
             elif added:
                 result = result + extra[n][:, at].astype(jnp.float32)
             if joined:
-                out_refs[0][:, to] = result.astype(jnp.bfloat16)
+                out_refs[0][:, to] = result.astype(out_refs[0].dtype)
             else:
-                out_refs[n][:, at] = result.astype(jnp.bfloat16)
+                out_refs[n][:, at] = result.astype(out_refs[n].dtype)
             return carry
 
         lax.fori_loop(0, width // tile, one, 0)
 
 
-def project(attention, weights, streamed, out_weight, mates, joined, kept, sizes, name, deps,
-            pieces=()):
+def project(attention, weights, mates, joined, dtype, sizes, name, deps, **fetch):
     attention, first, tokens = attention
-    count = len(weights) + len(streamed)
+    count = len(weights)
     if joined:
-        shapes = [jax.ShapeDtypeStruct((tokens, count * sizes.quarter), jnp.bfloat16)]
+        shapes = [jax.ShapeDtypeStruct((tokens, count * sizes.quarter), dtype)]
     else:
-        shapes = [jax.ShapeDtypeStruct((tokens, sizes.quarter), jnp.bfloat16)] * count
-    results = len(shapes)
+        shapes = [jax.ShapeDtypeStruct((tokens, sizes.quarter), dtype)] * count
     operands = [attention] + weights + mates
-    specs = [VMEM] * len(operands)
-    scratch = []
-    piece = (sizes.depth, sizes.quarter)
-    if streamed:
-        operands = operands + [out_weight]
-        specs = specs + [HBM]
-        if kept:
-            shapes = shapes + [jax.ShapeDtypeStruct(piece, jnp.bfloat16)] * len(streamed)
-        else:
-            scratch.append(pltpu.VMEM((len(streamed),) + piece, jnp.bfloat16))
-        scratch.append(pltpu.SemaphoreType.DMA((len(streamed),)))
-    result, new = run(
+    return run(
         functools.partial(
-            project_kernel, first=first, tokens=tokens, count=len(weights), streamed=streamed,
-            added=len(mates), joined=joined, kept=kept, sizes=sizes,
+            project_kernel, first=first, tokens=tokens, count=count, added=len(mates),
+            joined=joined, sizes=sizes,
         ),
-        [], operands, specs, deps, shapes, [VMEM] * len(shapes), name, sizes,
-        limit=FETCHING if streamed or pieces else 16, scratch=scratch,
-        pieces=pieces, weight=out_weight,
-    )
-    return result[:results], result[results:], new
-
-
-def final_kernel(ready, launch, attention, *refs, count, streamed, mates, fars, sizes):
+        [], operands, [VMEM] * len(operands), deps, shapes, [VMEM] * len(shapes), name, sizes,
+        **fetch,
+    )
+
+
+def finish_kernel(ready, launch, own, own_late, *refs, fars, sizes):
     z = sizes
     refs = list(refs)
 
@@ -546,46 +501,32 @@
         del refs[:n]
         return taken
 
-    weights, extra = take(count), take(mates)
-    low, second, high, late = take(fars), take(fars), take(fars), take(fars)
-    source = take(bool(streamed))
-    (out_hbm,) = take(1)
-    block_ref, block_sems = take(2)
-    copies = [None] * count
-    for n, piece in enumerate(streamed):
-        first = pl.multiple_of(piece_columns(piece, z), LANES)
-        copy = pltpu.make_async_copy(
-            source[0].at[:, pl.ds(first, z.quarter)], refs[0].at[n], refs[1].at[n]
-        )
-        copy.start()
-        copies.append(copy)
-        weights.append(refs[0].at[n])
+    low, high, second, late = take(fars), take(fars), take(fars), take(fars)
+    out_hbm, block_ref, sems = refs
+    rows = own_late.shape[0]
     tile = min(z.quarter, 256)
     writes = []
-    for n, (weight, copy) in enumerate(zip(weights, copies)):
-        if copy is not None:
-            copy.wait()
-
-        def one(j, carry, n=n, weight=weight):
+    for n in range(4):
+
+        def one(j, carry, n=n):
             start = pl.multiple_of(j * tile, tile)
-            at = pl.ds(start, tile)
-            whole = pl.ds(n * z.quarter + start, tile)
+            at = pl.ds(n * z.quarter + start, tile)
             half = pl.ds((n % 2) * z.quarter + start, tile)
-            sums = dot(attention[...], weight[:, at]) + extra[n][:, at].astype(jnp.float32)
+            begin = low[0].shape[0]
+            first = own[:begin, at]
+            rest = own[begin:-rows, at]
+            last = own_late[:, at]
             for k in range(fars):
-                if n < 2:
-                    parts = [low[k][:, half], second[k][:, half]]
-                else:
-                    parts = [high[k][:, half]]
-                rows = late[k].shape[0]
-                parts = parts[:-1] + [parts[-1][:-rows], late[k][:, whole]]
-                sums = sums + jnp.concatenate(parts, axis=0).astype(jnp.float32)
-            block_ref[n, at, :] = sums.T.astype(jnp.bfloat16)
+                first = first + (low if n < 2 else high)[k][:, half].astype(jnp.float32)
+                rest = rest + second[k][:-rows, at].astype(jnp.float32)
+                last = last + late[k][:, at].astype(jnp.float32)
+            sums = jnp.concatenate([first, rest, last], axis=0)
+            block_ref[n, pl.ds(start, tile), :] = sums.T.astype(jnp.bfloat16)
             return carry
 
         lax.fori_loop(0, z.quarter // tile, one, 0)
         write = pltpu.make_async_copy(
-            block_ref.at[n], out_hbm.at[pl.ds(n * z.quarter, z.quarter)], block_sems.at[n]
+            block_ref.at[n], out_hbm.at[pl.ds(n * z.quarter, z.quarter)], sems.at[n]
         )
         write.start()
         writes.append(write)
@@ -593,44 +534,19 @@
         write.wait()
 
 
-def final(attention, weights, streamed, out_weight, mates, low, second, high, late, sizes, deps):
+def finish(own, own_late, low, high, second, late, sizes, deps):
     z = sizes
-    tokens = attention.shape[0]
-    operands = [attention] + weights + mates + low + second + high + late
-    specs = [VMEM] * len(operands)
-    scratch = [
-        pltpu.VMEM((4, z.quarter, tokens), jnp.bfloat16), pltpu.SemaphoreType.DMA((4,))
-    ]
-    if streamed:
-        operands = operands + [out_weight]
-        specs = specs + [HBM]
-        scratch += [
-            pltpu.VMEM((len(streamed), z.depth, z.quarter), jnp.bfloat16),
-            pltpu.SemaphoreType.DMA((len(streamed),)),
-        ]
+    tokens = own.shape[0]
+    operands = [own, own_late] + low + high + second + late
     result, _ = run(
-        functools.partial(
-            final_kernel, count=len(weights), streamed=streamed, mates=len(mates),
-            fars=len(low), sizes=z,
-        ),
-        [], operands, specs, deps,
-        [jax.ShapeDtypeStruct((z.features, tokens), jnp.bfloat16)], [ANY], "final", z,
-        limit=FETCHING if streamed else 24, scratch=scratch,
+        functools.partial(finish_kernel, fars=len(low), sizes=z),
+        [], operands, [VMEM] * len(operands), deps,
+        [jax.ShapeDtypeStruct((z.features, tokens), jnp.bfloat16)], [ANY], "finish", z,
+        scratch=[
+            pltpu.VMEM((4, z.quarter, tokens), jnp.bfloat16), pltpu.SemaphoreType.DMA((4,))
+        ],
     )
     return result[0]
-
-
-def fetch_kernel(ready, launch, out_ref):
-    launch()
-    out_ref[...] = jnp.zeros_like(out_ref)
-
-
-def fetch_pieces(pieces, out_weight, sizes, deps):
-    _, new = run(
-        fetch_kernel, [], [], [], deps, [jax.ShapeDtypeStruct((8, LANES), jnp.float32)], [VMEM],
-        "fetch", sizes, pieces=pieces, weight=out_weight,
-    )
-    return new
 
 
 def shards(
@@ -648,8 +564,13 @@
     z = Sizes(queries, res_pool, res_table, src_table, mig_dest, out_weight)
     tps, chips = z.tps, z.chips
     table = res_table[0].T
-    query_rows = queries.reshape(z.batch * z.per, z.width)
-
+    out_weight, res_pool, out_pool, new_kv, query_rows, table, res_len, src_table, mig_dest, mig_len = (
+        pltpu.with_memory_space_constraint(x, pltpu.HBM)
+        for x in (
+            out_weight, res_pool, out_pool, new_kv, queries.reshape(z.batch * z.per, z.width),
+            table, res_len, src_table, mig_dest, mig_len,
+        )
+    )
     to_mate = [(i, i + 1 - 2 * (i % CORES)) for i in range(tps)]
     far = range(1, chips)
     held = {}
@@ -670,37 +591,31 @@
     def keeps(ks, parts):
         return [(k, True, part) for k in ks for part in parts]
 
-    def at_hand(pieces):
-        here = [held[piece] for piece in pieces if piece in held]
-        return here, [piece for piece in pieces if piece not in held]
-
     def hold(pieces, arrays):
         held.update(zip(pieces, arrays))
 
-    def give(attention, ks, parts, name, deps, pieces=(), kept=True, joined=False):
-        weights, streamed = at_hand(gives(ks, parts))
-        results, mine, new = project(
-            attention, weights, streamed, out_weight, [], joined, kept, z, name, deps, pieces
+    def give(attention, ks, parts, name, deps, pieces=(), joined=False):
+        weights = [held[piece] for piece in gives(ks, parts)]
+        results, new = project(
+            attention, weights, [], joined, jnp.bfloat16, z, name, deps, **bringing(pieces)
         )
-        if kept:
-            hold(streamed, mine)
         hold(pieces, new)
         return results[0], [mate_of(result) for result in results]
 
-    def keep(attention, ks, parts, mates, name, deps, kept=True):
+    def keep(attention, ks, parts, mates, name, deps, pieces=(), dtype=jnp.bfloat16):
         results = []
         for n, k in enumerate(ks):
-            weights, streamed = at_hand(keeps([k], parts))
+            weights = [held[piece] for piece in keeps([k], parts)]
             if len(mates) == 1:
                 width = mates[0].shape[1] // len(ks)
                 now = [mates[0][:, n * width : (n + 1) * width] if len(ks) > 1 else mates[0]]
             else:
                 now = mates[n * len(parts) : (n + 1) * len(parts)]
-            result, mine, _ = project(
-                attention, weights, streamed, out_weight, now, True, kept, z, name, deps
+            bring = pieces if n == 0 else ()
+            result, new = project(
+                attention, weights, now, True, dtype, z, name, deps, **bringing(bring)
             )
-            if kept:
-                hold(streamed, mine)
+            hold(bring, new)
             deps = [result[0]]
             results.append(result[0])
         return results
@@ -718,42 +633,39 @@
     pieces = gives(far, low) + keeps(far, low)
     rows, new = attend(
         table, res_len, query_rows, new_kv, res_pool, None, 0, half, z, [sends],
-        limit=LARGE_FIRST, **bringing(pieces),
+        **bringing(pieces),
     )
     hold(pieces, new)
-    given, mates = give((rows, 0, tokens), far, low, "give", [])
-    kept = keep((rows, 0, tokens), far, low, mates, "keep", [given])
+    a, b, whole = (rows, 0, tokens), None, None
+    given, mates = give(a, far, low, "give", [], gives(far, (2,)))
+    kept = keep(a, far, low, mates, "keep", [given], gives(far, (3,)))
     got_low = sent(kept)
-    pieces = gives(far, high) + keeps(far, high)
+    given, mates = give(a, far, high, "give", kept[-1:], keeps(far, high))
+    kept = keep(a, far, high, mates, "keep", [given])
+    got_high = sent(kept)
     rows, new = attend(
         table, res_len, query_rows, new_kv, res_pool, rows, half, half, z, kept[-1:],
-        **bringing(pieces),
-    )
-    hold(pieces, new)
-    given, mates_low = give((rows, tokens, tokens), far, low, "give", [])
-    given, mates = give((rows, 0, 2 * tokens), far, high, "give", [given])
-    kept = keep((rows, tokens, tokens), far, low, mates_low, "keep", [given] + got_low)
+        **bringing(gives([0], every)),
+    )
+    hold(gives([0], every), new)
+    b, whole = (rows, tokens, tokens), (rows, 0, 2 * tokens)
+    given, mates = give(b, far, every, "give", got_low, keeps([0], low))
+    kept = keep(b, far, every, mates, "keep", [given] + got_high, keeps([0], high))
     got_second = sent(kept)
-    kept = keep((rows, 0, 2 * tokens), far, high, mates, "keep", kept[-1:])
-    got_high = sent(kept)
-    early = gives([0], every)
-    new = fetch_pieces(early, out_weight, z, kept[-1:])
-    hold(early, new)
-    (rows, last, arrived), _ = settle(
-        mig_dest, mig_len, arriving, tail_q, tail_kv, rows, z, new[:1]
+
+    given, mates = give(whole, [0], every, "give_own", kept[-1:])
+    own = keep(whole, [0], every, mates, "keep_own", [given], dtype=jnp.float32)
+
+    (last, arrived), _ = settle(
+        mig_dest, mig_len, arriving, tail_q, tail_kv, rows, z, own
     )
     late = (last, 0, last.shape[0])
     given, mates = give(late, far, every, "give_last", [], joined=True)
+    given, own_mates = give(late, [0], every, "give_last", [given], joined=True)
     kept = keep(late, far, every, mates, "keep_last", [given])
     got_late = sent(kept)
-    whole = (rows, 0, 2 * tokens)
-    given, own_low = give(whole, [0], low, "give_own", kept[-1:] + got_second)
-    given, own_high = give(whole, [0], high, "give_own", [given] + got_late)
-    weights, streamed = at_hand(keeps([0], every))
-    hidden = final(
-        rows, weights, streamed, out_weight, own_low + own_high, got_low, got_second, got_high,
-        got_late, z, [given],
-    )
+    own_late = keep(late, [0], every, own_mates, "keep_last", kept[-1:], dtype=jnp.float32)
+    hidden = finish(own[0], own_late[0], got_low, got_high, got_second, got_late, z, [])
     return (arrived, hidden)
 
 

time: 100 us -> 100 us (level)
  Pallas kernels: 58.6 us -> 66 us
  local copies, waits for them, and re-layouts: 13 us -> 7.81 us
  waiting for transfers between devices: 13.3 us -> 10 us
  starting transfers between devices: 13.4 us -> 14.4 us
    pallas_call x16 -> x17, Pallas kernels: 58.6 us -> 66 us  [run(): pl.pallas_call(call, grid_spec=pltpu.PrefetchScalarGridSpec(num_scalar_pr...]
    unnamed x76 -> x72, local copies, waits for them, and re-layouts: 13 us -> 7.81 us
    ppermute x4, waiting for transfers between devices: 6.15 us -> 4.07 us  [across(): return lax.ppermute(x, 'tp', [(i, (i + shift) % tps) for i in range(tps)])]
    ppermute x11 -> x14, waiting for transfers between devices: 7.18 us -> 5.95 us  [mate_of(): return lax.ppermute(x, 'tp', to_mate)]
    ppermute x11 -> x14, starting transfers between devices: 2.74 us -> 3.68 us  [mate_of(): return lax.ppermute(x, 'tp', to_mate)]
  transfers between devices with their start and end apart: 16 -> 19, of which waited for: 8 -> 10; matrix products, arithmetic and copies ran while one was open for 0% -> 0% of each run, Pallas kernels for 45% -> 60%
where the time goes in v7:
time: 100 us; the launch traced here: 99.6 us
  Pallas kernels  66 us (66%)
  starting transfers between devices  14.4 us (14%)
  waiting for transfers between devices  10 us (10%)
  local copies, waits for them, and re-layouts  7.81 us (8%)
  between operations  1.3 us (1%)
    pallas_call x17, Pallas kernels, run(): pl.pallas_call(call, grid_spec=pltpu.PrefetchScalarGridSpec(num_scalar_pr...  66 us
    unnamed x72, local copies, waits for them, and re-layouts  7.81 us
    all_to_all x1, starting transfers between devices, shards(): lax.all_to_all(sends, 'inst', split_axis=0, concat_axis=0, tiled=True)  6.33 us
    ppermute x14, waiting for transfers between devices, mate_of(): return lax.ppermute(x, 'tp', to_mate)  5.95 us
    ppermute x4, starting transfers between devices, across(): return lax.ppermute(x, 'tp', [(i, (i + shift) % tps) for i in range(tps)])  4.37 us
    ppermute x4, waiting for transfers between devices, across(): return lax.ppermute(x, 'tp', [(i, (i + shift) % tps) for i in range(tps)])  4.07 us
    ppermute x14, starting transfers between devices, mate_of(): return lax.ppermute(x, 'tp', to_mate)  3.68 us
  transfers between devices with their start and end apart: 19, of which 10 were waited for; matrix products, arithmetic and copies ran while one was open for 0% of the time, Pallas kernels for 60%

profile of v7, /device:TPU:0, one launch (start us, length us, event | category | flops | bytes accessed | tf_op | source)
XLA Modules:
  0.0 99.6 jit_solution(593316127030902960)
XLA Ops:
  0.6 3.5 %pack.1 = (bf16[4,2,32,16,256]{4,3,2,1,0:T(8,128)(2,1)}, bf16[256,128]{1,0:T(8,128)(2,1)S(1)}, bf16[32,256]{1,0:T(8,128)(2,1)S(1)}) custom-call(s32[1,2,32]{2,1,0:T(2,128)} %refs_0_.2, s32[8]{0:T(128)} %refs_0_.3, bf16[1,2,64,16,256]{4,3,2,1,0:T(8,128)(2,1)} %refs_2_.1, bf16[8192,128]{1,0:T(8,128)(2,1)} %bitcast.4, bf16[128,4,2,256]{3,2,1,0:T(2,128)(2,1)} %refs_3_.7), custom_call_target="tpu_custom_call" | custom-call | bytes 1024 | tf_op jit(solution)/shard_map/pack/pallas_call | solution.py:135
  4.1 6.3 %all-to-all-start = ((bf16[4,2,32,16,256]{4,3,2,1,0:T(8,128)(2,1)}), bf16[4,2,32,16,256]{4,3,2,1,0:T(8,128)(2,1)}, u32[]{:S(2)}, u32[]{:S(2)}) async-start(bf16[4,2,32,16,256]{4,3,2,1,0:T(8,128)(2,1)} %get-tuple-element.39.refs_6_), calls=%async_computation | async-start | bytes 4194304 | tf_op jit(solution)/shard_map/all_to_all | solution.py:630
  10.4 1.6 %copy-done.19 = bf16[4,2,32,16,256]{4,3,2,1,0:T(8,128)(2,1)S(1)} copy-done((bf16[4,2,32,16,256]{4,3,2,1,0:T(8,128)(2,1)S(1)}, bf16[4,2,32,16,256]{4,3,2,1,0:T(8,128)(2,1)}, u32[]{:S(2)}) %copy-start.19) | copy-done | bytes 2097176
  12.1 7.8 %attend.2 = (bf16[512,2048]{1,0:T(8,128)(2,1)S(1)}, bf16[2048,512]{1,0:T(8,128)(2,1)S(1)}, bf16[2048,512]{1,0:T(8,128)(2,1)S(1)}, bf16[2048,512]{1,0:T(8,128)(2,1)S(1)}, bf16[2048,512]{1,0:T(8,128)(2,1)S(1)}) custom-call(s32[8,125]{1,0:T(8,128)} %bitcast.7, s32[1,125]{1,0:T(1,128)} %refs_1_.6, bf16[8192,128]{1,0:T(8,128)(2,1)} %bitcast.5, ...), custom_call_target="tpu_custom_call" | custom-call | bytes 1024 | tf_op jit(solution)/shard_map/attend/pallas_call | solution.py:135
  19.9 3.2 %give.3 = (bf16[256,512]{1,0:T(8,128)(2,1)S(1)}, bf16[256,512]{1,0:T(8,128)(2,1)S(1)}, bf16[2048,512]{1,0:T(8,128)(2,1)S(1)}) custom-call(bf16[512,2048]{1,0:T(8,128)(2,1)S(1)} %get-tuple-element.42.refs_0_.refs_6_, bf16[2048,512]{1,0:T(8,128)(2,1)S(1)} %get-tuple-element.43.refs_1_, bf16[2048,512]{1,0:T(8,128)(2,1)S(1)} %get-tuple-element.44.refs_2_, ...), custom_call_target="tpu_custom_call" | custom-call | bytes 1024 | tf_op jit(solution)/shard_map/give/pallas_call | solution.py:135
  23.8 1.0 %collective-permute-done.1.refs_4_ = bf16[256,512]{1,0:T(8,128)(2,1)S(1)} collective-permute-done((bf16[256,512]{1,0:T(8,128)(2,1)S(1)}, bf16[256,512]{1,0:T(8,128)(2,1)S(1)}, u32[]{:S(2)}, u32[]{:S(2)}) %collective-permute-start.1) | collective-permute-done | bytes 262176 | tf_op jit(solution)/shard_map/ppermute | solution.py:579
  25.2 1.8 %keep.3 = (bf16[256,1024]{1,0:T(8,128)(2,1)S(1)}, bf16[2048,512]{1,0:T(8,128)(2,1)S(1)}) custom-call(bf16[512,2048]{1,0:T(8,128)(2,1)S(1)} %get-tuple-element.42.refs_0_.refs_6_, bf16[2048,512]{1,0:T(8,128)(2,1)S(1)} %get-tuple-element.46.refs_1_, bf16[2048,512]{1,0:T(8,128)(2,1)S(1)} %get-tuple-element.47.refs_2_, ...), custom_call_target="tpu_custom_call" | custom-call | bytes 1024 | tf_op jit(solution)/shard_map/keep/pallas_call | solution.py:135
  27.0 1.6 %collective-permute-start.4 = (bf16[256,1024]{1,0:T(8,128)(2,1)S(1)}, bf16[256,1024]{1,0:T(8,128)(2,1)S(1)}, u32[]{:S(2)}, u32[]{:S(2)}) collective-permute-start(bf16[256,1024]{1,0:T(8,128)(2,1)S(1)} %get-tuple-element.51.refs_4_), channel_id=1, source_target_pairs={{0,2},{1,3},{2,0},{3,1},{4,6},{5,7},{6,4},{7,5},{8,10},{9,11},{10,... | collective-permute-start | bytes 1572872 | tf_op jit(solution)/shard_map/ppermute | solution.py:583
  28.6 2.3 %give.4 = (bf16[256,512]{1,0:T(8,128)(2,1)S(1)}, bf16[256,512]{1,0:T(8,128)(2,1)S(1)}, bf16[2048,512]{1,0:T(8,128)(2,1)S(1)}, bf16[2048,512]{1,0:T(8,128)(2,1)S(1)}) custom-call(bf16[512,2048]{1,0:T(8,128)(2,1)S(1)} %get-tuple-element.42.refs_0_.refs_6_, bf16[2048,512]{1,0:T(8,128)(2,1)S(1)} %get-tuple-element.45.refs_1_.refs_3_, ...), custom_call_target="tpu_custom_call" | custom-call | bytes 1024 | tf_op jit(solution)/shard_map/give/pallas_call | solution.py:135
  31.4 1.0 %collective-permute-done.3.refs_4_ = bf16[256,512]{1,0:T(8,128)(2,1)S(1)} collective-permute-done((bf16[256,512]{1,0:T(8,128)(2,1)S(1)}, bf16[256,512]{1,0:T(8,128)(2,1)S(1)}, u32[]{:S(2)}, u32[]{:S(2)}) %collective-permute-start.3) | collective-permute-done | bytes 262176 | tf_op jit(solution)/shard_map/ppermute | solution.py:579
  32.8 1.8 %keep.4.refs_7_ = bf16[256,1024]{1,0:T(8,128)(2,1)S(1)} custom-call(bf16[512,2048]{1,0:T(8,128)(2,1)S(1)} %get-tuple-element.42.refs_0_.refs_6_, bf16[2048,512]{1,0:T(8,128)(2,1)S(1)} %get-tuple-element.52.refs_1_.refs_3_, bf16[2048,512]{1,0:T(8,128)(2,1)S(1)} %get-tuple-element.53.refs_2_.refs_4_, bf16[256,512]{1,0:T(8,128)(2,1)S(1)} %collective-permute-done.2.refs_3_, ...), custom_call_target="tpu_custom_call" | custom-call | bytes 1024 | tf_op jit(solution)/shard_map/keep/pallas_call | solution.py:135
  34.6 0.7 collective-permute-start.9
  35.3 7.8 %attend.3 = (bf16[512,2048]{1,0:T(8,128)(2,1)S(1)}, bf16[2048,512]{1,0:T(8,128)(2,1)S(1)}, bf16[2048,512]{1,0:T(8,128)(2,1)S(1)}, bf16[2048,512]{1,0:T(8,128)(2,1)S(1)}, bf16[2048,512]{1,0:T(8,128)(2,1)S(1)}) custom-call(s32[8,125]{1,0:T(8,128)} %bitcast.8, s32[1,125]{1,0:T(1,128)} %refs_1_.6, ...), custom_call_target="tpu_custom_call", output_to_operand_aliasing={{0}: (6, {})} | custom-call | bytes 1024 | tf_op jit(solution)/shard_map/attend/pallas_call | solution.py:135
  43.3 5.1 %give.5 = (bf16[256,512]{1,0:T(8,128)(2,1)S(1)}, bf16[256,512]{1,0:T(8,128)(2,1)S(1)}, bf16[256,512]{1,0:T(8,128)(2,1)S(1)}, bf16[256,512]{1,0:T(8,128)(2,1)S(1)...) custom-call(bf16[512,2048]{1,0:T(8,128)(2,1)S(1)} %get-tuple-element.56.refs_0_.refs_5_, ...), custom_call_target="tpu_custom_call" | custom-call | bytes 1024 | tf_op jit(solution)/shard_map/give/pallas_call | solution.py:135
  49.5 2.8 %collective-permute-done.9.refs_11_.refs_3_ = bf16[256,1024]{1,0:T(8,128)(2,1)S(1)} collective-permute-done((bf16[256,1024]{1,0:T(8,128)(2,1)S(1)}, bf16[256,1024]{1,0:T(8,128)(2,1)S(1)}, u32[]{:S(2)}, u32[]{:S(2)}) %collective-permute-start.9) | collective-permute-done | bytes 524320 | tf_op jit(solution)/shard_map/ppermute | solution.py:583
  52.3 4.6 %keep.5 = (bf16[256,2048]{1,0:T(8,128)(2,1)}, bf16[2048,512]{1,0:T(8,128)(2,1)S(1)}, bf16[2048,512]{1,0:T(8,128)(2,1)S(1)}) custom-call(bf16[512,2048]{1,0:T(8,128)(2,1)S(1)} %get-tuple-element.56.refs_0_.refs_5_, bf16[2048,512]{1,0:T(8,128)(2,1)S(1)} %get-tuple-element.46.refs_1_, bf16[2048,512]{1,0:T(8,128)(2,1)S(1)} %get-tuple-element.47.refs_2_, ...), custom_call_target="tpu_custom_call" | custom-call | bytes 1024 | tf_op jit(solution)/shard_map/keep/pallas_call | solution.py:135
  57.0 1.6 %collective-permute-start.16 = (bf16[256,2048]{1,0:T(8,128)(2,1)}, bf16[256,2048]{1,0:T(8,128)(2,1)}, u32[]{:S(2)}, u32[]{:S(2)}) collective-permute-start(bf16[256,2048]{1,0:T(8,128)(2,1)} %get-tuple-element.69.refs_5_), channel_id=1, source_target_pairs={{0,2},{1,3},{2,0},{3,1},{4,6},{5,7},{6,4},{7,5},{8,10},{9,11},{10,... | collective-permute-start | bytes 3145736 | tf_op jit(solution)/shard_map/ppermute | solution.py:583
  58.6 5.8 %give_own.1 = (bf16[512,512]{1,0:T(8,128)(2,1)S(1)}, bf16[512,512]{1,0:T(8,128)(2,1)S(1)}, bf16[512,512]{1,0:T(8,128)(2,1)S(1)}, bf16[512,512]{1,0:T(8,128)(2,1)S(1)}) custom-call(bf16[512,2048]{1,0:T(8,128)(2,1)S(1)} %get-tuple-element.56.refs_0_.refs_5_, bf16[2048,512]{1,0:T(8,128)(2,1)S(1)} %get-tuple-element.65.refs_1_, ...), custom_call_target="tpu_custom_call" | custom-call | bytes 1024 | tf_op jit(solution)/shard_map/give_own/pallas_call | solution.py:135
  65.5 0.9 collective-permute-done.11.refs_6_
  66.3 0.7 collective-permute-done.12.refs_7_
  67.1 0.7 collective-permute-done.13.refs_8_
  67.8 0.7 collective-permute-done.10.refs_5_
  68.6 6.0 %keep_own.1.refs_6_.refs_0_ = f32[512,2048]{1,0:T(8,128)S(1)} custom-call(bf16[512,2048]{1,0:T(8,128)(2,1)S(1)} %get-tuple-element.56.refs_0_.refs_5_, bf16[2048,512]{1,0:T(8,128)(2,1)S(1)} %get-tuple-element.57.refs_1_, bf16[2048,512]{1,0:T(8,128)(2,1)S(1)} %get-tuple-element.58.refs_2_, bf16[2048,512]{1,0:T(8,128)(2,1)S(1)} %get-tuple-element.63.refs_3_, ...), custom_call_target="tpu_custom_call" | custom-call | bytes 1024 | tf_op jit(solution)/shard_map/keep_own/pallas_call | solution.py:135
  74.6 2.0 %copy-done = f32[512,2048]{1,0:T(8,128)} copy-done((f32[512,2048]{1,0:T(8,128)}, f32[512,2048]{1,0:T(8,128)S(1)}, u32[]{:S(2)}) %copy-start) | copy-done | bytes 4194328
  76.6 2.2 %copy-done.1 = f32[512,2048]{1,0:T(8,128)S(1)} copy-done((f32[512,2048]{1,0:T(8,128)S(1)}, f32[512,2048]{1,0:T(8,128)}, u32[]{:S(2)}) %copy-start.1) | copy-done | bytes 4194328
  78.8 4.9 %settle.1 = (bf16[16,2048]{1,0:T(8,128)(2,1)S(1)}, bf16[1,3,2,512,256]{4,3,2,1,0:T(8,128)(2,1)}) custom-call(s32[8]{0:T(128)} %refs_0_.3, s32[8]{0:T(128)} %refs_1_.7, bf16[4,2,32,16,256]{4,3,2,1,0:T(8,128)(2,1)} %all-to-all-done.refs_2_, bf16[256,128]{1,0:T(8,128)(2,1)S(1)} %get-tuple-element.40.refs_3_, bf16[32,256]{1,0:T(8,128)(2,1)S(1)} %get-tuple-element.41.refs_4_, ...), custom_call_target="tpu_custom_call" | custom-call | bytes 1024 | tf_op jit(solution)/shard_map/settle/pallas_call | solution.py:135
  83.7 2.0 %give_last.2.refs_5_ = bf16[16,2048]{1,0:T(8,128)(2,1)S(1)} custom-call(bf16[16,2048]{1,0:T(8,128)(2,1)S(1)} %get-tuple-element.75.refs_0_, bf16[2048,512]{1,0:T(8,128)(2,1)S(1)} %copy-done.8, bf16[2048,512]{1,0:T(8,128)(2,1)S(1)} %copy-done.10, bf16[2048,512]{1,0:T(8,128)(2,1)S(1)} %copy-done.12, bf16[2048,512]{1,0:T(8,128)(2,1)S(1)} %copy-done.14), custom_call_target="tpu_custom_call" | custom-call | bytes 1024 | tf_op jit(solution)/shard_map/give_last/pallas_call | solution.py:135
  87.1 2.0 %give_last.3.refs_6_ = bf16[16,2048]{1,0:T(8,128)(2,1)S(1)} custom-call(bf16[16,2048]{1,0:T(8,128)(2,1)S(1)} %get-tuple-element.75.refs_0_, bf16[2048,512]{1,0:T(8,128)(2,1)S(1)} %copy-done.29, bf16[2048,512]{1,0:T(8,128)(2,1)S(1)} %copy-done.31, bf16[2048,512]{1,0:T(8,128)(2,1)S(1)} %copy-done.33, bf16[2048,512]{1,0:T(8,128)(2,1)S(1)} %copy-done.35, ...), custom_call_target="tpu_custom_call" | custom-call | bytes 1024 | tf_op jit(solution)/shard_map/give_last/pallas_call | solution.py:135
  89.8 2.0 %keep_last.2.refs_6_ = bf16[16,2048]{1,0:T(8,128)(2,1)S(1)} custom-call(bf16[16,2048]{1,0:T(8,128)(2,1)S(1)} %get-tuple-element.75.refs_0_, bf16[2048,512]{1,0:T(8,128)(2,1)S(1)} %copy-done.4, bf16[2048,512]{1,0:T(8,128)(2,1)S(1)} %copy-done.6, bf16[2048,512]{1,0:T(8,128)(2,1)S(1)} %copy-done.16, bf16[2048,512]{1,0:T(8,128)(2,1)S(1)} %copy-done.18, ...), custom_call_target="tpu_custom_call" | custom-call | bytes 1024 | tf_op jit(solution)/shard_map/keep_last/pallas_call | solution.py:135
  92.8 2.0 %keep_last.3.refs_1_ = f32[16,2048]{1,0:T(8,128)S(1)} custom-call(bf16[16,2048]{1,0:T(8,128)(2,1)S(1)} %get-tuple-element.75.refs_0_, bf16[2048,512]{1,0:T(8,128)(2,1)S(1)} %copy-done.21, bf16[2048,512]{1,0:T(8,128)(2,1)S(1)} %copy-done.23, bf16[2048,512]{1,0:T(8,128)(2,1)S(1)} %copy-done.25, bf16[2048,512]{1,0:T(8,128)(2,1)S(1)} %copy-done.27, ...), custom_call_target="tpu_custom_call" | custom-call | bytes 1024 | tf_op jit(solution)/shard_map/keep_last/pallas_call | solution.py:135
  94.8 1.3 %collective-permute-done.17.refs_5_ = bf16[16,2048]{1,0:T(8,128)(2,1)S(1)} collective-permute-done((bf16[16,2048]{1,0:T(8,128)(2,1)S(1)}, bf16[16,2048]{1,0:T(8,128)(2,1)S(1)}, u32[]{:S(2)}, u32[]{:S(2)}) %collective-permute-start.17) | collective-permute-done | bytes 65568 | tf_op jit(solution)/shard_map/ppermute | solution.py:583
  96.1 3.3 %finish.1 = bf16[2048,512]{1,0:T(8,128)(2,1)} custom-call(f32[512,2048]{1,0:T(8,128)S(1)} %copy-done.2, f32[16,2048]{1,0:T(8,128)S(1)} %keep_last.3.refs_1_, bf16[256,1024]{1,0:T(8,128)(2,1)S(1)} %collective-permute-done.4.refs_6_.refs_2_, bf16[256,1024]{1,0:T(8,128)(2,1)S(1)} %collective-permute-done.9.refs_11_.refs_3_, ...), custom_call_target="tpu_custom_call" | custom-call | bytes 1024 | tf_op jit(solution)/shard_map/finish/pallas_call | solution.py:135
  (95 shorter events, 7.0 us)
Async XLA Ops:
  4.1 72.5 %all-to-all-start = ((bf16[4,2,32,16,256]{4,3,2,1,0:T(8,128)(2,1)}), bf16[4,2,32,16,256]{4,3,2,1,0:T(8,128)(2,1)}, u32[]{:S(2)}, u32[]{:S(2)}) async-start(bf16[4,2,32,16,256]{4,3,2,1,0:T(8,128)(2,1)} %get-tuple-element.39.refs_6_), calls=%async_computation | async-start | bytes 4194304 | tf_op jit(solution)/shard_map/all_to_all | solution.py:630
  19.9 23.3 %copy-start.7 = (bf16[2048,512]{1,0:T(8,128)(2,1)}, bf16[2048,512]{1,0:T(8,128)(2,1)S(1)}, u32[]{:S(2)}) copy-start(bf16[2048,512]{1,0:T(8,128)(2,1)S(1)} %get-tuple-element.43.refs_1_) | copy-start | bytes 6291460
  19.9 23.3 %copy-start.9 = (bf16[2048,512]{1,0:T(8,128)(2,1)}, bf16[2048,512]{1,0:T(8,128)(2,1)S(1)}, u32[]{:S(2)}) copy-start(bf16[2048,512]{1,0:T(8,128)(2,1)S(1)} %get-tuple-element.44.refs_2_) | copy-start | bytes 6291460
  19.9 32.4 %copy-start.3 = (bf16[2048,512]{1,0:T(8,128)(2,1)}, bf16[2048,512]{1,0:T(8,128)(2,1)S(1)}, u32[]{:S(2)}) copy-start(bf16[2048,512]{1,0:T(8,128)(2,1)S(1)} %get-tuple-element.46.refs_1_) | copy-start | bytes 6291460
  19.9 32.4 %copy-start.5 = (bf16[2048,512]{1,0:T(8,128)(2,1)}, bf16[2048,512]{1,0:T(8,128)(2,1)S(1)}, u32[]{:S(2)}) copy-start(bf16[2048,512]{1,0:T(8,128)(2,1)S(1)} %get-tuple-element.47.refs_2_) | copy-start | bytes 6291460
  23.2 20.1 %copy-start.11 = (bf16[2048,512]{1,0:T(8,128)(2,1)}, bf16[2048,512]{1,0:T(8,128)(2,1)S(1)}, u32[]{:S(2)}) copy-start(bf16[2048,512]{1,0:T(8,128)(2,1)S(1)} %get-tuple-element.45.refs_1_.refs_3_) | copy-start | bytes 6291460
  23.2 1.6 %collective-permute-start.1 = (bf16[256,512]{1,0:T(8,128)(2,1)S(1)}, bf16[256,512]{1,0:T(8,128)(2,1)S(1)}, u32[]{:S(2)}, u32[]{:S(2)}) collective-permute-start(bf16[256,512]{1,0:T(8,128)(2,1)S(1)} %get-tuple-element.49), channel_id=1, source_target_pairs={{0,1},{1,0},{2,3},{3,2},{4,5},{5,4},{6,7},{7,6},{8,9},{9,8},{10,11... | collective-permute-start | bytes 786440 | tf_op jit(solution)/shard_map/ppermute | solution.py:579
  23.3 1.9 %collective-permute-start = (bf16[256,512]{1,0:T(8,128)(2,1)S(1)}, bf16[256,512]{1,0:T(8,128)(2,1)S(1)}, u32[]{:S(2)}, u32[]{:S(2)}) collective-permute-start(bf16[256,512]{1,0:T(8,128)(2,1)S(1)} %get-tuple-element.48.refs_6_), channel_id=1, source_target_pairs={{0,1},{1,0},{2,3},{3,2},{4,5},{5,4},{6,7},{7,6},{8,9},{9,8},{10,11... | collective-permute-start | bytes 786440 | tf_op jit(solution)/shard_map/ppermute | solution.py:579
  27.0 16.3 %copy-start.13 = (bf16[2048,512]{1,0:T(8,128)(2,1)}, bf16[2048,512]{1,0:T(8,128)(2,1)S(1)}, u32[]{:S(2)}) copy-start(bf16[2048,512]{1,0:T(8,128)(2,1)S(1)} %get-tuple-element.50.refs_2_.refs_4_) | copy-start | bytes 6291460
  27.0 16.2 %collective-permute-start.4 = (bf16[256,1024]{1,0:T(8,128)(2,1)S(1)}, bf16[256,1024]{1,0:T(8,128)(2,1)S(1)}, u32[]{:S(2)}, u32[]{:S(2)}) collective-permute-start(bf16[256,1024]{1,0:T(8,128)(2,1)S(1)} %get-tuple-element.51.refs_4_), channel_id=1, source_target_pairs={{0,2},{1,3},{2,0},{3,1},{4,6},{5,7},{6,4},{7,5},{8,10},{9,11},{10,... | collective-permute-start | bytes 1572872 | tf_op jit(solution)/shard_map/ppermute | solution.py:583
  30.8 21.5 %copy-start.15 = (bf16[2048,512]{1,0:T(8,128)(2,1)}, bf16[2048,512]{1,0:T(8,128)(2,1)S(1)}, u32[]{:S(2)}) copy-start(bf16[2048,512]{1,0:T(8,128)(2,1)S(1)} %get-tuple-element.52.refs_1_.refs_3_) | copy-start | bytes 6291460
  30.8 21.5 %copy-start.17 = (bf16[2048,512]{1,0:T(8,128)(2,1)}, bf16[2048,512]{1,0:T(8,128)(2,1)S(1)}, u32[]{:S(2)}) copy-start(bf16[2048,512]{1,0:T(8,128)(2,1)S(1)} %get-tuple-element.53.refs_2_.refs_4_) | copy-start | bytes 6291460
  30.8 1.6 %collective-permute-start.3 = (bf16[256,512]{1,0:T(8,128)(2,1)S(1)}, bf16[256,512]{1,0:T(8,128)(2,1)S(1)}, u32[]{:S(2)}, u32[]{:S(2)}) collective-permute-start(bf16[256,512]{1,0:T(8,128)(2,1)S(1)} %get-tuple-element.55), channel_id=1, source_target_pairs={{0,1},{1,0},{2,3},{3,2},{4,5},{5,4},{6,7},{7,6},{8,9},{9,8},{10,11... | collective-permute-start | bytes 786440 | tf_op jit(solution)/shard_map/ppermute | solution.py:579
  30.9 1.9 %collective-permute-start.2 = (bf16[256,512]{1,0:T(8,128)(2,1)S(1)}, bf16[256,512]{1,0:T(8,128)(2,1)S(1)}, u32[]{:S(2)}, u32[]{:S(2)}) collective-permute-start(bf16[256,512]{1,0:T(8,128)(2,1)S(1)} %get-tuple-element.54.refs_5_), channel_id=1, source_target_pairs={{0,1},{1,0},{2,3},{3,2},{4,5},{5,4},{6,7},{7,6},{8,9},{9,8},{10,11... | collective-permute-start | bytes 786440 | tf_op jit(solution)/shard_map/ppermute | solution.py:579
  34.6 17.6 %collective-permute-start.9 = (bf16[256,1024]{1,0:T(8,128)(2,1)S(1)}, bf16[256,1024]{1,0:T(8,128)(2,1)S(1)}, u32[]{:S(2)}, u32[]{:S(2)}) collective-permute-start(bf16[256,1024]{1,0:T(8,128)(2,1)S(1)} %keep.4.refs_7_), channel_id=1, source_target_pairs={{0,2},{1,3},{2,0},{3,1},{4,6},{5,7},{6,4},{7,5},{8,10},{9,11},{10,... | collective-permute-start | bytes 1572872 | tf_op jit(solution)/shard_map/ppermute | solution.py:583
  43.2 15.4 %copy-start.28 = (bf16[2048,512]{1,0:T(8,128)(2,1)}, bf16[2048,512]{1,0:T(8,128)(2,1)S(1)}, u32[]{:S(2)}) copy-start(bf16[2048,512]{1,0:T(8,128)(2,1)S(1)} %get-tuple-element.65.refs_1_) | copy-start | bytes 6291460
  43.2 15.4 %copy-start.30 = (bf16[2048,512]{1,0:T(8,128)(2,1)}, bf16[2048,512]{1,0:T(8,128)(2,1)S(1)}, u32[]{:S(2)}) copy-start(bf16[2048,512]{1,0:T(8,128)(2,1)S(1)} %get-tuple-element.66.refs_2_) | copy-start | bytes 6291460
  43.2 15.4 %copy-start.32 = (bf16[2048,512]{1,0:T(8,128)(2,1)}, bf16[2048,512]{1,0:T(8,128)(2,1)S(1)}, u32[]{:S(2)}) copy-start(bf16[2048,512]{1,0:T(8,128)(2,1)S(1)} %get-tuple-element.67.refs_3_) | copy-start | bytes 6291460
  48.4 20.2 %copy-start.20 = (bf16[2048,512]{1,0:T(8,128)(2,1)}, bf16[2048,512]{1,0:T(8,128)(2,1)S(1)}, u32[]{:S(2)}) copy-start(bf16[2048,512]{1,0:T(8,128)(2,1)S(1)} %get-tuple-element.57.refs_1_) | copy-start | bytes 6291460
  48.4 20.2 %copy-start.22 = (bf16[2048,512]{1,0:T(8,128)(2,1)}, bf16[2048,512]{1,0:T(8,128)(2,1)S(1)}, u32[]{:S(2)}) copy-start(bf16[2048,512]{1,0:T(8,128)(2,1)S(1)} %get-tuple-element.58.refs_2_) | copy-start | bytes 6291460
  48.4 3.9 %collective-permute-start.6 = (bf16[256,512]{1,0:T(8,128)(2,1)S(1)}, bf16[256,512]{1,0:T(8,128)(2,1)S(1)}, u32[]{:S(2)}, u32[]{:S(2)}) collective-permute-start(bf16[256,512]{1,0:T(8,128)(2,1)S(1)} %get-tuple-element.60), channel_id=1, source_target_pairs={{0,1},{1,0},{2,3},{3,2},{4,5},{5,4},{6,7},{7,6},{8,9},{9,8},{10,11... | collective-permute-start | bytes 786440 | tf_op jit(solution)/shard_map/ppermute | solution.py:579
  48.5 3.8 %collective-permute-start.7 = (bf16[256,512]{1,0:T(8,128)(2,1)S(1)}, bf16[256,512]{1,0:T(8,128)(2,1)S(1)}, u32[]{:S(2)}, u32[]{:S(2)}) collective-permute-start(bf16[256,512]{1,0:T(8,128)(2,1)S(1)} %get-tuple-element.61), channel_id=1, source_target_pairs={{0,1},{1,0},{2,3},{3,2},{4,5},{5,4},{6,7},{7,6},{8,9},{9,8},{10,11... | collective-permute-start | bytes 786440 | tf_op jit(solution)/shard_map/ppermute | solution.py:579
  49.0 3.3 %collective-permute-start.8 = (bf16[256,512]{1,0:T(8,128)(2,1)S(1)}, bf16[256,512]{1,0:T(8,128)(2,1)S(1)}, u32[]{:S(2)}, u32[]{:S(2)}) collective-permute-start(bf16[256,512]{1,0:T(8,128)(2,1)S(1)} %get-tuple-element.62), channel_id=1, source_target_pairs={{0,1},{1,0},{2,3},{3,2},{4,5},{5,4},{6,7},{7,6},{8,9},{9,8},{10,11... | collective-permute-start | bytes 786440 | tf_op jit(solution)/shard_map/ppermute | solution.py:579
  49.0 3.2 %collective-permute-start.5 = (bf16[256,512]{1,0:T(8,128)(2,1)S(1)}, bf16[256,512]{1,0:T(8,128)(2,1)S(1)}, u32[]{:S(2)}, u32[]{:S(2)}) collective-permute-start(bf16[256,512]{1,0:T(8,128)(2,1)S(1)} %get-tuple-element.59.refs_10_), channel_id=1, source_target_pairs={{0,1},{1,0},{2,3},{3,2},{4,5},{5,4},{6,7},{7,6},{8,9},{9,8},{10,11... | collective-permute-start | bytes 786440 | tf_op jit(solution)/shard_map/ppermute | solution.py:579
  57.0 37.8 %collective-permute-start.16 = (bf16[256,2048]{1,0:T(8,128)(2,1)}, bf16[256,2048]{1,0:T(8,128)(2,1)}, u32[]{:S(2)}, u32[]{:S(2)}) collective-permute-start(bf16[256,2048]{1,0:T(8,128)(2,1)} %get-tuple-element.69.refs_5_), channel_id=1, source_target_pairs={{0,2},{1,3},{2,0},{3,1},{4,6},{5,7},{6,4},{7,5},{8,10},{9,11},{10,... | collective-permute-start | bytes 3145736 | tf_op jit(solution)/shard_map/ppermute | solution.py:583
  64.4 2.0 %collective-permute-start.11 = (bf16[512,512]{1,0:T(8,128)(2,1)S(1)}, bf16[512,512]{1,0:T(8,128)(2,1)S(1)}, u32[]{:S(2)}, u32[]{:S(2)}) collective-permute-start(bf16[512,512]{1,0:T(8,128)(2,1)S(1)} %get-tuple-element.71), channel_id=1, source_target_pairs={{0,1},{1,0},{2,3},{3,2},{4,5},{5,4},{6,7},{7,6},{8,9},{9,8},{10,11... | collective-permute-start | bytes 1572872 | tf_op jit(solution)/shard_map/ppermute | solution.py:579
  64.4 2.6 %collective-permute-start.12 = (bf16[512,512]{1,0:T(8,128)(2,1)S(1)}, bf16[512,512]{1,0:T(8,128)(2,1)S(1)}, u32[]{:S(2)}, u32[]{:S(2)}) collective-permute-start(bf16[512,512]{1,0:T(8,128)(2,1)S(1)} %get-tuple-element.72), channel_id=1, source_target_pairs={{0,1},{1,0},{2,3},{3,2},{4,5},{5,4},{6,7},{7,6},{8,9},{9,8},{10,11... | collective-permute-start | bytes 1572872 | tf_op jit(solution)/shard_map/ppermute | solution.py:579
  64.9 2.9 %collective-permute-start.13 = (bf16[512,512]{1,0:T(8,128)(2,1)S(1)}, bf16[512,512]{1,0:T(8,128)(2,1)S(1)}, u32[]{:S(2)}, u32[]{:S(2)}) collective-permute-start(bf16[512,512]{1,0:T(8,128)(2,1)S(1)} %get-tuple-element.73), channel_id=1, source_target_pairs={{0,1},{1,0},{2,3},{3,2},{4,5},{5,4},{6,7},{7,6},{8,9},{9,8},{10,11... | collective-permute-start | bytes 1572872 | tf_op jit(solution)/shard_map/ppermute | solution.py:579
  65.0 3.6 %collective-permute-start.10 = (bf16[512,512]{1,0:T(8,128)(2,1)S(1)}, bf16[512,512]{1,0:T(8,128)(2,1)S(1)}, u32[]{:S(2)}, u32[]{:S(2)}) collective-permute-start(bf16[512,512]{1,0:T(8,128)(2,1)S(1)} %get-tuple-element.70.refs_9_), channel_id=1, source_target_pairs={{0,1},{1,0},{2,3},{3,2},{4,5},{5,4},{6,7},{7,6},{8,9},{9,8},{10,11... | collective-permute-start | bytes 1572872 | tf_op jit(solution)/shard_map/ppermute | solution.py:579
  85.8 3.6 %collective-permute-start.15 = (bf16[16,2048]{1,0:T(8,128)(2,1)S(1)}, bf16[16,2048]{1,0:T(8,128)(2,1)S(1)}, u32[]{:S(2)}, u32[]{:S(2)}) collective-permute-start(bf16[16,2048]{1,0:T(8,128)(2,1)S(1)} %give_last.2.refs_5_), channel_id=1, source_target_pairs={{0,1},{1,0},{2,3},{3,2},{4,5},{5,4},{6,7},{7,6},{8,9},{9,8},{10,11... | collective-permute-start | bytes 196616 | tf_op jit(solution)/shard_map/ppermute | solution.py:579
  89.2 3.1 %collective-permute-start.14 = (bf16[16,2048]{1,0:T(8,128)(2,1)S(1)}, bf16[16,2048]{1,0:T(8,128)(2,1)S(1)}, u32[]{:S(2)}, u32[]{:S(2)}) collective-permute-start(bf16[16,2048]{1,0:T(8,128)(2,1)S(1)} %give_last.3.refs_6_), channel_id=1, source_target_pairs={{0,1},{1,0},{2,3},{3,2},{4,5},{5,4},{6,7},{7,6},{8,9},{9,8},{10,11... | collective-permute-start | bytes 196616 | tf_op jit(solution)/shard_map/ppermute | solution.py:579
  91.8 4.3 %collective-permute-start.17 = (bf16[16,2048]{1,0:T(8,128)(2,1)S(1)}, bf16[16,2048]{1,0:T(8,128)(2,1)S(1)}, u32[]{:S(2)}, u32[]{:S(2)}) collective-permute-start(bf16[16,2048]{1,0:T(8,128)(2,1)S(1)} %keep_last.2.refs_6_), channel_id=1, source_target_pairs={{0,2},{1,3},{2,0},{3,1},{4,6},{5,7},{6,4},{7,5},{8,10},{9,11},{10,... | collective-permute-start | bytes 196616 | tf_op jit(solution)/shard_map/ppermute | solution.py:583
  (23 other events, 106.2 us)

commit v8 on v7

--- a/solution.py
+++ b/solution.py
@@ -145,7 +145,7 @@
             + ([pltpu.SemaphoreType.DMA((fetches,))] if fetches else []),
         ),
         out_shape=list(out_shapes)
-        + [jax.ShapeDtypeStruct((sizes.depth, sizes.quarter), jnp.bfloat16)] * fetches,
+        + [pltpu.VMEM((sizes.depth, sizes.quarter), jnp.bfloat16)] * fetches,
         input_output_aliases=aliases or {},
         compiler_params=pltpu.CompilerParams(vmem_limit_bytes=limit * MIB),
         cost_estimate=pl.CostEstimate(flops=0, bytes_accessed=1024, transcendentals=0),
@@ -189,11 +189,13 @@
         ],
         [],
         [
-            pltpu.HBM((z.insts, z.slots, z.mig_blocks, z.block, 2 * z.width), out_pool.dtype),
+            jax.ShapeDtypeStruct(
+                (z.insts, z.slots, z.mig_blocks, z.block, 2 * z.width), out_pool.dtype
+            ),
             jax.ShapeDtypeStruct((z.tail_q, z.width), out_pool.dtype),
             jax.ShapeDtypeStruct((z.tail_kv, 2 * z.width), out_pool.dtype),
         ],
-        [VMEM] * 3, "pack", z, limit=16, grid=(1,),
+        [VMEM] * 3, "pack", z, limit=60, grid=(1,),
     )
     return result
 
@@ -477,7 +479,9 @@
 def project(attention, weights, mates, joined, dtype, sizes, name, deps, **fetch):
     attention, first, tokens = attention
     count = len(weights)
-    if joined:
+    if dtype == jnp.float32:
+        shapes = [pltpu.VMEM((tokens, count * sizes.quarter), dtype)]
+    elif joined:
         shapes = [jax.ShapeDtypeStruct((tokens, count * sizes.quarter), dtype)]
     else:
         shapes = [jax.ShapeDtypeStruct((tokens, sizes.quarter), dtype)] * count
@@ -492,7 +496,7 @@
     )
 
 
-def finish_kernel(ready, launch, own, own_late, *refs, fars, sizes):
+def finish_kernel(ready, launch, own_low, own_high, own_late, *refs, fars, sizes):
     z = sizes
     refs = list(refs)
 
@@ -513,8 +517,9 @@
             at = pl.ds(n * z.quarter + start, tile)
             half = pl.ds((n % 2) * z.quarter + start, tile)
             begin = low[0].shape[0]
-            first = own[:begin, at]
-            rest = own[begin:-rows, at]
+            own = own_low if n < 2 else own_high
+            first = own[:begin, half]
+            rest = own[begin:-rows, half]
             last = own_late[:, at]
             for k in range(fars):
                 first = first + (low if n < 2 else high)[k][:, half].astype(jnp.float32)
@@ -536,8 +541,8 @@
 
 def finish(own, own_late, low, high, second, late, sizes, deps):
     z = sizes
-    tokens = own.shape[0]
-    operands = [own, own_late] + low + high + second + late
+    tokens = own[0].shape[0]
+    operands = own + [own_late] + low + high + second + late
     result, _ = run(
         functools.partial(finish_kernel, fars=len(low), sizes=z),
         [], operands, [VMEM] * len(operands), deps,
@@ -650,14 +655,16 @@
     hold(gives([0], every), new)
     b, whole = (rows, tokens, tokens), (rows, 0, 2 * tokens)
     given, mates = give(b, far, every, "give", got_low, keeps([0], low))
-    kept = keep(b, far, every, mates, "keep", [given] + got_high, keeps([0], high))
+    kept = keep(b, far, every, mates, "keep", [given], keeps([0], high))
     got_second = sent(kept)
 
-    given, mates = give(whole, [0], every, "give_own", kept[-1:])
-    own = keep(whole, [0], every, mates, "keep_own", [given], dtype=jnp.float32)
+    given, mates_low = give(whole, [0], low, "give_own", kept[-1:] + got_high)
+    given, mates_high = give(whole, [0], high, "give_own", [given])
+    own = keep(whole, [0], low, mates_low, "keep_own", [given], dtype=jnp.float32)
+    own += keep(whole, [0], high, mates_high, "keep_own", own, dtype=jnp.float32)
 
     (last, arrived), _ = settle(
-        mig_dest, mig_len, arriving, tail_q, tail_kv, rows, z, own
+        mig_dest, mig_len, arriving, tail_q, tail_kv, rows, z, own[-1:]
     )
     late = (last, 0, last.shape[0])
     given, mates = give(late, far, every, "give_last", [], joined=True)
@@ -665,7 +672,7 @@
     kept = keep(late, far, every, mates, "keep_last", [given])
     got_late = sent(kept)
     own_late = keep(late, [0], every, own_mates, "keep_last", kept[-1:], dtype=jnp.float32)
-    hidden = finish(own[0], own_late[0], got_low, got_high, got_second, got_late, z, [])
+    hidden = finish(own, own_late[0], got_low, got_high, got_second, got_late, z, [])
     return (arrived, hidden)
 
 

time: 100 us -> 104 us (1.040)
  waiting for transfers between devices: 10 us -> 12.8 us
  local copies, waits for them, and re-layouts: 7.81 us -> 9.48 us
    ppermute x4, waiting for transfers between devices: 4.07 us -> 9.04 us  [across(): return lax.ppermute(x, 'tp', [(i, (i + shift) % tps) for i in range(tps)])]
    ppermute x14, waiting for transfers between devices: 5.95 us -> 3.81 us  [mate_of(): return lax.ppermute(x, 'tp', to_mate)]
    unnamed x72 -> x80, local copies, waits for them, and re-layouts: 7.81 us -> 9.48 us
    pallas_call x17 -> x19, Pallas kernels: 66 us -> 66.1 us  [run(): pl.pallas_call(call, grid_spec=pltpu.PrefetchScalarGridSpec(num_scalar_pr...]
  transfers between devices with their start and end apart: 19 -> 19, of which waited for: 10 -> 9; matrix products, arithmetic and copies ran while one was open for 0% -> 0% of each run, Pallas kernels for 60% -> 57%
where the time goes in v8:
time: 104 us; the launch traced here: 103 us
  Pallas kernels  66.1 us (64%)
  starting transfers between devices  13.6 us (13%)
  waiting for transfers between devices  12.8 us (12%)
  local copies, waits for them, and re-layouts  9.48 us (9%)
  between operations  1.3 us (1%)
    pallas_call x19, Pallas kernels, run(): pl.pallas_call(call, grid_spec=pltpu.PrefetchScalarGridSpec(num_scalar_pr...  66.1 us
    unnamed x80, local copies, waits for them, and re-layouts  9.48 us
    ppermute x4, waiting for transfers between devices, across(): return lax.ppermute(x, 'tp', [(i, (i + shift) % tps) for i in range(tps)])  9.04 us
    all_to_all x1, starting transfers between devices, shards(): lax.all_to_all(sends, 'inst', split_axis=0, concat_axis=0, tiled=True)  6.33 us
    ppermute x14, waiting for transfers between devices, mate_of(): return lax.ppermute(x, 'tp', to_mate)  3.81 us
    ppermute x14, starting transfers between devices, mate_of(): return lax.ppermute(x, 'tp', to_mate)  3.66 us
    ppermute x4, starting transfers between devices, across(): return lax.ppermute(x, 'tp', [(i, (i + shift) % tps) for i in range(tps)])  3.61 us
  transfers between devices with their start and end apart: 19, of which 9 were waited for; matrix products, arithmetic and copies ran while one was open for 0% of the time, Pallas kernels for 57%

profile of v8, /device:TPU:0, one launch (start us, length us, event | category | flops | bytes accessed | tf_op | source)
XLA Modules:
  0.0 103.3 jit_solution(7661191203741453875)
XLA Ops:
  0.6 3.5 %pack.1 = (bf16[4,2,32,16,256]{4,3,2,1,0:T(8,128)(2,1)}, bf16[256,128]{1,0:T(8,128)(2,1)}, bf16[32,256]{1,0:T(8,128)(2,1)}) custom-call(s32[1,2,32]{2,1,0:T(2,128)} %refs_0_.2, s32[8]{0:T(128)} %refs_0_.3, bf16[1,2,64,16,256]{4,3,2,1,0:T(8,128)(2,1)} %refs_2_.1, bf16[8192,128]{1,0:T(8,128)(2,1)} %bitcast.4, bf16[128,4,2,256]{3,2,1,0:T(2,128)(2,1)} %refs_3_.7), custom_call_target="tpu_custom_call" | custom-call | bytes 1024 | tf_op jit(solution)/shard_map/pack/pallas_call | solution.py:135
  4.1 6.3 %all-to-all-start = ((bf16[4,2,32,16,256]{4,3,2,1,0:T(8,128)(2,1)}), bf16[4,2,32,16,256]{4,3,2,1,0:T(8,128)(2,1)}, u32[]{:S(2)}, u32[]{:S(2)}) async-start(bf16[4,2,32,16,256]{4,3,2,1,0:T(8,128)(2,1)} %get-tuple-element.39.refs_6_), calls=%async_computation | async-start | bytes 4194304 | tf_op jit(solution)/shard_map/all_to_all | solution.py:635
  10.5 1.6 %copy-done.21 = bf16[4,2,32,16,256]{4,3,2,1,0:T(8,128)(2,1)S(1)} copy-done((bf16[4,2,32,16,256]{4,3,2,1,0:T(8,128)(2,1)S(1)}, bf16[4,2,32,16,256]{4,3,2,1,0:T(8,128)(2,1)}, u32[]{:S(2)}) %copy-start.21) | copy-done | bytes 2097176
  12.1 7.8 %attend.2 = (bf16[512,2048]{1,0:T(8,128)(2,1)S(1)}, bf16[2048,512]{1,0:T(8,128)(2,1)S(1)}, bf16[2048,512]{1,0:T(8,128)(2,1)S(1)}, bf16[2048,512]{1,0:T(8,128)(2,1)S(1)}, bf16[2048,512]{1,0:T(8,128)(2,1)S(1)}) custom-call(s32[8,125]{1,0:T(8,128)} %bitcast.7, s32[1,125]{1,0:T(1,128)} %refs_1_.6, bf16[8192,128]{1,0:T(8,128)(2,1)} %bitcast.5, ...), custom_call_target="tpu_custom_call" | custom-call | bytes 1024 | tf_op jit(solution)/shard_map/attend/pallas_call | solution.py:135
  20.0 3.2 %give.3 = (bf16[256,512]{1,0:T(8,128)(2,1)S(1)}, bf16[256,512]{1,0:T(8,128)(2,1)S(1)}, bf16[2048,512]{1,0:T(8,128)(2,1)S(1)}) custom-call(bf16[512,2048]{1,0:T(8,128)(2,1)S(1)} %get-tuple-element.42.refs_0_.refs_6_, bf16[2048,512]{1,0:T(8,128)(2,1)S(1)} %get-tuple-element.43.refs_1_, bf16[2048,512]{1,0:T(8,128)(2,1)S(1)} %get-tuple-element.44.refs_2_, ...), custom_call_target="tpu_custom_call" | custom-call | bytes 1024 | tf_op jit(solution)/shard_map/give/pallas_call | solution.py:135
  23.8 1.0 collective-permute-done.1.refs_4_
  25.2 1.8 %keep.3 = (bf16[256,1024]{1,0:T(8,128)(2,1)S(1)}, bf16[2048,512]{1,0:T(8,128)(2,1)S(1)}) custom-call(bf16[512,2048]{1,0:T(8,128)(2,1)S(1)} %get-tuple-element.42.refs_0_.refs_6_, bf16[2048,512]{1,0:T(8,128)(2,1)S(1)} %get-tuple-element.46.refs_1_, bf16[2048,512]{1,0:T(8,128)(2,1)S(1)} %get-tuple-element.47.refs_2_, ...), custom_call_target="tpu_custom_call" | custom-call | bytes 1024 | tf_op jit(solution)/shard_map/keep/pallas_call | solution.py:135
  27.0 1.6 %collective-permute-start.4 = (bf16[256,1024]{1,0:T(8,128)(2,1)S(1)}, bf16[256,1024]{1,0:T(8,128)(2,1)S(1)}, u32[]{:S(2)}, u32[]{:S(2)}) collective-permute-start(bf16[256,1024]{1,0:T(8,128)(2,1)S(1)} %get-tuple-element.51.refs_4_), channel_id=1, source_target_pairs={{0,2},{1,3},{2,0},{3,1},{4,6},{5,7},{6,4},{7,5},{8,10},{9,11},{10,... | collective-permute-start | bytes 1572872 | tf_op jit(solution)/shard_map/ppermute | solution.py:588
  28.6 2.3 %give.4 = (bf16[256,512]{1,0:T(8,128)(2,1)S(1)}, bf16[256,512]{1,0:T(8,128)(2,1)S(1)}, bf16[2048,512]{1,0:T(8,128)(2,1)S(1)}, bf16[2048,512]{1,0:T(8,128)(2,1)S(1)}) custom-call(bf16[512,2048]{1,0:T(8,128)(2,1)S(1)} %get-tuple-element.42.refs_0_.refs_6_, bf16[2048,512]{1,0:T(8,128)(2,1)S(1)} %get-tuple-element.45.refs_1_.refs_3_, ...), custom_call_target="tpu_custom_call" | custom-call | bytes 1024 | tf_op jit(solution)/shard_map/give/pallas_call | solution.py:135
  31.4 1.0 collective-permute-done.3.refs_4_
  32.8 1.8 %keep.4.refs_7_ = bf16[256,1024]{1,0:T(8,128)(2,1)S(1)} custom-call(bf16[512,2048]{1,0:T(8,128)(2,1)S(1)} %get-tuple-element.42.refs_0_.refs_6_, bf16[2048,512]{1,0:T(8,128)(2,1)S(1)} %get-tuple-element.52.refs_1_.refs_3_, bf16[2048,512]{1,0:T(8,128)(2,1)S(1)} %get-tuple-element.53.refs_2_.refs_4_, bf16[256,512]{1,0:T(8,128)(2,1)S(1)} %collective-permute-done.2.refs_3_, ...), custom_call_target="tpu_custom_call" | custom-call | bytes 1024 | tf_op jit(solution)/shard_map/keep/pallas_call | solution.py:135
  34.7 7.9 %attend.3 = (bf16[512,2048]{1,0:T(8,128)(2,1)S(1)}, bf16[2048,512]{1,0:T(8,128)(2,1)S(1)}, bf16[2048,512]{1,0:T(8,128)(2,1)S(1)}, bf16[2048,512]{1,0:T(8,128)(2,1)S(1)}, bf16[2048,512]{1,0:T(8,128)(2,1)S(1)}) custom-call(s32[8,125]{1,0:T(8,128)} %bitcast.8, s32[1,125]{1,0:T(1,128)} %refs_1_.6, ...), custom_call_target="tpu_custom_call", output_to_operand_aliasing={{0}: (6, {})} | custom-call | bytes 1024 | tf_op jit(solution)/shard_map/attend/pallas_call | solution.py:135
  42.6 5.1 %give.5 = (bf16[256,512]{1,0:T(8,128)(2,1)S(1)}, bf16[256,512]{1,0:T(8,128)(2,1)S(1)}, bf16[256,512]{1,0:T(8,128)(2,1)S(1)}, bf16[256,512]{1,0:T(8,128)(2,1)S(1)...) custom-call(bf16[512,2048]{1,0:T(8,128)(2,1)S(1)} %get-tuple-element.56.refs_0_.refs_5_, ...), custom_call_target="tpu_custom_call" | custom-call | bytes 1024 | tf_op jit(solution)/shard_map/give/pallas_call | solution.py:135
  50.5 4.7 %keep.5 = (bf16[256,2048]{1,0:T(8,128)(2,1)}, bf16[2048,512]{1,0:T(8,128)(2,1)S(1)}, bf16[2048,512]{1,0:T(8,128)(2,1)S(1)}) custom-call(bf16[512,2048]{1,0:T(8,128)(2,1)S(1)} %get-tuple-element.56.refs_0_.refs_5_, bf16[2048,512]{1,0:T(8,128)(2,1)S(1)} %get-tuple-element.46.refs_1_, bf16[2048,512]{1,0:T(8,128)(2,1)S(1)} %get-tuple-element.47.refs_2_, ...), custom_call_target="tpu_custom_call" | custom-call | bytes 1024 | tf_op jit(solution)/shard_map/keep/pallas_call | solution.py:135
  55.2 0.7 collective-permute-start.16
  55.9 7.7 %collective-permute-done.9.refs_4_ = bf16[256,1024]{1,0:T(8,128)(2,1)S(1)} collective-permute-done((bf16[256,1024]{1,0:T(8,128)(2,1)S(1)}, bf16[256,1024]{1,0:T(8,128)(2,1)S(1)}, u32[]{:S(2)}, u32[]{:S(2)}) %collective-permute-start.9) | collective-permute-done | bytes 524320 | tf_op jit(solution)/shard_map/ppermute | solution.py:588
  63.6 2.9 %give_own.2 = (bf16[512,512]{1,0:T(8,128)(2,1)S(1)}, bf16[512,512]{1,0:T(8,128)(2,1)S(1)}) custom-call(bf16[512,2048]{1,0:T(8,128)(2,1)S(1)} %get-tuple-element.56.refs_0_.refs_5_, bf16[2048,512]{1,0:T(8,128)(2,1)S(1)} %get-tuple-element.65.refs_1_, bf16[2048,512]{1,0:T(8,128)(2,1)S(1)} %get-tuple-element.66.refs_2_, ...), custom_call_target="tpu_custom_call" | custom-call | bytes 1024 | tf_op jit(solution)/shard_map/give_own/pallas_call | solution.py:135
  67.1 2.9 %give_own.3 = (bf16[512,512]{1,0:T(8,128)(2,1)S(1)}, bf16[512,512]{1,0:T(8,128)(2,1)S(1)}) custom-call(bf16[512,2048]{1,0:T(8,128)(2,1)S(1)} %get-tuple-element.56.refs_0_.refs_5_, bf16[2048,512]{1,0:T(8,128)(2,1)S(1)} %get-tuple-element.63.refs_1_.refs_3_, bf16[2048,512]{1,0:T(8,128)(2,1)S(1)} %get-tuple-element.64.refs_2_.refs_4_, ...), custom_call_target="tpu_custom_call" | custom-call | bytes 1024 | tf_op jit(solution)/shard_map/give_own/pallas_call | solution.py:135
  70.6 2.9 %keep_own.2.refs_5_.refs_0_ = f32[512,1024]{1,0:T(8,128)S(1)} custom-call(bf16[512,2048]{1,0:T(8,128)(2,1)S(1)} %get-tuple-element.56.refs_0_.refs_5_, bf16[2048,512]{1,0:T(8,128)(2,1)S(1)} %get-tuple-element.71.refs_1_, bf16[2048,512]{1,0:T(8,128)(2,1)S(1)} %get-tuple-element.72.refs_2_, bf16[512,512]{1,0:T(8,128)(2,1)S(1)} %collective-permute-done.12.refs_3_, ...), custom_call_target="tpu_custom_call" | custom-call | bytes 1024 | tf_op jit(solution)/shard_map/keep_own/pallas_call | solution.py:135
  73.5 3.1 %keep_own.3.refs_6_.refs_1_ = f32[512,1024]{1,0:T(8,128)S(1)} custom-call(bf16[512,2048]{1,0:T(8,128)(2,1)S(1)} %get-tuple-element.56.refs_0_.refs_5_, bf16[2048,512]{1,0:T(8,128)(2,1)S(1)} %get-tuple-element.61.refs_1_.refs_3_, bf16[2048,512]{1,0:T(8,128)(2,1)S(1)} %get-tuple-element.62.refs_2_.refs_4_, ...), custom_call_target="tpu_custom_call" | custom-call | bytes 1024 | tf_op jit(solution)/shard_map/keep_own/pallas_call | solution.py:135
  76.6 1.3 %copy-done.16 = f32[512,1024]{1,0:T(8,128)} copy-done((f32[512,1024]{1,0:T(8,128)}, f32[512,1024]{1,0:T(8,128)S(1)}, u32[]{:S(2)}) %copy-start.16) | copy-done | bytes 2097176
  78.0 1.3 %copy-done.18 = f32[512,1024]{1,0:T(8,128)} copy-done((f32[512,1024]{1,0:T(8,128)}, f32[512,1024]{1,0:T(8,128)S(1)}, u32[]{:S(2)}) %copy-start.18) | copy-done | bytes 2097176
  79.3 1.6 %copy-done.19 = f32[512,1024]{1,0:T(8,128)S(1)} copy-done((f32[512,1024]{1,0:T(8,128)S(1)}, f32[512,1024]{1,0:T(8,128)}, u32[]{:S(2)}) %copy-start.19) | copy-done | bytes 2097176
  80.9 4.8 %settle.1 = (bf16[16,2048]{1,0:T(8,128)(2,1)S(1)}, bf16[1,3,2,512,256]{4,3,2,1,0:T(8,128)(2,1)}) custom-call(s32[8]{0:T(128)} %refs_0_.3, s32[8]{0:T(128)} %refs_1_.7, bf16[4,2,32,16,256]{4,3,2,1,0:T(8,128)(2,1)} %all-to-all-done.refs_2_, bf16[256,128]{1,0:T(8,128)(2,1)S(1)} %copy-done.38, bf16[32,256]{1,0:T(8,128)(2,1)S(1)} %copy-done.39, ...), custom_call_target="tpu_custom_call" | custom-call | bytes 1024 | tf_op jit(solution)/shard_map/settle/pallas_call | solution.py:135
  85.8 1.6 %copy-done.11 = bf16[2048,512]{1,0:T(8,128)(2,1)S(1)} copy-done((bf16[2048,512]{1,0:T(8,128)(2,1)S(1)}, bf16[2048,512]{1,0:T(8,128)(2,1)}, u32[]{:S(2)}) %copy-start.11) | copy-done | bytes 2097176
  87.4 2.0 %give_last.2.refs_5_ = bf16[16,2048]{1,0:T(8,128)(2,1)S(1)} custom-call(bf16[16,2048]{1,0:T(8,128)(2,1)S(1)} %get-tuple-element.75.refs_0_, bf16[2048,512]{1,0:T(8,128)(2,1)S(1)} %copy-done.5, bf16[2048,512]{1,0:T(8,128)(2,1)S(1)} %copy-done.7, bf16[2048,512]{1,0:T(8,128)(2,1)S(1)} %copy-done.9, bf16[2048,512]{1,0:T(8,128)(2,1)S(1)} %copy-done.11), custom_call_target="tpu_custom_call" | custom-call | bytes 1024 | tf_op jit(solution)/shard_map/give_last/pallas_call | solution.py:135
  90.9 2.0 %give_last.3.refs_6_ = bf16[16,2048]{1,0:T(8,128)(2,1)S(1)} custom-call(bf16[16,2048]{1,0:T(8,128)(2,1)S(1)} %get-tuple-element.75.refs_0_, bf16[2048,512]{1,0:T(8,128)(2,1)S(1)} %copy-done.31, bf16[2048,512]{1,0:T(8,128)(2,1)S(1)} %copy-done.33, bf16[2048,512]{1,0:T(8,128)(2,1)S(1)} %copy-done.27, bf16[2048,512]{1,0:T(8,128)(2,1)S(1)} %copy-done.29, ...), custom_call_target="tpu_custom_call" | custom-call | bytes 1024 | tf_op jit(solution)/shard_map/give_last/pallas_call | solution.py:135
  93.5 2.0 %keep_last.2.refs_6_ = bf16[16,2048]{1,0:T(8,128)(2,1)S(1)} custom-call(bf16[16,2048]{1,0:T(8,128)(2,1)S(1)} %get-tuple-element.75.refs_0_, bf16[2048,512]{1,0:T(8,128)(2,1)S(1)} %copy-done.1, bf16[2048,512]{1,0:T(8,128)(2,1)S(1)} %copy-done.3, bf16[2048,512]{1,0:T(8,128)(2,1)S(1)} %copy-done.13, bf16[2048,512]{1,0:T(8,128)(2,1)S(1)} %copy-done.15, ...), custom_call_target="tpu_custom_call" | custom-call | bytes 1024 | tf_op jit(solution)/shard_map/keep_last/pallas_call | solution.py:135
  95.5 0.7 collective-permute-start.17
  96.5 2.0 %keep_last.3.refs_2_ = f32[16,2048]{1,0:T(8,128)S(1)} custom-call(bf16[16,2048]{1,0:T(8,128)(2,1)S(1)} %get-tuple-element.75.refs_0_, bf16[2048,512]{1,0:T(8,128)(2,1)S(1)} %copy-done.23, bf16[2048,512]{1,0:T(8,128)(2,1)S(1)} %copy-done.25, bf16[2048,512]{1,0:T(8,128)(2,1)S(1)} %copy-done.35, bf16[2048,512]{1,0:T(8,128)(2,1)S(1)} %copy-done.37, ...), custom_call_target="tpu_custom_call" | custom-call | bytes 1024 | tf_op jit(solution)/shard_map/keep_last/pallas_call | solution.py:135
  98.5 1.3 %collective-permute-done.17.refs_6_ = bf16[16,2048]{1,0:T(8,128)(2,1)S(1)} collective-permute-done((bf16[16,2048]{1,0:T(8,128)(2,1)S(1)}, bf16[16,2048]{1,0:T(8,128)(2,1)S(1)}, u32[]{:S(2)}, u32[]{:S(2)}) %collective-permute-start.17) | collective-permute-done | bytes 65568 | tf_op jit(solution)/shard_map/ppermute | solution.py:588
  99.8 3.3 %finish.1 = bf16[2048,512]{1,0:T(8,128)(2,1)} custom-call(f32[512,1024]{1,0:T(8,128)S(1)} %copy-done.17, f32[512,1024]{1,0:T(8,128)S(1)} %copy-done.20, f32[16,2048]{1,0:T(8,128)S(1)} %keep_last.3.refs_2_, bf16[256,1024]{1,0:T(8,128)(2,1)S(1)} %collective-permute-done.4.refs_6_.refs_3_, bf16[256,1024]{1,0:T(8,128)(2,1)S(1)} %collective-permute-done.9.refs_4_, ...), custom_call_target="tpu_custom_call" | custom-call | bytes 1024 | tf_op jit(solution)/shard_map/finish/pallas_call | solution.py:135
  (105 shorter events, 8.1 us)
Async XLA Ops:
  4.1 75.2 %all-to-all-start = ((bf16[4,2,32,16,256]{4,3,2,1,0:T(8,128)(2,1)}), bf16[4,2,32,16,256]{4,3,2,1,0:T(8,128)(2,1)}, u32[]{:S(2)}, u32[]{:S(2)}) async-start(bf16[4,2,32,16,256]{4,3,2,1,0:T(8,128)(2,1)} %get-tuple-element.39.refs_6_), calls=%async_computation | async-start | bytes 4194304 | tf_op jit(solution)/shard_map/all_to_all | solution.py:635
  19.9 22.7 %copy-start.4 = (bf16[2048,512]{1,0:T(8,128)(2,1)}, bf16[2048,512]{1,0:T(8,128)(2,1)S(1)}, u32[]{:S(2)}) copy-start(bf16[2048,512]{1,0:T(8,128)(2,1)S(1)} %get-tuple-element.43.refs_1_) | copy-start | bytes 6291460
  19.9 22.7 %copy-start.6 = (bf16[2048,512]{1,0:T(8,128)(2,1)}, bf16[2048,512]{1,0:T(8,128)(2,1)S(1)}, u32[]{:S(2)}) copy-start(bf16[2048,512]{1,0:T(8,128)(2,1)S(1)} %get-tuple-element.44.refs_2_) | copy-start | bytes 6291460
  19.9 30.5 %copy-start = (bf16[2048,512]{1,0:T(8,128)(2,1)}, bf16[2048,512]{1,0:T(8,128)(2,1)S(1)}, u32[]{:S(2)}) copy-start(bf16[2048,512]{1,0:T(8,128)(2,1)S(1)} %get-tuple-element.46.refs_1_) | copy-start | bytes 6291460
  19.9 30.5 %copy-start.2 = (bf16[2048,512]{1,0:T(8,128)(2,1)}, bf16[2048,512]{1,0:T(8,128)(2,1)S(1)}, u32[]{:S(2)}) copy-start(bf16[2048,512]{1,0:T(8,128)(2,1)S(1)} %get-tuple-element.47.refs_2_) | copy-start | bytes 6291460
  23.2 19.4 %copy-start.8 = (bf16[2048,512]{1,0:T(8,128)(2,1)}, bf16[2048,512]{1,0:T(8,128)(2,1)S(1)}, u32[]{:S(2)}) copy-start(bf16[2048,512]{1,0:T(8,128)(2,1)S(1)} %get-tuple-element.45.refs_1_.refs_3_) | copy-start | bytes 6291460
  23.2 1.6 %collective-permute-start.1 = (bf16[256,512]{1,0:T(8,128)(2,1)S(1)}, bf16[256,512]{1,0:T(8,128)(2,1)S(1)}, u32[]{:S(2)}, u32[]{:S(2)}) collective-permute-start(bf16[256,512]{1,0:T(8,128)(2,1)S(1)} %get-tuple-element.49), channel_id=1, source_target_pairs={{0,1},{1,0},{2,3},{3,2},{4,5},{5,4},{6,7},{7,6},{8,9},{9,8},{10,11... | collective-permute-start | bytes 786440 | tf_op jit(solution)/shard_map/ppermute | solution.py:584
  23.3 1.9 %collective-permute-start = (bf16[256,512]{1,0:T(8,128)(2,1)S(1)}, bf16[256,512]{1,0:T(8,128)(2,1)S(1)}, u32[]{:S(2)}, u32[]{:S(2)}) collective-permute-start(bf16[256,512]{1,0:T(8,128)(2,1)S(1)} %get-tuple-element.48.refs_6_), channel_id=1, source_target_pairs={{0,1},{1,0},{2,3},{3,2},{4,5},{5,4},{6,7},{7,6},{8,9},{9,8},{10,11... | collective-permute-start | bytes 786440 | tf_op jit(solution)/shard_map/ppermute | solution.py:584
  27.0 15.6 %collective-permute-start.4 = (bf16[256,1024]{1,0:T(8,128)(2,1)S(1)}, bf16[256,1024]{1,0:T(8,128)(2,1)S(1)}, u32[]{:S(2)}, u32[]{:S(2)}) collective-permute-start(bf16[256,1024]{1,0:T(8,128)(2,1)S(1)} %get-tuple-element.51.refs_4_), channel_id=1, source_target_pairs={{0,2},{1,3},{2,0},{3,1},{4,6},{5,7},{6,4},{7,5},{8,10},{9,11},{10,... | collective-permute-start | bytes 1572872 | tf_op jit(solution)/shard_map/ppermute | solution.py:588
  30.9 19.6 %copy-start.12 = (bf16[2048,512]{1,0:T(8,128)(2,1)}, bf16[2048,512]{1,0:T(8,128)(2,1)S(1)}, u32[]{:S(2)}) copy-start(bf16[2048,512]{1,0:T(8,128)(2,1)S(1)} %get-tuple-element.52.refs_1_.refs_3_) | copy-start | bytes 6291460
  30.9 19.6 %copy-start.14 = (bf16[2048,512]{1,0:T(8,128)(2,1)}, bf16[2048,512]{1,0:T(8,128)(2,1)S(1)}, u32[]{:S(2)}) copy-start(bf16[2048,512]{1,0:T(8,128)(2,1)S(1)} %get-tuple-element.53.refs_2_.refs_4_) | copy-start | bytes 6291460
  30.9 1.6 %collective-permute-start.3 = (bf16[256,512]{1,0:T(8,128)(2,1)S(1)}, bf16[256,512]{1,0:T(8,128)(2,1)S(1)}, u32[]{:S(2)}, u32[]{:S(2)}) collective-permute-start(bf16[256,512]{1,0:T(8,128)(2,1)S(1)} %get-tuple-element.55), channel_id=1, source_target_pairs={{0,1},{1,0},{2,3},{3,2},{4,5},{5,4},{6,7},{7,6},{8,9},{9,8},{10,11... | collective-permute-start | bytes 786440 | tf_op jit(solution)/shard_map/ppermute | solution.py:584
  30.9 1.9 %collective-permute-start.2 = (bf16[256,512]{1,0:T(8,128)(2,1)S(1)}, bf16[256,512]{1,0:T(8,128)(2,1)S(1)}, u32[]{:S(2)}, u32[]{:S(2)}) collective-permute-start(bf16[256,512]{1,0:T(8,128)(2,1)S(1)} %get-tuple-element.54.refs_5_), channel_id=1, source_target_pairs={{0,1},{1,0},{2,3},{3,2},{4,5},{5,4},{6,7},{7,6},{8,9},{9,8},{10,11... | collective-permute-start | bytes 786440 | tf_op jit(solution)/shard_map/ppermute | solution.py:584
  42.5 21.1 %copy-start.30 = (bf16[2048,512]{1,0:T(8,128)(2,1)}, bf16[2048,512]{1,0:T(8,128)(2,1)S(1)}, u32[]{:S(2)}) copy-start(bf16[2048,512]{1,0:T(8,128)(2,1)S(1)} %get-tuple-element.65.refs_1_) | copy-start | bytes 6291460
  42.5 21.1 %copy-start.32 = (bf16[2048,512]{1,0:T(8,128)(2,1)}, bf16[2048,512]{1,0:T(8,128)(2,1)S(1)}, u32[]{:S(2)}) copy-start(bf16[2048,512]{1,0:T(8,128)(2,1)S(1)} %get-tuple-element.66.refs_2_) | copy-start | bytes 6291460
  42.6 24.5 %copy-start.26 = (bf16[2048,512]{1,0:T(8,128)(2,1)}, bf16[2048,512]{1,0:T(8,128)(2,1)S(1)}, u32[]{:S(2)}) copy-start(bf16[2048,512]{1,0:T(8,128)(2,1)S(1)} %get-tuple-element.63.refs_1_.refs_3_) | copy-start | bytes 6291460
  42.6 24.5 %copy-start.28 = (bf16[2048,512]{1,0:T(8,128)(2,1)}, bf16[2048,512]{1,0:T(8,128)(2,1)S(1)}, u32[]{:S(2)}) copy-start(bf16[2048,512]{1,0:T(8,128)(2,1)S(1)} %get-tuple-element.64.refs_2_.refs_4_) | copy-start | bytes 6291460
  47.7 22.8 %copy-start.22 = (bf16[2048,512]{1,0:T(8,128)(2,1)}, bf16[2048,512]{1,0:T(8,128)(2,1)S(1)}, u32[]{:S(2)}) copy-start(bf16[2048,512]{1,0:T(8,128)(2,1)S(1)} %get-tuple-element.71.refs_1_) | copy-start | bytes 6291460
  47.7 22.8 %copy-start.24 = (bf16[2048,512]{1,0:T(8,128)(2,1)}, bf16[2048,512]{1,0:T(8,128)(2,1)S(1)}, u32[]{:S(2)}) copy-start(bf16[2048,512]{1,0:T(8,128)(2,1)S(1)} %get-tuple-element.72.refs_2_) | copy-start | bytes 6291460
  47.7 1.7 %collective-permute-start.6 = (bf16[256,512]{1,0:T(8,128)(2,1)S(1)}, bf16[256,512]{1,0:T(8,128)(2,1)S(1)}, u32[]{:S(2)}, u32[]{:S(2)}) collective-permute-start(bf16[256,512]{1,0:T(8,128)(2,1)S(1)} %get-tuple-element.58), channel_id=1, source_target_pairs={{0,1},{1,0},{2,3},{3,2},{4,5},{5,4},{6,7},{7,6},{8,9},{9,8},{10,11... | collective-permute-start | bytes 786440 | tf_op jit(solution)/shard_map/ppermute | solution.py:584
  47.9 1.8 %collective-permute-start.7 = (bf16[256,512]{1,0:T(8,128)(2,1)S(1)}, bf16[256,512]{1,0:T(8,128)(2,1)S(1)}, u32[]{:S(2)}, u32[]{:S(2)}) collective-permute-start(bf16[256,512]{1,0:T(8,128)(2,1)S(1)} %get-tuple-element.59), channel_id=1, source_target_pairs={{0,1},{1,0},{2,3},{3,2},{4,5},{5,4},{6,7},{7,6},{8,9},{9,8},{10,11... | collective-permute-start | bytes 786440 | tf_op jit(solution)/shard_map/ppermute | solution.py:584
  48.3 1.8 %collective-permute-start.8 = (bf16[256,512]{1,0:T(8,128)(2,1)S(1)}, bf16[256,512]{1,0:T(8,128)(2,1)S(1)}, u32[]{:S(2)}, u32[]{:S(2)}) collective-permute-start(bf16[256,512]{1,0:T(8,128)(2,1)S(1)} %get-tuple-element.60), channel_id=1, source_target_pairs={{0,1},{1,0},{2,3},{3,2},{4,5},{5,4},{6,7},{7,6},{8,9},{9,8},{10,11... | collective-permute-start | bytes 786440 | tf_op jit(solution)/shard_map/ppermute | solution.py:584
  48.4 2.0 %collective-permute-start.5 = (bf16[256,512]{1,0:T(8,128)(2,1)S(1)}, bf16[256,512]{1,0:T(8,128)(2,1)S(1)}, u32[]{:S(2)}, u32[]{:S(2)}) collective-permute-start(bf16[256,512]{1,0:T(8,128)(2,1)S(1)} %get-tuple-element.57.refs_10_), channel_id=1, source_target_pairs={{0,1},{1,0},{2,3},{3,2},{4,5},{5,4},{6,7},{7,6},{8,9},{9,8},{10,11... | collective-permute-start | bytes 786440 | tf_op jit(solution)/shard_map/ppermute | solution.py:584
  48.8 14.8 %collective-permute-start.9 = (bf16[256,1024]{1,0:T(8,128)(2,1)S(1)}, bf16[256,1024]{1,0:T(8,128)(2,1)S(1)}, u32[]{:S(2)}, u32[]{:S(2)}) collective-permute-start(bf16[256,1024]{1,0:T(8,128)(2,1)S(1)} %keep.4.refs_7_), channel_id=1, source_target_pairs={{0,2},{1,3},{2,0},{3,1},{4,6},{5,7},{6,4},{7,5},{8,10},{9,11},{10,... | collective-permute-start | bytes 1572872 | tf_op jit(solution)/shard_map/ppermute | solution.py:588
  55.2 43.3 %collective-permute-start.16 = (bf16[256,2048]{1,0:T(8,128)(2,1)}, bf16[256,2048]{1,0:T(8,128)(2,1)}, u32[]{:S(2)}, u32[]{:S(2)}) collective-permute-start(bf16[256,2048]{1,0:T(8,128)(2,1)} %get-tuple-element.67.refs_3_), channel_id=1, source_target_pairs={{0,2},{1,3},{2,0},{3,1},{4,6},{5,7},{6,4},{7,5},{8,10},{9,11},{10,... | collective-permute-start | bytes 3145736 | tf_op jit(solution)/shard_map/ppermute | solution.py:588
  66.5 4.1 %collective-permute-start.13 = (bf16[512,512]{1,0:T(8,128)(2,1)S(1)}, bf16[512,512]{1,0:T(8,128)(2,1)S(1)}, u32[]{:S(2)}, u32[]{:S(2)}) collective-permute-start(bf16[512,512]{1,0:T(8,128)(2,1)S(1)} %get-tuple-element.73), channel_id=1, source_target_pairs={{0,1},{1,0},{2,3},{3,2},{4,5},{5,4},{6,7},{7,6},{8,9},{9,8},{10,11... | collective-permute-start | bytes 1572872 | tf_op jit(solution)/shard_map/ppermute | solution.py:584
  66.6 4.0 %collective-permute-start.12 = (bf16[512,512]{1,0:T(8,128)(2,1)S(1)}, bf16[512,512]{1,0:T(8,128)(2,1)S(1)}, u32[]{:S(2)}, u32[]{:S(2)}) collective-permute-start(bf16[512,512]{1,0:T(8,128)(2,1)S(1)} %get-tuple-element.68.refs_3_), channel_id=1, source_target_pairs={{0,1},{1,0},{2,3},{3,2},{4,5},{5,4},{6,7},{7,6},{8,9},{9,8},{10,11... | collective-permute-start | bytes 1572872 | tf_op jit(solution)/shard_map/ppermute | solution.py:584
  70.0 3.5 %collective-permute-start.11 = (bf16[512,512]{1,0:T(8,128)(2,1)S(1)}, bf16[512,512]{1,0:T(8,128)(2,1)S(1)}, u32[]{:S(2)}, u32[]{:S(2)}) collective-permute-start(bf16[512,512]{1,0:T(8,128)(2,1)S(1)} %get-tuple-element.70), channel_id=1, source_target_pairs={{0,1},{1,0},{2,3},{3,2},{4,5},{5,4},{6,7},{7,6},{8,9},{9,8},{10,11... | collective-permute-start | bytes 1572872 | tf_op jit(solution)/shard_map/ppermute | solution.py:584
  70.1 3.4 %collective-permute-start.10 = (bf16[512,512]{1,0:T(8,128)(2,1)S(1)}, bf16[512,512]{1,0:T(8,128)(2,1)S(1)}, u32[]{:S(2)}, u32[]{:S(2)}) collective-permute-start(bf16[512,512]{1,0:T(8,128)(2,1)S(1)} %get-tuple-element.69.refs_5_), channel_id=1, source_target_pairs={{0,1},{1,0},{2,3},{3,2},{4,5},{5,4},{6,7},{7,6},{8,9},{9,8},{10,11... | collective-permute-start | bytes 1572872 | tf_op jit(solution)/shard_map/ppermute | solution.py:584
  89.5 3.6 %collective-permute-start.15 = (bf16[16,2048]{1,0:T(8,128)(2,1)S(1)}, bf16[16,2048]{1,0:T(8,128)(2,1)S(1)}, u32[]{:S(2)}, u32[]{:S(2)}) collective-permute-start(bf16[16,2048]{1,0:T(8,128)(2,1)S(1)} %give_last.2.refs_5_), channel_id=1, source_target_pairs={{0,1},{1,0},{2,3},{3,2},{4,5},{5,4},{6,7},{7,6},{8,9},{9,8},{10,11... | collective-permute-start | bytes 196616 | tf_op jit(solution)/shard_map/ppermute | solution.py:584
  92.9 3.3 %collective-permute-start.14 = (bf16[16,2048]{1,0:T(8,128)(2,1)S(1)}, bf16[16,2048]{1,0:T(8,128)(2,1)S(1)}, u32[]{:S(2)}, u32[]{:S(2)}) collective-permute-start(bf16[16,2048]{1,0:T(8,128)(2,1)S(1)} %give_last.3.refs_6_), channel_id=1, source_target_pairs={{0,1},{1,0},{2,3},{3,2},{4,5},{5,4},{6,7},{7,6},{8,9},{9,8},{10,11... | collective-permute-start | bytes 196616 | tf_op jit(solution)/shard_map/ppermute | solution.py:584
  95.5 4.3 %collective-permute-start.17 = (bf16[16,2048]{1,0:T(8,128)(2,1)S(1)}, bf16[16,2048]{1,0:T(8,128)(2,1)S(1)}, u32[]{:S(2)}, u32[]{:S(2)}) collective-permute-start(bf16[16,2048]{1,0:T(8,128)(2,1)S(1)} %keep_last.2.refs_6_), channel_id=1, source_target_pairs={{0,2},{1,3},{2,0},{3,1},{4,6},{5,7},{6,4},{7,5},{8,10},{9,11},{10,... | collective-permute-start | bytes 196616 | tf_op jit(solution)/shard_map/ppermute | solution.py:588
  (27 other events, 133.8 us)

commit v9 on v8

--- a/solution.py
+++ b/solution.py
@@ -369,7 +369,6 @@
     rows_ref, got_ref, keep_ref, sems, *, sizes
 ):
     z = sizes
-    launch()
     ready()
     inst = lax.axis_index("inst")
     requests = row_plan(dest_ref, inst, z.cap)
@@ -385,6 +384,7 @@
     ]
     for read in reads:
         read.start()
+    launch()
     new_kv = kv_ref[...]
     code = fresh_code(z.per, z.tail_kv, z)
     slot_of = slot_index(extent, z)
@@ -476,11 +476,11 @@
         lax.fori_loop(0, width // tile, one, 0)
 
 
-def project(attention, weights, mates, joined, dtype, sizes, name, deps, **fetch):
+def project(attention, weights, mates, joined, dtype, sizes, name, deps, place=None, **fetch):
     attention, first, tokens = attention
     count = len(weights)
-    if dtype == jnp.float32:
-        shapes = [pltpu.VMEM((tokens, count * sizes.quarter), dtype)]
+    if place is not None:
+        shapes = [place((tokens, count * sizes.quarter), dtype)]
     elif joined:
         shapes = [jax.ShapeDtypeStruct((tokens, count * sizes.quarter), dtype)]
     else:
@@ -518,8 +518,8 @@
             half = pl.ds((n % 2) * z.quarter + start, tile)
             begin = low[0].shape[0]
             own = own_low if n < 2 else own_high
-            first = own[:begin, half]
-            rest = own[begin:-rows, half]
+            first = own[:begin, half].astype(jnp.float32)
+            rest = own[begin:-rows, half].astype(jnp.float32)
             last = own_late[:, at]
             for k in range(fars):
                 first = first + (low if n < 2 else high)[k][:, half].astype(jnp.float32)
@@ -596,6 +596,9 @@
     def keeps(ks, parts):
         return [(k, True, part) for k in ks for part in parts]
 
+    def in_hbm(arrays):
+        return [pltpu.with_memory_space_constraint(x, pltpu.HBM) for x in arrays]
+
     def hold(pieces, arrays):
         held.update(zip(pieces, arrays))
 
@@ -607,7 +610,7 @@
         hold(pieces, new)
         return results[0], [mate_of(result) for result in results]
 
-    def keep(attention, ks, parts, mates, name, deps, pieces=(), dtype=jnp.bfloat16):
+    def keep(attention, ks, parts, mates, name, deps, pieces=(), dtype=jnp.bfloat16, place=None):
         results = []
         for n, k in enumerate(ks):
             weights = [held[piece] for piece in keeps([k], parts)]
@@ -618,7 +621,7 @@
                 now = mates[n * len(parts) : (n + 1) * len(parts)]
             bring = pieces if n == 0 else ()
             result, new = project(
-                attention, weights, now, True, dtype, z, name, deps, **bringing(bring)
+                attention, weights, now, True, dtype, z, name, deps, place, **bringing(bring)
             )
             hold(bring, new)
             deps = [result[0]]
@@ -655,21 +658,23 @@
     hold(gives([0], every), new)
     b, whole = (rows, tokens, tokens), (rows, 0, 2 * tokens)
     given, mates = give(b, far, every, "give", got_low, keeps([0], low))
-    kept = keep(b, far, every, mates, "keep", [given], keeps([0], high))
+    kept = keep(b, far, every, mates, "keep", [given] + got_high, keeps([0], high))
     got_second = sent(kept)
 
-    given, mates_low = give(whole, [0], low, "give_own", kept[-1:] + got_high)
+    given, mates_low = give(whole, [0], low, "give_own", kept[-1:])
     given, mates_high = give(whole, [0], high, "give_own", [given])
-    own = keep(whole, [0], low, mates_low, "keep_own", [given], dtype=jnp.float32)
-    own += keep(whole, [0], high, mates_high, "keep_own", own, dtype=jnp.float32)
-
-    (last, arrived), _ = settle(
-        mig_dest, mig_len, arriving, tail_q, tail_kv, rows, z, own[-1:]
-    )
+    own = keep(whole, [0], low, mates_low, "keep_own", [given], place=pltpu.HBM)
+    own += keep(whole, [0], high, mates_high, "keep_own", in_hbm(own), place=pltpu.HBM)
+
+    pieces = gives(far, every) + gives([0], every)
+    (last, arrived), new = settle(
+        mig_dest, mig_len, arriving, tail_q, tail_kv, rows, z, in_hbm(own[-1:]), **bringing(pieces)
+    )
+    hold(pieces, new)
     late = (last, 0, last.shape[0])
-    given, mates = give(late, far, every, "give_last", [], joined=True)
+    given, mates = give(late, far, every, "give_last", [], keeps(far, every), joined=True)
     given, own_mates = give(late, [0], every, "give_last", [given], joined=True)
-    kept = keep(late, far, every, mates, "keep_last", [given])
+    kept = keep(late, far, every, mates, "keep_last", [given], keeps([0], every))
     got_late = sent(kept)
     own_late = keep(late, [0], every, own_mates, "keep_last", kept[-1:], dtype=jnp.float32)
     hidden = finish(own, own_late[0], got_low, got_high, got_second, got_late, z, [])

time: 104 us -> 98.2 us (0.944)
  local copies, waits for them, and re-layouts: 9.48 us -> 1.64 us
  Pallas kernels: 66.1 us -> 71.6 us
  waiting for transfers between devices: 12.8 us -> 9 us
    unnamed x80 -> x10, local copies, waits for them, and re-layouts: 9.48 us -> 1.64 us
    pallas_call x19, Pallas kernels: 66.1 us -> 71.6 us  [run(): pl.pallas_call(call, grid_spec=pltpu.PrefetchScalarGridSpec(num_scalar_pr...]
    ppermute x4, waiting for transfers between devices: 9.04 us -> 6.17 us  [across(): return lax.ppermute(x, 'tp', [(i, (i + shift) % tps) for i in range(tps)])]
  transfers between devices with their start and end apart: 19 -> 19, of which waited for: 9 -> 6; matrix products, arithmetic and copies ran while one was open for 0% -> 0% of each run, Pallas kernels for 57% -> 66%
where the time goes in v9:
time: 98.2 us; the launch traced here: 97.8 us
  Pallas kernels  71.6 us (73%)
  starting transfers between devices  14.6 us (15%)
  waiting for transfers between devices  9 us (9%)
  local copies, waits for them, and re-layouts  1.64 us (2%)
  between operations  0.99 us (1%)
    pallas_call x19, Pallas kernels, run(): pl.pallas_call(call, grid_spec=pltpu.PrefetchScalarGridSpec(num_scalar_pr...  71.6 us
    all_to_all x1, starting transfers between devices, shards(): lax.all_to_all(sends, 'inst', split_axis=0, concat_axis=0, tiled=True)  6.33 us
    ppermute x4, waiting for transfers between devices, across(): return lax.ppermute(x, 'tp', [(i, (i + shift) % tps) for i in range(tps)])  6.17 us
    ppermute x4, starting transfers between devices, across(): return lax.ppermute(x, 'tp', [(i, (i + shift) % tps) for i in range(tps)])  4.31 us
    ppermute x14, starting transfers between devices, mate_of(): return lax.ppermute(x, 'tp', to_mate)  3.95 us
    ppermute x14, waiting for transfers between devices, mate_of(): return lax.ppermute(x, 'tp', to_mate)  2.82 us
  transfers between devices with their start and end apart: 19, of which 6 were waited for; matrix products, arithmetic and copies ran while one was open for 0% of the time, Pallas kernels for 66%

profile of v9, /device:TPU:0, one launch (start us, length us, event | category | flops | bytes accessed | tf_op | source)
XLA Modules:
  0.0 97.8 jit_solution(159020891640360825)
XLA Ops:
  0.6 3.5 %pack.1 = (bf16[4,2,32,16,256]{4,3,2,1,0:T(8,128)(2,1)}, bf16[256,128]{1,0:T(8,128)(2,1)}, bf16[32,256]{1,0:T(8,128)(2,1)}) custom-call(s32[1,2,32]{2,1,0:T(2,128)} %refs_0_.2, s32[8]{0:T(128)} %refs_0_.3, bf16[1,2,64,16,256]{4,3,2,1,0:T(8,128)(2,1)} %refs_2_.1, bf16[8192,128]{1,0:T(8,128)(2,1)} %bitcast.4, bf16[128,4,2,256]{3,2,1,0:T(2,128)(2,1)} %refs_3_.7), custom_call_target="tpu_custom_call" | custom-call | bytes 1024 | tf_op jit(solution)/shard_map/pack/pallas_call | solution.py:135
  4.1 6.3 %all-to-all-start = ((bf16[4,2,32,16,256]{4,3,2,1,0:T(8,128)(2,1)}), bf16[4,2,32,16,256]{4,3,2,1,0:T(8,128)(2,1)}, u32[]{:S(2)}, u32[]{:S(2)}) async-start(bf16[4,2,32,16,256]{4,3,2,1,0:T(8,128)(2,1)} %get-tuple-element.57.refs_6_), calls=%async_computation | async-start | bytes 4194304 | tf_op jit(solution)/shard_map/all_to_all | solution.py:638
  10.5 1.6 %copy-done.2 = bf16[4,2,32,16,256]{4,3,2,1,0:T(8,128)(2,1)S(1)} copy-done((bf16[4,2,32,16,256]{4,3,2,1,0:T(8,128)(2,1)S(1)}, bf16[4,2,32,16,256]{4,3,2,1,0:T(8,128)(2,1)}, u32[]{:S(2)}) %copy-start.2) | copy-done | bytes 2097176
  12.1 7.8 %attend.2 = (bf16[512,2048]{1,0:T(8,128)(2,1)S(1)}, bf16[2048,512]{1,0:T(8,128)(2,1)S(1)}, bf16[2048,512]{1,0:T(8,128)(2,1)S(1)}, bf16[2048,512]{1,0:T(8,128)(2,1)S(1)}, bf16[2048,512]{1,0:T(8,128)(2,1)S(1)}) custom-call(s32[8,125]{1,0:T(8,128)} %bitcast.7, s32[1,125]{1,0:T(1,128)} %refs_1_.6, bf16[8192,128]{1,0:T(8,128)(2,1)} %bitcast.5, ...), custom_call_target="tpu_custom_call" | custom-call | bytes 1024 | tf_op jit(solution)/shard_map/attend/pallas_call | solution.py:135
  19.9 1.8 %give.3 = (bf16[256,512]{1,0:T(8,128)(2,1)S(1)}, bf16[256,512]{1,0:T(8,128)(2,1)S(1)}, bf16[2048,512]{1,0:T(8,128)(2,1)S(1)}) custom-call(bf16[512,2048]{1,0:T(8,128)(2,1)S(1)} %get-tuple-element.60.refs_0_.refs_6_, bf16[2048,512]{1,0:T(8,128)(2,1)S(1)} %get-tuple-element.61.refs_1_, bf16[2048,512]{1,0:T(8,128)(2,1)S(1)} %get-tuple-element.62.refs_2_, ...), custom_call_target="tpu_custom_call" | custom-call | bytes 1024 | tf_op jit(solution)/shard_map/give/pallas_call | solution.py:135
  21.8 0.5 collective-permute-start
  22.3 1.0 %collective-permute-done.1.refs_4_ = bf16[256,512]{1,0:T(8,128)(2,1)S(1)} collective-permute-done((bf16[256,512]{1,0:T(8,128)(2,1)S(1)}, bf16[256,512]{1,0:T(8,128)(2,1)S(1)}, u32[]{:S(2)}, u32[]{:S(2)}) %collective-permute-start.1) | collective-permute-done | bytes 262176 | tf_op jit(solution)/shard_map/ppermute | solution.py:584
  23.7 1.8 %keep.3 = (bf16[256,1024]{1,0:T(8,128)(2,1)S(1)}, bf16[2048,512]{1,0:T(8,128)(2,1)S(1)}) custom-call(bf16[512,2048]{1,0:T(8,128)(2,1)S(1)} %get-tuple-element.60.refs_0_.refs_6_, bf16[2048,512]{1,0:T(8,128)(2,1)S(1)} %get-tuple-element.64.refs_1_, bf16[2048,512]{1,0:T(8,128)(2,1)S(1)} %get-tuple-element.65.refs_2_, ...), custom_call_target="tpu_custom_call" | custom-call | bytes 1024 | tf_op jit(solution)/shard_map/keep/pallas_call | solution.py:135
  25.6 1.6 %collective-permute-start.4 = (bf16[256,1024]{1,0:T(8,128)(2,1)S(1)}, bf16[256,1024]{1,0:T(8,128)(2,1)S(1)}, u32[]{:S(2)}, u32[]{:S(2)}) collective-permute-start(bf16[256,1024]{1,0:T(8,128)(2,1)S(1)} %get-tuple-element.69.refs_4_), channel_id=1, source_target_pairs={{0,2},{1,3},{2,0},{3,1},{4,6},{5,7},{6,4},{7,5},{8,10},{9,11},{10,... | collective-permute-start | bytes 1572872 | tf_op jit(solution)/shard_map/ppermute | solution.py:588
  27.1 2.3 %give.4 = (bf16[256,512]{1,0:T(8,128)(2,1)S(1)}, bf16[256,512]{1,0:T(8,128)(2,1)S(1)}, bf16[2048,512]{1,0:T(8,128)(2,1)S(1)}, bf16[2048,512]{1,0:T(8,128)(2,1)S(1)}) custom-call(bf16[512,2048]{1,0:T(8,128)(2,1)S(1)} %get-tuple-element.60.refs_0_.refs_6_, bf16[2048,512]{1,0:T(8,128)(2,1)S(1)} %get-tuple-element.63.refs_1_.refs_3_, ...), custom_call_target="tpu_custom_call" | custom-call | bytes 1024 | tf_op jit(solution)/shard_map/give/pallas_call | solution.py:135
  29.5 0.5 collective-permute-start.2
  30.0 1.0 %collective-permute-done.3.refs_4_ = bf16[256,512]{1,0:T(8,128)(2,1)S(1)} collective-permute-done((bf16[256,512]{1,0:T(8,128)(2,1)S(1)}, bf16[256,512]{1,0:T(8,128)(2,1)S(1)}, u32[]{:S(2)}, u32[]{:S(2)}) %collective-permute-start.3) | collective-permute-done | bytes 262176 | tf_op jit(solution)/shard_map/ppermute | solution.py:584
  31.4 1.8 %keep.4.refs_7_ = bf16[256,1024]{1,0:T(8,128)(2,1)S(1)} custom-call(bf16[512,2048]{1,0:T(8,128)(2,1)S(1)} %get-tuple-element.60.refs_0_.refs_6_, bf16[2048,512]{1,0:T(8,128)(2,1)S(1)} %get-tuple-element.70.refs_1_.refs_3_, bf16[2048,512]{1,0:T(8,128)(2,1)S(1)} %get-tuple-element.71.refs_2_.refs_4_, bf16[256,512]{1,0:T(8,128)(2,1)S(1)} %collective-permute-done.2.refs_3_, ...), custom_call_target="tpu_custom_call" | custom-call | bytes 1024 | tf_op jit(solution)/shard_map/keep/pallas_call | solution.py:135
  33.2 0.6 collective-permute-start.9
  33.8 7.8 %attend.3 = (bf16[512,2048]{1,0:T(8,128)(2,1)S(1)}, bf16[2048,512]{1,0:T(8,128)(2,1)S(1)}, bf16[2048,512]{1,0:T(8,128)(2,1)S(1)}, bf16[2048,512]{1,0:T(8,128)(2,1)S(1)}, bf16[2048,512]{1,0:T(8,128)(2,1)S(1)}) custom-call(s32[8,125]{1,0:T(8,128)} %bitcast.8, s32[1,125]{1,0:T(1,128)} %refs_1_.6, ...), custom_call_target="tpu_custom_call", output_to_operand_aliasing={{0}: (6, {})} | custom-call | bytes 1024 | tf_op jit(solution)/shard_map/attend/pallas_call | solution.py:135
  41.6 3.6 %give.5 = (bf16[256,512]{1,0:T(8,128)(2,1)S(1)}, bf16[256,512]{1,0:T(8,128)(2,1)S(1)}, bf16[256,512]{1,0:T(8,128)(2,1)S(1)}, bf16[256,512]{1,0:T(8,128)(2,1)S(1)...) custom-call(bf16[512,2048]{1,0:T(8,128)(2,1)S(1)} %get-tuple-element.74.refs_0_.refs_5_, ...), custom_call_target="tpu_custom_call" | custom-call | bytes 1024 | tf_op jit(solution)/shard_map/give/pallas_call | solution.py:135
  45.4 0.5 collective-permute-start.7
  46.4 4.5 %collective-permute-done.9.refs_11_.refs_4_ = bf16[256,1024]{1,0:T(8,128)(2,1)S(1)} collective-permute-done((bf16[256,1024]{1,0:T(8,128)(2,1)S(1)}, bf16[256,1024]{1,0:T(8,128)(2,1)S(1)}, u32[]{:S(2)}, u32[]{:S(2)}) %collective-permute-start.9) | collective-permute-done | bytes 524320 | tf_op jit(solution)/shard_map/ppermute | solution.py:588
  50.8 4.6 %keep.5 = (bf16[256,2048]{1,0:T(8,128)(2,1)}, bf16[2048,512]{1,0:T(8,128)(2,1)S(1)}, bf16[2048,512]{1,0:T(8,128)(2,1)S(1)}) custom-call(bf16[512,2048]{1,0:T(8,128)(2,1)S(1)} %get-tuple-element.74.refs_0_.refs_5_, bf16[2048,512]{1,0:T(8,128)(2,1)S(1)} %get-tuple-element.64.refs_1_, bf16[2048,512]{1,0:T(8,128)(2,1)S(1)} %get-tuple-element.65.refs_2_, ...), custom_call_target="tpu_custom_call" | custom-call | bytes 1024 | tf_op jit(solution)/shard_map/keep/pallas_call | solution.py:135
  55.5 1.6 %collective-permute-start.16 = (bf16[256,2048]{1,0:T(8,128)(2,1)}, bf16[256,2048]{1,0:T(8,128)(2,1)}, u32[]{:S(2)}, u32[]{:S(2)}) collective-permute-start(bf16[256,2048]{1,0:T(8,128)(2,1)} %get-tuple-element.85.refs_3_), channel_id=1, source_target_pairs={{0,2},{1,3},{2,0},{3,1},{4,6},{5,7},{6,4},{7,5},{8,10},{9,11},{10,... | collective-permute-start | bytes 3145736 | tf_op jit(solution)/shard_map/ppermute | solution.py:588
  57.1 2.9 %give_own.2 = (bf16[512,512]{1,0:T(8,128)(2,1)S(1)}, bf16[512,512]{1,0:T(8,128)(2,1)S(1)}) custom-call(bf16[512,2048]{1,0:T(8,128)(2,1)S(1)} %get-tuple-element.74.refs_0_.refs_5_, bf16[2048,512]{1,0:T(8,128)(2,1)S(1)} %get-tuple-element.83.refs_1_, bf16[2048,512]{1,0:T(8,128)(2,1)S(1)} %get-tuple-element.84.refs_2_, bf16[256,2048]{1,0:T(8,128)(2,1)} %get-tuple-element.85.refs_3_), custom_call_target="tpu_custom_call" | custom-call | bytes 1024 | tf_op jit(solution)/shard_map/give_own/pallas_call | solution.py:135
  60.6 2.9 %give_own.3 = (bf16[512,512]{1,0:T(8,128)(2,1)S(1)}, bf16[512,512]{1,0:T(8,128)(2,1)S(1)}) custom-call(bf16[512,2048]{1,0:T(8,128)(2,1)S(1)} %get-tuple-element.74.refs_0_.refs_5_, bf16[2048,512]{1,0:T(8,128)(2,1)S(1)} %get-tuple-element.81.refs_1_, bf16[2048,512]{1,0:T(8,128)(2,1)S(1)} %get-tuple-element.82.refs_2_, ...), custom_call_target="tpu_custom_call" | custom-call | bytes 1024 | tf_op jit(solution)/shard_map/give_own/pallas_call | solution.py:135
  64.0 3.9 %keep_own.2.refs_5_.refs_0_ = bf16[512,1024]{1,0:T(8,128)(2,1)} custom-call(bf16[512,2048]{1,0:T(8,128)(2,1)S(1)} %get-tuple-element.74.refs_0_.refs_5_, bf16[2048,512]{1,0:T(8,128)(2,1)S(1)} %get-tuple-element.89.refs_1_, bf16[2048,512]{1,0:T(8,128)(2,1)S(1)} %get-tuple-element.90.refs_2_, bf16[512,512]{1,0:T(8,128)(2,1)S(1)} %collective-permute-done.12.refs_3_, ...), custom_call_target="tpu_custom_call" | custom-call | bytes 1024 | tf_op jit(solution)/shard_map/keep_own/pallas_call | solution.py:135
  68.0 4.1 %keep_own.3.refs_7_.refs_1_ = bf16[512,1024]{1,0:T(8,128)(2,1)} custom-call(bf16[512,2048]{1,0:T(8,128)(2,1)S(1)} %get-tuple-element.74.refs_0_.refs_5_, bf16[2048,512]{1,0:T(8,128)(2,1)S(1)} %get-tuple-element.79.refs_1_, bf16[2048,512]{1,0:T(8,128)(2,1)S(1)} %get-tuple-element.80.refs_2_, bf16[512,512]{1,0:T(8,128)(2,1)S(1)} %collective-permute-done.10.refs_3_, ...), custom_call_target="tpu_custom_call" | custom-call | bytes 1024 | tf_op jit(solution)/shard_map/keep_own/pallas_call | solution.py:135
  72.1 8.3 %settle.1 = (bf16[16,2048]{1,0:T(8,128)(2,1)S(1)}, bf16[1,3,2,512,256]{4,3,2,1,0:T(8,128)(2,1)}, bf16[2048,512]{1,0:T(8,128)(2,1)S(1)}, bf16[2048,512]{1,0:T(8,1...) custom-call(s32[8]{0:T(128)} %refs_0_.3, ...), custom_call_target="tpu_custom_call" | custom-call | bytes 1024 | tf_op jit(solution)/shard_map/settle/pallas_call | solution.py:135
  80.3 3.6 %give_last.2 = (bf16[16,2048]{1,0:T(8,128)(2,1)S(1)}, bf16[2048,512]{1,0:T(8,128)(2,1)S(1)}, bf16[2048,512]{1,0:T(8,128)(2,1)S(1)}, bf16[2048,512]{1,0:T(8,128)(2,1)S(1)}, bf16[2048,512]{1,0:T(8,128)(2,1)S(1)}) custom-call(bf16[16,2048]{1,0:T(8,128)(2,1)S(1)} %get-tuple-element.93.refs_0_, bf16[2048,512]{1,0:T(8,128)(2,1)S(1)} %get-tuple-element.94.refs_1_, ...), custom_call_target="tpu_custom_call" | custom-call | bytes 1024 | tf_op jit(solution)/shard_map/give_last/pallas_call | solution.py:135
  84.1 2.0 %give_last.3.refs_7_ = bf16[16,2048]{1,0:T(8,128)(2,1)S(1)} custom-call(bf16[16,2048]{1,0:T(8,128)(2,1)S(1)} %get-tuple-element.93.refs_0_, bf16[2048,512]{1,0:T(8,128)(2,1)S(1)} %get-tuple-element.103.refs_1_, bf16[2048,512]{1,0:T(8,128)(2,1)S(1)} %get-tuple-element.104.refs_2_, bf16[2048,512]{1,0:T(8,128)(2,1)S(1)} %get-tuple-element.105.refs_3_, ...), custom_call_target="tpu_custom_call" | custom-call | bytes 1024 | tf_op jit(solution)/shard_map/give_last/pallas_call | solution.py:135
  86.5 3.5 %keep_last.2 = (bf16[16,2048]{1,0:T(8,128)(2,1)S(1)}, bf16[2048,512]{1,0:T(8,128)(2,1)S(1)}, bf16[2048,512]{1,0:T(8,128)(2,1)S(1)}, bf16[2048,512]{1,0:T(8,128)(2,1)S(1)}, bf16[2048,512]{1,0:T(8,128)(2,1)S(1)}) custom-call(bf16[16,2048]{1,0:T(8,128)(2,1)S(1)} %get-tuple-element.93.refs_0_, bf16[2048,512]{1,0:T(8,128)(2,1)S(1)} %get-tuple-element.98.refs_1_, ...), custom_call_target="tpu_custom_call" | custom-call | bytes 1024 | tf_op jit(solution)/shard_map/keep_last/pallas_call | solution.py:135
  90.1 0.6 collective-permute-start.17
  90.7 2.0 %keep_last.3.refs_2_ = f32[16,2048]{1,0:T(8,128)S(1)} custom-call(bf16[16,2048]{1,0:T(8,128)(2,1)S(1)} %get-tuple-element.93.refs_0_, bf16[2048,512]{1,0:T(8,128)(2,1)S(1)} %get-tuple-element.107.refs_1_, bf16[2048,512]{1,0:T(8,128)(2,1)S(1)} %get-tuple-element.108.refs_2_, bf16[2048,512]{1,0:T(8,128)(2,1)S(1)} %get-tuple-element.109.refs_3_, ...), custom_call_target="tpu_custom_call" | custom-call | bytes 1024 | tf_op jit(solution)/shard_map/keep_last/pallas_call | solution.py:135
  92.7 1.7 %collective-permute-done.17.refs_6_ = bf16[16,2048]{1,0:T(8,128)(2,1)S(1)} collective-permute-done((bf16[16,2048]{1,0:T(8,128)(2,1)S(1)}, bf16[16,2048]{1,0:T(8,128)(2,1)S(1)}, u32[]{:S(2)}, u32[]{:S(2)}) %collective-permute-start.17) | collective-permute-done | bytes 65568 | tf_op jit(solution)/shard_map/ppermute | solution.py:588
  94.4 3.2 %finish.1 = bf16[2048,512]{1,0:T(8,128)(2,1)} custom-call(bf16[512,1024]{1,0:T(8,128)(2,1)S(1)} %copy-done, bf16[512,1024]{1,0:T(8,128)(2,1)S(1)} %copy-done.1, f32[16,2048]{1,0:T(8,128)S(1)} %keep_last.3.refs_2_, bf16[256,1024]{1,0:T(8,128)(2,1)S(1)} %collective-permute-done.4.refs_6_.refs_3_, ...), custom_call_target="tpu_custom_call" | custom-call | bytes 1024 | tf_op jit(solution)/shard_map/finish/pallas_call | solution.py:135
  (35 shorter events, 3.3 us)
Async XLA Ops:
  4.1 67.9 %all-to-all-start = ((bf16[4,2,32,16,256]{4,3,2,1,0:T(8,128)(2,1)}), bf16[4,2,32,16,256]{4,3,2,1,0:T(8,128)(2,1)}, u32[]{:S(2)}, u32[]{:S(2)}) async-start(bf16[4,2,32,16,256]{4,3,2,1,0:T(8,128)(2,1)} %get-tuple-element.57.refs_6_), calls=%async_computation | async-start | bytes 4194304 | tf_op jit(solution)/shard_map/all_to_all | solution.py:638
  10.4 1.6 %copy-start.2 = (bf16[4,2,32,16,256]{4,3,2,1,0:T(8,128)(2,1)S(1)}, bf16[4,2,32,16,256]{4,3,2,1,0:T(8,128)(2,1)}, u32[]{:S(2)}) copy-start(bf16[4,2,32,16,256]{4,3,2,1,0:T(8,128)(2,1)} %get-tuple-element.57.refs_6_) | copy-start | bytes 6291460
  21.8 1.6 %collective-permute-start.1 = (bf16[256,512]{1,0:T(8,128)(2,1)S(1)}, bf16[256,512]{1,0:T(8,128)(2,1)S(1)}, u32[]{:S(2)}, u32[]{:S(2)}) collective-permute-start(bf16[256,512]{1,0:T(8,128)(2,1)S(1)} %get-tuple-element.67), channel_id=1, source_target_pairs={{0,1},{1,0},{2,3},{3,2},{4,5},{5,4},{6,7},{7,6},{8,9},{9,8},{10,11... | collective-permute-start | bytes 786440 | tf_op jit(solution)/shard_map/ppermute | solution.py:584
  21.8 1.9 %collective-permute-start = (bf16[256,512]{1,0:T(8,128)(2,1)S(1)}, bf16[256,512]{1,0:T(8,128)(2,1)S(1)}, u32[]{:S(2)}, u32[]{:S(2)}) collective-permute-start(bf16[256,512]{1,0:T(8,128)(2,1)S(1)} %get-tuple-element.66.refs_6_), channel_id=1, source_target_pairs={{0,1},{1,0},{2,3},{3,2},{4,5},{5,4},{6,7},{7,6},{8,9},{9,8},{10,11... | collective-permute-start | bytes 786440 | tf_op jit(solution)/shard_map/ppermute | solution.py:584
  25.6 16.1 %collective-permute-start.4 = (bf16[256,1024]{1,0:T(8,128)(2,1)S(1)}, bf16[256,1024]{1,0:T(8,128)(2,1)S(1)}, u32[]{:S(2)}, u32[]{:S(2)}) collective-permute-start(bf16[256,1024]{1,0:T(8,128)(2,1)S(1)} %get-tuple-element.69.refs_4_), channel_id=1, source_target_pairs={{0,2},{1,3},{2,0},{3,1},{4,6},{5,7},{6,4},{7,5},{8,10},{9,11},{10,... | collective-permute-start | bytes 1572872 | tf_op jit(solution)/shard_map/ppermute | solution.py:588
  29.4 1.6 %collective-permute-start.3 = (bf16[256,512]{1,0:T(8,128)(2,1)S(1)}, bf16[256,512]{1,0:T(8,128)(2,1)S(1)}, u32[]{:S(2)}, u32[]{:S(2)}) collective-permute-start(bf16[256,512]{1,0:T(8,128)(2,1)S(1)} %get-tuple-element.73), channel_id=1, source_target_pairs={{0,1},{1,0},{2,3},{3,2},{4,5},{5,4},{6,7},{7,6},{8,9},{9,8},{10,11... | collective-permute-start | bytes 786440 | tf_op jit(solution)/shard_map/ppermute | solution.py:584
  29.5 1.9 %collective-permute-start.2 = (bf16[256,512]{1,0:T(8,128)(2,1)S(1)}, bf16[256,512]{1,0:T(8,128)(2,1)S(1)}, u32[]{:S(2)}, u32[]{:S(2)}) collective-permute-start(bf16[256,512]{1,0:T(8,128)(2,1)S(1)} %get-tuple-element.72.refs_5_), channel_id=1, source_target_pairs={{0,1},{1,0},{2,3},{3,2},{4,5},{5,4},{6,7},{7,6},{8,9},{9,8},{10,11... | collective-permute-start | bytes 786440 | tf_op jit(solution)/shard_map/ppermute | solution.py:584
  33.2 17.6 %collective-permute-start.9 = (bf16[256,1024]{1,0:T(8,128)(2,1)S(1)}, bf16[256,1024]{1,0:T(8,128)(2,1)S(1)}, u32[]{:S(2)}, u32[]{:S(2)}) collective-permute-start(bf16[256,1024]{1,0:T(8,128)(2,1)S(1)} %keep.4.refs_7_), channel_id=1, source_target_pairs={{0,2},{1,3},{2,0},{3,1},{4,6},{5,7},{6,4},{7,5},{8,10},{9,11},{10,... | collective-permute-start | bytes 1572872 | tf_op jit(solution)/shard_map/ppermute | solution.py:588
  45.3 5.5 %collective-permute-start.6 = (bf16[256,512]{1,0:T(8,128)(2,1)S(1)}, bf16[256,512]{1,0:T(8,128)(2,1)S(1)}, u32[]{:S(2)}, u32[]{:S(2)}) collective-permute-start(bf16[256,512]{1,0:T(8,128)(2,1)S(1)} %get-tuple-element.76), channel_id=1, source_target_pairs={{0,1},{1,0},{2,3},{3,2},{4,5},{5,4},{6,7},{7,6},{8,9},{9,8},{10,11... | collective-permute-start | bytes 786440 | tf_op jit(solution)/shard_map/ppermute | solution.py:584
  45.4 5.5 %collective-permute-start.7 = (bf16[256,512]{1,0:T(8,128)(2,1)S(1)}, bf16[256,512]{1,0:T(8,128)(2,1)S(1)}, u32[]{:S(2)}, u32[]{:S(2)}) collective-permute-start(bf16[256,512]{1,0:T(8,128)(2,1)S(1)} %get-tuple-element.77), channel_id=1, source_target_pairs={{0,1},{1,0},{2,3},{3,2},{4,5},{5,4},{6,7},{7,6},{8,9},{9,8},{10,11... | collective-permute-start | bytes 786440 | tf_op jit(solution)/shard_map/ppermute | solution.py:584
  45.9 5.0 %collective-permute-start.8 = (bf16[256,512]{1,0:T(8,128)(2,1)S(1)}, bf16[256,512]{1,0:T(8,128)(2,1)S(1)}, u32[]{:S(2)}, u32[]{:S(2)}) collective-permute-start(bf16[256,512]{1,0:T(8,128)(2,1)S(1)} %get-tuple-element.78), channel_id=1, source_target_pairs={{0,1},{1,0},{2,3},{3,2},{4,5},{5,4},{6,7},{7,6},{8,9},{9,8},{10,11... | collective-permute-start | bytes 786440 | tf_op jit(solution)/shard_map/ppermute | solution.py:584
  45.9 4.9 %collective-permute-start.5 = (bf16[256,512]{1,0:T(8,128)(2,1)S(1)}, bf16[256,512]{1,0:T(8,128)(2,1)S(1)}, u32[]{:S(2)}, u32[]{:S(2)}) collective-permute-start(bf16[256,512]{1,0:T(8,128)(2,1)S(1)} %get-tuple-element.75.refs_10_), channel_id=1, source_target_pairs={{0,1},{1,0},{2,3},{3,2},{4,5},{5,4},{6,7},{7,6},{8,9},{9,8},{10,11... | collective-permute-start | bytes 786440 | tf_op jit(solution)/shard_map/ppermute | solution.py:584
  55.5 37.2 %collective-permute-start.16 = (bf16[256,2048]{1,0:T(8,128)(2,1)}, bf16[256,2048]{1,0:T(8,128)(2,1)}, u32[]{:S(2)}, u32[]{:S(2)}) collective-permute-start(bf16[256,2048]{1,0:T(8,128)(2,1)} %get-tuple-element.85.refs_3_), channel_id=1, source_target_pairs={{0,2},{1,3},{2,0},{3,1},{4,6},{5,7},{6,4},{7,5},{8,10},{9,11},{10,... | collective-permute-start | bytes 3145736 | tf_op jit(solution)/shard_map/ppermute | solution.py:588
  60.0 4.0 %collective-permute-start.13 = (bf16[512,512]{1,0:T(8,128)(2,1)S(1)}, bf16[512,512]{1,0:T(8,128)(2,1)S(1)}, u32[]{:S(2)}, u32[]{:S(2)}) collective-permute-start(bf16[512,512]{1,0:T(8,128)(2,1)S(1)} %get-tuple-element.91), channel_id=1, source_target_pairs={{0,1},{1,0},{2,3},{3,2},{4,5},{5,4},{6,7},{7,6},{8,9},{9,8},{10,11... | collective-permute-start | bytes 1572872 | tf_op jit(solution)/shard_map/ppermute | solution.py:584
  60.1 4.0 %collective-permute-start.12 = (bf16[512,512]{1,0:T(8,128)(2,1)S(1)}, bf16[512,512]{1,0:T(8,128)(2,1)S(1)}, u32[]{:S(2)}, u32[]{:S(2)}) collective-permute-start(bf16[512,512]{1,0:T(8,128)(2,1)S(1)} %get-tuple-element.86.refs_3_), channel_id=1, source_target_pairs={{0,1},{1,0},{2,3},{3,2},{4,5},{5,4},{6,7},{7,6},{8,9},{9,8},{10,11... | collective-permute-start | bytes 1572872 | tf_op jit(solution)/shard_map/ppermute | solution.py:584
  63.4 4.5 %collective-permute-start.11 = (bf16[512,512]{1,0:T(8,128)(2,1)S(1)}, bf16[512,512]{1,0:T(8,128)(2,1)S(1)}, u32[]{:S(2)}, u32[]{:S(2)}) collective-permute-start(bf16[512,512]{1,0:T(8,128)(2,1)S(1)} %get-tuple-element.88), channel_id=1, source_target_pairs={{0,1},{1,0},{2,3},{3,2},{4,5},{5,4},{6,7},{7,6},{8,9},{9,8},{10,11... | collective-permute-start | bytes 1572872 | tf_op jit(solution)/shard_map/ppermute | solution.py:584
  63.6 4.4 %collective-permute-start.10 = (bf16[512,512]{1,0:T(8,128)(2,1)S(1)}, bf16[512,512]{1,0:T(8,128)(2,1)S(1)}, u32[]{:S(2)}, u32[]{:S(2)}) collective-permute-start(bf16[512,512]{1,0:T(8,128)(2,1)S(1)} %get-tuple-element.87.refs_5_), channel_id=1, source_target_pairs={{0,1},{1,0},{2,3},{3,2},{4,5},{5,4},{6,7},{7,6},{8,9},{9,8},{10,11... | collective-permute-start | bytes 1572872 | tf_op jit(solution)/shard_map/ppermute | solution.py:584
  68.0 4.1 %copy-start.3 = (bf16[256,128]{1,0:T(8,128)(2,1)S(1)}, bf16[256,128]{1,0:T(8,128)(2,1)}, u32[]{:S(2)}) copy-start(bf16[256,128]{1,0:T(8,128)(2,1)} %get-tuple-element.58.refs_3_) | copy-start | bytes 196612
  68.0 4.1 %copy-start.4 = (bf16[32,256]{1,0:T(8,128)(2,1)S(1)}, bf16[32,256]{1,0:T(8,128)(2,1)}, u32[]{:S(2)}) copy-start(bf16[32,256]{1,0:T(8,128)(2,1)} %get-tuple-element.59.refs_4_) | copy-start | bytes 49156
  83.9 2.6 %collective-permute-start.14 = (bf16[16,2048]{1,0:T(8,128)(2,1)S(1)}, bf16[16,2048]{1,0:T(8,128)(2,1)S(1)}, u32[]{:S(2)}, u32[]{:S(2)}) collective-permute-start(bf16[16,2048]{1,0:T(8,128)(2,1)S(1)} %get-tuple-element.102.refs_5_), channel_id=1, source_target_pairs={{0,1},{1,0},{2,3},{3,2},{4,5},{5,4},{6,7},{7,6},{8,9},{9,8},{10,11... | collective-permute-start | bytes 196616 | tf_op jit(solution)/shard_map/ppermute | solution.py:584
  86.1 4.6 %collective-permute-start.15 = (bf16[16,2048]{1,0:T(8,128)(2,1)S(1)}, bf16[16,2048]{1,0:T(8,128)(2,1)S(1)}, u32[]{:S(2)}, u32[]{:S(2)}) collective-permute-start(bf16[16,2048]{1,0:T(8,128)(2,1)S(1)} %give_last.3.refs_7_), channel_id=1, source_target_pairs={{0,1},{1,0},{2,3},{3,2},{4,5},{5,4},{6,7},{7,6},{8,9},{9,8},{10,11... | collective-permute-start | bytes 196616 | tf_op jit(solution)/shard_map/ppermute | solution.py:584
  90.1 4.3 %collective-permute-start.17 = (bf16[16,2048]{1,0:T(8,128)(2,1)S(1)}, bf16[16,2048]{1,0:T(8,128)(2,1)S(1)}, u32[]{:S(2)}, u32[]{:S(2)}) collective-permute-start(bf16[16,2048]{1,0:T(8,128)(2,1)S(1)} %get-tuple-element.111.refs_6_), channel_id=1, source_target_pairs={{0,2},{1,3},{2,0},{3,1},{4,6},{5,7},{6,4},{7,5},{8,10},{9,11},{10,... | collective-permute-start | bytes 196616 | tf_op jit(solution)/shard_map/ppermute | solution.py:588
  90.7 3.8 %copy-start = (bf16[512,1024]{1,0:T(8,128)(2,1)S(1)}, bf16[512,1024]{1,0:T(8,128)(2,1)}, u32[]{:S(2)}) copy-start(bf16[512,1024]{1,0:T(8,128)(2,1)} %keep_own.2.refs_5_.refs_0_) | copy-start | bytes 3145732
  90.7 3.8 %copy-start.1 = (bf16[512,1024]{1,0:T(8,128)(2,1)S(1)}, bf16[512,1024]{1,0:T(8,128)(2,1)}, u32[]{:S(2)}) copy-start(bf16[512,1024]{1,0:T(8,128)(2,1)} %keep_own.3.refs_7_.refs_1_) | copy-start | bytes 3145732

commit v10 on v9

--- a/solution.py
+++ b/solution.py
@@ -155,24 +155,27 @@
 
 
 def pack_kernel(
-    ready, launch, table_ref, dest_ref, pool_ref, query_ref, kv_ref, send_ref, tail_q_ref,
-    tail_kv_ref, *, sizes
+    ready, launch, table_ref, dest_ref, pool_hbm, query_ref, kv_ref, send_hbm, tail_q_ref,
+    tail_kv_ref, sems, *, sizes
 ):
     inst = lax.axis_index("inst")
-    launch()
-    tail_q_ref[...] = query_ref[...]
-    tail_kv_ref[...] = kv_ref[...].reshape(sizes.tail_kv, 2 * sizes.width)
     ready()
-    for m in range(sizes.mig_per):
-        dest = dest_ref[inst * sizes.mig_per + m]
+    dests = [dest_ref[inst * sizes.mig_per + m] for m in range(sizes.mig_per)]
+    for m, dest in enumerate(dests):
 
         def copy_block(b, carry, m=m, dest=dest):
             block = table_ref[0, m, b]
             for s in range(sizes.slots):
-                send_ref[dest, s, b] = pool_ref[0, s, block]
+                pltpu.make_async_copy(
+                    pool_hbm.at[0, s, block], send_hbm.at[dest, s, b], sems.at[m]
+                ).start()
             return carry
 
         lax.fori_loop(0, sizes.mig_blocks, copy_block, 0, unroll=8)
+    tail_q_ref[...] = query_ref[...]
+    tail_kv_ref[...] = kv_ref[...].reshape(sizes.tail_kv, 2 * sizes.width)
+    for m, dest in enumerate(dests):
+        pltpu.make_async_copy(send_hbm.at[dest], send_hbm.at[dest], sems.at[m]).wait()
 
 
 def pack(src_table, mig_dest, out_pool, query_rows, new_kv, sizes):
@@ -183,19 +186,18 @@
         functools.partial(pack_kernel, sizes=z),
         [src_table, mig_dest], [out_pool, query_rows, new_kv],
         [
-            VMEM,
+            HBM,
             pl.BlockSpec((z.tail_q, z.width), lambda i: (last_q, 0)),
             pl.BlockSpec((z.insts,) + new_kv.shape[1:], lambda i: (last_kv, 0, 0, 0)),
         ],
         [],
         [
-            jax.ShapeDtypeStruct(
-                (z.insts, z.slots, z.mig_blocks, z.block, 2 * z.width), out_pool.dtype
-            ),
+            pltpu.HBM((z.insts, z.slots, z.mig_blocks, z.block, 2 * z.width), out_pool.dtype),
             jax.ShapeDtypeStruct((z.tail_q, z.width), out_pool.dtype),
             jax.ShapeDtypeStruct((z.tail_kv, 2 * z.width), out_pool.dtype),
         ],
-        [VMEM] * 3, "pack", z, limit=60, grid=(1,),
+        [ANY, VMEM, VMEM], "pack", z, limit=60, grid=(1,),
+        scratch=[pltpu.SemaphoreType.DMA((z.mig_per,))],
     )
     return result
 
@@ -365,8 +367,8 @@
 
 
 def settle_kernel(
-    ready, launch, dest_ref, len_ref, got_hbm, query_ref, kv_ref, old_ref, last_ref, arrived_hbm,
-    rows_ref, got_ref, keep_ref, sems, *, sizes
+    ready, launch, dest_ref, len_ref, got_hbm, query_ref, kv_ref, old_ref, out_ref, last_ref,
+    arrived_hbm, rows_ref, got_ref, keep_ref, sems, *, sizes
 ):
     z = sizes
     ready()
@@ -421,7 +423,9 @@
         at = slice(h * z.width, (h + 1) * z.width)
         column = rows_ref[pl.ds(h, tokens, stride=z.heads), :]
         old = old_ref[:, at].astype(jnp.float32)
-        last_ref[:, at] = jnp.where(filled, column, old).astype(jnp.bfloat16)
+        value = jnp.where(filled, column, old).astype(jnp.bfloat16)
+        out_ref[:, at] = value
+        last_ref[:, at] = value
     for write in writes:
         write.wait()
 
@@ -438,17 +442,18 @@
         [HBM, VMEM, VMEM, spec],
         deps,
         [
+            jax.ShapeDtypeStruct(attention.shape, jnp.bfloat16),
             jax.ShapeDtypeStruct((tokens, attention.shape[1]), jnp.bfloat16),
             jax.ShapeDtypeStruct((1, z.cap) + cache, jnp.bfloat16),
         ],
-        [VMEM, ANY], "settle", z, grid=(1,),
+        [spec, VMEM, ANY], "settle", z, grid=(1,),
         scratch=[
             pltpu.VMEM((z.insts * z.per, z.width), jnp.float32),
             pltpu.VMEM((z.cap,) + got.shape[1:], jnp.bfloat16),
             pltpu.VMEM((z.cap,) + cache, jnp.bfloat16),
             pltpu.SemaphoreType.DMA((2, z.cap)),
         ],
-        **fetch,
+        aliases={5: 0}, **fetch,
     )
 
 
@@ -496,7 +501,7 @@
     )
 
 
-def finish_kernel(ready, launch, own_low, own_high, own_late, *refs, fars, sizes):
+def finish_kernel(ready, launch, own_low, own_high, *refs, fars, sizes):
     z = sizes
     refs = list(refs)
 
@@ -507,7 +512,6 @@
 
     low, high, second, late = take(fars), take(fars), take(fars), take(fars)
     out_hbm, block_ref, sems = refs
-    rows = own_late.shape[0]
     tile = min(z.quarter, 256)
     writes = []
     for n in range(4):
@@ -516,16 +520,18 @@
             start = pl.multiple_of(j * tile, tile)
             at = pl.ds(n * z.quarter + start, tile)
             half = pl.ds((n % 2) * z.quarter + start, tile)
-            begin = low[0].shape[0]
-            own = own_low if n < 2 else own_high
-            first = own[:begin, half].astype(jnp.float32)
-            rest = own[begin:-rows, half].astype(jnp.float32)
-            last = own_late[:, at]
+            sums = (own_low if n < 2 else own_high)[:, half]
             for k in range(fars):
-                first = first + (low if n < 2 else high)[k][:, half].astype(jnp.float32)
-                rest = rest + second[k][:-rows, at].astype(jnp.float32)
-                last = last + late[k][:, at].astype(jnp.float32)
-            sums = jnp.concatenate([first, rest, last], axis=0)
+                rows = late[k].shape[0]
+                arrived = jnp.concatenate(
+                    [
+                        (low if n < 2 else high)[k][:, half],
+                        second[k][:-rows, at],
+                        late[k][:, at],
+                    ],
+                    axis=0,
+                )
+                sums = sums + arrived.astype(jnp.float32)
             block_ref[n, pl.ds(start, tile), :] = sums.T.astype(jnp.bfloat16)
             return carry
 
@@ -539,10 +545,10 @@
         write.wait()
 
 
-def finish(own, own_late, low, high, second, late, sizes, deps):
+def finish(own, low, high, second, late, sizes, deps):
     z = sizes
     tokens = own[0].shape[0]
-    operands = own + [own_late] + low + high + second + late
+    operands = own + low + high + second + late
     result, _ = run(
         functools.partial(finish_kernel, fars=len(low), sizes=z),
         [], operands, [VMEM] * len(operands), deps,
@@ -596,9 +602,6 @@
     def keeps(ks, parts):
         return [(k, True, part) for k in ks for part in parts]
 
-    def in_hbm(arrays):
-        return [pltpu.with_memory_space_constraint(x, pltpu.HBM) for x in arrays]
-
     def hold(pieces, arrays):
         held.update(zip(pieces, arrays))
 
@@ -638,46 +641,43 @@
     arriving = lax.all_to_all(sends, "inst", split_axis=0, concat_axis=0, tiled=True)
 
     tokens = half * z.steps
-    pieces = gives(far, low) + keeps(far, low)
+    pieces = gives(far, low) + keeps(far, low) + gives(far, high)
     rows, new = attend(
         table, res_len, query_rows, new_kv, res_pool, None, 0, half, z, [sends],
         **bringing(pieces),
     )
     hold(pieces, new)
-    a, b, whole = (rows, 0, tokens), None, None
-    given, mates = give(a, far, low, "give", [], gives(far, (2,)))
-    kept = keep(a, far, low, mates, "keep", [given], gives(far, (3,)))
+    a = (rows, 0, tokens)
+    given, mates_low = give(a, far, low, "give", [], keeps(far, high))
+    given, mates_high = give(a, far, high, "give", [given])
+    kept = keep(a, far, low, mates_low, "keep", [given])
     got_low = sent(kept)
-    given, mates = give(a, far, high, "give", kept[-1:], keeps(far, high))
-    kept = keep(a, far, high, mates, "keep", [given])
+    kept = keep(a, far, high, mates_high, "keep", kept[-1:])
     got_high = sent(kept)
-    rows, new = attend(
+    rows, _ = attend(
         table, res_len, query_rows, new_kv, res_pool, rows, half, half, z, kept[-1:],
-        **bringing(gives([0], every)),
-    )
-    hold(gives([0], every), new)
-    b, whole = (rows, tokens, tokens), (rows, 0, 2 * tokens)
-    given, mates = give(b, far, every, "give", got_low, keeps([0], low))
-    kept = keep(b, far, every, mates, "keep", [given] + got_high, keeps([0], high))
+    )
+    b = (rows, tokens, tokens)
+    given, mates = give(b, far, every, "give", [])
+    kept = keep(b, far, every, mates, "keep", [given] + got_low)
     got_second = sent(kept)
 
-    given, mates_low = give(whole, [0], low, "give_own", kept[-1:])
-    given, mates_high = give(whole, [0], high, "give_own", [given])
-    own = keep(whole, [0], low, mates_low, "keep_own", [given], place=pltpu.HBM)
-    own += keep(whole, [0], high, mates_high, "keep_own", in_hbm(own), place=pltpu.HBM)
-
-    pieces = gives(far, every) + gives([0], every)
-    (last, arrived), new = settle(
-        mig_dest, mig_len, arriving, tail_q, tail_kv, rows, z, in_hbm(own[-1:]), **bringing(pieces)
+    pieces = gives(far, every) + keeps(far, (0,))
+    (rows, last, arrived), new = settle(
+        mig_dest, mig_len, arriving, tail_q, tail_kv, rows, z, kept[-1:] + got_high,
+        **bringing(pieces),
     )
     hold(pieces, new)
-    late = (last, 0, last.shape[0])
-    given, mates = give(late, far, every, "give_last", [], keeps(far, every), joined=True)
-    given, own_mates = give(late, [0], every, "give_last", [given], joined=True)
-    kept = keep(late, far, every, mates, "keep_last", [given], keeps([0], every))
+    late, whole = (last, 0, last.shape[0]), (rows, 0, 2 * tokens)
+    given, mates = give(late, far, every, "give_last", [], gives([0], low), joined=True)
+    given, mates_low = give(whole, [0], low, "give_own", [given], keeps(far, (1, 2, 3)))
+    kept = keep(late, far, every, mates, "keep_last", [given], gives([0], high))
     got_late = sent(kept)
-    own_late = keep(late, [0], every, own_mates, "keep_last", kept[-1:], dtype=jnp.float32)
-    hidden = finish(own, own_late[0], got_low, got_high, got_second, got_late, z, [])
+    pieces = keeps([0], (0, 1, 2))
+    given, mates_high = give(whole, [0], high, "give_own", kept[-1:], pieces)
+    own = keep(whole, [0], low, mates_low, "keep_own", [given], keeps([0], (3,)), jnp.float32)
+    own += keep(whole, [0], high, mates_high, "keep_own", own, (), jnp.float32)
+    hidden = finish(own, got_low, got_high, got_second, got_late, z, [])
     return (arrived, hidden)
 
 

time: 98.2 us -> 121 us (1.23)
  Pallas kernels: 71.6 us -> 91.8 us
  local copies, waits for them, and re-layouts: 1.64 us -> 3.49 us
    pallas_call x19 -> x17, Pallas kernels: 71.6 us -> 91.8 us  [run(): pl.pallas_call(call, grid_spec=pltpu.PrefetchScalarGridSpec(num_scalar_pr...]
    ppermute x4, waiting for transfers between devices: 6.17 us -> 9.02 us  [across(): return lax.ppermute(x, 'tp', [(i, (i + shift) % tps) for i in range(tps)])]
    unnamed x10 -> x16, local copies, waits for them, and re-layouts: 1.64 us -> 3.49 us
    ppermute x14 -> x13, waiting for transfers between devices: 2.82 us -> 1.14 us  [mate_of(): return lax.ppermute(x, 'tp', to_mate)]
    ppermute x14 -> x13, starting transfers between devices: 3.95 us -> 3.48 us  [mate_of(): return lax.ppermute(x, 'tp', to_mate)]
  transfers between devices with their start and end apart: 19 -> 18, of which waited for: 6 -> 4; matrix products, arithmetic and copies ran while one was open for 0% -> 0% of each run, Pallas kernels for 66% -> 44%
where the time goes in v10:
time: 121 us
  Pallas kernels  91.8 us (76%)
  starting transfers between devices  14.2 us (12%)
  waiting for transfers between devices  10.2 us (8%)
  local copies, waits for them, and re-layouts  3.49 us (3%)
    pallas_call x17, Pallas kernels, run(): pl.pallas_call(call, grid_spec=pltpu.PrefetchScalarGridSpec(num_scalar_pr...  91.8 us
    ppermute x4, waiting for transfers between devices, across(): return lax.ppermute(x, 'tp', [(i, (i + shift) % tps) for i in range(tps)])  9.02 us
    all_to_all x1, starting transfers between devices, shards(): lax.all_to_all(sends, 'inst', split_axis=0, concat_axis=0, tiled=True)  6.33 us
    ppermute x4, starting transfers between devices, across(): return lax.ppermute(x, 'tp', [(i, (i + shift) % tps) for i in range(tps)])  4.37 us
    unnamed x16, local copies, waits for them, and re-layouts  3.49 us
    ppermute x13, starting transfers between devices, mate_of(): return lax.ppermute(x, 'tp', to_mate)  3.48 us
  transfers between devices with their start and end apart: 18, of which 4 were waited for; matrix products, arithmetic and copies ran while one was open for 0% of the time, Pallas kernels for 44%

profile of v10, /device:TPU:0, one launch (start us, length us, event | category | flops | bytes accessed | tf_op | source)
XLA Modules:
  0.0 120.6 jit_solution(5844554818439533684)
XLA Ops:
  0.6 35.1 %pack.1 = (bf16[4,2,32,16,256]{4,3,2,1,0:T(8,128)(2,1)}, bf16[256,128]{1,0:T(8,128)(2,1)}, bf16[32,256]{1,0:T(8,128)(2,1)}) custom-call(s32[1,2,32]{2,1,0:T(2,128)} %refs_0_.2, s32[8]{0:T(128)} %refs_0_.3, bf16[1,2,64,16,256]{4,3,2,1,0:T(8,128)(2,1)} %refs_2_.1, bf16[8192,128]{1,0:T(8,128)(2,1)} %bitcast.4, bf16[128,4,2,256]{3,2,1,0:T(2,128)(2,1)} %refs_3_.7), custom_call_target="tpu_custom_call" | custom-call | bytes 1024 | tf_op jit(solution)/shard_map/pack/pallas_call | solution.py:135
  35.7 6.3 %all-to-all-start = ((bf16[4,2,32,16,256]{4,3,2,1,0:T(8,128)(2,1)}), bf16[4,2,32,16,256]{4,3,2,1,0:T(8,128)(2,1)}, u32[]{:S(2)}, u32[]{:S(2)}) async-start(bf16[4,2,32,16,256]{4,3,2,1,0:T(8,128)(2,1)} %get-tuple-element.48.refs_6_), calls=%async_computation | async-start | bytes 4194304 | tf_op jit(solution)/shard_map/all_to_all | solution.py:641
  42.1 1.6 %copy-done = bf16[4,2,32,16,256]{4,3,2,1,0:T(8,128)(2,1)S(1)} copy-done((bf16[4,2,32,16,256]{4,3,2,1,0:T(8,128)(2,1)S(1)}, bf16[4,2,32,16,256]{4,3,2,1,0:T(8,128)(2,1)}, u32[]{:S(2)}) %copy-start) | copy-done | bytes 2097176
  43.7 7.9 %attend.2 = (bf16[512,2048]{1,0:T(8,128)(2,1)S(1)}, bf16[2048,512]{1,0:T(8,128)(2,1)S(1)}, bf16[2048,512]{1,0:T(8,128)(2,1)S(1)}, bf16[2048,512]{1,0:T(8,128)(2,...) custom-call(s32[8,125]{1,0:T(8,128)} %bitcast.7, ...), custom_call_target="tpu_custom_call" | custom-call | bytes 1024 | tf_op jit(solution)/shard_map/attend/pallas_call | solution.py:135
  51.6 2.3 %give.3 = (bf16[256,512]{1,0:T(8,128)(2,1)S(1)}, bf16[256,512]{1,0:T(8,128)(2,1)S(1)}, bf16[2048,512]{1,0:T(8,128)(2,1)S(1)}, bf16[2048,512]{1,0:T(8,128)(2,1)S(1)}) custom-call(bf16[512,2048]{1,0:T(8,128)(2,1)S(1)} %get-tuple-element.51.refs_0_.refs_5_, bf16[2048,512]{1,0:T(8,128)(2,1)S(1)} %get-tuple-element.52.refs_1_, ...), custom_call_target="tpu_custom_call" | custom-call | bytes 1024 | tf_op jit(solution)/shard_map/give/pallas_call | solution.py:135
  53.9 0.5 collective-permute-start.2
  54.4 1.8 %give.4 = (bf16[256,512]{1,0:T(8,128)(2,1)S(1)}, bf16[256,512]{1,0:T(8,128)(2,1)S(1)}) custom-call(bf16[512,2048]{1,0:T(8,128)(2,1)S(1)} %get-tuple-element.51.refs_0_.refs_5_, bf16[2048,512]{1,0:T(8,128)(2,1)S(1)} %get-tuple-element.56.refs_1_.refs_3_, bf16[2048,512]{1,0:T(8,128)(2,1)S(1)} %get-tuple-element.57.refs_2_.refs_4_, ...), custom_call_target="tpu_custom_call" | custom-call | bytes 1024 | tf_op jit(solution)/shard_map/give/pallas_call | solution.py:135
  56.4 0.4 collective-permute-start
  56.8 1.8 %keep.3.refs_5_ = bf16[256,1024]{1,0:T(8,128)(2,1)S(1)} custom-call(bf16[512,2048]{1,0:T(8,128)(2,1)S(1)} %get-tuple-element.51.refs_0_.refs_5_, bf16[2048,512]{1,0:T(8,128)(2,1)S(1)} %get-tuple-element.61.refs_1_, bf16[2048,512]{1,0:T(8,128)(2,1)S(1)} %get-tuple-element.62.refs_2_, bf16[256,512]{1,0:T(8,128)(2,1)S(1)} %collective-permute-done.2.refs_3_, ...), custom_call_target="tpu_custom_call" | custom-call | bytes 1024 | tf_op jit(solution)/shard_map/keep/pallas_call | solution.py:135
  58.6 1.6 %collective-permute-start.8 = (bf16[256,1024]{1,0:T(8,128)(2,1)S(1)}, bf16[256,1024]{1,0:T(8,128)(2,1)S(1)}, u32[]{:S(2)}, u32[]{:S(2)}) collective-permute-start(bf16[256,1024]{1,0:T(8,128)(2,1)S(1)} %keep.3.refs_5_), channel_id=1, source_target_pairs={{0,2},{1,3},{2,0},{3,1},{4,6},{5,7},{6,4},{7,5},{8,10},{9,11},{10,... | collective-permute-start | bytes 1572872 | tf_op jit(solution)/shard_map/ppermute | solution.py:594
  60.2 1.8 %keep.4.refs_6_ = bf16[256,1024]{1,0:T(8,128)(2,1)S(1)} custom-call(bf16[512,2048]{1,0:T(8,128)(2,1)S(1)} %get-tuple-element.51.refs_0_.refs_5_, bf16[2048,512]{1,0:T(8,128)(2,1)S(1)} %get-tuple-element.54.refs_1_.refs_3_, bf16[2048,512]{1,0:T(8,128)(2,1)S(1)} %get-tuple-element.55.refs_2_.refs_4_, bf16[256,512]{1,0:T(8,128)(2,1)S(1)} %collective-permute-done.refs_3_, ...), custom_call_target="tpu_custom_call" | custom-call | bytes 1024 | tf_op jit(solution)/shard_map/keep/pallas_call | solution.py:135
  62.0 7.8 %attend.3.refs_0_.refs_5_ = bf16[512,2048]{1,0:T(8,128)(2,1)S(1)} custom-call(s32[8,125]{1,0:T(8,128)} %bitcast.8, s32[1,125]{1,0:T(1,128)} %refs_1_.6, bf16[8192,128]{1,0:T(8,128)(2,1)} %bitcast.6, bf16[128,4,2,256]{3,2,1,0:T(2,128)(2,1)} %refs_3_.7, bf16[1,2,64,16,256]{4,3,2,1,0:T(8,128)(2,1)} %refs_4_.5, ...), custom_call_target="tpu_custom_call", output_to_operand_aliasing={{}: (5, {})} | custom-call | bytes 1024 | tf_op jit(solution)/shard_map/attend/pallas_call | solution.py:135
  69.8 3.6 %give.5 = (bf16[256,512]{1,0:T(8,128)(2,1)S(1)}, bf16[256,512]{1,0:T(8,128)(2,1)S(1)}, bf16[256,512]{1,0:T(8,128)(2,1)S(1)}, bf16[256,512]{1,0:T(8,128)(2,1)S(1)}) custom-call(bf16[512,2048]{1,0:T(8,128)(2,1)S(1)} %attend.3.refs_0_.refs_5_, bf16[2048,512]{1,0:T(8,128)(2,1)S(1)} %get-tuple-element.52.refs_1_, ...), custom_call_target="tpu_custom_call" | custom-call | bytes 1024 | tf_op jit(solution)/shard_map/give/pallas_call | solution.py:135
  73.5 0.5 collective-permute-start.6
  74.5 0.5 collective-permute-done.5.refs_6_
  75.0 0.5 collective-permute-start.9
  76.2 3.6 %keep.5.refs_7_ = bf16[256,2048]{1,0:T(8,128)(2,1)S(1)} custom-call(bf16[512,2048]{1,0:T(8,128)(2,1)S(1)} %attend.3.refs_0_.refs_5_, bf16[2048,512]{1,0:T(8,128)(2,1)S(1)} %get-tuple-element.61.refs_1_, bf16[2048,512]{1,0:T(8,128)(2,1)S(1)} %get-tuple-element.62.refs_2_, bf16[2048,512]{1,0:T(8,128)(2,1)S(1)} %get-tuple-element.54.refs_1_.refs_3_, ...), custom_call_target="tpu_custom_call" | custom-call | bytes 1024 | tf_op jit(solution)/shard_map/keep/pallas_call | solution.py:135
  79.8 1.0 collective-permute-start.15
  80.8 9.0 %collective-permute-done.9.refs_8_.refs_3_ = bf16[256,1024]{1,0:T(8,128)(2,1)S(1)} collective-permute-done((bf16[256,1024]{1,0:T(8,128)(2,1)S(1)}, bf16[256,1024]{1,0:T(8,128)(2,1)S(1)}, u32[]{:S(2)}, u32[]{:S(2)}) %collective-permute-start.9) | collective-permute-done | bytes 524320 | tf_op jit(solution)/shard_map/ppermute | solution.py:594
  89.8 0.8 copy-done.1
  90.6 1.0 copy-done.2
  91.7 6.4 %settle.1 = (bf16[512,2048]{1,0:T(8,128)(2,1)S(1)}, bf16[16,2048]{1,0:T(8,128)(2,1)S(1)}, bf16[1,3,2,512,256]{4,3,2,1,0:T(8,128)(2,1)}, bf16[2048,512]{1,0:T(8,1...) custom-call(s32[8]{0:T(128)} %refs_0_.3, ...), custom_call_target="tpu_custom_call", output_to_operand_aliasing={{0}: (5, {})} | custom-call | bytes 1024 | tf_op jit(solution)/shard_map/settle/pallas_call | solution.py:135
  98.0 2.3 %give_last.1 = (bf16[16,2048]{1,0:T(8,128)(2,1)S(1)}, bf16[2048,512]{1,0:T(8,128)(2,1)S(1)}, bf16[2048,512]{1,0:T(8,128)(2,1)S(1)}) custom-call(bf16[16,2048]{1,0:T(8,128)(2,1)S(1)} %get-tuple-element.70.refs_0_, bf16[2048,512]{1,0:T(8,128)(2,1)S(1)} %get-tuple-element.72.refs_1_, bf16[2048,512]{1,0:T(8,128)(2,1)S(1)} %get-tuple-element.73.refs_2_, ...), custom_call_target="tpu_custom_call" | custom-call | bytes 1024 | tf_op jit(solution)/shard_map/give_last/pallas_call | solution.py:135
  100.4 3.0 %give_own.2 = (bf16[512,512]{1,0:T(8,128)(2,1)S(1)}, bf16[512,512]{1,0:T(8,128)(2,1)S(1)}, bf16[2048,512]{1,0:T(8,128)(2,1)S(1)}, bf16[2048,512]{1,0:T(8,128)(2,1)S(1)}, bf16[2048,512]{1,0:T(8,128)(2,1)S(1)}) custom-call(bf16[512,2048]{1,0:T(8,128)(2,1)S(1)} %get-tuple-element.69.refs_0_, bf16[2048,512]{1,0:T(8,128)(2,1)S(1)} %get-tuple-element.76.refs_1_, ...), custom_call_target="tpu_custom_call" | custom-call | bytes 1024 | tf_op jit(solution)/shard_map/give_own/pallas_call | solution.py:135
  103.4 0.5 collective-permute-start.12
  104.0 2.3 %keep_last.1 = (bf16[16,2048]{1,0:T(8,128)(2,1)S(1)}, bf16[2048,512]{1,0:T(8,128)(2,1)S(1)}, bf16[2048,512]{1,0:T(8,128)(2,1)S(1)}) custom-call(bf16[16,2048]{1,0:T(8,128)(2,1)S(1)} %get-tuple-element.70.refs_0_, bf16[2048,512]{1,0:T(8,128)(2,1)S(1)} %get-tuple-element.71.refs_1_, bf16[2048,512]{1,0:T(8,128)(2,1)S(1)} %get-tuple-element.79.refs_2_, ...), custom_call_target="tpu_custom_call" | custom-call | bytes 1024 | tf_op jit(solution)/shard_map/keep_last/pallas_call | solution.py:135
  106.3 3.1 %give_own.3 = (bf16[512,512]{1,0:T(8,128)(2,1)S(1)}, bf16[512,512]{1,0:T(8,128)(2,1)S(1)}, bf16[2048,512]{1,0:T(8,128)(2,1)S(1)}, bf16[2048,512]{1,0:T(8,128)(2,1)S(1)}, bf16[2048,512]{1,0:T(8,128)(2,1)S(1)}) custom-call(bf16[512,2048]{1,0:T(8,128)(2,1)S(1)} %get-tuple-element.69.refs_0_, bf16[2048,512]{1,0:T(8,128)(2,1)S(1)} %get-tuple-element.83.refs_1_, ...), custom_call_target="tpu_custom_call" | custom-call | bytes 1024 | tf_op jit(solution)/shard_map/give_own/pallas_call | solution.py:135
  109.4 0.5 collective-permute-start.14
  110.0 1.3 %collective-permute-start.16 = (bf16[16,2048]{1,0:T(8,128)(2,1)S(1)}, bf16[16,2048]{1,0:T(8,128)(2,1)S(1)}, u32[]{:S(2)}, u32[]{:S(2)}) collective-permute-start(bf16[16,2048]{1,0:T(8,128)(2,1)S(1)} %get-tuple-element.85.refs_4_), channel_id=1, source_target_pairs={{0,2},{1,3},{2,0},{3,1},{4,6},{5,7},{6,4},{7,5},{8,10},{9,11},{10,... | collective-permute-start | bytes 196616 | tf_op jit(solution)/shard_map/ppermute | solution.py:594
  111.3 2.9 %keep_own.2 = (f32[512,1024]{1,0:T(8,128)S(1)}, bf16[2048,512]{1,0:T(8,128)(2,1)S(1)}) custom-call(bf16[512,2048]{1,0:T(8,128)(2,1)S(1)} %get-tuple-element.69.refs_0_, bf16[2048,512]{1,0:T(8,128)(2,1)S(1)} %get-tuple-element.86.refs_1_, bf16[2048,512]{1,0:T(8,128)(2,1)S(1)} %get-tuple-element.87.refs_2_, ...), custom_call_target="tpu_custom_call" | custom-call | bytes 1024 | tf_op jit(solution)/shard_map/keep_own/pallas_call | solution.py:135
  114.2 2.9 %keep_own.3.refs_1_ = f32[512,1024]{1,0:T(8,128)S(1)} custom-call(bf16[512,2048]{1,0:T(8,128)(2,1)S(1)} %get-tuple-element.69.refs_0_, bf16[2048,512]{1,0:T(8,128)(2,1)S(1)} %get-tuple-element.91.refs_1_, bf16[2048,512]{1,0:T(8,128)(2,1)S(1)} %get-tuple-element.92.refs_2_, bf16[512,512]{1,0:T(8,128)(2,1)S(1)} %collective-permute-done.13.refs_3_, ...), custom_call_target="tpu_custom_call" | custom-call | bytes 1024 | tf_op jit(solution)/shard_map/keep_own/pallas_call | solution.py:135
  117.2 3.3 %finish.1 = bf16[2048,512]{1,0:T(8,128)(2,1)} custom-call(f32[512,1024]{1,0:T(8,128)S(1)} %get-tuple-element.90.refs_5_.refs_0_, f32[512,1024]{1,0:T(8,128)S(1)} %keep_own.3.refs_1_, bf16[256,1024]{1,0:T(8,128)(2,1)S(1)} %copy-done.5, bf16[256,1024]{1,0:T(8,128)(2,1)S(1)} %copy-done.3, bf16[256,2048]{1,0:T(8,128)(2,1)} %collective-permute-done.15.refs_4_, ...), custom_call_target="tpu_custom_call" | custom-call | bytes 1024 | tf_op jit(solution)/shard_map/finish/pallas_call | solution.py:135
  (37 shorter events, 1.7 us)
Async XLA Ops:
  35.7 54.9 %all-to-all-start = ((bf16[4,2,32,16,256]{4,3,2,1,0:T(8,128)(2,1)}), bf16[4,2,32,16,256]{4,3,2,1,0:T(8,128)(2,1)}, u32[]{:S(2)}, u32[]{:S(2)}) async-start(bf16[4,2,32,16,256]{4,3,2,1,0:T(8,128)(2,1)} %get-tuple-element.48.refs_6_), calls=%async_computation | async-start | bytes 4194304 | tf_op jit(solution)/shard_map/all_to_all | solution.py:641
  42.1 1.6 %copy-start = (bf16[4,2,32,16,256]{4,3,2,1,0:T(8,128)(2,1)S(1)}, bf16[4,2,32,16,256]{4,3,2,1,0:T(8,128)(2,1)}, u32[]{:S(2)}) copy-start(bf16[4,2,32,16,256]{4,3,2,1,0:T(8,128)(2,1)} %get-tuple-element.48.refs_6_) | copy-start | bytes 6291460
  53.8 3.0 %collective-permute-start.3 = (bf16[256,512]{1,0:T(8,128)(2,1)S(1)}, bf16[256,512]{1,0:T(8,128)(2,1)S(1)}, u32[]{:S(2)}, u32[]{:S(2)}) collective-permute-start(bf16[256,512]{1,0:T(8,128)(2,1)S(1)} %get-tuple-element.63), channel_id=1, source_target_pairs={{0,1},{1,0},{2,3},{3,2},{4,5},{5,4},{6,7},{7,6},{8,9},{9,8},{10,11... | collective-permute-start | bytes 786440 | tf_op jit(solution)/shard_map/ppermute | solution.py:590
  53.9 2.9 %collective-permute-start.2 = (bf16[256,512]{1,0:T(8,128)(2,1)S(1)}, bf16[256,512]{1,0:T(8,128)(2,1)S(1)}, u32[]{:S(2)}, u32[]{:S(2)}) collective-permute-start(bf16[256,512]{1,0:T(8,128)(2,1)S(1)} %get-tuple-element.58.refs_3_), channel_id=1, source_target_pairs={{0,1},{1,0},{2,3},{3,2},{4,5},{5,4},{6,7},{7,6},{8,9},{9,8},{10,11... | collective-permute-start | bytes 786440 | tf_op jit(solution)/shard_map/ppermute | solution.py:590
  56.2 4.0 %collective-permute-start.1 = (bf16[256,512]{1,0:T(8,128)(2,1)S(1)}, bf16[256,512]{1,0:T(8,128)(2,1)S(1)}, u32[]{:S(2)}, u32[]{:S(2)}) collective-permute-start(bf16[256,512]{1,0:T(8,128)(2,1)S(1)} %get-tuple-element.60), channel_id=1, source_target_pairs={{0,1},{1,0},{2,3},{3,2},{4,5},{5,4},{6,7},{7,6},{8,9},{9,8},{10,11... | collective-permute-start | bytes 786440 | tf_op jit(solution)/shard_map/ppermute | solution.py:590
  56.4 3.9 %collective-permute-start = (bf16[256,512]{1,0:T(8,128)(2,1)S(1)}, bf16[256,512]{1,0:T(8,128)(2,1)S(1)}, u32[]{:S(2)}, u32[]{:S(2)}) collective-permute-start(bf16[256,512]{1,0:T(8,128)(2,1)S(1)} %get-tuple-element.59.refs_5_), channel_id=1, source_target_pairs={{0,1},{1,0},{2,3},{3,2},{4,5},{5,4},{6,7},{7,6},{8,9},{9,8},{10,11... | collective-permute-start | bytes 786440 | tf_op jit(solution)/shard_map/ppermute | solution.py:590
  58.6 17.5 %collective-permute-start.8 = (bf16[256,1024]{1,0:T(8,128)(2,1)S(1)}, bf16[256,1024]{1,0:T(8,128)(2,1)S(1)}, u32[]{:S(2)}, u32[]{:S(2)}) collective-permute-start(bf16[256,1024]{1,0:T(8,128)(2,1)S(1)} %keep.3.refs_5_), channel_id=1, source_target_pairs={{0,2},{1,3},{2,0},{3,1},{4,6},{5,7},{6,4},{7,5},{8,10},{9,11},{10,... | collective-permute-start | bytes 1572872 | tf_op jit(solution)/shard_map/ppermute | solution.py:594
  73.4 1.6 %collective-permute-start.5 = (bf16[256,512]{1,0:T(8,128)(2,1)S(1)}, bf16[256,512]{1,0:T(8,128)(2,1)S(1)}, u32[]{:S(2)}, u32[]{:S(2)}) collective-permute-start(bf16[256,512]{1,0:T(8,128)(2,1)S(1)} %get-tuple-element.65), channel_id=1, source_target_pairs={{0,1},{1,0},{2,3},{3,2},{4,5},{5,4},{6,7},{7,6},{8,9},{9,8},{10,11... | collective-permute-start | bytes 786440 | tf_op jit(solution)/shard_map/ppermute | solution.py:590
  73.5 2.0 %collective-permute-start.6 = (bf16[256,512]{1,0:T(8,128)(2,1)S(1)}, bf16[256,512]{1,0:T(8,128)(2,1)S(1)}, u32[]{:S(2)}, u32[]{:S(2)}) collective-permute-start(bf16[256,512]{1,0:T(8,128)(2,1)S(1)} %get-tuple-element.66), channel_id=1, source_target_pairs={{0,1},{1,0},{2,3},{3,2},{4,5},{5,4},{6,7},{7,6},{8,9},{9,8},{10,11... | collective-permute-start | bytes 786440 | tf_op jit(solution)/shard_map/ppermute | solution.py:590
  74.0 1.8 %collective-permute-start.7 = (bf16[256,512]{1,0:T(8,128)(2,1)S(1)}, bf16[256,512]{1,0:T(8,128)(2,1)S(1)}, u32[]{:S(2)}, u32[]{:S(2)}) collective-permute-start(bf16[256,512]{1,0:T(8,128)(2,1)S(1)} %get-tuple-element.67), channel_id=1, source_target_pairs={{0,1},{1,0},{2,3},{3,2},{4,5},{5,4},{6,7},{7,6},{8,9},{9,8},{10,11... | collective-permute-start | bytes 786440 | tf_op jit(solution)/shard_map/ppermute | solution.py:590
  74.1 16.5 %copy-start.6 = (bf16[256,128]{1,0:T(8,128)(2,1)S(1)}, bf16[256,128]{1,0:T(8,128)(2,1)}, u32[]{:S(2)}) copy-start(bf16[256,128]{1,0:T(8,128)(2,1)} %get-tuple-element.49.refs_3_) | copy-start | bytes 196612
  74.1 16.5 %copy-start.7 = (bf16[32,256]{1,0:T(8,128)(2,1)S(1)}, bf16[32,256]{1,0:T(8,128)(2,1)}, u32[]{:S(2)}) copy-start(bf16[32,256]{1,0:T(8,128)(2,1)} %get-tuple-element.50.refs_4_) | copy-start | bytes 49156
  74.1 2.1 %collective-permute-start.4 = (bf16[256,512]{1,0:T(8,128)(2,1)S(1)}, bf16[256,512]{1,0:T(8,128)(2,1)S(1)}, u32[]{:S(2)}, u32[]{:S(2)}) collective-permute-start(bf16[256,512]{1,0:T(8,128)(2,1)S(1)} %get-tuple-element.64.refs_9_), channel_id=1, source_target_pairs={{0,1},{1,0},{2,3},{3,2},{4,5},{5,4},{6,7},{7,6},{8,9},{9,8},{10,11... | collective-permute-start | bytes 786440 | tf_op jit(solution)/shard_map/ppermute | solution.py:590
  75.0 14.8 %collective-permute-start.9 = (bf16[256,1024]{1,0:T(8,128)(2,1)S(1)}, bf16[256,1024]{1,0:T(8,128)(2,1)S(1)}, u32[]{:S(2)}, u32[]{:S(2)}) collective-permute-start(bf16[256,1024]{1,0:T(8,128)(2,1)S(1)} %keep.4.refs_6_), channel_id=1, source_target_pairs={{0,2},{1,3},{2,0},{3,1},{4,6},{5,7},{6,4},{7,5},{8,10},{9,11},{10,... | collective-permute-start | bytes 1572872 | tf_op jit(solution)/shard_map/ppermute | solution.py:594
  76.2 3.6 %copy-start.4 = (bf16[256,1024]{1,0:T(8,128)(2,1)}, bf16[256,1024]{1,0:T(8,128)(2,1)S(1)}, u32[]{:S(2)}) copy-start(bf16[256,1024]{1,0:T(8,128)(2,1)S(1)} %collective-permute-done.8.refs_10_.refs_2_) | copy-start | bytes 1572868
  79.8 37.3 %collective-permute-start.15 = (bf16[256,2048]{1,0:T(8,128)(2,1)S(1)}, bf16[256,2048]{1,0:T(8,128)(2,1)}, u32[]{:S(2)}, u32[]{:S(2)}) collective-permute-start(bf16[256,2048]{1,0:T(8,128)(2,1)S(1)} %keep.5.refs_7_), channel_id=1, source_target_pairs={{0,2},{1,3},{2,0},{3,1},{4,6},{5,7},{6,4},{7,5},{8,10},{9,11},{10,... | collective-permute-start | bytes 3145736 | tf_op jit(solution)/shard_map/ppermute | solution.py:594
  89.8 0.8 copy-start.1
  90.6 1.0 copy-start.2
  100.3 3.7 %collective-permute-start.10 = (bf16[16,2048]{1,0:T(8,128)(2,1)S(1)}, bf16[16,2048]{1,0:T(8,128)(2,1)S(1)}, u32[]{:S(2)}, u32[]{:S(2)}) collective-permute-start(bf16[16,2048]{1,0:T(8,128)(2,1)S(1)} %get-tuple-element.78.refs_4_), channel_id=1, source_target_pairs={{0,1},{1,0},{2,3},{3,2},{4,5},{5,4},{6,7},{7,6},{8,9},{9,8},{10,11... | collective-permute-start | bytes 196616 | tf_op jit(solution)/shard_map/ppermute | solution.py:590
  103.4 6.6 %collective-permute-start.12 = (bf16[512,512]{1,0:T(8,128)(2,1)S(1)}, bf16[512,512]{1,0:T(8,128)(2,1)S(1)}, u32[]{:S(2)}, u32[]{:S(2)}) collective-permute-start(bf16[512,512]{1,0:T(8,128)(2,1)S(1)} %get-tuple-element.88), channel_id=1, source_target_pairs={{0,1},{1,0},{2,3},{3,2},{4,5},{5,4},{6,7},{7,6},{8,9},{9,8},{10,11... | collective-permute-start | bytes 1572872 | tf_op jit(solution)/shard_map/ppermute | solution.py:590
  103.9 7.4 %collective-permute-start.11 = (bf16[512,512]{1,0:T(8,128)(2,1)S(1)}, bf16[512,512]{1,0:T(8,128)(2,1)S(1)}, u32[]{:S(2)}, u32[]{:S(2)}) collective-permute-start(bf16[512,512]{1,0:T(8,128)(2,1)S(1)} %get-tuple-element.82.refs_7_), channel_id=1, source_target_pairs={{0,1},{1,0},{2,3},{3,2},{4,5},{5,4},{6,7},{7,6},{8,9},{9,8},{10,11... | collective-permute-start | bytes 1572872 | tf_op jit(solution)/shard_map/ppermute | solution.py:590
  109.4 4.8 %collective-permute-start.14 = (bf16[512,512]{1,0:T(8,128)(2,1)S(1)}, bf16[512,512]{1,0:T(8,128)(2,1)S(1)}, u32[]{:S(2)}, u32[]{:S(2)}) collective-permute-start(bf16[512,512]{1,0:T(8,128)(2,1)S(1)} %get-tuple-element.93), channel_id=1, source_target_pairs={{0,1},{1,0},{2,3},{3,2},{4,5},{5,4},{6,7},{7,6},{8,9},{9,8},{10,11... | collective-permute-start | bytes 1572872 | tf_op jit(solution)/shard_map/ppermute | solution.py:590
  109.9 4.3 %collective-permute-start.13 = (bf16[512,512]{1,0:T(8,128)(2,1)S(1)}, bf16[512,512]{1,0:T(8,128)(2,1)S(1)}, u32[]{:S(2)}, u32[]{:S(2)}) collective-permute-start(bf16[512,512]{1,0:T(8,128)(2,1)S(1)} %get-tuple-element.89.refs_6_), channel_id=1, source_target_pairs={{0,1},{1,0},{2,3},{3,2},{4,5},{5,4},{6,7},{7,6},{8,9},{9,8},{10,11... | collective-permute-start | bytes 1572872 | tf_op jit(solution)/shard_map/ppermute | solution.py:590
  110.0 7.2 %collective-permute-start.16 = (bf16[16,2048]{1,0:T(8,128)(2,1)S(1)}, bf16[16,2048]{1,0:T(8,128)(2,1)S(1)}, u32[]{:S(2)}, u32[]{:S(2)}) collective-permute-start(bf16[16,2048]{1,0:T(8,128)(2,1)S(1)} %get-tuple-element.85.refs_4_), channel_id=1, source_target_pairs={{0,2},{1,3},{2,0},{3,1},{4,6},{5,7},{6,4},{7,5},{8,10},{9,11},{10,... | collective-permute-start | bytes 196616 | tf_op jit(solution)/shard_map/ppermute | solution.py:594
  114.2 2.9 %copy-start.3 = (bf16[256,1024]{1,0:T(8,128)(2,1)S(1)}, bf16[256,1024]{1,0:T(8,128)(2,1)}, u32[]{:S(2)}) copy-start(bf16[256,1024]{1,0:T(8,128)(2,1)} %copy-done.1) | copy-start | bytes 1572868
  114.2 2.9 %copy-start.5 = (bf16[256,1024]{1,0:T(8,128)(2,1)S(1)}, bf16[256,1024]{1,0:T(8,128)(2,1)}, u32[]{:S(2)}) copy-start(bf16[256,1024]{1,0:T(8,128)(2,1)} %copy-done.4) | copy-start | bytes 1572868

commit v11 on v10

--- a/solution.py
+++ b/solution.py
@@ -155,49 +155,54 @@
 
 
 def pack_kernel(
-    ready, launch, table_ref, dest_ref, pool_hbm, query_ref, kv_ref, send_hbm, tail_q_ref,
-    tail_kv_ref, sems, *, sizes
+    ready, launch, table_ref, dest_ref, pool_ref, query_ref, kv_ref, send_hbm, tail_q_ref,
+    tail_kv_ref, pack_ref, sems, *, sizes
 ):
     inst = lax.axis_index("inst")
     ready()
-    dests = [dest_ref[inst * sizes.mig_per + m] for m in range(sizes.mig_per)]
-    for m, dest in enumerate(dests):
-
-        def copy_block(b, carry, m=m, dest=dest):
+    copies = []
+    for m in range(sizes.mig_per):
+        dest = dest_ref[inst * sizes.mig_per + m]
+
+        def copy_block(b, carry, m=m):
             block = table_ref[0, m, b]
             for s in range(sizes.slots):
-                pltpu.make_async_copy(
-                    pool_hbm.at[0, s, block], send_hbm.at[dest, s, b], sems.at[m]
-                ).start()
+                pack_ref[m, s, b] = pool_ref[0, s, block]
             return carry
 
         lax.fori_loop(0, sizes.mig_blocks, copy_block, 0, unroll=8)
+        copies.append(pltpu.make_async_copy(pack_ref.at[m], send_hbm.at[dest], sems.at[m]))
+        copies[-1].start()
     tail_q_ref[...] = query_ref[...]
     tail_kv_ref[...] = kv_ref[...].reshape(sizes.tail_kv, 2 * sizes.width)
-    for m, dest in enumerate(dests):
-        pltpu.make_async_copy(send_hbm.at[dest], send_hbm.at[dest], sems.at[m]).wait()
+    for copy in copies:
+        copy.wait()
 
 
 def pack(src_table, mig_dest, out_pool, query_rows, new_kv, sizes):
     z = sizes
     last_q = query_rows.shape[0] // z.tail_q - 1
     last_kv = z.batch // z.insts - 1
+    request = (z.slots, z.mig_blocks, z.block, 2 * z.width)
     result, _ = run(
         functools.partial(pack_kernel, sizes=z),
         [src_table, mig_dest], [out_pool, query_rows, new_kv],
         [
-            HBM,
+            VMEM,
             pl.BlockSpec((z.tail_q, z.width), lambda i: (last_q, 0)),
             pl.BlockSpec((z.insts,) + new_kv.shape[1:], lambda i: (last_kv, 0, 0, 0)),
         ],
         [],
         [
-            pltpu.HBM((z.insts, z.slots, z.mig_blocks, z.block, 2 * z.width), out_pool.dtype),
-            jax.ShapeDtypeStruct((z.tail_q, z.width), out_pool.dtype),
-            jax.ShapeDtypeStruct((z.tail_kv, 2 * z.width), out_pool.dtype),
+            pltpu.HBM((z.insts,) + request, out_pool.dtype),
+            pltpu.HBM((z.tail_q, z.width), out_pool.dtype),
+            pltpu.HBM((z.tail_kv, 2 * z.width), out_pool.dtype),
         ],
         [ANY, VMEM, VMEM], "pack", z, limit=60, grid=(1,),
-        scratch=[pltpu.SemaphoreType.DMA((z.mig_per,))],
+        scratch=[
+            pltpu.VMEM((z.mig_per,) + request, out_pool.dtype),
+            pltpu.SemaphoreType.DMA((z.mig_per,)),
+        ],
     )
     return result
 
@@ -501,7 +506,7 @@
     )
 
 
-def finish_kernel(ready, launch, own_low, own_high, *refs, fars, sizes):
+def final_kernel(ready, launch, attention, *refs, count, streamed, mates, fars, sizes):
     z = sizes
     refs = list(refs)
 
@@ -510,34 +515,48 @@
         del refs[:n]
         return taken
 
+    weights, extra = take(count), take(mates)
     low, high, second, late = take(fars), take(fars), take(fars), take(fars)
-    out_hbm, block_ref, sems = refs
+    source = take(bool(streamed))
+    (out_hbm,) = take(1)
+    block_ref, block_sems = take(2)
+    copies = [None] * count
+    for n, piece in enumerate(streamed):
+        begin = pl.multiple_of(piece_columns(piece, z), LANES)
+        copy = pltpu.make_async_copy(
+            source[0].at[:, pl.ds(begin, z.quarter)], refs[0].at[n], refs[1].at[n]
+        )
+        copy.start()
+        copies.append(copy)
+        weights.append(refs[0].at[n])
     tile = min(z.quarter, 256)
     writes = []
-    for n in range(4):
-
-        def one(j, carry, n=n):
+    for n, (weight, copy) in enumerate(zip(weights, copies)):
+        if copy is not None:
+            copy.wait()
+
+        def one(j, carry, n=n, weight=weight):
             start = pl.multiple_of(j * tile, tile)
-            at = pl.ds(n * z.quarter + start, tile)
-            half = pl.ds((n % 2) * z.quarter + start, tile)
-            sums = (own_low if n < 2 else own_high)[:, half]
+            at = pl.ds(start, tile)
+            whole = pl.ds(n * z.quarter + start, tile)
+            sums = dot(attention[...], weight[:, at]) + extra[n][:, at].astype(jnp.float32)
             for k in range(fars):
                 rows = late[k].shape[0]
                 arrived = jnp.concatenate(
                     [
-                        (low if n < 2 else high)[k][:, half],
-                        second[k][:-rows, at],
-                        late[k][:, at],
+                        low[k][:, whole] if n < 3 else high[k][:, at],
+                        second[k][:-rows, whole],
+                        late[k][:, whole],
                     ],
                     axis=0,
                 )
                 sums = sums + arrived.astype(jnp.float32)
-            block_ref[n, pl.ds(start, tile), :] = sums.T.astype(jnp.bfloat16)
+            block_ref[n, at, :] = sums.T.astype(jnp.bfloat16)
             return carry
 
         lax.fori_loop(0, z.quarter // tile, one, 0)
         write = pltpu.make_async_copy(
-            block_ref.at[n], out_hbm.at[pl.ds(n * z.quarter, z.quarter)], sems.at[n]
+            block_ref.at[n], out_hbm.at[pl.ds(n * z.quarter, z.quarter)], block_sems.at[n]
         )
         write.start()
         writes.append(write)
@@ -545,16 +564,22 @@
         write.wait()
 
 
-def finish(own, low, high, second, late, sizes, deps):
+def final(attention, weights, streamed, out_weight, mates, low, high, second, late, sizes, deps):
     z = sizes
-    tokens = own[0].shape[0]
-    operands = own + low + high + second + late
+    tokens = attention.shape[0]
+    operands = [attention] + weights + mates + low + high + second + late + [out_weight]
+    specs = [VMEM] * (len(operands) - 1) + [HBM]
     result, _ = run(
-        functools.partial(finish_kernel, fars=len(low), sizes=z),
-        [], operands, [VMEM] * len(operands), deps,
-        [jax.ShapeDtypeStruct((z.features, tokens), jnp.bfloat16)], [ANY], "finish", z,
+        functools.partial(
+            final_kernel, count=len(weights), streamed=streamed, mates=len(mates),
+            fars=len(low), sizes=z,
+        ),
+        [], operands, specs, deps,
+        [jax.ShapeDtypeStruct((z.features, tokens), jnp.bfloat16)], [ANY], "final", z,
         scratch=[
-            pltpu.VMEM((4, z.quarter, tokens), jnp.bfloat16), pltpu.SemaphoreType.DMA((4,))
+            pltpu.VMEM((4, z.quarter, tokens), jnp.bfloat16), pltpu.SemaphoreType.DMA((4,)),
+            pltpu.VMEM((len(streamed), z.depth, z.quarter), jnp.bfloat16),
+            pltpu.SemaphoreType.DMA((len(streamed),)),
         ],
     )
     return result[0]
@@ -650,9 +675,10 @@
     a = (rows, 0, tokens)
     given, mates_low = give(a, far, low, "give", [], keeps(far, high))
     given, mates_high = give(a, far, high, "give", [given])
-    kept = keep(a, far, low, mates_low, "keep", [given])
+    mates = [mates_low[2 * n : 2 * n + 2] + mates_high[2 * n : 2 * n + 2] for n in range(chips - 1)]
+    kept = keep(a, far, (0, 1, 2), sum((m[:3] for m in mates), []), "keep", [given])
     got_low = sent(kept)
-    kept = keep(a, far, high, mates_high, "keep", kept[-1:])
+    kept = keep(a, far, (3,), sum((m[3:] for m in mates), []), "keep", kept[-1:])
     got_high = sent(kept)
     rows, _ = attend(
         table, res_len, query_rows, new_kv, res_pool, rows, half, half, z, kept[-1:],
@@ -663,6 +689,9 @@
     got_second = sent(kept)
 
     pieces = gives(far, every) + keeps(far, (0,))
+    tail_q, tail_kv = (
+        pltpu.with_memory_space_constraint(x, pltpu.HBM) for x in (tail_q, tail_kv)
+    )
     (rows, last, arrived), new = settle(
         mig_dest, mig_len, arriving, tail_q, tail_kv, rows, z, kept[-1:] + got_high,
         **bringing(pieces),
@@ -675,9 +704,11 @@
     got_late = sent(kept)
     pieces = keeps([0], (0, 1, 2))
     given, mates_high = give(whole, [0], high, "give_own", kept[-1:], pieces)
-    own = keep(whole, [0], low, mates_low, "keep_own", [given], keeps([0], (3,)), jnp.float32)
-    own += keep(whole, [0], high, mates_high, "keep_own", own, (), jnp.float32)
-    hidden = finish(own, got_low, got_high, got_second, got_late, z, [])
+    weights = [held[piece] for piece in pieces]
+    hidden = final(
+        rows, weights, keeps([0], (3,)), out_weight, mates_low + mates_high, got_low, got_high,
+        got_second, got_late, z, [given],
+    )
     return (arrived, hidden)
 
 

time: 121 us -> 115 us (0.950)
  Pallas kernels: 91.8 us -> 60.4 us
  waiting for transfers between devices: 10.2 us -> 37 us
  local copies, waits for them, and re-layouts: 3.49 us -> 1.63 us
    pallas_call x17 -> x15, Pallas kernels: 91.8 us -> 60.4 us  [run(): pl.pallas_call(call, grid_spec=pltpu.PrefetchScalarGridSpec(num_scalar_pr...]
    ppermute x4, waiting for transfers between devices: 9.02 us -> 32.3 us  [across(): return lax.ppermute(x, 'tp', [(i, (i + shift) % tps) for i in range(tps)])]
    ppermute x13, waiting for transfers between devices: 1.14 us -> 4.65 us  [mate_of(): return lax.ppermute(x, 'tp', to_mate)]
    unnamed x16 -> x6, local copies, waits for them, and re-layouts: 3.49 us -> 1.63 us
  transfers between devices with their start and end apart: 18 -> 18, of which waited for: 4 -> 9; matrix products, arithmetic and copies ran while one was open for 0% -> 0% of each run, Pallas kernels for 44% -> 42%
where the time goes in v11:
time: 115 us
  Pallas kernels  60.4 us (53%)
  waiting for transfers between devices  37 us (32%)
  starting transfers between devices  14.6 us (13%)
  local copies, waits for them, and re-layouts  1.63 us (1%)
    pallas_call x15, Pallas kernels, run(): pl.pallas_call(call, grid_spec=pltpu.PrefetchScalarGridSpec(num_scalar_pr...  60.4 us
    ppermute x4, waiting for transfers between devices, across(): return lax.ppermute(x, 'tp', [(i, (i + shift) % tps) for i in range(tps)])  32.3 us
    all_to_all x1, starting transfers between devices, shards(): lax.all_to_all(sends, 'inst', split_axis=0, concat_axis=0, tiled=True)  6.33 us
    ppermute x4, starting transfers between devices, across(): return lax.ppermute(x, 'tp', [(i, (i + shift) % tps) for i in range(tps)])  5.19 us
    ppermute x13, waiting for transfers between devices, mate_of(): return lax.ppermute(x, 'tp', to_mate)  4.65 us
    ppermute x13, starting transfers between devices, mate_of(): return lax.ppermute(x, 'tp', to_mate)  3.05 us
  transfers between devices with their start and end apart: 18, of which 9 were waited for; matrix products, arithmetic and copies ran while one was open for 0% of the time, Pallas kernels for 42%

profile of v11, /device:TPU:0, one launch (start us, length us, event | category | flops | bytes accessed | tf_op | source)
XLA Modules:
  0.0 114.6 jit_solution(12573184582660399195)
XLA Ops:
  0.6 3.6 %pack.1 = (bf16[4,2,32,16,256]{4,3,2,1,0:T(8,128)(2,1)}, bf16[256,128]{1,0:T(8,128)(2,1)}, bf16[32,256]{1,0:T(8,128)(2,1)}) custom-call(s32[1,2,32]{2,1,0:T(2,128)} %refs_0_.2, s32[8]{0:T(128)} %refs_0_.3, bf16[1,2,64,16,256]{4,3,2,1,0:T(8,128)(2,1)} %refs_2_.1, bf16[8192,128]{1,0:T(8,128)(2,1)} %bitcast.4, bf16[128,4,2,256]{3,2,1,0:T(2,128)(2,1)} %refs_3_.7), custom_call_target="tpu_custom_call" | custom-call | bytes 1024 | tf_op jit(solution)/shard_map/pack/pallas_call | solution.py:135
  4.3 6.3 %all-to-all-start = ((bf16[4,2,32,16,256]{4,3,2,1,0:T(8,128)(2,1)}), bf16[4,2,32,16,256]{4,3,2,1,0:T(8,128)(2,1)}, u32[]{:S(2)}, u32[]{:S(2)}) async-start(bf16[4,2,32,16,256]{4,3,2,1,0:T(8,128)(2,1)} %get-tuple-element.46.refs_6_), calls=%async_computation | async-start | bytes 4194304 | tf_op jit(solution)/shard_map/all_to_all | solution.py:666
  10.6 1.6 %copy-done = bf16[4,2,32,16,256]{4,3,2,1,0:T(8,128)(2,1)S(1)} copy-done((bf16[4,2,32,16,256]{4,3,2,1,0:T(8,128)(2,1)S(1)}, bf16[4,2,32,16,256]{4,3,2,1,0:T(8,128)(2,1)}, u32[]{:S(2)}) %copy-start) | copy-done | bytes 2097176
  12.2 7.8 %attend.2 = (bf16[512,2048]{1,0:T(8,128)(2,1)S(1)}, bf16[2048,512]{1,0:T(8,128)(2,1)S(1)}, bf16[2048,512]{1,0:T(8,128)(2,1)S(1)}, bf16[2048,512]{1,0:T(8,128)(2,...) custom-call(s32[8,125]{1,0:T(8,128)} %bitcast.7, ...), custom_call_target="tpu_custom_call" | custom-call | bytes 1024 | tf_op jit(solution)/shard_map/attend/pallas_call | solution.py:135
  20.1 2.3 %give.3 = (bf16[256,512]{1,0:T(8,128)(2,1)S(1)}, bf16[256,512]{1,0:T(8,128)(2,1)S(1)}, bf16[2048,512]{1,0:T(8,128)(2,1)S(1)}, bf16[2048,512]{1,0:T(8,128)(2,1)S(1)}) custom-call(bf16[512,2048]{1,0:T(8,128)(2,1)S(1)} %get-tuple-element.49.refs_0_.refs_5_, bf16[2048,512]{1,0:T(8,128)(2,1)S(1)} %get-tuple-element.50.refs_1_, ...), custom_call_target="tpu_custom_call" | custom-call | bytes 1024 | tf_op jit(solution)/shard_map/give/pallas_call | solution.py:135
  22.4 0.5 collective-permute-start.1
  22.9 1.8 %give.4 = (bf16[256,512]{1,0:T(8,128)(2,1)S(1)}, bf16[256,512]{1,0:T(8,128)(2,1)S(1)}) custom-call(bf16[512,2048]{1,0:T(8,128)(2,1)S(1)} %get-tuple-element.49.refs_0_.refs_5_, bf16[2048,512]{1,0:T(8,128)(2,1)S(1)} %get-tuple-element.53.refs_1_.refs_3_, bf16[2048,512]{1,0:T(8,128)(2,1)S(1)} %get-tuple-element.54.refs_2_.refs_4_, ...), custom_call_target="tpu_custom_call" | custom-call | bytes 1024 | tf_op jit(solution)/shard_map/give/pallas_call | solution.py:135
  24.9 1.5 %collective-permute-done.3.refs_6_ = bf16[256,512]{1,0:T(8,128)(2,1)S(1)} collective-permute-done((bf16[256,512]{1,0:T(8,128)(2,1)S(1)}, bf16[256,512]{1,0:T(8,128)(2,1)S(1)}, u32[]{:S(2)}, u32[]{:S(2)}) %collective-permute-start.3) | collective-permute-done | bytes 262176 | tf_op jit(solution)/shard_map/ppermute | solution.py:615
  26.4 2.7 %keep.3.refs_3_ = bf16[256,1536]{1,0:T(8,128)(2,1)S(1)} custom-call(bf16[512,2048]{1,0:T(8,128)(2,1)S(1)} %get-tuple-element.49.refs_0_.refs_5_, bf16[2048,512]{1,0:T(8,128)(2,1)S(1)} %get-tuple-element.57.refs_1_, bf16[2048,512]{1,0:T(8,128)(2,1)S(1)} %get-tuple-element.58.refs_2_, bf16[2048,512]{1,0:T(8,128)(2,1)S(1)} %get-tuple-element.59.refs_3_, ...), custom_call_target="tpu_custom_call" | custom-call | bytes 1024 | tf_op jit(solution)/shard_map/keep/pallas_call | solution.py:135
  29.1 1.6 %collective-permute-start.8 = (bf16[256,1536]{1,0:T(8,128)(2,1)S(1)}, bf16[256,1536]{1,0:T(8,128)(2,1)S(1)}, u32[]{:S(2)}, u32[]{:S(2)}) collective-permute-start(bf16[256,1536]{1,0:T(8,128)(2,1)S(1)} %keep.3.refs_3_), channel_id=1, source_target_pairs={{0,2},{1,3},{2,0},{3,1},{4,6},{5,7},{6,4},{7,5},{8,10},{9,11},{10,... | collective-permute-start | bytes 2359304 | tf_op jit(solution)/shard_map/ppermute | solution.py:619
  30.7 1.5 %collective-permute-done.refs_2_ = bf16[256,512]{1,0:T(8,128)(2,1)S(1)} collective-permute-done((bf16[256,512]{1,0:T(8,128)(2,1)S(1)}, bf16[256,512]{1,0:T(8,128)(2,1)S(1)}, u32[]{:S(2)}, u32[]{:S(2)}) %collective-permute-start) | collective-permute-done | bytes 262176 | tf_op jit(solution)/shard_map/ppermute | solution.py:615
  32.2 0.9 keep.4.refs_6_
  33.1 7.8 %attend.3.refs_0_.refs_5_ = bf16[512,2048]{1,0:T(8,128)(2,1)S(1)} custom-call(s32[8,125]{1,0:T(8,128)} %bitcast.8, s32[1,125]{1,0:T(1,128)} %refs_1_.6, bf16[8192,128]{1,0:T(8,128)(2,1)} %bitcast.6, bf16[128,4,2,256]{3,2,1,0:T(2,128)(2,1)} %refs_3_.7, bf16[1,2,64,16,256]{4,3,2,1,0:T(8,128)(2,1)} %refs_4_.5, ...), custom_call_target="tpu_custom_call", output_to_operand_aliasing={{}: (5, {})} | custom-call | bytes 1024 | tf_op jit(solution)/shard_map/attend/pallas_call | solution.py:135
  40.9 3.6 %give.5 = (bf16[256,512]{1,0:T(8,128)(2,1)S(1)}, bf16[256,512]{1,0:T(8,128)(2,1)S(1)}, bf16[256,512]{1,0:T(8,128)(2,1)S(1)}, bf16[256,512]{1,0:T(8,128)(2,1)S(1)}) custom-call(bf16[512,2048]{1,0:T(8,128)(2,1)S(1)} %attend.3.refs_0_.refs_5_, bf16[2048,512]{1,0:T(8,128)(2,1)S(1)} %get-tuple-element.50.refs_1_, ...), custom_call_target="tpu_custom_call" | custom-call | bytes 1024 | tf_op jit(solution)/shard_map/give/pallas_call | solution.py:135
  45.6 0.5 collective-permute-done.5.refs_6_
  46.1 0.4 collective-permute-done.6.refs_7_
  46.5 0.4 collective-permute-done.7.refs_8_
  47.2 1.5 %collective-permute-done.8.refs_10_.refs_8_ = bf16[256,1536]{1,0:T(8,128)(2,1)S(1)} collective-permute-done((bf16[256,1536]{1,0:T(8,128)(2,1)S(1)}, bf16[256,1536]{1,0:T(8,128)(2,1)S(1)}, u32[]{:S(2)}, u32[]{:S(2)}) %collective-permute-start.8) | collective-permute-done | bytes 786464 | tf_op jit(solution)/shard_map/ppermute | solution.py:619
  48.7 3.6 %keep.5.refs_7_ = bf16[256,2048]{1,0:T(8,128)(2,1)S(1)} custom-call(bf16[512,2048]{1,0:T(8,128)(2,1)S(1)} %attend.3.refs_0_.refs_5_, bf16[2048,512]{1,0:T(8,128)(2,1)S(1)} %get-tuple-element.57.refs_1_, bf16[2048,512]{1,0:T(8,128)(2,1)S(1)} %get-tuple-element.58.refs_2_, bf16[2048,512]{1,0:T(8,128)(2,1)S(1)} %get-tuple-element.59.refs_3_, ...), custom_call_target="tpu_custom_call" | custom-call | bytes 1024 | tf_op jit(solution)/shard_map/keep/pallas_call | solution.py:135
  52.4 1.6 %collective-permute-start.15 = (bf16[256,2048]{1,0:T(8,128)(2,1)S(1)}, bf16[256,2048]{1,0:T(8,128)(2,1)}, u32[]{:S(2)}, u32[]{:S(2)}) collective-permute-start(bf16[256,2048]{1,0:T(8,128)(2,1)S(1)} %keep.5.refs_7_), channel_id=1, source_target_pairs={{0,2},{1,3},{2,0},{3,1},{4,6},{5,7},{6,4},{7,5},{8,10},{9,11},{10,... | collective-permute-start | bytes 3145736 | tf_op jit(solution)/shard_map/ppermute | solution.py:619
  53.9 0.5 collective-permute-start.9
  54.4 27.9 %collective-permute-done.9.refs_8_.refs_9_ = bf16[256,512]{1,0:T(8,128)(2,1)S(1)} collective-permute-done((bf16[256,512]{1,0:T(8,128)(2,1)S(1)}, bf16[256,512]{1,0:T(8,128)(2,1)S(1)}, u32[]{:S(2)}, u32[]{:S(2)}) %collective-permute-start.9) | collective-permute-done | bytes 262176 | tf_op jit(solution)/shard_map/ppermute | solution.py:619
  82.4 7.2 %settle.1 = (bf16[512,2048]{1,0:T(8,128)(2,1)S(1)}, bf16[16,2048]{1,0:T(8,128)(2,1)S(1)}, bf16[1,3,2,512,256]{4,3,2,1,0:T(8,128)(2,1)}, bf16[2048,512]{1,0:T(8,1...) custom-call(s32[8]{0:T(128)} %refs_0_.3, ...), custom_call_target="tpu_custom_call", output_to_operand_aliasing={{0}: (5, {})} | custom-call | bytes 1024 | tf_op jit(solution)/shard_map/settle/pallas_call | solution.py:135
  89.6 2.3 %give_last.1 = (bf16[16,2048]{1,0:T(8,128)(2,1)S(1)}, bf16[2048,512]{1,0:T(8,128)(2,1)S(1)}, bf16[2048,512]{1,0:T(8,128)(2,1)S(1)}) custom-call(bf16[16,2048]{1,0:T(8,128)(2,1)S(1)} %get-tuple-element.68.refs_0_, bf16[2048,512]{1,0:T(8,128)(2,1)S(1)} %get-tuple-element.70.refs_1_, bf16[2048,512]{1,0:T(8,128)(2,1)S(1)} %get-tuple-element.71.refs_2_, ...), custom_call_target="tpu_custom_call" | custom-call | bytes 1024 | tf_op jit(solution)/shard_map/give_last/pallas_call | solution.py:135
  92.0 2.9 %give_own.2 = (bf16[512,512]{1,0:T(8,128)(2,1)S(1)}, bf16[512,512]{1,0:T(8,128)(2,1)S(1)}, bf16[2048,512]{1,0:T(8,128)(2,1)S(1)}, bf16[2048,512]{1,0:T(8,128)(2,1)S(1)}, bf16[2048,512]{1,0:T(8,128)(2,1)S(1)}) custom-call(bf16[512,2048]{1,0:T(8,128)(2,1)S(1)} %get-tuple-element.67.refs_0_, bf16[2048,512]{1,0:T(8,128)(2,1)S(1)} %get-tuple-element.74.refs_1_, ...), custom_call_target="tpu_custom_call" | custom-call | bytes 1024 | tf_op jit(solution)/shard_map/give_own/pallas_call | solution.py:135
  94.9 0.5 collective-permute-start.12
  95.6 2.3 %keep_last.1 = (bf16[16,2048]{1,0:T(8,128)(2,1)S(1)}, bf16[2048,512]{1,0:T(8,128)(2,1)S(1)}, bf16[2048,512]{1,0:T(8,128)(2,1)S(1)}) custom-call(bf16[16,2048]{1,0:T(8,128)(2,1)S(1)} %get-tuple-element.68.refs_0_, bf16[2048,512]{1,0:T(8,128)(2,1)S(1)} %get-tuple-element.69.refs_1_, bf16[2048,512]{1,0:T(8,128)(2,1)S(1)} %get-tuple-element.77.refs_2_, ...), custom_call_target="tpu_custom_call" | custom-call | bytes 1024 | tf_op jit(solution)/shard_map/keep_last/pallas_call | solution.py:135
  97.8 3.1 %give_own.3 = (bf16[512,512]{1,0:T(8,128)(2,1)S(1)}, bf16[512,512]{1,0:T(8,128)(2,1)S(1)}, bf16[2048,512]{1,0:T(8,128)(2,1)S(1)}, bf16[2048,512]{1,0:T(8,128)(2,1)S(1)}, bf16[2048,512]{1,0:T(8,128)(2,1)S(1)}) custom-call(bf16[512,2048]{1,0:T(8,128)(2,1)S(1)} %get-tuple-element.67.refs_0_, bf16[2048,512]{1,0:T(8,128)(2,1)S(1)} %get-tuple-element.81.refs_1_, ...), custom_call_target="tpu_custom_call" | custom-call | bytes 1024 | tf_op jit(solution)/shard_map/give_own/pallas_call | solution.py:135
  101.0 0.5 collective-permute-start.14
  101.5 1.5 %collective-permute-start.16 = (bf16[16,2048]{1,0:T(8,128)(2,1)S(1)}, bf16[16,2048]{1,0:T(8,128)(2,1)S(1)}, u32[]{:S(2)}, u32[]{:S(2)}) collective-permute-start(bf16[16,2048]{1,0:T(8,128)(2,1)S(1)} %get-tuple-element.83.refs_4_), channel_id=1, source_target_pairs={{0,2},{1,3},{2,0},{3,1},{4,6},{5,7},{6,4},{7,5},{8,10},{9,11},{10,... | collective-permute-start | bytes 196616 | tf_op jit(solution)/shard_map/ppermute | solution.py:619
  103.1 2.9 %collective-permute-done.16.refs_11_ = bf16[16,2048]{1,0:T(8,128)(2,1)S(1)} collective-permute-done((bf16[16,2048]{1,0:T(8,128)(2,1)S(1)}, bf16[16,2048]{1,0:T(8,128)(2,1)S(1)}, u32[]{:S(2)}, u32[]{:S(2)}) %collective-permute-start.16) | collective-permute-done | bytes 65568 | tf_op jit(solution)/shard_map/ppermute | solution.py:619
  106.0 8.4 %final.1 = bf16[2048,512]{1,0:T(8,128)(2,1)} custom-call(bf16[512,2048]{1,0:T(8,128)(2,1)S(1)} %get-tuple-element.67.refs_0_, bf16[2048,512]{1,0:T(8,128)(2,1)S(1)} %get-tuple-element.84.refs_1_, bf16[2048,512]{1,0:T(8,128)(2,1)S(1)} %get-tuple-element.85.refs_2_, bf16[2048,512]{1,0:T(8,128)(2,1)S(1)} %get-tuple-element.86.refs_3_, ...), custom_call_target="tpu_custom_call" | custom-call | bytes 1024 | tf_op jit(solution)/shard_map/final/pallas_call | solution.py:135
  (25 shorter events, 1.9 us)
Async XLA Ops:
  4.3 78.1 %all-to-all-start = ((bf16[4,2,32,16,256]{4,3,2,1,0:T(8,128)(2,1)}), bf16[4,2,32,16,256]{4,3,2,1,0:T(8,128)(2,1)}, u32[]{:S(2)}, u32[]{:S(2)}) async-start(bf16[4,2,32,16,256]{4,3,2,1,0:T(8,128)(2,1)} %get-tuple-element.46.refs_6_), calls=%async_computation | async-start | bytes 4194304 | tf_op jit(solution)/shard_map/all_to_all | solution.py:666
  10.6 1.6 %copy-start = (bf16[4,2,32,16,256]{4,3,2,1,0:T(8,128)(2,1)S(1)}, bf16[4,2,32,16,256]{4,3,2,1,0:T(8,128)(2,1)}, u32[]{:S(2)}) copy-start(bf16[4,2,32,16,256]{4,3,2,1,0:T(8,128)(2,1)} %get-tuple-element.46.refs_6_) | copy-start | bytes 6291460
  22.4 2.5 %collective-permute-start.2 = (bf16[256,512]{1,0:T(8,128)(2,1)S(1)}, bf16[256,512]{1,0:T(8,128)(2,1)S(1)}, u32[]{:S(2)}, u32[]{:S(2)}) collective-permute-start(bf16[256,512]{1,0:T(8,128)(2,1)S(1)} %get-tuple-element.60), channel_id=1, source_target_pairs={{0,1},{1,0},{2,3},{3,2},{4,5},{5,4},{6,7},{7,6},{8,9},{9,8},{10,11... | collective-permute-start | bytes 786440 | tf_op jit(solution)/shard_map/ppermute | solution.py:615
  22.4 2.5 %collective-permute-start.1 = (bf16[256,512]{1,0:T(8,128)(2,1)S(1)}, bf16[256,512]{1,0:T(8,128)(2,1)S(1)}, u32[]{:S(2)}, u32[]{:S(2)}) collective-permute-start(bf16[256,512]{1,0:T(8,128)(2,1)S(1)} %get-tuple-element.55.refs_3_), channel_id=1, source_target_pairs={{0,1},{1,0},{2,3},{3,2},{4,5},{5,4},{6,7},{7,6},{8,9},{9,8},{10,11... | collective-permute-start | bytes 786440 | tf_op jit(solution)/shard_map/ppermute | solution.py:615
  24.8 1.6 %collective-permute-start.3 = (bf16[256,512]{1,0:T(8,128)(2,1)S(1)}, bf16[256,512]{1,0:T(8,128)(2,1)S(1)}, u32[]{:S(2)}, u32[]{:S(2)}) collective-permute-start(bf16[256,512]{1,0:T(8,128)(2,1)S(1)} %get-tuple-element.61.refs_7_), channel_id=1, source_target_pairs={{0,1},{1,0},{2,3},{3,2},{4,5},{5,4},{6,7},{7,6},{8,9},{9,8},{10,11... | collective-permute-start | bytes 786440 | tf_op jit(solution)/shard_map/ppermute | solution.py:615
  29.1 19.6 %collective-permute-start.8 = (bf16[256,1536]{1,0:T(8,128)(2,1)S(1)}, bf16[256,1536]{1,0:T(8,128)(2,1)S(1)}, u32[]{:S(2)}, u32[]{:S(2)}) collective-permute-start(bf16[256,1536]{1,0:T(8,128)(2,1)S(1)} %keep.3.refs_3_), channel_id=1, source_target_pairs={{0,2},{1,3},{2,0},{3,1},{4,6},{5,7},{6,4},{7,5},{8,10},{9,11},{10,... | collective-permute-start | bytes 2359304 | tf_op jit(solution)/shard_map/ppermute | solution.py:619
  30.7 1.5 %collective-permute-start = (bf16[256,512]{1,0:T(8,128)(2,1)S(1)}, bf16[256,512]{1,0:T(8,128)(2,1)S(1)}, u32[]{:S(2)}, u32[]{:S(2)}) collective-permute-start(bf16[256,512]{1,0:T(8,128)(2,1)S(1)} %get-tuple-element.56), channel_id=1, source_target_pairs={{0,1},{1,0},{2,3},{3,2},{4,5},{5,4},{6,7},{7,6},{8,9},{9,8},{10,11... | collective-permute-start | bytes 786440 | tf_op jit(solution)/shard_map/ppermute | solution.py:615
  44.5 1.6 %collective-permute-start.5 = (bf16[256,512]{1,0:T(8,128)(2,1)S(1)}, bf16[256,512]{1,0:T(8,128)(2,1)S(1)}, u32[]{:S(2)}, u32[]{:S(2)}) collective-permute-start(bf16[256,512]{1,0:T(8,128)(2,1)S(1)} %get-tuple-element.63), channel_id=1, source_target_pairs={{0,1},{1,0},{2,3},{3,2},{4,5},{5,4},{6,7},{7,6},{8,9},{9,8},{10,11... | collective-permute-start | bytes 786440 | tf_op jit(solution)/shard_map/ppermute | solution.py:615
  44.7 1.8 %collective-permute-start.6 = (bf16[256,512]{1,0:T(8,128)(2,1)S(1)}, bf16[256,512]{1,0:T(8,128)(2,1)S(1)}, u32[]{:S(2)}, u32[]{:S(2)}) collective-permute-start(bf16[256,512]{1,0:T(8,128)(2,1)S(1)} %get-tuple-element.64), channel_id=1, source_target_pairs={{0,1},{1,0},{2,3},{3,2},{4,5},{5,4},{6,7},{7,6},{8,9},{9,8},{10,11... | collective-permute-start | bytes 786440 | tf_op jit(solution)/shard_map/ppermute | solution.py:615
  45.1 1.8 %collective-permute-start.7 = (bf16[256,512]{1,0:T(8,128)(2,1)S(1)}, bf16[256,512]{1,0:T(8,128)(2,1)S(1)}, u32[]{:S(2)}, u32[]{:S(2)}) collective-permute-start(bf16[256,512]{1,0:T(8,128)(2,1)S(1)} %get-tuple-element.65), channel_id=1, source_target_pairs={{0,1},{1,0},{2,3},{3,2},{4,5},{5,4},{6,7},{7,6},{8,9},{9,8},{10,11... | collective-permute-start | bytes 786440 | tf_op jit(solution)/shard_map/ppermute | solution.py:615
  45.2 2.0 %collective-permute-start.4 = (bf16[256,512]{1,0:T(8,128)(2,1)S(1)}, bf16[256,512]{1,0:T(8,128)(2,1)S(1)}, u32[]{:S(2)}, u32[]{:S(2)}) collective-permute-start(bf16[256,512]{1,0:T(8,128)(2,1)S(1)} %get-tuple-element.62.refs_9_), channel_id=1, source_target_pairs={{0,1},{1,0},{2,3},{3,2},{4,5},{5,4},{6,7},{7,6},{8,9},{9,8},{10,11... | collective-permute-start | bytes 786440 | tf_op jit(solution)/shard_map/ppermute | solution.py:615
  48.7 3.6 %copy-start.1 = (bf16[256,1536]{1,0:T(8,128)(2,1)}, bf16[256,1536]{1,0:T(8,128)(2,1)S(1)}, u32[]{:S(2)}) copy-start(bf16[256,1536]{1,0:T(8,128)(2,1)S(1)} %collective-permute-done.8.refs_10_.refs_8_) | copy-start | bytes 2359300
  52.4 49.2 %collective-permute-start.15 = (bf16[256,2048]{1,0:T(8,128)(2,1)S(1)}, bf16[256,2048]{1,0:T(8,128)(2,1)}, u32[]{:S(2)}, u32[]{:S(2)}) collective-permute-start(bf16[256,2048]{1,0:T(8,128)(2,1)S(1)} %keep.5.refs_7_), channel_id=1, source_target_pairs={{0,2},{1,3},{2,0},{3,1},{4,6},{5,7},{6,4},{7,5},{8,10},{9,11},{10,... | collective-permute-start | bytes 3145736 | tf_op jit(solution)/shard_map/ppermute | solution.py:619
  53.9 28.4 %collective-permute-start.9 = (bf16[256,512]{1,0:T(8,128)(2,1)S(1)}, bf16[256,512]{1,0:T(8,128)(2,1)S(1)}, u32[]{:S(2)}, u32[]{:S(2)}) collective-permute-start(bf16[256,512]{1,0:T(8,128)(2,1)S(1)} %keep.4.refs_6_), channel_id=1, source_target_pairs={{0,2},{1,3},{2,0},{3,1},{4,6},{5,7},{6,4},{7,5},{8,10},{9,11},{10,... | collective-permute-start | bytes 786440 | tf_op jit(solution)/shard_map/ppermute | solution.py:619
  91.9 3.7 %collective-permute-start.10 = (bf16[16,2048]{1,0:T(8,128)(2,1)S(1)}, bf16[16,2048]{1,0:T(8,128)(2,1)S(1)}, u32[]{:S(2)}, u32[]{:S(2)}) collective-permute-start(bf16[16,2048]{1,0:T(8,128)(2,1)S(1)} %get-tuple-element.76.refs_4_), channel_id=1, source_target_pairs={{0,1},{1,0},{2,3},{3,2},{4,5},{5,4},{6,7},{7,6},{8,9},{9,8},{10,11... | collective-permute-start | bytes 196616 | tf_op jit(solution)/shard_map/ppermute | solution.py:615
  94.9 11.1 %collective-permute-start.12 = (bf16[512,512]{1,0:T(8,128)(2,1)S(1)}, bf16[512,512]{1,0:T(8,128)(2,1)S(1)}, u32[]{:S(2)}, u32[]{:S(2)}) collective-permute-start(bf16[512,512]{1,0:T(8,128)(2,1)S(1)} %get-tuple-element.87), channel_id=1, source_target_pairs={{0,1},{1,0},{2,3},{3,2},{4,5},{5,4},{6,7},{7,6},{8,9},{9,8},{10,11... | collective-permute-start | bytes 1572872 | tf_op jit(solution)/shard_map/ppermute | solution.py:615
  95.5 10.5 %collective-permute-start.11 = (bf16[512,512]{1,0:T(8,128)(2,1)S(1)}, bf16[512,512]{1,0:T(8,128)(2,1)S(1)}, u32[]{:S(2)}, u32[]{:S(2)}) collective-permute-start(bf16[512,512]{1,0:T(8,128)(2,1)S(1)} %get-tuple-element.80.refs_7_), channel_id=1, source_target_pairs={{0,1},{1,0},{2,3},{3,2},{4,5},{5,4},{6,7},{7,6},{8,9},{9,8},{10,11... | collective-permute-start | bytes 1572872 | tf_op jit(solution)/shard_map/ppermute | solution.py:615
  97.8 8.2 %copy-start.2 = (bf16[256,1536]{1,0:T(8,128)(2,1)S(1)}, bf16[256,1536]{1,0:T(8,128)(2,1)}, u32[]{:S(2)}) copy-start(bf16[256,1536]{1,0:T(8,128)(2,1)} %copy-done.1) | copy-start | bytes 2359300
  101.0 5.0 %collective-permute-start.14 = (bf16[512,512]{1,0:T(8,128)(2,1)S(1)}, bf16[512,512]{1,0:T(8,128)(2,1)S(1)}, u32[]{:S(2)}, u32[]{:S(2)}) collective-permute-start(bf16[512,512]{1,0:T(8,128)(2,1)S(1)} %get-tuple-element.89), channel_id=1, source_target_pairs={{0,1},{1,0},{2,3},{3,2},{4,5},{5,4},{6,7},{7,6},{8,9},{9,8},{10,11... | collective-permute-start | bytes 1572872 | tf_op jit(solution)/shard_map/ppermute | solution.py:615
  101.5 4.5 %collective-permute-start.13 = (bf16[512,512]{1,0:T(8,128)(2,1)S(1)}, bf16[512,512]{1,0:T(8,128)(2,1)S(1)}, u32[]{:S(2)}, u32[]{:S(2)}) collective-permute-start(bf16[512,512]{1,0:T(8,128)(2,1)S(1)} %get-tuple-element.88.refs_13_), channel_id=1, source_target_pairs={{0,1},{1,0},{2,3},{3,2},{4,5},{5,4},{6,7},{7,6},{8,9},{9,8},{10,11... | collective-permute-start | bytes 1572872 | tf_op jit(solution)/shard_map/ppermute | solution.py:615
  101.5 4.4 %collective-permute-start.16 = (bf16[16,2048]{1,0:T(8,128)(2,1)S(1)}, bf16[16,2048]{1,0:T(8,128)(2,1)S(1)}, u32[]{:S(2)}, u32[]{:S(2)}) collective-permute-start(bf16[16,2048]{1,0:T(8,128)(2,1)S(1)} %get-tuple-element.83.refs_4_), channel_id=1, source_target_pairs={{0,2},{1,3},{2,0},{3,1},{4,6},{5,7},{6,4},{7,5},{8,10},{9,11},{10,... | collective-permute-start | bytes 196616 | tf_op jit(solution)/shard_map/ppermute | solution.py:619

commit v12 on v11

--- a/solution.py
+++ b/solution.py
@@ -539,12 +539,13 @@
             start = pl.multiple_of(j * tile, tile)
             at = pl.ds(start, tile)
             whole = pl.ds(n * z.quarter + start, tile)
+            half = pl.ds((n % 2) * z.quarter + start, tile)
             sums = dot(attention[...], weight[:, at]) + extra[n][:, at].astype(jnp.float32)
             for k in range(fars):
                 rows = late[k].shape[0]
                 arrived = jnp.concatenate(
                     [
-                        low[k][:, whole] if n < 3 else high[k][:, at],
+                        (low if n < 2 else high)[k][:, half],
                         second[k][:-rows, whole],
                         late[k][:, whole],
                     ],
@@ -675,10 +676,9 @@
     a = (rows, 0, tokens)
     given, mates_low = give(a, far, low, "give", [], keeps(far, high))
     given, mates_high = give(a, far, high, "give", [given])
-    mates = [mates_low[2 * n : 2 * n + 2] + mates_high[2 * n : 2 * n + 2] for n in range(chips - 1)]
-    kept = keep(a, far, (0, 1, 2), sum((m[:3] for m in mates), []), "keep", [given])
+    kept = keep(a, far, low, mates_low, "keep", [given])
     got_low = sent(kept)
-    kept = keep(a, far, (3,), sum((m[3:] for m in mates), []), "keep", kept[-1:])
+    kept = keep(a, far, high, mates_high, "keep", kept[-1:])
     got_high = sent(kept)
     rows, _ = attend(
         table, res_len, query_rows, new_kv, res_pool, rows, half, half, z, kept[-1:],

time: 115 us -> 93.5 us (0.81)
  waiting for transfers between devices: 37 us -> 14.6 us
  local copies, waits for them, and re-layouts: 1.63 us -> 3.47 us
    ppermute x4, waiting for transfers between devices: 32.3 us -> 13.4 us  [across(): return lax.ppermute(x, 'tp', [(i, (i + shift) % tps) for i in range(tps)])]
    ppermute x13, waiting for transfers between devices: 4.65 us -> 1.15 us  [mate_of(): return lax.ppermute(x, 'tp', to_mate)]
    unnamed x6 -> x12, local copies, waits for them, and re-layouts: 1.63 us -> 3.47 us
    ppermute x4, starting transfers between devices: 5.19 us -> 3.69 us  [across(): return lax.ppermute(x, 'tp', [(i, (i + shift) % tps) for i in range(tps)])]
  transfers between devices with their start and end apart: 18 -> 18, of which waited for: 9 -> 6; matrix products, arithmetic and copies ran while one was open for 0% -> 0% of each run, Pallas kernels for 42% -> 52%
where the time goes in v12:
time: 93.5 us; the launch traced here: 92.9 us
  Pallas kernels  60.4 us (65%)
  waiting for transfers between devices  14.6 us (16%)
  starting transfers between devices  13.5 us (14%)
  local copies, waits for them, and re-layouts  3.47 us (4%)
  between operations  1 us (1%)
    pallas_call x15, Pallas kernels, run(): pl.pallas_call(call, grid_spec=pltpu.PrefetchScalarGridSpec(num_scalar_pr...  60.4 us
    ppermute x4, waiting for transfers between devices, across(): return lax.ppermute(x, 'tp', [(i, (i + shift) % tps) for i in range(tps)])  13.4 us
    all_to_all x1, starting transfers between devices, shards(): lax.all_to_all(sends, 'inst', split_axis=0, concat_axis=0, tiled=True)  6.33 us
    ppermute x4, starting transfers between devices, across(): return lax.ppermute(x, 'tp', [(i, (i + shift) % tps) for i in range(tps)])  3.69 us
    ppermute x13, starting transfers between devices, mate_of(): return lax.ppermute(x, 'tp', to_mate)  3.48 us
    unnamed x12, local copies, waits for them, and re-layouts  3.47 us
  transfers between devices with their start and end apart: 18, of which 6 were waited for; matrix products, arithmetic and copies ran while one was open for 0% of the time, Pallas kernels for 52%

profile of v12, /device:TPU:0, one launch (start us, length us, event | category | flops | bytes accessed | tf_op | source)
XLA Modules:
  0.0 92.9 jit_solution(2582847048176407385)
XLA Ops:
  0.6 3.6 %pack.1 = (bf16[4,2,32,16,256]{4,3,2,1,0:T(8,128)(2,1)}, bf16[256,128]{1,0:T(8,128)(2,1)}, bf16[32,256]{1,0:T(8,128)(2,1)}) custom-call(s32[1,2,32]{2,1,0:T(2,128)} %refs_0_.2, s32[8]{0:T(128)} %refs_0_.3, bf16[1,2,64,16,256]{4,3,2,1,0:T(8,128)(2,1)} %refs_2_.1, bf16[8192,128]{1,0:T(8,128)(2,1)} %bitcast.4, bf16[128,4,2,256]{3,2,1,0:T(2,128)(2,1)} %refs_3_.7), custom_call_target="tpu_custom_call" | custom-call | bytes 1024 | tf_op jit(solution)/shard_map/pack/pallas_call | solution.py:135
  4.3 6.3 %all-to-all-start = ((bf16[4,2,32,16,256]{4,3,2,1,0:T(8,128)(2,1)}), bf16[4,2,32,16,256]{4,3,2,1,0:T(8,128)(2,1)}, u32[]{:S(2)}, u32[]{:S(2)}) async-start(bf16[4,2,32,16,256]{4,3,2,1,0:T(8,128)(2,1)} %get-tuple-element.46.refs_6_), calls=%async_computation | async-start | bytes 4194304 | tf_op jit(solution)/shard_map/all_to_all | solution.py:667
  10.6 1.6 %copy-done = bf16[4,2,32,16,256]{4,3,2,1,0:T(8,128)(2,1)S(1)} copy-done((bf16[4,2,32,16,256]{4,3,2,1,0:T(8,128)(2,1)S(1)}, bf16[4,2,32,16,256]{4,3,2,1,0:T(8,128)(2,1)}, u32[]{:S(2)}) %copy-start) | copy-done | bytes 2097176
  12.2 7.8 %attend.2 = (bf16[512,2048]{1,0:T(8,128)(2,1)S(1)}, bf16[2048,512]{1,0:T(8,128)(2,1)S(1)}, bf16[2048,512]{1,0:T(8,128)(2,1)S(1)}, bf16[2048,512]{1,0:T(8,128)(2,...) custom-call(s32[8,125]{1,0:T(8,128)} %bitcast.7, ...), custom_call_target="tpu_custom_call" | custom-call | bytes 1024 | tf_op jit(solution)/shard_map/attend/pallas_call | solution.py:135
  20.1 2.3 %give.3 = (bf16[256,512]{1,0:T(8,128)(2,1)S(1)}, bf16[256,512]{1,0:T(8,128)(2,1)S(1)}, bf16[2048,512]{1,0:T(8,128)(2,1)S(1)}, bf16[2048,512]{1,0:T(8,128)(2,1)S(1)}) custom-call(bf16[512,2048]{1,0:T(8,128)(2,1)S(1)} %get-tuple-element.49.refs_0_.refs_5_, bf16[2048,512]{1,0:T(8,128)(2,1)S(1)} %get-tuple-element.50.refs_1_, ...), custom_call_target="tpu_custom_call" | custom-call | bytes 1024 | tf_op jit(solution)/shard_map/give/pallas_call | solution.py:135
  22.4 0.5 collective-permute-start.2
  22.9 1.8 %give.4 = (bf16[256,512]{1,0:T(8,128)(2,1)S(1)}, bf16[256,512]{1,0:T(8,128)(2,1)S(1)}) custom-call(bf16[512,2048]{1,0:T(8,128)(2,1)S(1)} %get-tuple-element.49.refs_0_.refs_5_, bf16[2048,512]{1,0:T(8,128)(2,1)S(1)} %get-tuple-element.54.refs_1_.refs_3_, bf16[2048,512]{1,0:T(8,128)(2,1)S(1)} %get-tuple-element.55.refs_2_.refs_4_, ...), custom_call_target="tpu_custom_call" | custom-call | bytes 1024 | tf_op jit(solution)/shard_map/give/pallas_call | solution.py:135
  24.9 0.4 collective-permute-start
  25.3 1.8 %keep.3.refs_5_ = bf16[256,1024]{1,0:T(8,128)(2,1)S(1)} custom-call(bf16[512,2048]{1,0:T(8,128)(2,1)S(1)} %get-tuple-element.49.refs_0_.refs_5_, bf16[2048,512]{1,0:T(8,128)(2,1)S(1)} %get-tuple-element.59.refs_1_, bf16[2048,512]{1,0:T(8,128)(2,1)S(1)} %get-tuple-element.60.refs_2_, bf16[256,512]{1,0:T(8,128)(2,1)S(1)} %collective-permute-done.2.refs_3_, ...), custom_call_target="tpu_custom_call" | custom-call | bytes 1024 | tf_op jit(solution)/shard_map/keep/pallas_call | solution.py:135
  27.1 1.6 %collective-permute-start.8 = (bf16[256,1024]{1,0:T(8,128)(2,1)S(1)}, bf16[256,1024]{1,0:T(8,128)(2,1)S(1)}, u32[]{:S(2)}, u32[]{:S(2)}) collective-permute-start(bf16[256,1024]{1,0:T(8,128)(2,1)S(1)} %keep.3.refs_5_), channel_id=1, source_target_pairs={{0,2},{1,3},{2,0},{3,1},{4,6},{5,7},{6,4},{7,5},{8,10},{9,11},{10,... | collective-permute-start | bytes 1572872 | tf_op jit(solution)/shard_map/ppermute | solution.py:620
  28.7 1.8 %keep.4.refs_6_ = bf16[256,1024]{1,0:T(8,128)(2,1)S(1)} custom-call(bf16[512,2048]{1,0:T(8,128)(2,1)S(1)} %get-tuple-element.49.refs_0_.refs_5_, bf16[2048,512]{1,0:T(8,128)(2,1)S(1)} %get-tuple-element.52.refs_1_.refs_3_, bf16[2048,512]{1,0:T(8,128)(2,1)S(1)} %get-tuple-element.53.refs_2_.refs_4_, bf16[256,512]{1,0:T(8,128)(2,1)S(1)} %collective-permute-done.refs_3_, ...), custom_call_target="tpu_custom_call" | custom-call | bytes 1024 | tf_op jit(solution)/shard_map/keep/pallas_call | solution.py:135
  30.5 7.7 %attend.3.refs_0_.refs_5_ = bf16[512,2048]{1,0:T(8,128)(2,1)S(1)} custom-call(s32[8,125]{1,0:T(8,128)} %bitcast.8, s32[1,125]{1,0:T(1,128)} %refs_1_.6, bf16[8192,128]{1,0:T(8,128)(2,1)} %bitcast.6, bf16[128,4,2,256]{3,2,1,0:T(2,128)(2,1)} %refs_3_.7, bf16[1,2,64,16,256]{4,3,2,1,0:T(8,128)(2,1)} %refs_4_.5, ...), custom_call_target="tpu_custom_call", output_to_operand_aliasing={{}: (5, {})} | custom-call | bytes 1024 | tf_op jit(solution)/shard_map/attend/pallas_call | solution.py:135
  38.3 3.6 %give.5 = (bf16[256,512]{1,0:T(8,128)(2,1)S(1)}, bf16[256,512]{1,0:T(8,128)(2,1)S(1)}, bf16[256,512]{1,0:T(8,128)(2,1)S(1)}, bf16[256,512]{1,0:T(8,128)(2,1)S(1)}) custom-call(bf16[512,2048]{1,0:T(8,128)(2,1)S(1)} %attend.3.refs_0_.refs_5_, bf16[2048,512]{1,0:T(8,128)(2,1)S(1)} %get-tuple-element.50.refs_1_, ...), custom_call_target="tpu_custom_call" | custom-call | bytes 1024 | tf_op jit(solution)/shard_map/give/pallas_call | solution.py:135
  42.0 0.5 collective-permute-start.6
  43.0 0.5 collective-permute-done.5.refs_6_
  43.5 0.5 collective-permute-start.9
  44.6 3.6 %keep.5.refs_7_ = bf16[256,2048]{1,0:T(8,128)(2,1)S(1)} custom-call(bf16[512,2048]{1,0:T(8,128)(2,1)S(1)} %attend.3.refs_0_.refs_5_, bf16[2048,512]{1,0:T(8,128)(2,1)S(1)} %get-tuple-element.59.refs_1_, bf16[2048,512]{1,0:T(8,128)(2,1)S(1)} %get-tuple-element.60.refs_2_, bf16[2048,512]{1,0:T(8,128)(2,1)S(1)} %get-tuple-element.52.refs_1_.refs_3_, ...), custom_call_target="tpu_custom_call" | custom-call | bytes 1024 | tf_op jit(solution)/shard_map/keep/pallas_call | solution.py:135
  48.3 1.0 %collective-permute-start.15 = (bf16[256,2048]{1,0:T(8,128)(2,1)S(1)}, bf16[256,2048]{1,0:T(8,128)(2,1)}, u32[]{:S(2)}, u32[]{:S(2)}) collective-permute-start(bf16[256,2048]{1,0:T(8,128)(2,1)S(1)} %keep.5.refs_7_), channel_id=1, source_target_pairs={{0,2},{1,3},{2,0},{3,1},{4,6},{5,7},{6,4},{7,5},{8,10},{9,11},{10,... | collective-permute-start | bytes 3145736 | tf_op jit(solution)/shard_map/ppermute | solution.py:620
  49.3 9.0 %collective-permute-done.9.refs_8_.refs_9_ = bf16[256,1024]{1,0:T(8,128)(2,1)S(1)} collective-permute-done((bf16[256,1024]{1,0:T(8,128)(2,1)S(1)}, bf16[256,1024]{1,0:T(8,128)(2,1)S(1)}, u32[]{:S(2)}, u32[]{:S(2)}) %collective-permute-start.9) | collective-permute-done | bytes 524320 | tf_op jit(solution)/shard_map/ppermute | solution.py:620
  58.3 0.8 copy-done.1
  59.1 1.0 %copy-done.2 = bf16[256,1024]{1,0:T(8,128)(2,1)S(1)} copy-done((bf16[256,1024]{1,0:T(8,128)(2,1)S(1)}, bf16[256,1024]{1,0:T(8,128)(2,1)}, u32[]{:S(2)}) %copy-start.2) | copy-done | bytes 524312
  60.1 7.2 %settle.1 = (bf16[512,2048]{1,0:T(8,128)(2,1)S(1)}, bf16[16,2048]{1,0:T(8,128)(2,1)S(1)}, bf16[1,3,2,512,256]{4,3,2,1,0:T(8,128)(2,1)}, bf16[2048,512]{1,0:T(8,1...) custom-call(s32[8]{0:T(128)} %refs_0_.3, ...), custom_call_target="tpu_custom_call", output_to_operand_aliasing={{0}: (5, {})} | custom-call | bytes 1024 | tf_op jit(solution)/shard_map/settle/pallas_call | solution.py:135
  67.3 2.3 %give_last.1 = (bf16[16,2048]{1,0:T(8,128)(2,1)S(1)}, bf16[2048,512]{1,0:T(8,128)(2,1)S(1)}, bf16[2048,512]{1,0:T(8,128)(2,1)S(1)}) custom-call(bf16[16,2048]{1,0:T(8,128)(2,1)S(1)} %get-tuple-element.68.refs_0_, bf16[2048,512]{1,0:T(8,128)(2,1)S(1)} %get-tuple-element.70.refs_1_, bf16[2048,512]{1,0:T(8,128)(2,1)S(1)} %get-tuple-element.71.refs_2_, ...), custom_call_target="tpu_custom_call" | custom-call | bytes 1024 | tf_op jit(solution)/shard_map/give_last/pallas_call | solution.py:135
  69.7 3.0 %give_own.2 = (bf16[512,512]{1,0:T(8,128)(2,1)S(1)}, bf16[512,512]{1,0:T(8,128)(2,1)S(1)}, bf16[2048,512]{1,0:T(8,128)(2,1)S(1)}, bf16[2048,512]{1,0:T(8,128)(2,1)S(1)}, bf16[2048,512]{1,0:T(8,128)(2,1)S(1)}) custom-call(bf16[512,2048]{1,0:T(8,128)(2,1)S(1)} %get-tuple-element.67.refs_0_, bf16[2048,512]{1,0:T(8,128)(2,1)S(1)} %get-tuple-element.74.refs_1_, ...), custom_call_target="tpu_custom_call" | custom-call | bytes 1024 | tf_op jit(solution)/shard_map/give_own/pallas_call | solution.py:135
  72.7 0.5 collective-permute-start.12
  73.3 2.3 %keep_last.1 = (bf16[16,2048]{1,0:T(8,128)(2,1)S(1)}, bf16[2048,512]{1,0:T(8,128)(2,1)S(1)}, bf16[2048,512]{1,0:T(8,128)(2,1)S(1)}) custom-call(bf16[16,2048]{1,0:T(8,128)(2,1)S(1)} %get-tuple-element.68.refs_0_, bf16[2048,512]{1,0:T(8,128)(2,1)S(1)} %get-tuple-element.69.refs_1_, bf16[2048,512]{1,0:T(8,128)(2,1)S(1)} %get-tuple-element.77.refs_2_, ...), custom_call_target="tpu_custom_call" | custom-call | bytes 1024 | tf_op jit(solution)/shard_map/keep_last/pallas_call | solution.py:135
  75.6 3.1 %give_own.3 = (bf16[512,512]{1,0:T(8,128)(2,1)S(1)}, bf16[512,512]{1,0:T(8,128)(2,1)S(1)}, bf16[2048,512]{1,0:T(8,128)(2,1)S(1)}, bf16[2048,512]{1,0:T(8,128)(2,1)S(1)}, bf16[2048,512]{1,0:T(8,128)(2,1)S(1)}) custom-call(bf16[512,2048]{1,0:T(8,128)(2,1)S(1)} %get-tuple-element.67.refs_0_, bf16[2048,512]{1,0:T(8,128)(2,1)S(1)} %get-tuple-element.81.refs_1_, ...), custom_call_target="tpu_custom_call" | custom-call | bytes 1024 | tf_op jit(solution)/shard_map/give_own/pallas_call | solution.py:135
  78.7 0.5 collective-permute-start.14
  79.3 0.8 collective-permute-done.15.refs_10_
  80.0 0.6 collective-permute-start.16
  80.6 3.7 %collective-permute-done.16.refs_11_ = bf16[16,2048]{1,0:T(8,128)(2,1)S(1)} collective-permute-done((bf16[16,2048]{1,0:T(8,128)(2,1)S(1)}, bf16[16,2048]{1,0:T(8,128)(2,1)S(1)}, u32[]{:S(2)}, u32[]{:S(2)}) %collective-permute-start.16) | collective-permute-done | bytes 65568 | tf_op jit(solution)/shard_map/ppermute | solution.py:620
  84.3 8.4 %final.1 = bf16[2048,512]{1,0:T(8,128)(2,1)} custom-call(bf16[512,2048]{1,0:T(8,128)(2,1)S(1)} %get-tuple-element.67.refs_0_, bf16[2048,512]{1,0:T(8,128)(2,1)S(1)} %get-tuple-element.84.refs_1_, bf16[2048,512]{1,0:T(8,128)(2,1)S(1)} %get-tuple-element.85.refs_2_, bf16[2048,512]{1,0:T(8,128)(2,1)S(1)} %get-tuple-element.86.refs_3_, ...), custom_call_target="tpu_custom_call" | custom-call | bytes 1024 | tf_op jit(solution)/shard_map/final/pallas_call | solution.py:135
  (31 shorter events, 1.7 us)
Async XLA Ops:
  4.3 54.8 %all-to-all-start = ((bf16[4,2,32,16,256]{4,3,2,1,0:T(8,128)(2,1)}), bf16[4,2,32,16,256]{4,3,2,1,0:T(8,128)(2,1)}, u32[]{:S(2)}, u32[]{:S(2)}) async-start(bf16[4,2,32,16,256]{4,3,2,1,0:T(8,128)(2,1)} %get-tuple-element.46.refs_6_), calls=%async_computation | async-start | bytes 4194304 | tf_op jit(solution)/shard_map/all_to_all | solution.py:667
  10.6 1.6 %copy-start = (bf16[4,2,32,16,256]{4,3,2,1,0:T(8,128)(2,1)S(1)}, bf16[4,2,32,16,256]{4,3,2,1,0:T(8,128)(2,1)}, u32[]{:S(2)}) copy-start(bf16[4,2,32,16,256]{4,3,2,1,0:T(8,128)(2,1)} %get-tuple-element.46.refs_6_) | copy-start | bytes 6291460
  22.4 3.0 %collective-permute-start.3 = (bf16[256,512]{1,0:T(8,128)(2,1)S(1)}, bf16[256,512]{1,0:T(8,128)(2,1)S(1)}, u32[]{:S(2)}, u32[]{:S(2)}) collective-permute-start(bf16[256,512]{1,0:T(8,128)(2,1)S(1)} %get-tuple-element.61), channel_id=1, source_target_pairs={{0,1},{1,0},{2,3},{3,2},{4,5},{5,4},{6,7},{7,6},{8,9},{9,8},{10,11... | collective-permute-start | bytes 786440 | tf_op jit(solution)/shard_map/ppermute | solution.py:616
  22.4 2.9 %collective-permute-start.2 = (bf16[256,512]{1,0:T(8,128)(2,1)S(1)}, bf16[256,512]{1,0:T(8,128)(2,1)S(1)}, u32[]{:S(2)}, u32[]{:S(2)}) collective-permute-start(bf16[256,512]{1,0:T(8,128)(2,1)S(1)} %get-tuple-element.56.refs_3_), channel_id=1, source_target_pairs={{0,1},{1,0},{2,3},{3,2},{4,5},{5,4},{6,7},{7,6},{8,9},{9,8},{10,11... | collective-permute-start | bytes 786440 | tf_op jit(solution)/shard_map/ppermute | solution.py:616
  24.7 4.0 %collective-permute-start.1 = (bf16[256,512]{1,0:T(8,128)(2,1)S(1)}, bf16[256,512]{1,0:T(8,128)(2,1)S(1)}, u32[]{:S(2)}, u32[]{:S(2)}) collective-permute-start(bf16[256,512]{1,0:T(8,128)(2,1)S(1)} %get-tuple-element.58), channel_id=1, source_target_pairs={{0,1},{1,0},{2,3},{3,2},{4,5},{5,4},{6,7},{7,6},{8,9},{9,8},{10,11... | collective-permute-start | bytes 786440 | tf_op jit(solution)/shard_map/ppermute | solution.py:616
  24.9 3.8 %collective-permute-start = (bf16[256,512]{1,0:T(8,128)(2,1)S(1)}, bf16[256,512]{1,0:T(8,128)(2,1)S(1)}, u32[]{:S(2)}, u32[]{:S(2)}) collective-permute-start(bf16[256,512]{1,0:T(8,128)(2,1)S(1)} %get-tuple-element.57.refs_5_), channel_id=1, source_target_pairs={{0,1},{1,0},{2,3},{3,2},{4,5},{5,4},{6,7},{7,6},{8,9},{9,8},{10,11... | collective-permute-start | bytes 786440 | tf_op jit(solution)/shard_map/ppermute | solution.py:616
  27.1 17.5 %collective-permute-start.8 = (bf16[256,1024]{1,0:T(8,128)(2,1)S(1)}, bf16[256,1024]{1,0:T(8,128)(2,1)S(1)}, u32[]{:S(2)}, u32[]{:S(2)}) collective-permute-start(bf16[256,1024]{1,0:T(8,128)(2,1)S(1)} %keep.3.refs_5_), channel_id=1, source_target_pairs={{0,2},{1,3},{2,0},{3,1},{4,6},{5,7},{6,4},{7,5},{8,10},{9,11},{10,... | collective-permute-start | bytes 1572872 | tf_op jit(solution)/shard_map/ppermute | solution.py:620
  41.9 1.6 %collective-permute-start.5 = (bf16[256,512]{1,0:T(8,128)(2,1)S(1)}, bf16[256,512]{1,0:T(8,128)(2,1)S(1)}, u32[]{:S(2)}, u32[]{:S(2)}) collective-permute-start(bf16[256,512]{1,0:T(8,128)(2,1)S(1)} %get-tuple-element.63), channel_id=1, source_target_pairs={{0,1},{1,0},{2,3},{3,2},{4,5},{5,4},{6,7},{7,6},{8,9},{9,8},{10,11... | collective-permute-start | bytes 786440 | tf_op jit(solution)/shard_map/ppermute | solution.py:616
  42.0 2.0 %collective-permute-start.6 = (bf16[256,512]{1,0:T(8,128)(2,1)S(1)}, bf16[256,512]{1,0:T(8,128)(2,1)S(1)}, u32[]{:S(2)}, u32[]{:S(2)}) collective-permute-start(bf16[256,512]{1,0:T(8,128)(2,1)S(1)} %get-tuple-element.64), channel_id=1, source_target_pairs={{0,1},{1,0},{2,3},{3,2},{4,5},{5,4},{6,7},{7,6},{8,9},{9,8},{10,11... | collective-permute-start | bytes 786440 | tf_op jit(solution)/shard_map/ppermute | solution.py:616
  42.5 1.8 %collective-permute-start.7 = (bf16[256,512]{1,0:T(8,128)(2,1)S(1)}, bf16[256,512]{1,0:T(8,128)(2,1)S(1)}, u32[]{:S(2)}, u32[]{:S(2)}) collective-permute-start(bf16[256,512]{1,0:T(8,128)(2,1)S(1)} %get-tuple-element.65), channel_id=1, source_target_pairs={{0,1},{1,0},{2,3},{3,2},{4,5},{5,4},{6,7},{7,6},{8,9},{9,8},{10,11... | collective-permute-start | bytes 786440 | tf_op jit(solution)/shard_map/ppermute | solution.py:616
  42.6 2.1 %collective-permute-start.4 = (bf16[256,512]{1,0:T(8,128)(2,1)S(1)}, bf16[256,512]{1,0:T(8,128)(2,1)S(1)}, u32[]{:S(2)}, u32[]{:S(2)}) collective-permute-start(bf16[256,512]{1,0:T(8,128)(2,1)S(1)} %get-tuple-element.62.refs_9_), channel_id=1, source_target_pairs={{0,1},{1,0},{2,3},{3,2},{4,5},{5,4},{6,7},{7,6},{8,9},{9,8},{10,11... | collective-permute-start | bytes 786440 | tf_op jit(solution)/shard_map/ppermute | solution.py:616
  43.5 14.8 %collective-permute-start.9 = (bf16[256,1024]{1,0:T(8,128)(2,1)S(1)}, bf16[256,1024]{1,0:T(8,128)(2,1)S(1)}, u32[]{:S(2)}, u32[]{:S(2)}) collective-permute-start(bf16[256,1024]{1,0:T(8,128)(2,1)S(1)} %keep.4.refs_6_), channel_id=1, source_target_pairs={{0,2},{1,3},{2,0},{3,1},{4,6},{5,7},{6,4},{7,5},{8,10},{9,11},{10,... | collective-permute-start | bytes 1572872 | tf_op jit(solution)/shard_map/ppermute | solution.py:620
  44.6 3.6 %copy-start.4 = (bf16[256,1024]{1,0:T(8,128)(2,1)}, bf16[256,1024]{1,0:T(8,128)(2,1)S(1)}, u32[]{:S(2)}) copy-start(bf16[256,1024]{1,0:T(8,128)(2,1)S(1)} %collective-permute-done.8.refs_10_.refs_8_) | copy-start | bytes 1572868
  48.3 31.8 %collective-permute-start.15 = (bf16[256,2048]{1,0:T(8,128)(2,1)S(1)}, bf16[256,2048]{1,0:T(8,128)(2,1)}, u32[]{:S(2)}, u32[]{:S(2)}) collective-permute-start(bf16[256,2048]{1,0:T(8,128)(2,1)S(1)} %keep.5.refs_7_), channel_id=1, source_target_pairs={{0,2},{1,3},{2,0},{3,1},{4,6},{5,7},{6,4},{7,5},{8,10},{9,11},{10,... | collective-permute-start | bytes 3145736 | tf_op jit(solution)/shard_map/ppermute | solution.py:620
  58.3 0.8 copy-start.1
  59.1 1.0 %copy-start.2 = (bf16[256,1024]{1,0:T(8,128)(2,1)S(1)}, bf16[256,1024]{1,0:T(8,128)(2,1)}, u32[]{:S(2)}) copy-start(bf16[256,1024]{1,0:T(8,128)(2,1)} %copy-done.1) | copy-start | bytes 1572868
  69.6 3.7 %collective-permute-start.10 = (bf16[16,2048]{1,0:T(8,128)(2,1)S(1)}, bf16[16,2048]{1,0:T(8,128)(2,1)S(1)}, u32[]{:S(2)}, u32[]{:S(2)}) collective-permute-start(bf16[16,2048]{1,0:T(8,128)(2,1)S(1)} %get-tuple-element.76.refs_4_), channel_id=1, source_target_pairs={{0,1},{1,0},{2,3},{3,2},{4,5},{5,4},{6,7},{7,6},{8,9},{9,8},{10,11... | collective-permute-start | bytes 196616 | tf_op jit(solution)/shard_map/ppermute | solution.py:616
  72.7 11.6 %collective-permute-start.12 = (bf16[512,512]{1,0:T(8,128)(2,1)S(1)}, bf16[512,512]{1,0:T(8,128)(2,1)S(1)}, u32[]{:S(2)}, u32[]{:S(2)}) collective-permute-start(bf16[512,512]{1,0:T(8,128)(2,1)S(1)} %get-tuple-element.87), channel_id=1, source_target_pairs={{0,1},{1,0},{2,3},{3,2},{4,5},{5,4},{6,7},{7,6},{8,9},{9,8},{10,11... | collective-permute-start | bytes 1572872 | tf_op jit(solution)/shard_map/ppermute | solution.py:616
  73.2 11.1 %collective-permute-start.11 = (bf16[512,512]{1,0:T(8,128)(2,1)S(1)}, bf16[512,512]{1,0:T(8,128)(2,1)S(1)}, u32[]{:S(2)}, u32[]{:S(2)}) collective-permute-start(bf16[512,512]{1,0:T(8,128)(2,1)S(1)} %get-tuple-element.80.refs_7_), channel_id=1, source_target_pairs={{0,1},{1,0},{2,3},{3,2},{4,5},{5,4},{6,7},{7,6},{8,9},{9,8},{10,11... | collective-permute-start | bytes 1572872 | tf_op jit(solution)/shard_map/ppermute | solution.py:616
  75.5 8.8 %copy-start.3 = (bf16[256,1024]{1,0:T(8,128)(2,1)S(1)}, bf16[256,1024]{1,0:T(8,128)(2,1)}, u32[]{:S(2)}) copy-start(bf16[256,1024]{1,0:T(8,128)(2,1)} %copy-done.1) | copy-start | bytes 1572868
  75.6 8.8 %copy-start.5 = (bf16[256,1024]{1,0:T(8,128)(2,1)S(1)}, bf16[256,1024]{1,0:T(8,128)(2,1)}, u32[]{:S(2)}) copy-start(bf16[256,1024]{1,0:T(8,128)(2,1)} %copy-done.4) | copy-start | bytes 1572868
  78.7 5.6 %collective-permute-start.14 = (bf16[512,512]{1,0:T(8,128)(2,1)S(1)}, bf16[512,512]{1,0:T(8,128)(2,1)S(1)}, u32[]{:S(2)}, u32[]{:S(2)}) collective-permute-start(bf16[512,512]{1,0:T(8,128)(2,1)S(1)} %get-tuple-element.89), channel_id=1, source_target_pairs={{0,1},{1,0},{2,3},{3,2},{4,5},{5,4},{6,7},{7,6},{8,9},{9,8},{10,11... | collective-permute-start | bytes 1572872 | tf_op jit(solution)/shard_map/ppermute | solution.py:616
  79.2 5.1 %collective-permute-start.13 = (bf16[512,512]{1,0:T(8,128)(2,1)S(1)}, bf16[512,512]{1,0:T(8,128)(2,1)S(1)}, u32[]{:S(2)}, u32[]{:S(2)}) collective-permute-start(bf16[512,512]{1,0:T(8,128)(2,1)S(1)} %get-tuple-element.88.refs_13_), channel_id=1, source_target_pairs={{0,1},{1,0},{2,3},{3,2},{4,5},{5,4},{6,7},{7,6},{8,9},{9,8},{10,11... | collective-permute-start | bytes 1572872 | tf_op jit(solution)/shard_map/ppermute | solution.py:616
  80.0 4.3 %collective-permute-start.16 = (bf16[16,2048]{1,0:T(8,128)(2,1)S(1)}, bf16[16,2048]{1,0:T(8,128)(2,1)S(1)}, u32[]{:S(2)}, u32[]{:S(2)}) collective-permute-start(bf16[16,2048]{1,0:T(8,128)(2,1)S(1)} %get-tuple-element.83.refs_4_), channel_id=1, source_target_pairs={{0,2},{1,3},{2,0},{3,1},{4,6},{5,7},{6,4},{7,5},{8,10},{9,11},{10,... | collective-permute-start | bytes 196616 | tf_op jit(solution)/shard_map/ppermute | solution.py:620

commit v13 on v10

--- a/solution.py
+++ b/solution.py
@@ -155,49 +155,54 @@
 
 
 def pack_kernel(
-    ready, launch, table_ref, dest_ref, pool_hbm, query_ref, kv_ref, send_hbm, tail_q_ref,
-    tail_kv_ref, sems, *, sizes
+    ready, launch, table_ref, dest_ref, pool_ref, query_ref, kv_ref, send_hbm, tail_q_ref,
+    tail_kv_ref, pack_ref, sems, *, sizes
 ):
     inst = lax.axis_index("inst")
     ready()
-    dests = [dest_ref[inst * sizes.mig_per + m] for m in range(sizes.mig_per)]
-    for m, dest in enumerate(dests):
-
-        def copy_block(b, carry, m=m, dest=dest):
+    copies = []
+    for m in range(sizes.mig_per):
+        dest = dest_ref[inst * sizes.mig_per + m]
+
+        def copy_block(b, carry, m=m):
             block = table_ref[0, m, b]
             for s in range(sizes.slots):
-                pltpu.make_async_copy(
-                    pool_hbm.at[0, s, block], send_hbm.at[dest, s, b], sems.at[m]
-                ).start()
+                pack_ref[m, s, b] = pool_ref[0, s, block]
             return carry
 
         lax.fori_loop(0, sizes.mig_blocks, copy_block, 0, unroll=8)
+        copies.append(pltpu.make_async_copy(pack_ref.at[m], send_hbm.at[dest], sems.at[m]))
+        copies[-1].start()
     tail_q_ref[...] = query_ref[...]
     tail_kv_ref[...] = kv_ref[...].reshape(sizes.tail_kv, 2 * sizes.width)
-    for m, dest in enumerate(dests):
-        pltpu.make_async_copy(send_hbm.at[dest], send_hbm.at[dest], sems.at[m]).wait()
+    for copy in copies:
+        copy.wait()
 
 
 def pack(src_table, mig_dest, out_pool, query_rows, new_kv, sizes):
     z = sizes
     last_q = query_rows.shape[0] // z.tail_q - 1
     last_kv = z.batch // z.insts - 1
+    request = (z.slots, z.mig_blocks, z.block, 2 * z.width)
     result, _ = run(
         functools.partial(pack_kernel, sizes=z),
         [src_table, mig_dest], [out_pool, query_rows, new_kv],
         [
-            HBM,
+            VMEM,
             pl.BlockSpec((z.tail_q, z.width), lambda i: (last_q, 0)),
             pl.BlockSpec((z.insts,) + new_kv.shape[1:], lambda i: (last_kv, 0, 0, 0)),
         ],
         [],
         [
-            pltpu.HBM((z.insts, z.slots, z.mig_blocks, z.block, 2 * z.width), out_pool.dtype),
-            jax.ShapeDtypeStruct((z.tail_q, z.width), out_pool.dtype),
-            jax.ShapeDtypeStruct((z.tail_kv, 2 * z.width), out_pool.dtype),
+            pltpu.HBM((z.insts,) + request, out_pool.dtype),
+            pltpu.HBM((z.tail_q, z.width), out_pool.dtype),
+            pltpu.HBM((z.tail_kv, 2 * z.width), out_pool.dtype),
         ],
         [ANY, VMEM, VMEM], "pack", z, limit=60, grid=(1,),
-        scratch=[pltpu.SemaphoreType.DMA((z.mig_per,))],
+        scratch=[
+            pltpu.VMEM((z.mig_per,) + request, out_pool.dtype),
+            pltpu.SemaphoreType.DMA((z.mig_per,)),
+        ],
     )
     return result
 
@@ -662,20 +667,24 @@
     kept = keep(b, far, every, mates, "keep", [given] + got_low)
     got_second = sent(kept)
 
-    pieces = gives(far, every) + keeps(far, (0,))
+    tail_q, tail_kv = (
+        pltpu.with_memory_space_constraint(x, pltpu.HBM) for x in (tail_q, tail_kv)
+    )
+    pieces = gives([0], low) + gives(far, (0,))
     (rows, last, arrived), new = settle(
         mig_dest, mig_len, arriving, tail_q, tail_kv, rows, z, kept[-1:] + got_high,
         **bringing(pieces),
     )
     hold(pieces, new)
     late, whole = (last, 0, last.shape[0]), (rows, 0, 2 * tokens)
-    given, mates = give(late, far, every, "give_last", [], gives([0], low), joined=True)
-    given, mates_low = give(whole, [0], low, "give_own", [given], keeps(far, (1, 2, 3)))
-    kept = keep(late, far, every, mates, "keep_last", [given], gives([0], high))
+    given, mates_low = give(whole, [0], low, "give_own", [], gives(far, (1, 2, 3)))
+    given, mates = give(late, far, every, "give_last", [given], gives([0], high), joined=True)
+    given, mates_high = give(whole, [0], high, "give_own", [given], keeps(far, every))
+    kept = keep(late, far, every, mates, "keep_last", [given], keeps([0], low))
     got_late = sent(kept)
-    pieces = keeps([0], (0, 1, 2))
-    given, mates_high = give(whole, [0], high, "give_own", kept[-1:], pieces)
-    own = keep(whole, [0], low, mates_low, "keep_own", [given], keeps([0], (3,)), jnp.float32)
+    own = keep(
+        whole, [0], low, mates_low, "keep_own", kept[-1:], keeps([0], high), jnp.float32
+    )
     own += keep(whole, [0], high, mates_high, "keep_own", own, (), jnp.float32)
     hidden = finish(own, got_low, got_high, got_second, got_late, z, [])
     return (arrived, hidden)

time: 121 us -> 89.8 us (0.74)
  Pallas kernels: 91.8 us -> 60.3 us
    pallas_call x17, Pallas kernels: 91.8 us -> 60.3 us  [run(): pl.pallas_call(call, grid_spec=pltpu.PrefetchScalarGridSpec(num_scalar_pr...]
    unnamed x16 -> x12, local copies, waits for them, and re-layouts: 3.49 us -> 3.48 us
  transfers between devices with their start and end apart: 18 -> 18, of which waited for: 4 -> 4; matrix products, arithmetic and copies ran while one was open for 0% -> 0% of each run, Pallas kernels for 44% -> 60%
where the time goes in v13:
time: 89.8 us; the launch traced here: 89.3 us
  Pallas kernels  60.3 us (67%)
  starting transfers between devices  14.2 us (16%)
  waiting for transfers between devices  10.2 us (11%)
  local copies, waits for them, and re-layouts  3.48 us (4%)
  between operations  1.04 us (1%)
    pallas_call x17, Pallas kernels, run(): pl.pallas_call(call, grid_spec=pltpu.PrefetchScalarGridSpec(num_scalar_pr...  60.3 us
    ppermute x4, waiting for transfers between devices, across(): return lax.ppermute(x, 'tp', [(i, (i + shift) % tps) for i in range(tps)])  9.01 us
    all_to_all x1, starting transfers between devices, shards(): lax.all_to_all(sends, 'inst', split_axis=0, concat_axis=0, tiled=True)  6.33 us
    ppermute x4, starting transfers between devices, across(): return lax.ppermute(x, 'tp', [(i, (i + shift) % tps) for i in range(tps)])  4.43 us
    unnamed x12, local copies, waits for them, and re-layouts  3.48 us
    ppermute x13, starting transfers between devices, mate_of(): return lax.ppermute(x, 'tp', to_mate)  3.45 us
  transfers between devices with their start and end apart: 18, of which 4 were waited for; matrix products, arithmetic and copies ran while one was open for 0% of the time, Pallas kernels for 60%

profile of v13, /device:TPU:0, one launch (start us, length us, event | category | flops | bytes accessed | tf_op | source)
XLA Modules:
  0.0 89.3 jit_solution(17285939960375688396)
XLA Ops:
  0.6 3.7 %pack.1 = (bf16[4,2,32,16,256]{4,3,2,1,0:T(8,128)(2,1)}, bf16[256,128]{1,0:T(8,128)(2,1)}, bf16[32,256]{1,0:T(8,128)(2,1)}) custom-call(s32[1,2,32]{2,1,0:T(2,128)} %refs_0_.2, s32[8]{0:T(128)} %refs_0_.3, bf16[1,2,64,16,256]{4,3,2,1,0:T(8,128)(2,1)} %refs_2_.1, bf16[8192,128]{1,0:T(8,128)(2,1)} %bitcast.4, bf16[128,4,2,256]{3,2,1,0:T(2,128)(2,1)} %refs_3_.7), custom_call_target="tpu_custom_call" | custom-call | bytes 1024 | tf_op jit(solution)/shard_map/pack/pallas_call | solution.py:135
  4.3 6.3 %all-to-all-start = ((bf16[4,2,32,16,256]{4,3,2,1,0:T(8,128)(2,1)}), bf16[4,2,32,16,256]{4,3,2,1,0:T(8,128)(2,1)}, u32[]{:S(2)}, u32[]{:S(2)}) async-start(bf16[4,2,32,16,256]{4,3,2,1,0:T(8,128)(2,1)} %get-tuple-element.48.refs_6_), calls=%async_computation | async-start | bytes 4194304 | tf_op jit(solution)/shard_map/all_to_all | solution.py:646
  10.6 1.6 %copy-done = bf16[4,2,32,16,256]{4,3,2,1,0:T(8,128)(2,1)S(1)} copy-done((bf16[4,2,32,16,256]{4,3,2,1,0:T(8,128)(2,1)S(1)}, bf16[4,2,32,16,256]{4,3,2,1,0:T(8,128)(2,1)}, u32[]{:S(2)}) %copy-start) | copy-done | bytes 2097176
  12.2 7.8 %attend.2 = (bf16[512,2048]{1,0:T(8,128)(2,1)S(1)}, bf16[2048,512]{1,0:T(8,128)(2,1)S(1)}, bf16[2048,512]{1,0:T(8,128)(2,1)S(1)}, bf16[2048,512]{1,0:T(8,128)(2,...) custom-call(s32[8,125]{1,0:T(8,128)} %bitcast.7, ...), custom_call_target="tpu_custom_call" | custom-call | bytes 1024 | tf_op jit(solution)/shard_map/attend/pallas_call | solution.py:135
  20.1 2.3 %give.3 = (bf16[256,512]{1,0:T(8,128)(2,1)S(1)}, bf16[256,512]{1,0:T(8,128)(2,1)S(1)}, bf16[2048,512]{1,0:T(8,128)(2,1)S(1)}, bf16[2048,512]{1,0:T(8,128)(2,1)S(1)}) custom-call(bf16[512,2048]{1,0:T(8,128)(2,1)S(1)} %get-tuple-element.51.refs_0_.refs_5_, bf16[2048,512]{1,0:T(8,128)(2,1)S(1)} %get-tuple-element.52.refs_1_, ...), custom_call_target="tpu_custom_call" | custom-call | bytes 1024 | tf_op jit(solution)/shard_map/give/pallas_call | solution.py:135
  22.5 0.5 collective-permute-start.2
  23.0 1.8 %give.4 = (bf16[256,512]{1,0:T(8,128)(2,1)S(1)}, bf16[256,512]{1,0:T(8,128)(2,1)S(1)}) custom-call(bf16[512,2048]{1,0:T(8,128)(2,1)S(1)} %get-tuple-element.51.refs_0_.refs_5_, bf16[2048,512]{1,0:T(8,128)(2,1)S(1)} %get-tuple-element.56.refs_1_.refs_3_, bf16[2048,512]{1,0:T(8,128)(2,1)S(1)} %get-tuple-element.57.refs_2_.refs_4_, ...), custom_call_target="tpu_custom_call" | custom-call | bytes 1024 | tf_op jit(solution)/shard_map/give/pallas_call | solution.py:135
  24.9 0.4 collective-permute-start
  25.3 1.8 %keep.3.refs_5_ = bf16[256,1024]{1,0:T(8,128)(2,1)S(1)} custom-call(bf16[512,2048]{1,0:T(8,128)(2,1)S(1)} %get-tuple-element.51.refs_0_.refs_5_, bf16[2048,512]{1,0:T(8,128)(2,1)S(1)} %get-tuple-element.61.refs_1_, bf16[2048,512]{1,0:T(8,128)(2,1)S(1)} %get-tuple-element.62.refs_2_, bf16[256,512]{1,0:T(8,128)(2,1)S(1)} %collective-permute-done.2.refs_3_, ...), custom_call_target="tpu_custom_call" | custom-call | bytes 1024 | tf_op jit(solution)/shard_map/keep/pallas_call | solution.py:135
  27.2 1.6 %collective-permute-start.8 = (bf16[256,1024]{1,0:T(8,128)(2,1)S(1)}, bf16[256,1024]{1,0:T(8,128)(2,1)S(1)}, u32[]{:S(2)}, u32[]{:S(2)}) collective-permute-start(bf16[256,1024]{1,0:T(8,128)(2,1)S(1)} %keep.3.refs_5_), channel_id=1, source_target_pairs={{0,2},{1,3},{2,0},{3,1},{4,6},{5,7},{6,4},{7,5},{8,10},{9,11},{10,... | collective-permute-start | bytes 1572872 | tf_op jit(solution)/shard_map/ppermute | solution.py:599
  28.8 1.8 %keep.4.refs_6_ = bf16[256,1024]{1,0:T(8,128)(2,1)S(1)} custom-call(bf16[512,2048]{1,0:T(8,128)(2,1)S(1)} %get-tuple-element.51.refs_0_.refs_5_, bf16[2048,512]{1,0:T(8,128)(2,1)S(1)} %get-tuple-element.54.refs_1_.refs_3_, bf16[2048,512]{1,0:T(8,128)(2,1)S(1)} %get-tuple-element.55.refs_2_.refs_4_, bf16[256,512]{1,0:T(8,128)(2,1)S(1)} %collective-permute-done.refs_3_, ...), custom_call_target="tpu_custom_call" | custom-call | bytes 1024 | tf_op jit(solution)/shard_map/keep/pallas_call | solution.py:135
  30.6 7.8 %attend.3.refs_0_.refs_5_ = bf16[512,2048]{1,0:T(8,128)(2,1)S(1)} custom-call(s32[8,125]{1,0:T(8,128)} %bitcast.8, s32[1,125]{1,0:T(1,128)} %refs_1_.6, bf16[8192,128]{1,0:T(8,128)(2,1)} %bitcast.6, bf16[128,4,2,256]{3,2,1,0:T(2,128)(2,1)} %refs_3_.7, bf16[1,2,64,16,256]{4,3,2,1,0:T(8,128)(2,1)} %refs_4_.5, ...), custom_call_target="tpu_custom_call", output_to_operand_aliasing={{}: (5, {})} | custom-call | bytes 1024 | tf_op jit(solution)/shard_map/attend/pallas_call | solution.py:135
  38.4 3.6 %give.5 = (bf16[256,512]{1,0:T(8,128)(2,1)S(1)}, bf16[256,512]{1,0:T(8,128)(2,1)S(1)}, bf16[256,512]{1,0:T(8,128)(2,1)S(1)}, bf16[256,512]{1,0:T(8,128)(2,1)S(1)}) custom-call(bf16[512,2048]{1,0:T(8,128)(2,1)S(1)} %attend.3.refs_0_.refs_5_, bf16[2048,512]{1,0:T(8,128)(2,1)S(1)} %get-tuple-element.52.refs_1_, ...), custom_call_target="tpu_custom_call" | custom-call | bytes 1024 | tf_op jit(solution)/shard_map/give/pallas_call | solution.py:135
  42.1 0.5 collective-permute-start.6
  43.1 0.5 collective-permute-done.5.refs_6_
  43.6 0.5 collective-permute-start.9
  44.7 3.6 %keep.5.refs_7_ = bf16[256,2048]{1,0:T(8,128)(2,1)S(1)} custom-call(bf16[512,2048]{1,0:T(8,128)(2,1)S(1)} %attend.3.refs_0_.refs_5_, bf16[2048,512]{1,0:T(8,128)(2,1)S(1)} %get-tuple-element.61.refs_1_, bf16[2048,512]{1,0:T(8,128)(2,1)S(1)} %get-tuple-element.62.refs_2_, bf16[2048,512]{1,0:T(8,128)(2,1)S(1)} %get-tuple-element.54.refs_1_.refs_3_, ...), custom_call_target="tpu_custom_call" | custom-call | bytes 1024 | tf_op jit(solution)/shard_map/keep/pallas_call | solution.py:135
  48.3 1.0 %collective-permute-start.15 = (bf16[256,2048]{1,0:T(8,128)(2,1)S(1)}, bf16[256,2048]{1,0:T(8,128)(2,1)}, u32[]{:S(2)}, u32[]{:S(2)}) collective-permute-start(bf16[256,2048]{1,0:T(8,128)(2,1)S(1)} %keep.5.refs_7_), channel_id=1, source_target_pairs={{0,2},{1,3},{2,0},{3,1},{4,6},{5,7},{6,4},{7,5},{8,10},{9,11},{10,... | collective-permute-start | bytes 3145736 | tf_op jit(solution)/shard_map/ppermute | solution.py:599
  49.3 9.0 %collective-permute-done.9.refs_8_.refs_3_ = bf16[256,1024]{1,0:T(8,128)(2,1)S(1)} collective-permute-done((bf16[256,1024]{1,0:T(8,128)(2,1)S(1)}, bf16[256,1024]{1,0:T(8,128)(2,1)S(1)}, u32[]{:S(2)}, u32[]{:S(2)}) %collective-permute-start.9) | collective-permute-done | bytes 524320 | tf_op jit(solution)/shard_map/ppermute | solution.py:599
  58.4 0.8 copy-done.1
  59.2 1.0 %copy-done.2 = bf16[256,1024]{1,0:T(8,128)(2,1)S(1)} copy-done((bf16[256,1024]{1,0:T(8,128)(2,1)S(1)}, bf16[256,1024]{1,0:T(8,128)(2,1)}, u32[]{:S(2)}) %copy-start.2) | copy-done | bytes 524312
  60.2 6.0 %settle.1 = (bf16[512,2048]{1,0:T(8,128)(2,1)S(1)}, bf16[16,2048]{1,0:T(8,128)(2,1)S(1)}, bf16[1,3,2,512,256]{4,3,2,1,0:T(8,128)(2,1)}, bf16[2048,512]{1,0:T(8,1...) custom-call(s32[8]{0:T(128)} %refs_0_.3, s32[8]{0:T(128)} %refs_1_.7, ...), custom_call_target="tpu_custom_call", output_to_operand_aliasing={{0}: (5, {})} | custom-call | bytes 1024 | tf_op jit(solution)/shard_map/settle/pallas_call | solution.py:135
  66.2 3.0 %give_own.2 = (bf16[512,512]{1,0:T(8,128)(2,1)S(1)}, bf16[512,512]{1,0:T(8,128)(2,1)S(1)}, bf16[2048,512]{1,0:T(8,128)(2,1)S(1)}, bf16[2048,512]{1,0:T(8,128)(2,1)S(1)}, bf16[2048,512]{1,0:T(8,128)(2,1)S(1)}) custom-call(bf16[512,2048]{1,0:T(8,128)(2,1)S(1)} %get-tuple-element.69.refs_0_, bf16[2048,512]{1,0:T(8,128)(2,1)S(1)} %get-tuple-element.72.refs_1_, ...), custom_call_target="tpu_custom_call" | custom-call | bytes 1024 | tf_op jit(solution)/shard_map/give_own/pallas_call | solution.py:135
  69.2 2.3 %give_last.1 = (bf16[16,2048]{1,0:T(8,128)(2,1)S(1)}, bf16[2048,512]{1,0:T(8,128)(2,1)S(1)}, bf16[2048,512]{1,0:T(8,128)(2,1)S(1)}) custom-call(bf16[16,2048]{1,0:T(8,128)(2,1)S(1)} %get-tuple-element.70.refs_0_, bf16[2048,512]{1,0:T(8,128)(2,1)S(1)} %get-tuple-element.71.refs_1_, bf16[2048,512]{1,0:T(8,128)(2,1)S(1)} %get-tuple-element.74.refs_2_, ...), custom_call_target="tpu_custom_call" | custom-call | bytes 1024 | tf_op jit(solution)/shard_map/give_last/pallas_call | solution.py:135
  71.5 0.5 collective-permute-start.12
  72.1 3.5 %give_own.3 = (bf16[512,512]{1,0:T(8,128)(2,1)S(1)}, bf16[512,512]{1,0:T(8,128)(2,1)S(1)}, bf16[2048,512]{1,0:T(8,128)(2,1)S(1)}, bf16[2048,512]{1,0:T(8,128)(2,...) custom-call(bf16[512,2048]{1,0:T(8,128)(2,1)S(1)} %get-tuple-element.69.refs_0_, ...), custom_call_target="tpu_custom_call" | custom-call | bytes 1024 | tf_op jit(solution)/shard_map/give_own/pallas_call | solution.py:135
  75.7 0.5 collective-permute-start.14
  76.3 2.3 %keep_last.1 = (bf16[16,2048]{1,0:T(8,128)(2,1)S(1)}, bf16[2048,512]{1,0:T(8,128)(2,1)S(1)}, bf16[2048,512]{1,0:T(8,128)(2,1)S(1)}) custom-call(bf16[16,2048]{1,0:T(8,128)(2,1)S(1)} %get-tuple-element.70.refs_0_, bf16[2048,512]{1,0:T(8,128)(2,1)S(1)} %get-tuple-element.81.refs_1_, bf16[2048,512]{1,0:T(8,128)(2,1)S(1)} %get-tuple-element.82.refs_2_, ...), custom_call_target="tpu_custom_call" | custom-call | bytes 1024 | tf_op jit(solution)/shard_map/keep_last/pallas_call | solution.py:135
  78.5 1.3 %collective-permute-start.16 = (bf16[16,2048]{1,0:T(8,128)(2,1)S(1)}, bf16[16,2048]{1,0:T(8,128)(2,1)S(1)}, u32[]{:S(2)}, u32[]{:S(2)}) collective-permute-start(bf16[16,2048]{1,0:T(8,128)(2,1)S(1)} %get-tuple-element.89.refs_6_), channel_id=1, source_target_pairs={{0,2},{1,3},{2,0},{3,1},{4,6},{5,7},{6,4},{7,5},{8,10},{9,11},{10,... | collective-permute-start | bytes 196616 | tf_op jit(solution)/shard_map/ppermute | solution.py:599
  79.9 2.9 %keep_own.2 = (f32[512,1024]{1,0:T(8,128)S(1)}, bf16[2048,512]{1,0:T(8,128)(2,1)S(1)}, bf16[2048,512]{1,0:T(8,128)(2,1)S(1)}) custom-call(bf16[512,2048]{1,0:T(8,128)(2,1)S(1)} %get-tuple-element.69.refs_0_, bf16[2048,512]{1,0:T(8,128)(2,1)S(1)} %get-tuple-element.86.refs_1_, bf16[2048,512]{1,0:T(8,128)(2,1)S(1)} %get-tuple-element.87.refs_2_, ...), custom_call_target="tpu_custom_call" | custom-call | bytes 1024 | tf_op jit(solution)/shard_map/keep_own/pallas_call | solution.py:135
  82.8 2.9 %keep_own.3.refs_1_ = f32[512,1024]{1,0:T(8,128)S(1)} custom-call(bf16[512,2048]{1,0:T(8,128)(2,1)S(1)} %get-tuple-element.69.refs_0_, bf16[2048,512]{1,0:T(8,128)(2,1)S(1)} %get-tuple-element.91.refs_1_, bf16[2048,512]{1,0:T(8,128)(2,1)S(1)} %get-tuple-element.92.refs_2_, bf16[512,512]{1,0:T(8,128)(2,1)S(1)} %collective-permute-done.13.refs_3_, ...), custom_call_target="tpu_custom_call" | custom-call | bytes 1024 | tf_op jit(solution)/shard_map/keep_own/pallas_call | solution.py:135
  85.8 3.3 %finish.1 = bf16[2048,512]{1,0:T(8,128)(2,1)} custom-call(f32[512,1024]{1,0:T(8,128)S(1)} %get-tuple-element.90.refs_5_.refs_0_, f32[512,1024]{1,0:T(8,128)S(1)} %keep_own.3.refs_1_, bf16[256,1024]{1,0:T(8,128)(2,1)S(1)} %copy-done.5, bf16[256,1024]{1,0:T(8,128)(2,1)S(1)} %copy-done.3, bf16[256,2048]{1,0:T(8,128)(2,1)} %collective-permute-done.15.refs_4_, ...), custom_call_target="tpu_custom_call" | custom-call | bytes 1024 | tf_op jit(solution)/shard_map/finish/pallas_call | solution.py:135
  (33 shorter events, 1.7 us)
Async XLA Ops:
  4.3 54.9 %all-to-all-start = ((bf16[4,2,32,16,256]{4,3,2,1,0:T(8,128)(2,1)}), bf16[4,2,32,16,256]{4,3,2,1,0:T(8,128)(2,1)}, u32[]{:S(2)}, u32[]{:S(2)}) async-start(bf16[4,2,32,16,256]{4,3,2,1,0:T(8,128)(2,1)} %get-tuple-element.48.refs_6_), calls=%async_computation | async-start | bytes 4194304 | tf_op jit(solution)/shard_map/all_to_all | solution.py:646
  10.6 1.6 %copy-start = (bf16[4,2,32,16,256]{4,3,2,1,0:T(8,128)(2,1)S(1)}, bf16[4,2,32,16,256]{4,3,2,1,0:T(8,128)(2,1)}, u32[]{:S(2)}) copy-start(bf16[4,2,32,16,256]{4,3,2,1,0:T(8,128)(2,1)} %get-tuple-element.48.refs_6_) | copy-start | bytes 6291460
  22.4 3.0 %collective-permute-start.3 = (bf16[256,512]{1,0:T(8,128)(2,1)S(1)}, bf16[256,512]{1,0:T(8,128)(2,1)S(1)}, u32[]{:S(2)}, u32[]{:S(2)}) collective-permute-start(bf16[256,512]{1,0:T(8,128)(2,1)S(1)} %get-tuple-element.63), channel_id=1, source_target_pairs={{0,1},{1,0},{2,3},{3,2},{4,5},{5,4},{6,7},{7,6},{8,9},{9,8},{10,11... | collective-permute-start | bytes 786440 | tf_op jit(solution)/shard_map/ppermute | solution.py:595
  22.5 2.9 %collective-permute-start.2 = (bf16[256,512]{1,0:T(8,128)(2,1)S(1)}, bf16[256,512]{1,0:T(8,128)(2,1)S(1)}, u32[]{:S(2)}, u32[]{:S(2)}) collective-permute-start(bf16[256,512]{1,0:T(8,128)(2,1)S(1)} %get-tuple-element.58.refs_3_), channel_id=1, source_target_pairs={{0,1},{1,0},{2,3},{3,2},{4,5},{5,4},{6,7},{7,6},{8,9},{9,8},{10,11... | collective-permute-start | bytes 786440 | tf_op jit(solution)/shard_map/ppermute | solution.py:595
  24.8 4.0 %collective-permute-start.1 = (bf16[256,512]{1,0:T(8,128)(2,1)S(1)}, bf16[256,512]{1,0:T(8,128)(2,1)S(1)}, u32[]{:S(2)}, u32[]{:S(2)}) collective-permute-start(bf16[256,512]{1,0:T(8,128)(2,1)S(1)} %get-tuple-element.60), channel_id=1, source_target_pairs={{0,1},{1,0},{2,3},{3,2},{4,5},{5,4},{6,7},{7,6},{8,9},{9,8},{10,11... | collective-permute-start | bytes 786440 | tf_op jit(solution)/shard_map/ppermute | solution.py:595
  24.9 3.9 %collective-permute-start = (bf16[256,512]{1,0:T(8,128)(2,1)S(1)}, bf16[256,512]{1,0:T(8,128)(2,1)S(1)}, u32[]{:S(2)}, u32[]{:S(2)}) collective-permute-start(bf16[256,512]{1,0:T(8,128)(2,1)S(1)} %get-tuple-element.59.refs_5_), channel_id=1, source_target_pairs={{0,1},{1,0},{2,3},{3,2},{4,5},{5,4},{6,7},{7,6},{8,9},{9,8},{10,11... | collective-permute-start | bytes 786440 | tf_op jit(solution)/shard_map/ppermute | solution.py:595
  27.2 17.5 %collective-permute-start.8 = (bf16[256,1024]{1,0:T(8,128)(2,1)S(1)}, bf16[256,1024]{1,0:T(8,128)(2,1)S(1)}, u32[]{:S(2)}, u32[]{:S(2)}) collective-permute-start(bf16[256,1024]{1,0:T(8,128)(2,1)S(1)} %keep.3.refs_5_), channel_id=1, source_target_pairs={{0,2},{1,3},{2,0},{3,1},{4,6},{5,7},{6,4},{7,5},{8,10},{9,11},{10,... | collective-permute-start | bytes 1572872 | tf_op jit(solution)/shard_map/ppermute | solution.py:599
  42.0 1.6 %collective-permute-start.5 = (bf16[256,512]{1,0:T(8,128)(2,1)S(1)}, bf16[256,512]{1,0:T(8,128)(2,1)S(1)}, u32[]{:S(2)}, u32[]{:S(2)}) collective-permute-start(bf16[256,512]{1,0:T(8,128)(2,1)S(1)} %get-tuple-element.65), channel_id=1, source_target_pairs={{0,1},{1,0},{2,3},{3,2},{4,5},{5,4},{6,7},{7,6},{8,9},{9,8},{10,11... | collective-permute-start | bytes 786440 | tf_op jit(solution)/shard_map/ppermute | solution.py:595
  42.1 2.0 %collective-permute-start.6 = (bf16[256,512]{1,0:T(8,128)(2,1)S(1)}, bf16[256,512]{1,0:T(8,128)(2,1)S(1)}, u32[]{:S(2)}, u32[]{:S(2)}) collective-permute-start(bf16[256,512]{1,0:T(8,128)(2,1)S(1)} %get-tuple-element.66), channel_id=1, source_target_pairs={{0,1},{1,0},{2,3},{3,2},{4,5},{5,4},{6,7},{7,6},{8,9},{9,8},{10,11... | collective-permute-start | bytes 786440 | tf_op jit(solution)/shard_map/ppermute | solution.py:595
  42.6 1.8 %collective-permute-start.7 = (bf16[256,512]{1,0:T(8,128)(2,1)S(1)}, bf16[256,512]{1,0:T(8,128)(2,1)S(1)}, u32[]{:S(2)}, u32[]{:S(2)}) collective-permute-start(bf16[256,512]{1,0:T(8,128)(2,1)S(1)} %get-tuple-element.67), channel_id=1, source_target_pairs={{0,1},{1,0},{2,3},{3,2},{4,5},{5,4},{6,7},{7,6},{8,9},{9,8},{10,11... | collective-permute-start | bytes 786440 | tf_op jit(solution)/shard_map/ppermute | solution.py:595
  42.6 2.1 %collective-permute-start.4 = (bf16[256,512]{1,0:T(8,128)(2,1)S(1)}, bf16[256,512]{1,0:T(8,128)(2,1)S(1)}, u32[]{:S(2)}, u32[]{:S(2)}) collective-permute-start(bf16[256,512]{1,0:T(8,128)(2,1)S(1)} %get-tuple-element.64.refs_9_), channel_id=1, source_target_pairs={{0,1},{1,0},{2,3},{3,2},{4,5},{5,4},{6,7},{7,6},{8,9},{9,8},{10,11... | collective-permute-start | bytes 786440 | tf_op jit(solution)/shard_map/ppermute | solution.py:595
  43.6 14.8 %collective-permute-start.9 = (bf16[256,1024]{1,0:T(8,128)(2,1)S(1)}, bf16[256,1024]{1,0:T(8,128)(2,1)S(1)}, u32[]{:S(2)}, u32[]{:S(2)}) collective-permute-start(bf16[256,1024]{1,0:T(8,128)(2,1)S(1)} %keep.4.refs_6_), channel_id=1, source_target_pairs={{0,2},{1,3},{2,0},{3,1},{4,6},{5,7},{6,4},{7,5},{8,10},{9,11},{10,... | collective-permute-start | bytes 1572872 | tf_op jit(solution)/shard_map/ppermute | solution.py:599
  44.7 3.6 %copy-start.4 = (bf16[256,1024]{1,0:T(8,128)(2,1)}, bf16[256,1024]{1,0:T(8,128)(2,1)S(1)}, u32[]{:S(2)}) copy-start(bf16[256,1024]{1,0:T(8,128)(2,1)S(1)} %collective-permute-done.8.refs_10_.refs_2_) | copy-start | bytes 1572868
  48.3 37.4 %collective-permute-start.15 = (bf16[256,2048]{1,0:T(8,128)(2,1)S(1)}, bf16[256,2048]{1,0:T(8,128)(2,1)}, u32[]{:S(2)}, u32[]{:S(2)}) collective-permute-start(bf16[256,2048]{1,0:T(8,128)(2,1)S(1)} %keep.5.refs_7_), channel_id=1, source_target_pairs={{0,2},{1,3},{2,0},{3,1},{4,6},{5,7},{6,4},{7,5},{8,10},{9,11},{10,... | collective-permute-start | bytes 3145736 | tf_op jit(solution)/shard_map/ppermute | solution.py:599
  58.4 0.8 copy-start.1
  59.2 1.0 %copy-start.2 = (bf16[256,1024]{1,0:T(8,128)(2,1)S(1)}, bf16[256,1024]{1,0:T(8,128)(2,1)}, u32[]{:S(2)}) copy-start(bf16[256,1024]{1,0:T(8,128)(2,1)} %copy-done.1) | copy-start | bytes 1572868
  71.5 4.7 %collective-permute-start.10 = (bf16[16,2048]{1,0:T(8,128)(2,1)S(1)}, bf16[16,2048]{1,0:T(8,128)(2,1)S(1)}, u32[]{:S(2)}, u32[]{:S(2)}) collective-permute-start(bf16[16,2048]{1,0:T(8,128)(2,1)S(1)} %get-tuple-element.80.refs_4_), channel_id=1, source_target_pairs={{0,1},{1,0},{2,3},{3,2},{4,5},{5,4},{6,7},{7,6},{8,9},{9,8},{10,11... | collective-permute-start | bytes 196616 | tf_op jit(solution)/shard_map/ppermute | solution.py:595
  71.5 7.0 %collective-permute-start.12 = (bf16[512,512]{1,0:T(8,128)(2,1)S(1)}, bf16[512,512]{1,0:T(8,128)(2,1)S(1)}, u32[]{:S(2)}, u32[]{:S(2)}) collective-permute-start(bf16[512,512]{1,0:T(8,128)(2,1)S(1)} %get-tuple-element.88), channel_id=1, source_target_pairs={{0,1},{1,0},{2,3},{3,2},{4,5},{5,4},{6,7},{7,6},{8,9},{9,8},{10,11... | collective-permute-start | bytes 1572872 | tf_op jit(solution)/shard_map/ppermute | solution.py:595
  72.0 7.8 %collective-permute-start.11 = (bf16[512,512]{1,0:T(8,128)(2,1)S(1)}, bf16[512,512]{1,0:T(8,128)(2,1)S(1)}, u32[]{:S(2)}, u32[]{:S(2)}) collective-permute-start(bf16[512,512]{1,0:T(8,128)(2,1)S(1)} %get-tuple-element.77.refs_6_), channel_id=1, source_target_pairs={{0,1},{1,0},{2,3},{3,2},{4,5},{5,4},{6,7},{7,6},{8,9},{9,8},{10,11... | collective-permute-start | bytes 1572872 | tf_op jit(solution)/shard_map/ppermute | solution.py:595
  75.7 7.1 %collective-permute-start.14 = (bf16[512,512]{1,0:T(8,128)(2,1)S(1)}, bf16[512,512]{1,0:T(8,128)(2,1)S(1)}, u32[]{:S(2)}, u32[]{:S(2)}) collective-permute-start(bf16[512,512]{1,0:T(8,128)(2,1)S(1)} %get-tuple-element.93), channel_id=1, source_target_pairs={{0,1},{1,0},{2,3},{3,2},{4,5},{5,4},{6,7},{7,6},{8,9},{9,8},{10,11... | collective-permute-start | bytes 1572872 | tf_op jit(solution)/shard_map/ppermute | solution.py:595
  76.2 6.6 %collective-permute-start.13 = (bf16[512,512]{1,0:T(8,128)(2,1)S(1)}, bf16[512,512]{1,0:T(8,128)(2,1)S(1)}, u32[]{:S(2)}, u32[]{:S(2)}) collective-permute-start(bf16[512,512]{1,0:T(8,128)(2,1)S(1)} %get-tuple-element.85.refs_7_), channel_id=1, source_target_pairs={{0,1},{1,0},{2,3},{3,2},{4,5},{5,4},{6,7},{7,6},{8,9},{9,8},{10,11... | collective-permute-start | bytes 1572872 | tf_op jit(solution)/shard_map/ppermute | solution.py:595
  78.5 7.2 %collective-permute-start.16 = (bf16[16,2048]{1,0:T(8,128)(2,1)S(1)}, bf16[16,2048]{1,0:T(8,128)(2,1)S(1)}, u32[]{:S(2)}, u32[]{:S(2)}) collective-permute-start(bf16[16,2048]{1,0:T(8,128)(2,1)S(1)} %get-tuple-element.89.refs_6_), channel_id=1, source_target_pairs={{0,2},{1,3},{2,0},{3,1},{4,6},{5,7},{6,4},{7,5},{8,10},{9,11},{10,... | collective-permute-start | bytes 196616 | tf_op jit(solution)/shard_map/ppermute | solution.py:599
  82.8 2.9 %copy-start.3 = (bf16[256,1024]{1,0:T(8,128)(2,1)S(1)}, bf16[256,1024]{1,0:T(8,128)(2,1)}, u32[]{:S(2)}) copy-start(bf16[256,1024]{1,0:T(8,128)(2,1)} %copy-done.1) | copy-start | bytes 1572868
  82.8 2.9 %copy-start.5 = (bf16[256,1024]{1,0:T(8,128)(2,1)S(1)}, bf16[256,1024]{1,0:T(8,128)(2,1)}, u32[]{:S(2)}) copy-start(bf16[256,1024]{1,0:T(8,128)(2,1)} %copy-done.4) | copy-start | bytes 1572868

commit v14 on v13

--- a/solution.py
+++ b/solution.py
@@ -155,11 +155,14 @@
 
 
 def pack_kernel(
-    ready, launch, table_ref, dest_ref, pool_ref, query_ref, kv_ref, send_hbm, tail_q_ref,
-    tail_kv_ref, pack_ref, sems, *, sizes
+    ready, launch, table_ref, dest_ref, pool_hbm, query_ref, kv_ref, send_hbm, tail_q_ref,
+    tail_kv_ref, pool_ref, pack_ref, sems, *, sizes
 ):
     inst = lax.axis_index("inst")
+    pool_copy = pltpu.make_async_copy(pool_hbm, pool_ref, sems.at[sizes.mig_per])
+    pool_copy.start()
     ready()
+    pool_copy.wait()
     copies = []
     for m in range(sizes.mig_per):
         dest = dest_ref[inst * sizes.mig_per + m]
@@ -188,7 +191,7 @@
         functools.partial(pack_kernel, sizes=z),
         [src_table, mig_dest], [out_pool, query_rows, new_kv],
         [
-            VMEM,
+            HBM,
             pl.BlockSpec((z.tail_q, z.width), lambda i: (last_q, 0)),
             pl.BlockSpec((z.insts,) + new_kv.shape[1:], lambda i: (last_kv, 0, 0, 0)),
         ],
@@ -200,8 +203,9 @@
         ],
         [ANY, VMEM, VMEM], "pack", z, limit=60, grid=(1,),
         scratch=[
+            pltpu.VMEM(out_pool.shape, out_pool.dtype),
             pltpu.VMEM((z.mig_per,) + request, out_pool.dtype),
-            pltpu.SemaphoreType.DMA((z.mig_per,)),
+            pltpu.SemaphoreType.DMA((z.mig_per + 1,)),
         ],
     )
     return result
@@ -376,14 +380,13 @@
     arrived_hbm, rows_ref, got_ref, keep_ref, sems, *, sizes
 ):
     z = sizes
-    ready()
     inst = lax.axis_index("inst")
-    requests = row_plan(dest_ref, inst, z.cap)
-    known = [jnp.maximum(request, 0) for request in requests]
     extent = z.mig_blocks * z.block
     reads = [
-        pltpu.make_async_copy(got_hbm.at[known[a] // z.mig_per], got_ref.at[a], sems.at[0, a])
-        for a in range(z.cap)
+        pltpu.make_async_copy(
+            got_hbm.at[lax.rem(inst + k, z.insts)], got_ref.at[k - 1], sems.at[0, k - 1]
+        )
+        for k in range(1, z.insts)
     ]
     writes = [
         pltpu.make_async_copy(keep_ref.at[a], arrived_hbm.at[0, a], sems.at[1, a])
@@ -392,6 +395,9 @@
     for read in reads:
         read.start()
     launch()
+    ready()
+    requests = row_plan(dest_ref, inst, z.cap)
+    known = [jnp.maximum(request, 0) for request in requests]
     new_kv = kv_ref[...]
     code = fresh_code(z.per, z.tail_kv, z)
     slot_of = slot_index(extent, z)
@@ -401,15 +407,18 @@
     place = lax.broadcasted_iota(jnp.int32, (z.block, 2 * z.width), 0)
     filled = row < 0
     rows_ref[: z.per, :] = jnp.zeros((z.per, z.width), jnp.float32)
+    for read in reads:
+        read.wait()
     for a in range(z.cap):
         length = jnp.where(requests[a] >= 0, len_ref[known[a]], 0)
-        reads[a].wait()
-
-        def one(b, carry, a=a, length=length):
+        ahead = lax.rem(known[a] // z.mig_per - inst + z.insts, z.insts)
+        at_hand = jnp.maximum(ahead - 1, 0)
+
+        def one(b, carry, a=a, length=length, at_hand=at_hand):
             inside = place + b * z.block < length
             at = pl.ds(pl.multiple_of(b * z.block, z.block), z.block)
             for s in range(z.slots):
-                value = got_ref[a, s, b].astype(jnp.float32)
+                value = got_ref[at_hand, s, b].astype(jnp.float32)
                 keep_ref[a, s, at, :] = jnp.where(inside, value, 0.0).astype(jnp.bfloat16)
             return carry
 
@@ -664,7 +673,7 @@
     )
     b = (rows, tokens, tokens)
     given, mates = give(b, far, every, "give", [])
-    kept = keep(b, far, every, mates, "keep", [given] + got_low)
+    kept = keep(b, far, every, mates, "keep", [given] + got_low + got_high)
     got_second = sent(kept)
 
     tail_q, tail_kv = (
@@ -672,7 +681,7 @@
     )
     pieces = gives([0], low) + gives(far, (0,))
     (rows, last, arrived), new = settle(
-        mig_dest, mig_len, arriving, tail_q, tail_kv, rows, z, kept[-1:] + got_high,
+        mig_dest, mig_len, arriving, tail_q, tail_kv, rows, z, kept[-1:],
         **bringing(pieces),
     )
     hold(pieces, new)

time: 89.8 us -> 100 us (1.11)
  waiting for transfers between devices: 10.2 us -> 23 us
  local copies, waits for them, and re-layouts: 3.48 us -> 1.64 us
    ppermute x4, waiting for transfers between devices: 9.01 us -> 21.2 us  [across(): return lax.ppermute(x, 'tp', [(i, (i + shift) % tps) for i in range(tps)])]
    unnamed x12 -> x10, local copies, waits for them, and re-layouts: 3.48 us -> 1.64 us
  transfers between devices with their start and end apart: 18 -> 18, of which waited for: 4 -> 5; matrix products, arithmetic and copies ran while one was open for 0% -> 0% of each run, Pallas kernels for 60% -> 54%
where the time goes in v14:
time: 100 us; the launch traced here: 99.7 us
  Pallas kernels  60.4 us (60%)
  waiting for transfers between devices  23 us (23%)
  starting transfers between devices  13.5 us (14%)
  local copies, waits for them, and re-layouts  1.64 us (2%)
  between operations  1.05 us (1%)
    pallas_call x17, Pallas kernels, run(): pl.pallas_call(call, grid_spec=pltpu.PrefetchScalarGridSpec(num_scalar_pr...  60.4 us
    ppermute x4, waiting for transfers between devices, across(): return lax.ppermute(x, 'tp', [(i, (i + shift) % tps) for i in range(tps)])  21.2 us
    all_to_all x1, starting transfers between devices, shards(): lax.all_to_all(sends, 'inst', split_axis=0, concat_axis=0, tiled=True)  6.33 us
    ppermute x4, starting transfers between devices, across(): return lax.ppermute(x, 'tp', [(i, (i + shift) % tps) for i in range(tps)])  4.18 us
    ppermute x13, starting transfers between devices, mate_of(): return lax.ppermute(x, 'tp', to_mate)  3.03 us
  transfers between devices with their start and end apart: 18, of which 5 were waited for; matrix products, arithmetic and copies ran while one was open for 0% of the time, Pallas kernels for 54%

profile of v14, /device:TPU:0, one launch (start us, length us, event | category | flops | bytes accessed | tf_op | source)
XLA Modules:
  0.0 99.7 jit_solution(17368627668560090024)
XLA Ops:
  0.6 3.7 %pack.1 = (bf16[4,2,32,16,256]{4,3,2,1,0:T(8,128)(2,1)}, bf16[256,128]{1,0:T(8,128)(2,1)}, bf16[32,256]{1,0:T(8,128)(2,1)}) custom-call(s32[1,2,32]{2,1,0:T(2,128)} %refs_0_.2, s32[8]{0:T(128)} %refs_0_.3, bf16[1,2,64,16,256]{4,3,2,1,0:T(8,128)(2,1)} %refs_2_.1, bf16[8192,128]{1,0:T(8,128)(2,1)} %bitcast.4, bf16[128,4,2,256]{3,2,1,0:T(2,128)(2,1)} %refs_3_.7), custom_call_target="tpu_custom_call" | custom-call | bytes 1024 | tf_op jit(solution)/shard_map/pack/pallas_call | solution.py:135
  4.4 6.3 %all-to-all-start = ((bf16[4,2,32,16,256]{4,3,2,1,0:T(8,128)(2,1)}), bf16[4,2,32,16,256]{4,3,2,1,0:T(8,128)(2,1)}, u32[]{:S(2)}, u32[]{:S(2)}) async-start(bf16[4,2,32,16,256]{4,3,2,1,0:T(8,128)(2,1)} %get-tuple-element.48.refs_6_), calls=%async_computation | async-start | bytes 4194304 | tf_op jit(solution)/shard_map/all_to_all | solution.py:655
  10.7 1.6 %copy-done = bf16[4,2,32,16,256]{4,3,2,1,0:T(8,128)(2,1)S(1)} copy-done((bf16[4,2,32,16,256]{4,3,2,1,0:T(8,128)(2,1)S(1)}, bf16[4,2,32,16,256]{4,3,2,1,0:T(8,128)(2,1)}, u32[]{:S(2)}) %copy-start) | copy-done | bytes 2097176
  12.3 7.8 %attend.2 = (bf16[512,2048]{1,0:T(8,128)(2,1)S(1)}, bf16[2048,512]{1,0:T(8,128)(2,1)S(1)}, bf16[2048,512]{1,0:T(8,128)(2,1)S(1)}, bf16[2048,512]{1,0:T(8,128)(2,...) custom-call(s32[8,125]{1,0:T(8,128)} %bitcast.7, ...), custom_call_target="tpu_custom_call" | custom-call | bytes 1024 | tf_op jit(solution)/shard_map/attend/pallas_call | solution.py:135
  20.2 2.3 %give.3 = (bf16[256,512]{1,0:T(8,128)(2,1)S(1)}, bf16[256,512]{1,0:T(8,128)(2,1)S(1)}, bf16[2048,512]{1,0:T(8,128)(2,1)S(1)}, bf16[2048,512]{1,0:T(8,128)(2,1)S(1)}) custom-call(bf16[512,2048]{1,0:T(8,128)(2,1)S(1)} %get-tuple-element.51.refs_0_.refs_5_, bf16[2048,512]{1,0:T(8,128)(2,1)S(1)} %get-tuple-element.52.refs_1_, ...), custom_call_target="tpu_custom_call" | custom-call | bytes 1024 | tf_op jit(solution)/shard_map/give/pallas_call | solution.py:135
  22.5 0.5 collective-permute-start.2
  23.0 1.8 %give.4 = (bf16[256,512]{1,0:T(8,128)(2,1)S(1)}, bf16[256,512]{1,0:T(8,128)(2,1)S(1)}) custom-call(bf16[512,2048]{1,0:T(8,128)(2,1)S(1)} %get-tuple-element.51.refs_0_.refs_5_, bf16[2048,512]{1,0:T(8,128)(2,1)S(1)} %get-tuple-element.56.refs_1_.refs_3_, bf16[2048,512]{1,0:T(8,128)(2,1)S(1)} %get-tuple-element.57.refs_2_.refs_4_, ...), custom_call_target="tpu_custom_call" | custom-call | bytes 1024 | tf_op jit(solution)/shard_map/give/pallas_call | solution.py:135
  25.0 0.4 collective-permute-start
  25.4 1.8 %keep.3.refs_5_ = bf16[256,1024]{1,0:T(8,128)(2,1)S(1)} custom-call(bf16[512,2048]{1,0:T(8,128)(2,1)S(1)} %get-tuple-element.51.refs_0_.refs_5_, bf16[2048,512]{1,0:T(8,128)(2,1)S(1)} %get-tuple-element.61.refs_1_, bf16[2048,512]{1,0:T(8,128)(2,1)S(1)} %get-tuple-element.62.refs_2_, bf16[256,512]{1,0:T(8,128)(2,1)S(1)} %collective-permute-done.2.refs_3_, ...), custom_call_target="tpu_custom_call" | custom-call | bytes 1024 | tf_op jit(solution)/shard_map/keep/pallas_call | solution.py:135
  27.3 1.8 %keep.4.refs_6_ = bf16[256,1024]{1,0:T(8,128)(2,1)S(1)} custom-call(bf16[512,2048]{1,0:T(8,128)(2,1)S(1)} %get-tuple-element.51.refs_0_.refs_5_, bf16[2048,512]{1,0:T(8,128)(2,1)S(1)} %get-tuple-element.54.refs_1_.refs_3_, bf16[2048,512]{1,0:T(8,128)(2,1)S(1)} %get-tuple-element.55.refs_2_.refs_4_, bf16[256,512]{1,0:T(8,128)(2,1)S(1)} %collective-permute-done.refs_3_, ...), custom_call_target="tpu_custom_call" | custom-call | bytes 1024 | tf_op jit(solution)/shard_map/keep/pallas_call | solution.py:135
  29.1 7.7 %attend.3.refs_0_.refs_5_ = bf16[512,2048]{1,0:T(8,128)(2,1)S(1)} custom-call(s32[8,125]{1,0:T(8,128)} %bitcast.8, s32[1,125]{1,0:T(1,128)} %refs_1_.6, bf16[8192,128]{1,0:T(8,128)(2,1)} %bitcast.6, bf16[128,4,2,256]{3,2,1,0:T(2,128)(2,1)} %refs_3_.7, bf16[1,2,64,16,256]{4,3,2,1,0:T(8,128)(2,1)} %refs_4_.5, ...), custom_call_target="tpu_custom_call", output_to_operand_aliasing={{}: (5, {})} | custom-call | bytes 1024 | tf_op jit(solution)/shard_map/attend/pallas_call | solution.py:135
  36.8 3.6 %give.5 = (bf16[256,512]{1,0:T(8,128)(2,1)S(1)}, bf16[256,512]{1,0:T(8,128)(2,1)S(1)}, bf16[256,512]{1,0:T(8,128)(2,1)S(1)}, bf16[256,512]{1,0:T(8,128)(2,1)S(1)}) custom-call(bf16[512,2048]{1,0:T(8,128)(2,1)S(1)} %attend.3.refs_0_.refs_5_, bf16[2048,512]{1,0:T(8,128)(2,1)S(1)} %get-tuple-element.52.refs_1_, ...), custom_call_target="tpu_custom_call" | custom-call | bytes 1024 | tf_op jit(solution)/shard_map/give/pallas_call | solution.py:135
  40.6 1.5 %collective-permute-start.9 = (bf16[256,1024]{1,0:T(8,128)(2,1)S(1)}, bf16[256,1024]{1,0:T(8,128)(2,1)S(1)}, u32[]{:S(2)}, u32[]{:S(2)}) collective-permute-start(bf16[256,1024]{1,0:T(8,128)(2,1)S(1)} %keep.4.refs_6_), channel_id=1, source_target_pairs={{0,2},{1,3},{2,0},{3,1},{4,6},{5,7},{6,4},{7,5},{8,10},{9,11},{10,... | collective-permute-start | bytes 1572872 | tf_op jit(solution)/shard_map/ppermute | solution.py:608
  42.1 0.5 collective-permute-start.8
  42.6 0.5 collective-permute-start.7
  43.1 1.0 %collective-permute-done.6.refs_7_ = bf16[256,512]{1,0:T(8,128)(2,1)S(1)} collective-permute-done((bf16[256,512]{1,0:T(8,128)(2,1)S(1)}, bf16[256,512]{1,0:T(8,128)(2,1)S(1)}, u32[]{:S(2)}, u32[]{:S(2)}) %collective-permute-start.6) | collective-permute-done | bytes 262176 | tf_op jit(solution)/shard_map/ppermute | solution.py:604
  44.5 0.4 collective-permute-done.4.refs_5_
  44.9 10.4 %collective-permute-done.9.refs_11_.refs_3_ = bf16[256,1024]{1,0:T(8,128)(2,1)S(1)} collective-permute-done((bf16[256,1024]{1,0:T(8,128)(2,1)S(1)}, bf16[256,1024]{1,0:T(8,128)(2,1)S(1)}, u32[]{:S(2)}, u32[]{:S(2)}) %collective-permute-start.9) | collective-permute-done | bytes 524320 | tf_op jit(solution)/shard_map/ppermute | solution.py:608
  55.3 10.8 %collective-permute-done.8.refs_10_.refs_2_ = bf16[256,1024]{1,0:T(8,128)(2,1)S(1)} collective-permute-done((bf16[256,1024]{1,0:T(8,128)(2,1)S(1)}, bf16[256,1024]{1,0:T(8,128)(2,1)S(1)}, u32[]{:S(2)}, u32[]{:S(2)}) %collective-permute-start.8) | collective-permute-done | bytes 524320 | tf_op jit(solution)/shard_map/ppermute | solution.py:608
  66.1 3.6 %keep.5.refs_7_ = bf16[256,2048]{1,0:T(8,128)(2,1)S(1)} custom-call(bf16[512,2048]{1,0:T(8,128)(2,1)S(1)} %attend.3.refs_0_.refs_5_, bf16[2048,512]{1,0:T(8,128)(2,1)S(1)} %get-tuple-element.61.refs_1_, bf16[2048,512]{1,0:T(8,128)(2,1)S(1)} %get-tuple-element.62.refs_2_, bf16[2048,512]{1,0:T(8,128)(2,1)S(1)} %get-tuple-element.54.refs_1_.refs_3_, ...), custom_call_target="tpu_custom_call" | custom-call | bytes 1024 | tf_op jit(solution)/shard_map/keep/pallas_call | solution.py:135
  69.7 1.6 %collective-permute-start.15 = (bf16[256,2048]{1,0:T(8,128)(2,1)S(1)}, bf16[256,2048]{1,0:T(8,128)(2,1)}, u32[]{:S(2)}, u32[]{:S(2)}) collective-permute-start(bf16[256,2048]{1,0:T(8,128)(2,1)S(1)} %keep.5.refs_7_), channel_id=1, source_target_pairs={{0,2},{1,3},{2,0},{3,1},{4,6},{5,7},{6,4},{7,5},{8,10},{9,11},{10,... | collective-permute-start | bytes 3145736 | tf_op jit(solution)/shard_map/ppermute | solution.py:608
  71.3 6.1 %settle.1 = (bf16[512,2048]{1,0:T(8,128)(2,1)S(1)}, bf16[16,2048]{1,0:T(8,128)(2,1)S(1)}, bf16[1,3,2,512,256]{4,3,2,1,0:T(8,128)(2,1)}, bf16[2048,512]{1,0:T(8,1...) custom-call(s32[8]{0:T(128)} %refs_0_.3, s32[8]{0:T(128)} %refs_1_.7, ...), custom_call_target="tpu_custom_call", output_to_operand_aliasing={{0}: (5, {})} | custom-call | bytes 1024 | tf_op jit(solution)/shard_map/settle/pallas_call | solution.py:135
  77.4 2.9 %give_own.2 = (bf16[512,512]{1,0:T(8,128)(2,1)S(1)}, bf16[512,512]{1,0:T(8,128)(2,1)S(1)}, bf16[2048,512]{1,0:T(8,128)(2,1)S(1)}, bf16[2048,512]{1,0:T(8,128)(2,1)S(1)}, bf16[2048,512]{1,0:T(8,128)(2,1)S(1)}) custom-call(bf16[512,2048]{1,0:T(8,128)(2,1)S(1)} %get-tuple-element.69.refs_0_, bf16[2048,512]{1,0:T(8,128)(2,1)S(1)} %get-tuple-element.72.refs_1_, ...), custom_call_target="tpu_custom_call" | custom-call | bytes 1024 | tf_op jit(solution)/shard_map/give_own/pallas_call | solution.py:135
  80.4 2.3 %give_last.1 = (bf16[16,2048]{1,0:T(8,128)(2,1)S(1)}, bf16[2048,512]{1,0:T(8,128)(2,1)S(1)}, bf16[2048,512]{1,0:T(8,128)(2,1)S(1)}) custom-call(bf16[16,2048]{1,0:T(8,128)(2,1)S(1)} %get-tuple-element.70.refs_0_, bf16[2048,512]{1,0:T(8,128)(2,1)S(1)} %get-tuple-element.71.refs_1_, bf16[2048,512]{1,0:T(8,128)(2,1)S(1)} %get-tuple-element.74.refs_2_, ...), custom_call_target="tpu_custom_call" | custom-call | bytes 1024 | tf_op jit(solution)/shard_map/give_last/pallas_call | solution.py:135
  82.7 0.5 collective-permute-start.12
  83.3 3.5 %give_own.3 = (bf16[512,512]{1,0:T(8,128)(2,1)S(1)}, bf16[512,512]{1,0:T(8,128)(2,1)S(1)}, bf16[2048,512]{1,0:T(8,128)(2,1)S(1)}, bf16[2048,512]{1,0:T(8,128)(2,...) custom-call(bf16[512,2048]{1,0:T(8,128)(2,1)S(1)} %get-tuple-element.69.refs_0_, ...), custom_call_target="tpu_custom_call" | custom-call | bytes 1024 | tf_op jit(solution)/shard_map/give_own/pallas_call | solution.py:135
  86.9 0.5 collective-permute-start.14
  87.5 2.3 %keep_last.1 = (bf16[16,2048]{1,0:T(8,128)(2,1)S(1)}, bf16[2048,512]{1,0:T(8,128)(2,1)S(1)}, bf16[2048,512]{1,0:T(8,128)(2,1)S(1)}) custom-call(bf16[16,2048]{1,0:T(8,128)(2,1)S(1)} %get-tuple-element.70.refs_0_, bf16[2048,512]{1,0:T(8,128)(2,1)S(1)} %get-tuple-element.81.refs_1_, bf16[2048,512]{1,0:T(8,128)(2,1)S(1)} %get-tuple-element.82.refs_2_, ...), custom_call_target="tpu_custom_call" | custom-call | bytes 1024 | tf_op jit(solution)/shard_map/keep_last/pallas_call | solution.py:135
  89.7 0.6 collective-permute-start.16
  90.3 2.9 %keep_own.2 = (f32[512,1024]{1,0:T(8,128)S(1)}, bf16[2048,512]{1,0:T(8,128)(2,1)S(1)}, bf16[2048,512]{1,0:T(8,128)(2,1)S(1)}) custom-call(bf16[512,2048]{1,0:T(8,128)(2,1)S(1)} %get-tuple-element.69.refs_0_, bf16[2048,512]{1,0:T(8,128)(2,1)S(1)} %get-tuple-element.86.refs_1_, bf16[2048,512]{1,0:T(8,128)(2,1)S(1)} %get-tuple-element.87.refs_2_, ...), custom_call_target="tpu_custom_call" | custom-call | bytes 1024 | tf_op jit(solution)/shard_map/keep_own/pallas_call | solution.py:135
  93.3 2.9 %keep_own.3.refs_1_ = f32[512,1024]{1,0:T(8,128)S(1)} custom-call(bf16[512,2048]{1,0:T(8,128)(2,1)S(1)} %get-tuple-element.69.refs_0_, bf16[2048,512]{1,0:T(8,128)(2,1)S(1)} %get-tuple-element.91.refs_1_, bf16[2048,512]{1,0:T(8,128)(2,1)S(1)} %get-tuple-element.92.refs_2_, bf16[512,512]{1,0:T(8,128)(2,1)S(1)} %collective-permute-done.13.refs_3_, ...), custom_call_target="tpu_custom_call" | custom-call | bytes 1024 | tf_op jit(solution)/shard_map/keep_own/pallas_call | solution.py:135
  96.2 3.3 %finish.1 = bf16[2048,512]{1,0:T(8,128)(2,1)} custom-call(f32[512,1024]{1,0:T(8,128)S(1)} %get-tuple-element.90.refs_5_.refs_0_, f32[512,1024]{1,0:T(8,128)S(1)} %keep_own.3.refs_1_, bf16[256,1024]{1,0:T(8,128)(2,1)S(1)} %copy-done.4, bf16[256,1024]{1,0:T(8,128)(2,1)S(1)} %copy-done.2, bf16[256,2048]{1,0:T(8,128)(2,1)} %collective-permute-done.15.refs_4_, ...), custom_call_target="tpu_custom_call" | custom-call | bytes 1024 | tf_op jit(solution)/shard_map/finish/pallas_call | solution.py:135
  (31 shorter events, 1.0 us)
Async XLA Ops:
  4.4 67.0 %all-to-all-start = ((bf16[4,2,32,16,256]{4,3,2,1,0:T(8,128)(2,1)}), bf16[4,2,32,16,256]{4,3,2,1,0:T(8,128)(2,1)}, u32[]{:S(2)}, u32[]{:S(2)}) async-start(bf16[4,2,32,16,256]{4,3,2,1,0:T(8,128)(2,1)} %get-tuple-element.48.refs_6_), calls=%async_computation | async-start | bytes 4194304 | tf_op jit(solution)/shard_map/all_to_all | solution.py:655
  10.7 1.6 %copy-start = (bf16[4,2,32,16,256]{4,3,2,1,0:T(8,128)(2,1)S(1)}, bf16[4,2,32,16,256]{4,3,2,1,0:T(8,128)(2,1)}, u32[]{:S(2)}) copy-start(bf16[4,2,32,16,256]{4,3,2,1,0:T(8,128)(2,1)} %get-tuple-element.48.refs_6_) | copy-start | bytes 6291460
  22.5 3.0 %collective-permute-start.3 = (bf16[256,512]{1,0:T(8,128)(2,1)S(1)}, bf16[256,512]{1,0:T(8,128)(2,1)S(1)}, u32[]{:S(2)}, u32[]{:S(2)}) collective-permute-start(bf16[256,512]{1,0:T(8,128)(2,1)S(1)} %get-tuple-element.63), channel_id=1, source_target_pairs={{0,1},{1,0},{2,3},{3,2},{4,5},{5,4},{6,7},{7,6},{8,9},{9,8},{10,11... | collective-permute-start | bytes 786440 | tf_op jit(solution)/shard_map/ppermute | solution.py:604
  22.5 2.9 %collective-permute-start.2 = (bf16[256,512]{1,0:T(8,128)(2,1)S(1)}, bf16[256,512]{1,0:T(8,128)(2,1)S(1)}, u32[]{:S(2)}, u32[]{:S(2)}) collective-permute-start(bf16[256,512]{1,0:T(8,128)(2,1)S(1)} %get-tuple-element.58.refs_3_), channel_id=1, source_target_pairs={{0,1},{1,0},{2,3},{3,2},{4,5},{5,4},{6,7},{7,6},{8,9},{9,8},{10,11... | collective-permute-start | bytes 786440 | tf_op jit(solution)/shard_map/ppermute | solution.py:604
  24.8 2.4 %collective-permute-start.1 = (bf16[256,512]{1,0:T(8,128)(2,1)S(1)}, bf16[256,512]{1,0:T(8,128)(2,1)S(1)}, u32[]{:S(2)}, u32[]{:S(2)}) collective-permute-start(bf16[256,512]{1,0:T(8,128)(2,1)S(1)} %get-tuple-element.60), channel_id=1, source_target_pairs={{0,1},{1,0},{2,3},{3,2},{4,5},{5,4},{6,7},{7,6},{8,9},{9,8},{10,11... | collective-permute-start | bytes 786440 | tf_op jit(solution)/shard_map/ppermute | solution.py:604
  25.0 2.3 %collective-permute-start = (bf16[256,512]{1,0:T(8,128)(2,1)S(1)}, bf16[256,512]{1,0:T(8,128)(2,1)S(1)}, u32[]{:S(2)}, u32[]{:S(2)}) collective-permute-start(bf16[256,512]{1,0:T(8,128)(2,1)S(1)} %get-tuple-element.59.refs_5_), channel_id=1, source_target_pairs={{0,1},{1,0},{2,3},{3,2},{4,5},{5,4},{6,7},{7,6},{8,9},{9,8},{10,11... | collective-permute-start | bytes 786440 | tf_op jit(solution)/shard_map/ppermute | solution.py:604
  40.4 2.7 %collective-permute-start.5 = (bf16[256,512]{1,0:T(8,128)(2,1)S(1)}, bf16[256,512]{1,0:T(8,128)(2,1)S(1)}, u32[]{:S(2)}, u32[]{:S(2)}) collective-permute-start(bf16[256,512]{1,0:T(8,128)(2,1)S(1)} %get-tuple-element.65), channel_id=1, source_target_pairs={{0,1},{1,0},{2,3},{3,2},{4,5},{5,4},{6,7},{7,6},{8,9},{9,8},{10,11... | collective-permute-start | bytes 786440 | tf_op jit(solution)/shard_map/ppermute | solution.py:604
  40.6 14.7 %collective-permute-start.9 = (bf16[256,1024]{1,0:T(8,128)(2,1)S(1)}, bf16[256,1024]{1,0:T(8,128)(2,1)S(1)}, u32[]{:S(2)}, u32[]{:S(2)}) collective-permute-start(bf16[256,1024]{1,0:T(8,128)(2,1)S(1)} %keep.4.refs_6_), channel_id=1, source_target_pairs={{0,2},{1,3},{2,0},{3,1},{4,6},{5,7},{6,4},{7,5},{8,10},{9,11},{10,... | collective-permute-start | bytes 1572872 | tf_op jit(solution)/shard_map/ppermute | solution.py:608
  42.1 24.0 %collective-permute-start.8 = (bf16[256,1024]{1,0:T(8,128)(2,1)S(1)}, bf16[256,1024]{1,0:T(8,128)(2,1)S(1)}, u32[]{:S(2)}, u32[]{:S(2)}) collective-permute-start(bf16[256,1024]{1,0:T(8,128)(2,1)S(1)} %keep.3.refs_5_), channel_id=1, source_target_pairs={{0,2},{1,3},{2,0},{3,1},{4,6},{5,7},{6,4},{7,5},{8,10},{9,11},{10,... | collective-permute-start | bytes 1572872 | tf_op jit(solution)/shard_map/ppermute | solution.py:608
  42.6 1.5 %collective-permute-start.6 = (bf16[256,512]{1,0:T(8,128)(2,1)S(1)}, bf16[256,512]{1,0:T(8,128)(2,1)S(1)}, u32[]{:S(2)}, u32[]{:S(2)}) collective-permute-start(bf16[256,512]{1,0:T(8,128)(2,1)S(1)} %get-tuple-element.66), channel_id=1, source_target_pairs={{0,1},{1,0},{2,3},{3,2},{4,5},{5,4},{6,7},{7,6},{8,9},{9,8},{10,11... | collective-permute-start | bytes 786440 | tf_op jit(solution)/shard_map/ppermute | solution.py:604
  42.6 1.9 %collective-permute-start.7 = (bf16[256,512]{1,0:T(8,128)(2,1)S(1)}, bf16[256,512]{1,0:T(8,128)(2,1)S(1)}, u32[]{:S(2)}, u32[]{:S(2)}) collective-permute-start(bf16[256,512]{1,0:T(8,128)(2,1)S(1)} %get-tuple-element.67), channel_id=1, source_target_pairs={{0,1},{1,0},{2,3},{3,2},{4,5},{5,4},{6,7},{7,6},{8,9},{9,8},{10,11... | collective-permute-start | bytes 786440 | tf_op jit(solution)/shard_map/ppermute | solution.py:604
  43.1 1.8 %collective-permute-start.4 = (bf16[256,512]{1,0:T(8,128)(2,1)S(1)}, bf16[256,512]{1,0:T(8,128)(2,1)S(1)}, u32[]{:S(2)}, u32[]{:S(2)}) collective-permute-start(bf16[256,512]{1,0:T(8,128)(2,1)S(1)} %get-tuple-element.64.refs_9_), channel_id=1, source_target_pairs={{0,1},{1,0},{2,3},{3,2},{4,5},{5,4},{6,7},{7,6},{8,9},{9,8},{10,11... | collective-permute-start | bytes 786440 | tf_op jit(solution)/shard_map/ppermute | solution.py:604
  55.3 14.4 %copy-start.1 = (bf16[256,1024]{1,0:T(8,128)(2,1)}, bf16[256,1024]{1,0:T(8,128)(2,1)S(1)}, u32[]{:S(2)}) copy-start(bf16[256,1024]{1,0:T(8,128)(2,1)S(1)} %collective-permute-done.9.refs_11_.refs_3_) | copy-start | bytes 1572868
  66.1 3.6 %copy-start.3 = (bf16[256,1024]{1,0:T(8,128)(2,1)}, bf16[256,1024]{1,0:T(8,128)(2,1)S(1)}, u32[]{:S(2)}) copy-start(bf16[256,1024]{1,0:T(8,128)(2,1)S(1)} %collective-permute-done.8.refs_10_.refs_2_) | copy-start | bytes 1572868
  69.7 26.4 %collective-permute-start.15 = (bf16[256,2048]{1,0:T(8,128)(2,1)S(1)}, bf16[256,2048]{1,0:T(8,128)(2,1)}, u32[]{:S(2)}, u32[]{:S(2)}) collective-permute-start(bf16[256,2048]{1,0:T(8,128)(2,1)S(1)} %keep.5.refs_7_), channel_id=1, source_target_pairs={{0,2},{1,3},{2,0},{3,1},{4,6},{5,7},{6,4},{7,5},{8,10},{9,11},{10,... | collective-permute-start | bytes 3145736 | tf_op jit(solution)/shard_map/ppermute | solution.py:608
  82.7 4.7 %collective-permute-start.10 = (bf16[16,2048]{1,0:T(8,128)(2,1)S(1)}, bf16[16,2048]{1,0:T(8,128)(2,1)S(1)}, u32[]{:S(2)}, u32[]{:S(2)}) collective-permute-start(bf16[16,2048]{1,0:T(8,128)(2,1)S(1)} %get-tuple-element.80.refs_4_), channel_id=1, source_target_pairs={{0,1},{1,0},{2,3},{3,2},{4,5},{5,4},{6,7},{7,6},{8,9},{9,8},{10,11... | collective-permute-start | bytes 196616 | tf_op jit(solution)/shard_map/ppermute | solution.py:604
  82.7 7.0 %collective-permute-start.12 = (bf16[512,512]{1,0:T(8,128)(2,1)S(1)}, bf16[512,512]{1,0:T(8,128)(2,1)S(1)}, u32[]{:S(2)}, u32[]{:S(2)}) collective-permute-start(bf16[512,512]{1,0:T(8,128)(2,1)S(1)} %get-tuple-element.88), channel_id=1, source_target_pairs={{0,1},{1,0},{2,3},{3,2},{4,5},{5,4},{6,7},{7,6},{8,9},{9,8},{10,11... | collective-permute-start | bytes 1572872 | tf_op jit(solution)/shard_map/ppermute | solution.py:604
  83.2 7.1 %collective-permute-start.11 = (bf16[512,512]{1,0:T(8,128)(2,1)S(1)}, bf16[512,512]{1,0:T(8,128)(2,1)S(1)}, u32[]{:S(2)}, u32[]{:S(2)}) collective-permute-start(bf16[512,512]{1,0:T(8,128)(2,1)S(1)} %get-tuple-element.77.refs_6_), channel_id=1, source_target_pairs={{0,1},{1,0},{2,3},{3,2},{4,5},{5,4},{6,7},{7,6},{8,9},{9,8},{10,11... | collective-permute-start | bytes 1572872 | tf_op jit(solution)/shard_map/ppermute | solution.py:604
  86.9 6.3 %collective-permute-start.14 = (bf16[512,512]{1,0:T(8,128)(2,1)S(1)}, bf16[512,512]{1,0:T(8,128)(2,1)S(1)}, u32[]{:S(2)}, u32[]{:S(2)}) collective-permute-start(bf16[512,512]{1,0:T(8,128)(2,1)S(1)} %get-tuple-element.93), channel_id=1, source_target_pairs={{0,1},{1,0},{2,3},{3,2},{4,5},{5,4},{6,7},{7,6},{8,9},{9,8},{10,11... | collective-permute-start | bytes 1572872 | tf_op jit(solution)/shard_map/ppermute | solution.py:604
  87.4 5.9 %collective-permute-start.13 = (bf16[512,512]{1,0:T(8,128)(2,1)S(1)}, bf16[512,512]{1,0:T(8,128)(2,1)S(1)}, u32[]{:S(2)}, u32[]{:S(2)}) collective-permute-start(bf16[512,512]{1,0:T(8,128)(2,1)S(1)} %get-tuple-element.85.refs_7_), channel_id=1, source_target_pairs={{0,1},{1,0},{2,3},{3,2},{4,5},{5,4},{6,7},{7,6},{8,9},{9,8},{10,11... | collective-permute-start | bytes 1572872 | tf_op jit(solution)/shard_map/ppermute | solution.py:604
  89.7 6.4 %collective-permute-start.16 = (bf16[16,2048]{1,0:T(8,128)(2,1)S(1)}, bf16[16,2048]{1,0:T(8,128)(2,1)S(1)}, u32[]{:S(2)}, u32[]{:S(2)}) collective-permute-start(bf16[16,2048]{1,0:T(8,128)(2,1)S(1)} %get-tuple-element.89.refs_6_), channel_id=1, source_target_pairs={{0,2},{1,3},{2,0},{3,1},{4,6},{5,7},{6,4},{7,5},{8,10},{9,11},{10,... | collective-permute-start | bytes 196616 | tf_op jit(solution)/shard_map/ppermute | solution.py:608
  93.2 2.9 %copy-start.2 = (bf16[256,1024]{1,0:T(8,128)(2,1)S(1)}, bf16[256,1024]{1,0:T(8,128)(2,1)}, u32[]{:S(2)}) copy-start(bf16[256,1024]{1,0:T(8,128)(2,1)} %copy-done.1) | copy-start | bytes 1572868
  93.2 2.9 %copy-start.4 = (bf16[256,1024]{1,0:T(8,128)(2,1)S(1)}, bf16[256,1024]{1,0:T(8,128)(2,1)}, u32[]{:S(2)}) copy-start(bf16[256,1024]{1,0:T(8,128)(2,1)} %copy-done.3) | copy-start | bytes 1572868

commit v15 on v13

--- a/solution.py
+++ b/solution.py
@@ -663,8 +663,8 @@
         table, res_len, query_rows, new_kv, res_pool, rows, half, half, z, kept[-1:],
     )
     b = (rows, tokens, tokens)
-    given, mates = give(b, far, every, "give", [])
-    kept = keep(b, far, every, mates, "keep", [given] + got_low)
+    given, mates = give(b, far, every, "give", got_low)
+    kept = keep(b, far, every, mates, "keep", [given] + got_high)
     got_second = sent(kept)
 
     tail_q, tail_kv = (
@@ -672,7 +672,7 @@
     )
     pieces = gives([0], low) + gives(far, (0,))
     (rows, last, arrived), new = settle(
-        mig_dest, mig_len, arriving, tail_q, tail_kv, rows, z, kept[-1:] + got_high,
+        mig_dest, mig_len, arriving, tail_q, tail_kv, rows, z, kept[-1:],
         **bringing(pieces),
     )
     hold(pieces, new)

time: 89.8 us -> 88.7 us (0.988)
  local copies, waits for them, and re-layouts: 3.48 us -> 1.64 us
    ppermute x4, waiting for transfers between devices: 9.01 us -> 6.88 us  [across(): return lax.ppermute(x, 'tp', [(i, (i + shift) % tps) for i in range(tps)])]
    all_to_all x1, waiting for transfers between devices: 0.01 us -> 1.87 us  [shards(): lax.all_to_all(sends, 'inst', split_axis=0, concat_axis=0, tiled=True)]
    unnamed x12 -> x10, local copies, waits for them, and re-layouts: 3.48 us -> 1.64 us
  transfers between devices with their start and end apart: 18 -> 18, of which waited for: 4 -> 5; matrix products, arithmetic and copies ran while one was open for 0% -> 0% of each run, Pallas kernels for 60% -> 60%
where the time goes in v15:
time: 88.7 us; the launch traced here: 88.2 us
  Pallas kernels  60.3 us (68%)
  starting transfers between devices  15 us (17%)
  waiting for transfers between devices  10.2 us (11%)
  local copies, waits for them, and re-layouts  1.64 us (2%)
  between operations  1.08 us (1%)
    pallas_call x17, Pallas kernels, run(): pl.pallas_call(call, grid_spec=pltpu.PrefetchScalarGridSpec(num_scalar_pr...  60.3 us
    ppermute x4, waiting for transfers between devices, across(): return lax.ppermute(x, 'tp', [(i, (i + shift) % tps) for i in range(tps)])  6.88 us
    all_to_all x1, starting transfers between devices, shards(): lax.all_to_all(sends, 'inst', split_axis=0, concat_axis=0, tiled=True)  6.33 us
    ppermute x4, starting transfers between devices, across(): return lax.ppermute(x, 'tp', [(i, (i + shift) % tps) for i in range(tps)])  5.33 us
    ppermute x13, starting transfers between devices, mate_of(): return lax.ppermute(x, 'tp', to_mate)  3.38 us
    all_to_all x1, waiting for transfers between devices, shards(): lax.all_to_all(sends, 'inst', split_axis=0, concat_axis=0, tiled=True)  1.87 us
  transfers between devices with their start and end apart: 18, of which 5 were waited for; matrix products, arithmetic and copies ran while one was open for 0% of the time, Pallas kernels for 60%

profile of v15, /device:TPU:0, one launch (start us, length us, event | category | flops | bytes accessed | tf_op | source)
XLA Modules:
  0.0 88.2 jit_solution(15418758155225457992)
XLA Ops:
  0.6 3.6 %pack.1 = (bf16[4,2,32,16,256]{4,3,2,1,0:T(8,128)(2,1)}, bf16[256,128]{1,0:T(8,128)(2,1)}, bf16[32,256]{1,0:T(8,128)(2,1)}) custom-call(s32[1,2,32]{2,1,0:T(2,128)} %refs_0_.2, s32[8]{0:T(128)} %refs_0_.3, bf16[1,2,64,16,256]{4,3,2,1,0:T(8,128)(2,1)} %refs_2_.1, bf16[8192,128]{1,0:T(8,128)(2,1)} %bitcast.4, bf16[128,4,2,256]{3,2,1,0:T(2,128)(2,1)} %refs_3_.7), custom_call_target="tpu_custom_call" | custom-call | bytes 1024 | tf_op jit(solution)/shard_map/pack/pallas_call | solution.py:135
  4.3 6.3 %all-to-all-start = ((bf16[4,2,32,16,256]{4,3,2,1,0:T(8,128)(2,1)}), bf16[4,2,32,16,256]{4,3,2,1,0:T(8,128)(2,1)}, u32[]{:S(2)}, u32[]{:S(2)}) async-start(bf16[4,2,32,16,256]{4,3,2,1,0:T(8,128)(2,1)} %get-tuple-element.48.refs_6_), calls=%async_computation | async-start | bytes 4194304 | tf_op jit(solution)/shard_map/all_to_all | solution.py:646
  10.6 1.6 %copy-done = bf16[4,2,32,16,256]{4,3,2,1,0:T(8,128)(2,1)S(1)} copy-done((bf16[4,2,32,16,256]{4,3,2,1,0:T(8,128)(2,1)S(1)}, bf16[4,2,32,16,256]{4,3,2,1,0:T(8,128)(2,1)}, u32[]{:S(2)}) %copy-start) | copy-done | bytes 2097176
  12.2 7.8 %attend.2 = (bf16[512,2048]{1,0:T(8,128)(2,1)S(1)}, bf16[2048,512]{1,0:T(8,128)(2,1)S(1)}, bf16[2048,512]{1,0:T(8,128)(2,1)S(1)}, bf16[2048,512]{1,0:T(8,128)(2,...) custom-call(s32[8,125]{1,0:T(8,128)} %bitcast.7, ...), custom_call_target="tpu_custom_call" | custom-call | bytes 1024 | tf_op jit(solution)/shard_map/attend/pallas_call | solution.py:135
  20.1 2.3 %give.3 = (bf16[256,512]{1,0:T(8,128)(2,1)S(1)}, bf16[256,512]{1,0:T(8,128)(2,1)S(1)}, bf16[2048,512]{1,0:T(8,128)(2,1)S(1)}, bf16[2048,512]{1,0:T(8,128)(2,1)S(1)}) custom-call(bf16[512,2048]{1,0:T(8,128)(2,1)S(1)} %get-tuple-element.51.refs_0_.refs_5_, bf16[2048,512]{1,0:T(8,128)(2,1)S(1)} %get-tuple-element.52.refs_1_, ...), custom_call_target="tpu_custom_call" | custom-call | bytes 1024 | tf_op jit(solution)/shard_map/give/pallas_call | solution.py:135
  22.4 0.5 collective-permute-start.2
  22.9 1.8 %give.4 = (bf16[256,512]{1,0:T(8,128)(2,1)S(1)}, bf16[256,512]{1,0:T(8,128)(2,1)S(1)}) custom-call(bf16[512,2048]{1,0:T(8,128)(2,1)S(1)} %get-tuple-element.51.refs_0_.refs_5_, bf16[2048,512]{1,0:T(8,128)(2,1)S(1)} %get-tuple-element.56.refs_1_.refs_3_, bf16[2048,512]{1,0:T(8,128)(2,1)S(1)} %get-tuple-element.57.refs_2_.refs_4_, ...), custom_call_target="tpu_custom_call" | custom-call | bytes 1024 | tf_op jit(solution)/shard_map/give/pallas_call | solution.py:135
  24.8 1.8 %keep.3.refs_5_ = bf16[256,1024]{1,0:T(8,128)(2,1)S(1)} custom-call(bf16[512,2048]{1,0:T(8,128)(2,1)S(1)} %get-tuple-element.51.refs_0_.refs_5_, bf16[2048,512]{1,0:T(8,128)(2,1)S(1)} %get-tuple-element.61.refs_1_, bf16[2048,512]{1,0:T(8,128)(2,1)S(1)} %get-tuple-element.62.refs_2_, bf16[256,512]{1,0:T(8,128)(2,1)S(1)} %collective-permute-done.2.refs_3_, ...), custom_call_target="tpu_custom_call" | custom-call | bytes 1024 | tf_op jit(solution)/shard_map/keep/pallas_call | solution.py:135
  26.6 1.6 %collective-permute-start.4 = (bf16[256,1024]{1,0:T(8,128)(2,1)S(1)}, bf16[256,1024]{1,0:T(8,128)(2,1)S(1)}, u32[]{:S(2)}, u32[]{:S(2)}) collective-permute-start(bf16[256,1024]{1,0:T(8,128)(2,1)S(1)} %keep.3.refs_5_), channel_id=1, source_target_pairs={{0,2},{1,3},{2,0},{3,1},{4,6},{5,7},{6,4},{7,5},{8,10},{9,11},{10,... | collective-permute-start | bytes 1572872 | tf_op jit(solution)/shard_map/ppermute | solution.py:599
  28.2 0.5 collective-permute-start
  28.7 1.0 %collective-permute-done.1.refs_4_ = bf16[256,512]{1,0:T(8,128)(2,1)S(1)} collective-permute-done((bf16[256,512]{1,0:T(8,128)(2,1)S(1)}, bf16[256,512]{1,0:T(8,128)(2,1)S(1)}, u32[]{:S(2)}, u32[]{:S(2)}) %collective-permute-start.1) | collective-permute-done | bytes 262176 | tf_op jit(solution)/shard_map/ppermute | solution.py:595
  30.1 1.8 %keep.4.refs_6_ = bf16[256,1024]{1,0:T(8,128)(2,1)S(1)} custom-call(bf16[512,2048]{1,0:T(8,128)(2,1)S(1)} %get-tuple-element.51.refs_0_.refs_5_, bf16[2048,512]{1,0:T(8,128)(2,1)S(1)} %get-tuple-element.54.refs_1_.refs_3_, bf16[2048,512]{1,0:T(8,128)(2,1)S(1)} %get-tuple-element.55.refs_2_.refs_4_, bf16[256,512]{1,0:T(8,128)(2,1)S(1)} %collective-permute-done.refs_3_, ...), custom_call_target="tpu_custom_call" | custom-call | bytes 1024 | tf_op jit(solution)/shard_map/keep/pallas_call | solution.py:135
  31.9 0.6 collective-permute-start.9
  32.5 7.7 %attend.3.refs_0_.refs_5_ = bf16[512,2048]{1,0:T(8,128)(2,1)S(1)} custom-call(s32[8,125]{1,0:T(8,128)} %bitcast.8, s32[1,125]{1,0:T(1,128)} %refs_1_.6, bf16[8192,128]{1,0:T(8,128)(2,1)} %bitcast.6, bf16[128,4,2,256]{3,2,1,0:T(2,128)(2,1)} %refs_3_.7, bf16[1,2,64,16,256]{4,3,2,1,0:T(8,128)(2,1)} %refs_4_.5, ...), custom_call_target="tpu_custom_call", output_to_operand_aliasing={{}: (5, {})} | custom-call | bytes 1024 | tf_op jit(solution)/shard_map/attend/pallas_call | solution.py:135
  40.2 1.2 %collective-permute-done.4.refs_5_.refs_2_ = bf16[256,1024]{1,0:T(8,128)(2,1)S(1)} collective-permute-done((bf16[256,1024]{1,0:T(8,128)(2,1)S(1)}, bf16[256,1024]{1,0:T(8,128)(2,1)S(1)}, u32[]{:S(2)}, u32[]{:S(2)}) %collective-permute-start.4) | collective-permute-done | bytes 524320 | tf_op jit(solution)/shard_map/ppermute | solution.py:599
  41.4 3.6 %give.5 = (bf16[256,512]{1,0:T(8,128)(2,1)S(1)}, bf16[256,512]{1,0:T(8,128)(2,1)S(1)}, bf16[256,512]{1,0:T(8,128)(2,1)S(1)}, bf16[256,512]{1,0:T(8,128)(2,1)S(1)}) custom-call(bf16[512,2048]{1,0:T(8,128)(2,1)S(1)} %attend.3.refs_0_.refs_5_, bf16[2048,512]{1,0:T(8,128)(2,1)S(1)} %get-tuple-element.52.refs_1_, ...), custom_call_target="tpu_custom_call" | custom-call | bytes 1024 | tf_op jit(solution)/shard_map/give/pallas_call | solution.py:135
  45.1 0.5 collective-permute-start.7
  46.1 5.7 %collective-permute-done.9.refs_10_.refs_3_ = bf16[256,1024]{1,0:T(8,128)(2,1)S(1)} collective-permute-done((bf16[256,1024]{1,0:T(8,128)(2,1)S(1)}, bf16[256,1024]{1,0:T(8,128)(2,1)S(1)}, u32[]{:S(2)}, u32[]{:S(2)}) %collective-permute-start.9) | collective-permute-done | bytes 524320 | tf_op jit(solution)/shard_map/ppermute | solution.py:599
  51.8 3.6 %keep.5.refs_7_ = bf16[256,2048]{1,0:T(8,128)(2,1)S(1)} custom-call(bf16[512,2048]{1,0:T(8,128)(2,1)S(1)} %attend.3.refs_0_.refs_5_, bf16[2048,512]{1,0:T(8,128)(2,1)S(1)} %get-tuple-element.61.refs_1_, bf16[2048,512]{1,0:T(8,128)(2,1)S(1)} %get-tuple-element.62.refs_2_, bf16[2048,512]{1,0:T(8,128)(2,1)S(1)} %get-tuple-element.54.refs_1_.refs_3_, ...), custom_call_target="tpu_custom_call" | custom-call | bytes 1024 | tf_op jit(solution)/shard_map/keep/pallas_call | solution.py:135
  55.5 1.6 %collective-permute-start.15 = (bf16[256,2048]{1,0:T(8,128)(2,1)S(1)}, bf16[256,2048]{1,0:T(8,128)(2,1)}, u32[]{:S(2)}, u32[]{:S(2)}) collective-permute-start(bf16[256,2048]{1,0:T(8,128)(2,1)S(1)} %keep.5.refs_7_), channel_id=1, source_target_pairs={{0,2},{1,3},{2,0},{3,1},{4,6},{5,7},{6,4},{7,5},{8,10},{9,11},{10,... | collective-permute-start | bytes 3145736 | tf_op jit(solution)/shard_map/ppermute | solution.py:599
  57.0 1.9 %all-to-all-done.refs_2_ = bf16[4,2,32,16,256]{4,3,2,1,0:T(8,128)(2,1)} async-done(((bf16[4,2,32,16,256]{4,3,2,1,0:T(8,128)(2,1)}), bf16[4,2,32,16,256]{4,3,2,1,0:T(8,128)(2,1)}, u32[]{:S(2)}, u32[]{:S(2)}) %all-to-all-start) | async-done | bytes 2097184 | tf_op jit(solution)/shard_map/all_to_all | solution.py:646
  58.9 6.0 %settle.1 = (bf16[512,2048]{1,0:T(8,128)(2,1)S(1)}, bf16[16,2048]{1,0:T(8,128)(2,1)S(1)}, bf16[1,3,2,512,256]{4,3,2,1,0:T(8,128)(2,1)}, bf16[2048,512]{1,0:T(8,1...) custom-call(s32[8]{0:T(128)} %refs_0_.3, s32[8]{0:T(128)} %refs_1_.7, ...), custom_call_target="tpu_custom_call", output_to_operand_aliasing={{0}: (5, {})} | custom-call | bytes 1024 | tf_op jit(solution)/shard_map/settle/pallas_call | solution.py:135
  64.9 3.0 %give_own.2 = (bf16[512,512]{1,0:T(8,128)(2,1)S(1)}, bf16[512,512]{1,0:T(8,128)(2,1)S(1)}, bf16[2048,512]{1,0:T(8,128)(2,1)S(1)}, bf16[2048,512]{1,0:T(8,128)(2,1)S(1)}, bf16[2048,512]{1,0:T(8,128)(2,1)S(1)}) custom-call(bf16[512,2048]{1,0:T(8,128)(2,1)S(1)} %get-tuple-element.69.refs_0_, bf16[2048,512]{1,0:T(8,128)(2,1)S(1)} %get-tuple-element.72.refs_1_, ...), custom_call_target="tpu_custom_call" | custom-call | bytes 1024 | tf_op jit(solution)/shard_map/give_own/pallas_call | solution.py:135
  67.9 2.3 %give_last.1 = (bf16[16,2048]{1,0:T(8,128)(2,1)S(1)}, bf16[2048,512]{1,0:T(8,128)(2,1)S(1)}, bf16[2048,512]{1,0:T(8,128)(2,1)S(1)}) custom-call(bf16[16,2048]{1,0:T(8,128)(2,1)S(1)} %get-tuple-element.70.refs_0_, bf16[2048,512]{1,0:T(8,128)(2,1)S(1)} %get-tuple-element.71.refs_1_, bf16[2048,512]{1,0:T(8,128)(2,1)S(1)} %get-tuple-element.74.refs_2_, ...), custom_call_target="tpu_custom_call" | custom-call | bytes 1024 | tf_op jit(solution)/shard_map/give_last/pallas_call | solution.py:135
  70.2 0.5 collective-permute-start.12
  70.8 3.5 %give_own.3 = (bf16[512,512]{1,0:T(8,128)(2,1)S(1)}, bf16[512,512]{1,0:T(8,128)(2,1)S(1)}, bf16[2048,512]{1,0:T(8,128)(2,1)S(1)}, bf16[2048,512]{1,0:T(8,128)(2,...) custom-call(bf16[512,2048]{1,0:T(8,128)(2,1)S(1)} %get-tuple-element.69.refs_0_, ...), custom_call_target="tpu_custom_call" | custom-call | bytes 1024 | tf_op jit(solution)/shard_map/give_own/pallas_call | solution.py:135
  74.4 0.5 collective-permute-start.14
  75.0 2.3 %keep_last.1 = (bf16[16,2048]{1,0:T(8,128)(2,1)S(1)}, bf16[2048,512]{1,0:T(8,128)(2,1)S(1)}, bf16[2048,512]{1,0:T(8,128)(2,1)S(1)}) custom-call(bf16[16,2048]{1,0:T(8,128)(2,1)S(1)} %get-tuple-element.70.refs_0_, bf16[2048,512]{1,0:T(8,128)(2,1)S(1)} %get-tuple-element.81.refs_1_, bf16[2048,512]{1,0:T(8,128)(2,1)S(1)} %get-tuple-element.82.refs_2_, ...), custom_call_target="tpu_custom_call" | custom-call | bytes 1024 | tf_op jit(solution)/shard_map/keep_last/pallas_call | solution.py:135
  77.2 1.6 %collective-permute-start.16 = (bf16[16,2048]{1,0:T(8,128)(2,1)S(1)}, bf16[16,2048]{1,0:T(8,128)(2,1)S(1)}, u32[]{:S(2)}, u32[]{:S(2)}) collective-permute-start(bf16[16,2048]{1,0:T(8,128)(2,1)S(1)} %get-tuple-element.89.refs_6_), channel_id=1, source_target_pairs={{0,2},{1,3},{2,0},{3,1},{4,6},{5,7},{6,4},{7,5},{8,10},{9,11},{10,... | collective-permute-start | bytes 196616 | tf_op jit(solution)/shard_map/ppermute | solution.py:599
  78.8 2.9 %keep_own.2 = (f32[512,1024]{1,0:T(8,128)S(1)}, bf16[2048,512]{1,0:T(8,128)(2,1)S(1)}, bf16[2048,512]{1,0:T(8,128)(2,1)S(1)}) custom-call(bf16[512,2048]{1,0:T(8,128)(2,1)S(1)} %get-tuple-element.69.refs_0_, bf16[2048,512]{1,0:T(8,128)(2,1)S(1)} %get-tuple-element.86.refs_1_, bf16[2048,512]{1,0:T(8,128)(2,1)S(1)} %get-tuple-element.87.refs_2_, ...), custom_call_target="tpu_custom_call" | custom-call | bytes 1024 | tf_op jit(solution)/shard_map/keep_own/pallas_call | solution.py:135
  81.8 2.9 %keep_own.3.refs_1_ = f32[512,1024]{1,0:T(8,128)S(1)} custom-call(bf16[512,2048]{1,0:T(8,128)(2,1)S(1)} %get-tuple-element.69.refs_0_, bf16[2048,512]{1,0:T(8,128)(2,1)S(1)} %get-tuple-element.91.refs_1_, bf16[2048,512]{1,0:T(8,128)(2,1)S(1)} %get-tuple-element.92.refs_2_, bf16[512,512]{1,0:T(8,128)(2,1)S(1)} %collective-permute-done.13.refs_3_, ...), custom_call_target="tpu_custom_call" | custom-call | bytes 1024 | tf_op jit(solution)/shard_map/keep_own/pallas_call | solution.py:135
  84.7 3.3 %finish.1 = bf16[2048,512]{1,0:T(8,128)(2,1)} custom-call(f32[512,1024]{1,0:T(8,128)S(1)} %get-tuple-element.90.refs_5_.refs_0_, f32[512,1024]{1,0:T(8,128)S(1)} %keep_own.3.refs_1_, bf16[256,1024]{1,0:T(8,128)(2,1)S(1)} %copy-done.4, bf16[256,1024]{1,0:T(8,128)(2,1)S(1)} %copy-done.2, bf16[256,2048]{1,0:T(8,128)(2,1)} %collective-permute-done.15.refs_4_, ...), custom_call_target="tpu_custom_call" | custom-call | bytes 1024 | tf_op jit(solution)/shard_map/finish/pallas_call | solution.py:135
  (31 shorter events, 1.3 us)
Async XLA Ops:
  4.3 54.6 %all-to-all-start = ((bf16[4,2,32,16,256]{4,3,2,1,0:T(8,128)(2,1)}), bf16[4,2,32,16,256]{4,3,2,1,0:T(8,128)(2,1)}, u32[]{:S(2)}, u32[]{:S(2)}) async-start(bf16[4,2,32,16,256]{4,3,2,1,0:T(8,128)(2,1)} %get-tuple-element.48.refs_6_), calls=%async_computation | async-start | bytes 4194304 | tf_op jit(solution)/shard_map/all_to_all | solution.py:646
  10.6 1.6 %copy-start = (bf16[4,2,32,16,256]{4,3,2,1,0:T(8,128)(2,1)S(1)}, bf16[4,2,32,16,256]{4,3,2,1,0:T(8,128)(2,1)}, u32[]{:S(2)}) copy-start(bf16[4,2,32,16,256]{4,3,2,1,0:T(8,128)(2,1)} %get-tuple-element.48.refs_6_) | copy-start | bytes 6291460
  22.4 2.4 %collective-permute-start.3 = (bf16[256,512]{1,0:T(8,128)(2,1)S(1)}, bf16[256,512]{1,0:T(8,128)(2,1)S(1)}, u32[]{:S(2)}, u32[]{:S(2)}) collective-permute-start(bf16[256,512]{1,0:T(8,128)(2,1)S(1)} %get-tuple-element.63), channel_id=1, source_target_pairs={{0,1},{1,0},{2,3},{3,2},{4,5},{5,4},{6,7},{7,6},{8,9},{9,8},{10,11... | collective-permute-start | bytes 786440 | tf_op jit(solution)/shard_map/ppermute | solution.py:595
  22.4 2.3 %collective-permute-start.2 = (bf16[256,512]{1,0:T(8,128)(2,1)S(1)}, bf16[256,512]{1,0:T(8,128)(2,1)S(1)}, u32[]{:S(2)}, u32[]{:S(2)}) collective-permute-start(bf16[256,512]{1,0:T(8,128)(2,1)S(1)} %get-tuple-element.58.refs_3_), channel_id=1, source_target_pairs={{0,1},{1,0},{2,3},{3,2},{4,5},{5,4},{6,7},{7,6},{8,9},{9,8},{10,11... | collective-permute-start | bytes 786440 | tf_op jit(solution)/shard_map/ppermute | solution.py:595
  26.6 14.8 %collective-permute-start.4 = (bf16[256,1024]{1,0:T(8,128)(2,1)S(1)}, bf16[256,1024]{1,0:T(8,128)(2,1)S(1)}, u32[]{:S(2)}, u32[]{:S(2)}) collective-permute-start(bf16[256,1024]{1,0:T(8,128)(2,1)S(1)} %keep.3.refs_5_), channel_id=1, source_target_pairs={{0,2},{1,3},{2,0},{3,1},{4,6},{5,7},{6,4},{7,5},{8,10},{9,11},{10,... | collective-permute-start | bytes 1572872 | tf_op jit(solution)/shard_map/ppermute | solution.py:599
  28.2 1.5 %collective-permute-start.1 = (bf16[256,512]{1,0:T(8,128)(2,1)S(1)}, bf16[256,512]{1,0:T(8,128)(2,1)S(1)}, u32[]{:S(2)}, u32[]{:S(2)}) collective-permute-start(bf16[256,512]{1,0:T(8,128)(2,1)S(1)} %get-tuple-element.60), channel_id=1, source_target_pairs={{0,1},{1,0},{2,3},{3,2},{4,5},{5,4},{6,7},{7,6},{8,9},{9,8},{10,11... | collective-permute-start | bytes 786440 | tf_op jit(solution)/shard_map/ppermute | solution.py:595
  28.2 1.9 %collective-permute-start = (bf16[256,512]{1,0:T(8,128)(2,1)S(1)}, bf16[256,512]{1,0:T(8,128)(2,1)S(1)}, u32[]{:S(2)}, u32[]{:S(2)}) collective-permute-start(bf16[256,512]{1,0:T(8,128)(2,1)S(1)} %get-tuple-element.59.refs_5_), channel_id=1, source_target_pairs={{0,1},{1,0},{2,3},{3,2},{4,5},{5,4},{6,7},{7,6},{8,9},{9,8},{10,11... | collective-permute-start | bytes 786440 | tf_op jit(solution)/shard_map/ppermute | solution.py:595
  31.9 19.9 %collective-permute-start.9 = (bf16[256,1024]{1,0:T(8,128)(2,1)S(1)}, bf16[256,1024]{1,0:T(8,128)(2,1)S(1)}, u32[]{:S(2)}, u32[]{:S(2)}) collective-permute-start(bf16[256,1024]{1,0:T(8,128)(2,1)S(1)} %keep.4.refs_6_), channel_id=1, source_target_pairs={{0,2},{1,3},{2,0},{3,1},{4,6},{5,7},{6,4},{7,5},{8,10},{9,11},{10,... | collective-permute-start | bytes 1572872 | tf_op jit(solution)/shard_map/ppermute | solution.py:599
  41.4 3.6 %copy-start.3 = (bf16[256,1024]{1,0:T(8,128)(2,1)}, bf16[256,1024]{1,0:T(8,128)(2,1)S(1)}, u32[]{:S(2)}) copy-start(bf16[256,1024]{1,0:T(8,128)(2,1)S(1)} %collective-permute-done.4.refs_5_.refs_2_) | copy-start | bytes 1572868
  45.0 6.8 %collective-permute-start.6 = (bf16[256,512]{1,0:T(8,128)(2,1)S(1)}, bf16[256,512]{1,0:T(8,128)(2,1)S(1)}, u32[]{:S(2)}, u32[]{:S(2)}) collective-permute-start(bf16[256,512]{1,0:T(8,128)(2,1)S(1)} %get-tuple-element.65), channel_id=1, source_target_pairs={{0,1},{1,0},{2,3},{3,2},{4,5},{5,4},{6,7},{7,6},{8,9},{9,8},{10,11... | collective-permute-start | bytes 786440 | tf_op jit(solution)/shard_map/ppermute | solution.py:595
  45.1 6.7 %collective-permute-start.7 = (bf16[256,512]{1,0:T(8,128)(2,1)S(1)}, bf16[256,512]{1,0:T(8,128)(2,1)S(1)}, u32[]{:S(2)}, u32[]{:S(2)}) collective-permute-start(bf16[256,512]{1,0:T(8,128)(2,1)S(1)} %get-tuple-element.66), channel_id=1, source_target_pairs={{0,1},{1,0},{2,3},{3,2},{4,5},{5,4},{6,7},{7,6},{8,9},{9,8},{10,11... | collective-permute-start | bytes 786440 | tf_op jit(solution)/shard_map/ppermute | solution.py:595
  45.6 6.2 %collective-permute-start.8 = (bf16[256,512]{1,0:T(8,128)(2,1)S(1)}, bf16[256,512]{1,0:T(8,128)(2,1)S(1)}, u32[]{:S(2)}, u32[]{:S(2)}) collective-permute-start(bf16[256,512]{1,0:T(8,128)(2,1)S(1)} %get-tuple-element.67), channel_id=1, source_target_pairs={{0,1},{1,0},{2,3},{3,2},{4,5},{5,4},{6,7},{7,6},{8,9},{9,8},{10,11... | collective-permute-start | bytes 786440 | tf_op jit(solution)/shard_map/ppermute | solution.py:595
  45.7 6.1 %collective-permute-start.5 = (bf16[256,512]{1,0:T(8,128)(2,1)S(1)}, bf16[256,512]{1,0:T(8,128)(2,1)S(1)}, u32[]{:S(2)}, u32[]{:S(2)}) collective-permute-start(bf16[256,512]{1,0:T(8,128)(2,1)S(1)} %get-tuple-element.64.refs_9_), channel_id=1, source_target_pairs={{0,1},{1,0},{2,3},{3,2},{4,5},{5,4},{6,7},{7,6},{8,9},{9,8},{10,11... | collective-permute-start | bytes 786440 | tf_op jit(solution)/shard_map/ppermute | solution.py:595
  51.8 3.7 %copy-start.1 = (bf16[256,1024]{1,0:T(8,128)(2,1)}, bf16[256,1024]{1,0:T(8,128)(2,1)S(1)}, u32[]{:S(2)}) copy-start(bf16[256,1024]{1,0:T(8,128)(2,1)S(1)} %collective-permute-done.9.refs_10_.refs_3_) | copy-start | bytes 1572868
  55.5 29.2 %collective-permute-start.15 = (bf16[256,2048]{1,0:T(8,128)(2,1)S(1)}, bf16[256,2048]{1,0:T(8,128)(2,1)}, u32[]{:S(2)}, u32[]{:S(2)}) collective-permute-start(bf16[256,2048]{1,0:T(8,128)(2,1)S(1)} %keep.5.refs_7_), channel_id=1, source_target_pairs={{0,2},{1,3},{2,0},{3,1},{4,6},{5,7},{6,4},{7,5},{8,10},{9,11},{10,... | collective-permute-start | bytes 3145736 | tf_op jit(solution)/shard_map/ppermute | solution.py:599
  70.2 4.7 %collective-permute-start.10 = (bf16[16,2048]{1,0:T(8,128)(2,1)S(1)}, bf16[16,2048]{1,0:T(8,128)(2,1)S(1)}, u32[]{:S(2)}, u32[]{:S(2)}) collective-permute-start(bf16[16,2048]{1,0:T(8,128)(2,1)S(1)} %get-tuple-element.80.refs_4_), channel_id=1, source_target_pairs={{0,1},{1,0},{2,3},{3,2},{4,5},{5,4},{6,7},{7,6},{8,9},{9,8},{10,11... | collective-permute-start | bytes 196616 | tf_op jit(solution)/shard_map/ppermute | solution.py:595
  70.2 7.0 %collective-permute-start.12 = (bf16[512,512]{1,0:T(8,128)(2,1)S(1)}, bf16[512,512]{1,0:T(8,128)(2,1)S(1)}, u32[]{:S(2)}, u32[]{:S(2)}) collective-permute-start(bf16[512,512]{1,0:T(8,128)(2,1)S(1)} %get-tuple-element.88), channel_id=1, source_target_pairs={{0,1},{1,0},{2,3},{3,2},{4,5},{5,4},{6,7},{7,6},{8,9},{9,8},{10,11... | collective-permute-start | bytes 1572872 | tf_op jit(solution)/shard_map/ppermute | solution.py:595
  70.7 8.1 %collective-permute-start.11 = (bf16[512,512]{1,0:T(8,128)(2,1)S(1)}, bf16[512,512]{1,0:T(8,128)(2,1)S(1)}, u32[]{:S(2)}, u32[]{:S(2)}) collective-permute-start(bf16[512,512]{1,0:T(8,128)(2,1)S(1)} %get-tuple-element.77.refs_6_), channel_id=1, source_target_pairs={{0,1},{1,0},{2,3},{3,2},{4,5},{5,4},{6,7},{7,6},{8,9},{9,8},{10,11... | collective-permute-start | bytes 1572872 | tf_op jit(solution)/shard_map/ppermute | solution.py:595
  74.4 7.4 %collective-permute-start.14 = (bf16[512,512]{1,0:T(8,128)(2,1)S(1)}, bf16[512,512]{1,0:T(8,128)(2,1)S(1)}, u32[]{:S(2)}, u32[]{:S(2)}) collective-permute-start(bf16[512,512]{1,0:T(8,128)(2,1)S(1)} %get-tuple-element.93), channel_id=1, source_target_pairs={{0,1},{1,0},{2,3},{3,2},{4,5},{5,4},{6,7},{7,6},{8,9},{9,8},{10,11... | collective-permute-start | bytes 1572872 | tf_op jit(solution)/shard_map/ppermute | solution.py:595
  74.9 6.9 %collective-permute-start.13 = (bf16[512,512]{1,0:T(8,128)(2,1)S(1)}, bf16[512,512]{1,0:T(8,128)(2,1)S(1)}, u32[]{:S(2)}, u32[]{:S(2)}) collective-permute-start(bf16[512,512]{1,0:T(8,128)(2,1)S(1)} %get-tuple-element.85.refs_7_), channel_id=1, source_target_pairs={{0,1},{1,0},{2,3},{3,2},{4,5},{5,4},{6,7},{7,6},{8,9},{9,8},{10,11... | collective-permute-start | bytes 1572872 | tf_op jit(solution)/shard_map/ppermute | solution.py:595
  77.2 7.5 %collective-permute-start.16 = (bf16[16,2048]{1,0:T(8,128)(2,1)S(1)}, bf16[16,2048]{1,0:T(8,128)(2,1)S(1)}, u32[]{:S(2)}, u32[]{:S(2)}) collective-permute-start(bf16[16,2048]{1,0:T(8,128)(2,1)S(1)} %get-tuple-element.89.refs_6_), channel_id=1, source_target_pairs={{0,2},{1,3},{2,0},{3,1},{4,6},{5,7},{6,4},{7,5},{8,10},{9,11},{10,... | collective-permute-start | bytes 196616 | tf_op jit(solution)/shard_map/ppermute | solution.py:599
  81.8 2.9 %copy-start.2 = (bf16[256,1024]{1,0:T(8,128)(2,1)S(1)}, bf16[256,1024]{1,0:T(8,128)(2,1)}, u32[]{:S(2)}) copy-start(bf16[256,1024]{1,0:T(8,128)(2,1)} %copy-done.1) | copy-start | bytes 1572868
  81.8 2.9 %copy-start.4 = (bf16[256,1024]{1,0:T(8,128)(2,1)S(1)}, bf16[256,1024]{1,0:T(8,128)(2,1)}, u32[]{:S(2)}) copy-start(bf16[256,1024]{1,0:T(8,128)(2,1)} %copy-done.3) | copy-start | bytes 1572868

commit v16 on v15

--- a/solution.py
+++ b/solution.py
@@ -155,11 +155,13 @@
 
 
 def pack_kernel(
-    ready, launch, table_ref, dest_ref, pool_ref, query_ref, kv_ref, send_hbm, tail_q_ref,
-    tail_kv_ref, pack_ref, sems, *, sizes
+    ready, launch, table_ref, dest_ref, pool_hbm, send_hbm, pool_ref, pack_ref, sems, *, sizes
 ):
     inst = lax.axis_index("inst")
+    pool_copy = pltpu.make_async_copy(pool_hbm, pool_ref, sems.at[sizes.mig_per])
+    pool_copy.start()
     ready()
+    pool_copy.wait()
     copies = []
     for m in range(sizes.mig_per):
         dest = dest_ref[inst * sizes.mig_per + m]
@@ -173,38 +175,24 @@
         lax.fori_loop(0, sizes.mig_blocks, copy_block, 0, unroll=8)
         copies.append(pltpu.make_async_copy(pack_ref.at[m], send_hbm.at[dest], sems.at[m]))
         copies[-1].start()
-    tail_q_ref[...] = query_ref[...]
-    tail_kv_ref[...] = kv_ref[...].reshape(sizes.tail_kv, 2 * sizes.width)
     for copy in copies:
         copy.wait()
 
 
-def pack(src_table, mig_dest, out_pool, query_rows, new_kv, sizes):
+def pack(src_table, mig_dest, out_pool, sizes):
     z = sizes
-    last_q = query_rows.shape[0] // z.tail_q - 1
-    last_kv = z.batch // z.insts - 1
     request = (z.slots, z.mig_blocks, z.block, 2 * z.width)
     result, _ = run(
         functools.partial(pack_kernel, sizes=z),
-        [src_table, mig_dest], [out_pool, query_rows, new_kv],
-        [
-            VMEM,
-            pl.BlockSpec((z.tail_q, z.width), lambda i: (last_q, 0)),
-            pl.BlockSpec((z.insts,) + new_kv.shape[1:], lambda i: (last_kv, 0, 0, 0)),
+        [src_table, mig_dest], [out_pool], [HBM], [],
+        [pltpu.HBM((z.insts,) + request, out_pool.dtype)], [ANY], "pack", z, limit=60,
+        scratch=[
+            pltpu.VMEM(out_pool.shape, out_pool.dtype),
+            pltpu.VMEM((z.mig_per,) + request, out_pool.dtype),
+            pltpu.SemaphoreType.DMA((z.mig_per + 1,)),
         ],
-        [],
-        [
-            pltpu.HBM((z.insts,) + request, out_pool.dtype),
-            pltpu.HBM((z.tail_q, z.width), out_pool.dtype),
-            pltpu.HBM((z.tail_kv, 2 * z.width), out_pool.dtype),
-        ],
-        [ANY, VMEM, VMEM], "pack", z, limit=60, grid=(1,),
-        scratch=[
-            pltpu.VMEM((z.mig_per,) + request, out_pool.dtype),
-            pltpu.SemaphoreType.DMA((z.mig_per,)),
-        ],
-    )
-    return result
+    )
+    return result[0]
 
 
 def fresh_code(rows, keys, sizes):
@@ -392,7 +380,7 @@
     for read in reads:
         read.start()
     launch()
-    new_kv = kv_ref[...]
+    new_kv = kv_ref[...].reshape(z.tail_kv, 2 * z.width)
     code = fresh_code(z.per, z.tail_kv, z)
     slot_of = slot_index(extent, z)
     scale = math.log2(math.e) / math.sqrt(z.width)
@@ -435,16 +423,23 @@
         write.wait()
 
 
-def settle(mig_dest, mig_len, got, tail_q, tail_kv, attention, sizes, deps, **fetch):
+def settle(mig_dest, mig_len, got, query_rows, new_kv, attention, sizes, deps, **fetch):
     z = sizes
     tokens = z.insts * z.steps
     last = attention.shape[0] // tokens - 1
+    last_q = query_rows.shape[0] // z.tail_q - 1
+    last_kv = z.batch // z.insts - 1
     spec = pl.BlockSpec((tokens, attention.shape[1]), lambda i: (last, 0))
     cache = (z.slots, z.mig_blocks * z.block, 2 * z.width)
     return run(
         functools.partial(settle_kernel, sizes=z),
-        [mig_dest, mig_len], [got, tail_q, tail_kv, attention],
-        [HBM, VMEM, VMEM, spec],
+        [mig_dest, mig_len], [got, query_rows, new_kv, attention],
+        [
+            HBM,
+            pl.BlockSpec((z.tail_q, z.width), lambda i: (last_q, 0)),
+            pl.BlockSpec((z.insts,) + new_kv.shape[1:], lambda i: (last_kv, 0, 0, 0)),
+            spec,
+        ],
         deps,
         [
             jax.ShapeDtypeStruct(attention.shape, jnp.bfloat16),
@@ -642,7 +637,7 @@
     half = z.batch // 2
     low, high, every = (0, 1), (2, 3), (0, 1, 2, 3)
 
-    sends, tail_q, tail_kv = pack(src_table, mig_dest, out_pool, query_rows, new_kv, z)
+    sends = pack(src_table, mig_dest, out_pool, z)
     arriving = lax.all_to_all(sends, "inst", split_axis=0, concat_axis=0, tiled=True)
 
     tokens = half * z.steps
@@ -667,12 +662,9 @@
     kept = keep(b, far, every, mates, "keep", [given] + got_high)
     got_second = sent(kept)
 
-    tail_q, tail_kv = (
-        pltpu.with_memory_space_constraint(x, pltpu.HBM) for x in (tail_q, tail_kv)
-    )
     pieces = gives([0], low) + gives(far, (0,))
     (rows, last, arrived), new = settle(
-        mig_dest, mig_len, arriving, tail_q, tail_kv, rows, z, kept[-1:],
+        mig_dest, mig_len, arriving, query_rows, new_kv, rows, z, kept[-1:],
         **bringing(pieces),
     )
     hold(pieces, new)

time: 88.7 us -> 87.3 us (0.984)
  Pallas kernels: 60.3 us -> 58.9 us
    pallas_call x17, Pallas kernels: 60.3 us -> 58.9 us  [run(): pl.pallas_call(call, grid_spec=pltpu.PrefetchScalarGridSpec(num_scalar_pr...]
  transfers between devices with their start and end apart: 18 -> 18, of which waited for: 5 -> 5; matrix products, arithmetic and copies ran while one was open for 0% -> 0% of each run, Pallas kernels for 60% -> 61%
where the time goes in v16:
time: 87.3 us; the launch traced here: 86.8 us
  Pallas kernels  58.9 us (67%)
  starting transfers between devices  15 us (17%)
  waiting for transfers between devices  10.2 us (12%)
  local copies, waits for them, and re-layouts  1.64 us (2%)
  between operations  1.08 us (1%)
    pallas_call x17, Pallas kernels, run(): pl.pallas_call(call, grid_spec=pltpu.PrefetchScalarGridSpec(num_scalar_pr...  58.9 us
    ppermute x4, waiting for transfers between devices, across(): return lax.ppermute(x, 'tp', [(i, (i + shift) % tps) for i in range(tps)])  6.87 us
    all_to_all x1, starting transfers between devices, shards(): lax.all_to_all(sends, 'inst', split_axis=0, concat_axis=0, tiled=True)  6.33 us
    ppermute x4, starting transfers between devices, across(): return lax.ppermute(x, 'tp', [(i, (i + shift) % tps) for i in range(tps)])  5.33 us
    ppermute x13, starting transfers between devices, mate_of(): return lax.ppermute(x, 'tp', to_mate)  3.38 us
    all_to_all x1, waiting for transfers between devices, shards(): lax.all_to_all(sends, 'inst', split_axis=0, concat_axis=0, tiled=True)  1.87 us
  transfers between devices with their start and end apart: 18, of which 5 were waited for; matrix products, arithmetic and copies ran while one was open for 0% of the time, Pallas kernels for 61%

profile of v16, /device:TPU:0, one launch (start us, length us, event | category | flops | bytes accessed | tf_op | source)
XLA Modules:
  0.0 86.8 jit_solution(18246506042029831549)
XLA Ops:
  0.6 2.3 %pack.1.refs_6_ = bf16[4,2,32,16,256]{4,3,2,1,0:T(8,128)(2,1)} custom-call(s32[1,2,32]{2,1,0:T(2,128)} %refs_0_.2, s32[8]{0:T(128)} %refs_0_.3, bf16[1,2,64,16,256]{4,3,2,1,0:T(8,128)(2,1)} %refs_2_.1), custom_call_target="tpu_custom_call" | custom-call | bytes 1024 | tf_op jit(solution)/shard_map/pack/pallas_call | solution.py:135
  2.9 6.3 %all-to-all-start = ((bf16[4,2,32,16,256]{4,3,2,1,0:T(8,128)(2,1)}), bf16[4,2,32,16,256]{4,3,2,1,0:T(8,128)(2,1)}, u32[]{:S(2)}, u32[]{:S(2)}) async-start(bf16[4,2,32,16,256]{4,3,2,1,0:T(8,128)(2,1)} %pack.1.refs_6_), calls=%async_computation | async-start | bytes 4194304 | tf_op jit(solution)/shard_map/all_to_all | solution.py:641
  9.2 1.6 %copy-done = bf16[4,2,32,16,256]{4,3,2,1,0:T(8,128)(2,1)S(1)} copy-done((bf16[4,2,32,16,256]{4,3,2,1,0:T(8,128)(2,1)S(1)}, bf16[4,2,32,16,256]{4,3,2,1,0:T(8,128)(2,1)}, u32[]{:S(2)}) %copy-start) | copy-done | bytes 2097176
  10.9 7.8 %attend.2 = (bf16[512,2048]{1,0:T(8,128)(2,1)S(1)}, bf16[2048,512]{1,0:T(8,128)(2,1)S(1)}, bf16[2048,512]{1,0:T(8,128)(2,1)S(1)}, bf16[2048,512]{1,0:T(8,128)(2,...) custom-call(s32[8,125]{1,0:T(8,128)} %bitcast.7, ...), custom_call_target="tpu_custom_call" | custom-call | bytes 1024 | tf_op jit(solution)/shard_map/attend/pallas_call | solution.py:135
  18.7 2.3 %give.3 = (bf16[256,512]{1,0:T(8,128)(2,1)S(1)}, bf16[256,512]{1,0:T(8,128)(2,1)S(1)}, bf16[2048,512]{1,0:T(8,128)(2,1)S(1)}, bf16[2048,512]{1,0:T(8,128)(2,1)S(1)}) custom-call(bf16[512,2048]{1,0:T(8,128)(2,1)S(1)} %get-tuple-element.45.refs_0_.refs_5_, bf16[2048,512]{1,0:T(8,128)(2,1)S(1)} %get-tuple-element.46.refs_1_, ...), custom_call_target="tpu_custom_call" | custom-call | bytes 1024 | tf_op jit(solution)/shard_map/give/pallas_call | solution.py:135
  21.1 0.5 collective-permute-start.2
  21.6 1.8 %give.4 = (bf16[256,512]{1,0:T(8,128)(2,1)S(1)}, bf16[256,512]{1,0:T(8,128)(2,1)S(1)}) custom-call(bf16[512,2048]{1,0:T(8,128)(2,1)S(1)} %get-tuple-element.45.refs_0_.refs_5_, bf16[2048,512]{1,0:T(8,128)(2,1)S(1)} %get-tuple-element.50.refs_1_.refs_3_, bf16[2048,512]{1,0:T(8,128)(2,1)S(1)} %get-tuple-element.51.refs_2_.refs_4_, ...), custom_call_target="tpu_custom_call" | custom-call | bytes 1024 | tf_op jit(solution)/shard_map/give/pallas_call | solution.py:135
  23.4 1.8 %keep.3.refs_5_ = bf16[256,1024]{1,0:T(8,128)(2,1)S(1)} custom-call(bf16[512,2048]{1,0:T(8,128)(2,1)S(1)} %get-tuple-element.45.refs_0_.refs_5_, bf16[2048,512]{1,0:T(8,128)(2,1)S(1)} %get-tuple-element.55.refs_1_, bf16[2048,512]{1,0:T(8,128)(2,1)S(1)} %get-tuple-element.56.refs_2_, bf16[256,512]{1,0:T(8,128)(2,1)S(1)} %collective-permute-done.2.refs_3_, ...), custom_call_target="tpu_custom_call" | custom-call | bytes 1024 | tf_op jit(solution)/shard_map/keep/pallas_call | solution.py:135
  25.2 1.6 %collective-permute-start.4 = (bf16[256,1024]{1,0:T(8,128)(2,1)S(1)}, bf16[256,1024]{1,0:T(8,128)(2,1)S(1)}, u32[]{:S(2)}, u32[]{:S(2)}) collective-permute-start(bf16[256,1024]{1,0:T(8,128)(2,1)S(1)} %keep.3.refs_5_), channel_id=1, source_target_pairs={{0,2},{1,3},{2,0},{3,1},{4,6},{5,7},{6,4},{7,5},{8,10},{9,11},{10,... | collective-permute-start | bytes 1572872 | tf_op jit(solution)/shard_map/ppermute | solution.py:594
  26.8 0.5 collective-permute-start
  27.3 1.0 %collective-permute-done.1.refs_4_ = bf16[256,512]{1,0:T(8,128)(2,1)S(1)} collective-permute-done((bf16[256,512]{1,0:T(8,128)(2,1)S(1)}, bf16[256,512]{1,0:T(8,128)(2,1)S(1)}, u32[]{:S(2)}, u32[]{:S(2)}) %collective-permute-start.1) | collective-permute-done | bytes 262176 | tf_op jit(solution)/shard_map/ppermute | solution.py:590
  28.7 1.8 %keep.4.refs_6_ = bf16[256,1024]{1,0:T(8,128)(2,1)S(1)} custom-call(bf16[512,2048]{1,0:T(8,128)(2,1)S(1)} %get-tuple-element.45.refs_0_.refs_5_, bf16[2048,512]{1,0:T(8,128)(2,1)S(1)} %get-tuple-element.48.refs_1_.refs_3_, bf16[2048,512]{1,0:T(8,128)(2,1)S(1)} %get-tuple-element.49.refs_2_.refs_4_, bf16[256,512]{1,0:T(8,128)(2,1)S(1)} %collective-permute-done.refs_3_, ...), custom_call_target="tpu_custom_call" | custom-call | bytes 1024 | tf_op jit(solution)/shard_map/keep/pallas_call | solution.py:135
  30.5 0.6 collective-permute-start.9
  31.1 7.7 %attend.3.refs_0_.refs_5_ = bf16[512,2048]{1,0:T(8,128)(2,1)S(1)} custom-call(s32[8,125]{1,0:T(8,128)} %bitcast.8, s32[1,125]{1,0:T(1,128)} %refs_1_.6, bf16[8192,128]{1,0:T(8,128)(2,1)} %bitcast.5, bf16[128,4,2,256]{3,2,1,0:T(2,128)(2,1)} %refs_4_.5, bf16[1,2,64,16,256]{4,3,2,1,0:T(8,128)(2,1)} %refs_4_.4, ...), custom_call_target="tpu_custom_call", output_to_operand_aliasing={{}: (5, {})} | custom-call | bytes 1024 | tf_op jit(solution)/shard_map/attend/pallas_call | solution.py:135
  38.9 1.2 %collective-permute-done.4.refs_5_.refs_2_ = bf16[256,1024]{1,0:T(8,128)(2,1)S(1)} collective-permute-done((bf16[256,1024]{1,0:T(8,128)(2,1)S(1)}, bf16[256,1024]{1,0:T(8,128)(2,1)S(1)}, u32[]{:S(2)}, u32[]{:S(2)}) %collective-permute-start.4) | collective-permute-done | bytes 524320 | tf_op jit(solution)/shard_map/ppermute | solution.py:594
  40.1 3.6 %give.5 = (bf16[256,512]{1,0:T(8,128)(2,1)S(1)}, bf16[256,512]{1,0:T(8,128)(2,1)S(1)}, bf16[256,512]{1,0:T(8,128)(2,1)S(1)}, bf16[256,512]{1,0:T(8,128)(2,1)S(1)}) custom-call(bf16[512,2048]{1,0:T(8,128)(2,1)S(1)} %attend.3.refs_0_.refs_5_, bf16[2048,512]{1,0:T(8,128)(2,1)S(1)} %get-tuple-element.46.refs_1_, ...), custom_call_target="tpu_custom_call" | custom-call | bytes 1024 | tf_op jit(solution)/shard_map/give/pallas_call | solution.py:135
  43.8 0.5 collective-permute-start.7
  44.8 5.7 %collective-permute-done.9.refs_10_.refs_3_ = bf16[256,1024]{1,0:T(8,128)(2,1)S(1)} collective-permute-done((bf16[256,1024]{1,0:T(8,128)(2,1)S(1)}, bf16[256,1024]{1,0:T(8,128)(2,1)S(1)}, u32[]{:S(2)}, u32[]{:S(2)}) %collective-permute-start.9) | collective-permute-done | bytes 524320 | tf_op jit(solution)/shard_map/ppermute | solution.py:594
  50.5 3.6 %keep.5.refs_7_ = bf16[256,2048]{1,0:T(8,128)(2,1)S(1)} custom-call(bf16[512,2048]{1,0:T(8,128)(2,1)S(1)} %attend.3.refs_0_.refs_5_, bf16[2048,512]{1,0:T(8,128)(2,1)S(1)} %get-tuple-element.55.refs_1_, bf16[2048,512]{1,0:T(8,128)(2,1)S(1)} %get-tuple-element.56.refs_2_, bf16[2048,512]{1,0:T(8,128)(2,1)S(1)} %get-tuple-element.48.refs_1_.refs_3_, ...), custom_call_target="tpu_custom_call" | custom-call | bytes 1024 | tf_op jit(solution)/shard_map/keep/pallas_call | solution.py:135
  54.1 1.6 %collective-permute-start.15 = (bf16[256,2048]{1,0:T(8,128)(2,1)S(1)}, bf16[256,2048]{1,0:T(8,128)(2,1)}, u32[]{:S(2)}, u32[]{:S(2)}) collective-permute-start(bf16[256,2048]{1,0:T(8,128)(2,1)S(1)} %keep.5.refs_7_), channel_id=1, source_target_pairs={{0,2},{1,3},{2,0},{3,1},{4,6},{5,7},{6,4},{7,5},{8,10},{9,11},{10,... | collective-permute-start | bytes 3145736 | tf_op jit(solution)/shard_map/ppermute | solution.py:594
  55.7 1.9 %all-to-all-done.refs_2_ = bf16[4,2,32,16,256]{4,3,2,1,0:T(8,128)(2,1)} async-done(((bf16[4,2,32,16,256]{4,3,2,1,0:T(8,128)(2,1)}), bf16[4,2,32,16,256]{4,3,2,1,0:T(8,128)(2,1)}, u32[]{:S(2)}, u32[]{:S(2)}) %all-to-all-start) | async-done | bytes 2097184 | tf_op jit(solution)/shard_map/all_to_all | solution.py:641
  57.5 6.0 %settle.1 = (bf16[512,2048]{1,0:T(8,128)(2,1)S(1)}, bf16[16,2048]{1,0:T(8,128)(2,1)S(1)}, bf16[1,3,2,512,256]{4,3,2,1,0:T(8,128)(2,1)}, bf16[2048,512]{1,0:T(8,1...) custom-call(s32[8]{0:T(128)} %refs_0_.3, s32[8]{0:T(128)} %refs_1_.7, ...), custom_call_target="tpu_custom_call", output_to_operand_aliasing={{0}: (5, {})} | custom-call | bytes 1024 | tf_op jit(solution)/shard_map/settle/pallas_call | solution.py:135
  63.6 3.0 %give_own.2 = (bf16[512,512]{1,0:T(8,128)(2,1)S(1)}, bf16[512,512]{1,0:T(8,128)(2,1)S(1)}, bf16[2048,512]{1,0:T(8,128)(2,1)S(1)}, bf16[2048,512]{1,0:T(8,128)(2,1)S(1)}, bf16[2048,512]{1,0:T(8,128)(2,1)S(1)}) custom-call(bf16[512,2048]{1,0:T(8,128)(2,1)S(1)} %get-tuple-element.63.refs_0_, bf16[2048,512]{1,0:T(8,128)(2,1)S(1)} %get-tuple-element.66.refs_1_, ...), custom_call_target="tpu_custom_call" | custom-call | bytes 1024 | tf_op jit(solution)/shard_map/give_own/pallas_call | solution.py:135
  66.5 2.3 %give_last.1 = (bf16[16,2048]{1,0:T(8,128)(2,1)S(1)}, bf16[2048,512]{1,0:T(8,128)(2,1)S(1)}, bf16[2048,512]{1,0:T(8,128)(2,1)S(1)}) custom-call(bf16[16,2048]{1,0:T(8,128)(2,1)S(1)} %get-tuple-element.64.refs_0_, bf16[2048,512]{1,0:T(8,128)(2,1)S(1)} %get-tuple-element.65.refs_1_, bf16[2048,512]{1,0:T(8,128)(2,1)S(1)} %get-tuple-element.68.refs_2_, ...), custom_call_target="tpu_custom_call" | custom-call | bytes 1024 | tf_op jit(solution)/shard_map/give_last/pallas_call | solution.py:135
  68.9 0.5 collective-permute-start.12
  69.5 3.5 %give_own.3 = (bf16[512,512]{1,0:T(8,128)(2,1)S(1)}, bf16[512,512]{1,0:T(8,128)(2,1)S(1)}, bf16[2048,512]{1,0:T(8,128)(2,1)S(1)}, bf16[2048,512]{1,0:T(8,128)(2,...) custom-call(bf16[512,2048]{1,0:T(8,128)(2,1)S(1)} %get-tuple-element.63.refs_0_, ...), custom_call_target="tpu_custom_call" | custom-call | bytes 1024 | tf_op jit(solution)/shard_map/give_own/pallas_call | solution.py:135
  73.0 0.5 collective-permute-start.14
  73.6 2.3 %keep_last.1 = (bf16[16,2048]{1,0:T(8,128)(2,1)S(1)}, bf16[2048,512]{1,0:T(8,128)(2,1)S(1)}, bf16[2048,512]{1,0:T(8,128)(2,1)S(1)}) custom-call(bf16[16,2048]{1,0:T(8,128)(2,1)S(1)} %get-tuple-element.64.refs_0_, bf16[2048,512]{1,0:T(8,128)(2,1)S(1)} %get-tuple-element.75.refs_1_, bf16[2048,512]{1,0:T(8,128)(2,1)S(1)} %get-tuple-element.76.refs_2_, ...), custom_call_target="tpu_custom_call" | custom-call | bytes 1024 | tf_op jit(solution)/shard_map/keep_last/pallas_call | solution.py:135
  75.9 1.6 %collective-permute-start.16 = (bf16[16,2048]{1,0:T(8,128)(2,1)S(1)}, bf16[16,2048]{1,0:T(8,128)(2,1)S(1)}, u32[]{:S(2)}, u32[]{:S(2)}) collective-permute-start(bf16[16,2048]{1,0:T(8,128)(2,1)S(1)} %get-tuple-element.83.refs_6_), channel_id=1, source_target_pairs={{0,2},{1,3},{2,0},{3,1},{4,6},{5,7},{6,4},{7,5},{8,10},{9,11},{10,... | collective-permute-start | bytes 196616 | tf_op jit(solution)/shard_map/ppermute | solution.py:594
  77.5 2.9 %keep_own.2 = (f32[512,1024]{1,0:T(8,128)S(1)}, bf16[2048,512]{1,0:T(8,128)(2,1)S(1)}, bf16[2048,512]{1,0:T(8,128)(2,1)S(1)}) custom-call(bf16[512,2048]{1,0:T(8,128)(2,1)S(1)} %get-tuple-element.63.refs_0_, bf16[2048,512]{1,0:T(8,128)(2,1)S(1)} %get-tuple-element.80.refs_1_, bf16[2048,512]{1,0:T(8,128)(2,1)S(1)} %get-tuple-element.81.refs_2_, ...), custom_call_target="tpu_custom_call" | custom-call | bytes 1024 | tf_op jit(solution)/shard_map/keep_own/pallas_call | solution.py:135
  80.4 2.9 %keep_own.3.refs_1_ = f32[512,1024]{1,0:T(8,128)S(1)} custom-call(bf16[512,2048]{1,0:T(8,128)(2,1)S(1)} %get-tuple-element.63.refs_0_, bf16[2048,512]{1,0:T(8,128)(2,1)S(1)} %get-tuple-element.85.refs_1_, bf16[2048,512]{1,0:T(8,128)(2,1)S(1)} %get-tuple-element.86.refs_2_, bf16[512,512]{1,0:T(8,128)(2,1)S(1)} %collective-permute-done.13.refs_3_, ...), custom_call_target="tpu_custom_call" | custom-call | bytes 1024 | tf_op jit(solution)/shard_map/keep_own/pallas_call | solution.py:135
  83.4 3.3 %finish.1 = bf16[2048,512]{1,0:T(8,128)(2,1)} custom-call(f32[512,1024]{1,0:T(8,128)S(1)} %get-tuple-element.84.refs_5_.refs_0_, f32[512,1024]{1,0:T(8,128)S(1)} %keep_own.3.refs_1_, bf16[256,1024]{1,0:T(8,128)(2,1)S(1)} %copy-done.4, bf16[256,1024]{1,0:T(8,128)(2,1)S(1)} %copy-done.2, bf16[256,2048]{1,0:T(8,128)(2,1)} %collective-permute-done.15.refs_4_, ...), custom_call_target="tpu_custom_call" | custom-call | bytes 1024 | tf_op jit(solution)/shard_map/finish/pallas_call | solution.py:135
  (31 shorter events, 1.3 us)
Async XLA Ops:
  2.9 54.6 %all-to-all-start = ((bf16[4,2,32,16,256]{4,3,2,1,0:T(8,128)(2,1)}), bf16[4,2,32,16,256]{4,3,2,1,0:T(8,128)(2,1)}, u32[]{:S(2)}, u32[]{:S(2)}) async-start(bf16[4,2,32,16,256]{4,3,2,1,0:T(8,128)(2,1)} %pack.1.refs_6_), calls=%async_computation | async-start | bytes 4194304 | tf_op jit(solution)/shard_map/all_to_all | solution.py:641
  9.2 1.6 %copy-start = (bf16[4,2,32,16,256]{4,3,2,1,0:T(8,128)(2,1)S(1)}, bf16[4,2,32,16,256]{4,3,2,1,0:T(8,128)(2,1)}, u32[]{:S(2)}) copy-start(bf16[4,2,32,16,256]{4,3,2,1,0:T(8,128)(2,1)} %pack.1.refs_6_) | copy-start | bytes 6291460
  21.0 2.4 %collective-permute-start.3 = (bf16[256,512]{1,0:T(8,128)(2,1)S(1)}, bf16[256,512]{1,0:T(8,128)(2,1)S(1)}, u32[]{:S(2)}, u32[]{:S(2)}) collective-permute-start(bf16[256,512]{1,0:T(8,128)(2,1)S(1)} %get-tuple-element.57), channel_id=1, source_target_pairs={{0,1},{1,0},{2,3},{3,2},{4,5},{5,4},{6,7},{7,6},{8,9},{9,8},{10,11... | collective-permute-start | bytes 786440 | tf_op jit(solution)/shard_map/ppermute | solution.py:590
  21.1 2.3 %collective-permute-start.2 = (bf16[256,512]{1,0:T(8,128)(2,1)S(1)}, bf16[256,512]{1,0:T(8,128)(2,1)S(1)}, u32[]{:S(2)}, u32[]{:S(2)}) collective-permute-start(bf16[256,512]{1,0:T(8,128)(2,1)S(1)} %get-tuple-element.52.refs_3_), channel_id=1, source_target_pairs={{0,1},{1,0},{2,3},{3,2},{4,5},{5,4},{6,7},{7,6},{8,9},{9,8},{10,11... | collective-permute-start | bytes 786440 | tf_op jit(solution)/shard_map/ppermute | solution.py:590
  25.2 14.8 %collective-permute-start.4 = (bf16[256,1024]{1,0:T(8,128)(2,1)S(1)}, bf16[256,1024]{1,0:T(8,128)(2,1)S(1)}, u32[]{:S(2)}, u32[]{:S(2)}) collective-permute-start(bf16[256,1024]{1,0:T(8,128)(2,1)S(1)} %keep.3.refs_5_), channel_id=1, source_target_pairs={{0,2},{1,3},{2,0},{3,1},{4,6},{5,7},{6,4},{7,5},{8,10},{9,11},{10,... | collective-permute-start | bytes 1572872 | tf_op jit(solution)/shard_map/ppermute | solution.py:594
  26.8 1.5 %collective-permute-start.1 = (bf16[256,512]{1,0:T(8,128)(2,1)S(1)}, bf16[256,512]{1,0:T(8,128)(2,1)S(1)}, u32[]{:S(2)}, u32[]{:S(2)}) collective-permute-start(bf16[256,512]{1,0:T(8,128)(2,1)S(1)} %get-tuple-element.54), channel_id=1, source_target_pairs={{0,1},{1,0},{2,3},{3,2},{4,5},{5,4},{6,7},{7,6},{8,9},{9,8},{10,11... | collective-permute-start | bytes 786440 | tf_op jit(solution)/shard_map/ppermute | solution.py:590
  26.8 1.9 %collective-permute-start = (bf16[256,512]{1,0:T(8,128)(2,1)S(1)}, bf16[256,512]{1,0:T(8,128)(2,1)S(1)}, u32[]{:S(2)}, u32[]{:S(2)}) collective-permute-start(bf16[256,512]{1,0:T(8,128)(2,1)S(1)} %get-tuple-element.53.refs_5_), channel_id=1, source_target_pairs={{0,1},{1,0},{2,3},{3,2},{4,5},{5,4},{6,7},{7,6},{8,9},{9,8},{10,11... | collective-permute-start | bytes 786440 | tf_op jit(solution)/shard_map/ppermute | solution.py:590
  30.5 19.9 %collective-permute-start.9 = (bf16[256,1024]{1,0:T(8,128)(2,1)S(1)}, bf16[256,1024]{1,0:T(8,128)(2,1)S(1)}, u32[]{:S(2)}, u32[]{:S(2)}) collective-permute-start(bf16[256,1024]{1,0:T(8,128)(2,1)S(1)} %keep.4.refs_6_), channel_id=1, source_target_pairs={{0,2},{1,3},{2,0},{3,1},{4,6},{5,7},{6,4},{7,5},{8,10},{9,11},{10,... | collective-permute-start | bytes 1572872 | tf_op jit(solution)/shard_map/ppermute | solution.py:594
  40.1 3.6 %copy-start.3 = (bf16[256,1024]{1,0:T(8,128)(2,1)}, bf16[256,1024]{1,0:T(8,128)(2,1)S(1)}, u32[]{:S(2)}) copy-start(bf16[256,1024]{1,0:T(8,128)(2,1)S(1)} %collective-permute-done.4.refs_5_.refs_2_) | copy-start | bytes 1572868
  43.7 6.8 %collective-permute-start.6 = (bf16[256,512]{1,0:T(8,128)(2,1)S(1)}, bf16[256,512]{1,0:T(8,128)(2,1)S(1)}, u32[]{:S(2)}, u32[]{:S(2)}) collective-permute-start(bf16[256,512]{1,0:T(8,128)(2,1)S(1)} %get-tuple-element.59), channel_id=1, source_target_pairs={{0,1},{1,0},{2,3},{3,2},{4,5},{5,4},{6,7},{7,6},{8,9},{9,8},{10,11... | collective-permute-start | bytes 786440 | tf_op jit(solution)/shard_map/ppermute | solution.py:590
  43.8 6.7 %collective-permute-start.7 = (bf16[256,512]{1,0:T(8,128)(2,1)S(1)}, bf16[256,512]{1,0:T(8,128)(2,1)S(1)}, u32[]{:S(2)}, u32[]{:S(2)}) collective-permute-start(bf16[256,512]{1,0:T(8,128)(2,1)S(1)} %get-tuple-element.60), channel_id=1, source_target_pairs={{0,1},{1,0},{2,3},{3,2},{4,5},{5,4},{6,7},{7,6},{8,9},{9,8},{10,11... | collective-permute-start | bytes 786440 | tf_op jit(solution)/shard_map/ppermute | solution.py:590
  44.3 6.2 %collective-permute-start.8 = (bf16[256,512]{1,0:T(8,128)(2,1)S(1)}, bf16[256,512]{1,0:T(8,128)(2,1)S(1)}, u32[]{:S(2)}, u32[]{:S(2)}) collective-permute-start(bf16[256,512]{1,0:T(8,128)(2,1)S(1)} %get-tuple-element.61), channel_id=1, source_target_pairs={{0,1},{1,0},{2,3},{3,2},{4,5},{5,4},{6,7},{7,6},{8,9},{9,8},{10,11... | collective-permute-start | bytes 786440 | tf_op jit(solution)/shard_map/ppermute | solution.py:590
  44.3 6.1 %collective-permute-start.5 = (bf16[256,512]{1,0:T(8,128)(2,1)S(1)}, bf16[256,512]{1,0:T(8,128)(2,1)S(1)}, u32[]{:S(2)}, u32[]{:S(2)}) collective-permute-start(bf16[256,512]{1,0:T(8,128)(2,1)S(1)} %get-tuple-element.58.refs_9_), channel_id=1, source_target_pairs={{0,1},{1,0},{2,3},{3,2},{4,5},{5,4},{6,7},{7,6},{8,9},{9,8},{10,11... | collective-permute-start | bytes 786440 | tf_op jit(solution)/shard_map/ppermute | solution.py:590
  50.4 3.7 %copy-start.1 = (bf16[256,1024]{1,0:T(8,128)(2,1)}, bf16[256,1024]{1,0:T(8,128)(2,1)S(1)}, u32[]{:S(2)}) copy-start(bf16[256,1024]{1,0:T(8,128)(2,1)S(1)} %collective-permute-done.9.refs_10_.refs_3_) | copy-start | bytes 1572868
  54.1 29.2 %collective-permute-start.15 = (bf16[256,2048]{1,0:T(8,128)(2,1)S(1)}, bf16[256,2048]{1,0:T(8,128)(2,1)}, u32[]{:S(2)}, u32[]{:S(2)}) collective-permute-start(bf16[256,2048]{1,0:T(8,128)(2,1)S(1)} %keep.5.refs_7_), channel_id=1, source_target_pairs={{0,2},{1,3},{2,0},{3,1},{4,6},{5,7},{6,4},{7,5},{8,10},{9,11},{10,... | collective-permute-start | bytes 3145736 | tf_op jit(solution)/shard_map/ppermute | solution.py:594
  68.8 4.7 %collective-permute-start.10 = (bf16[16,2048]{1,0:T(8,128)(2,1)S(1)}, bf16[16,2048]{1,0:T(8,128)(2,1)S(1)}, u32[]{:S(2)}, u32[]{:S(2)}) collective-permute-start(bf16[16,2048]{1,0:T(8,128)(2,1)S(1)} %get-tuple-element.74.refs_4_), channel_id=1, source_target_pairs={{0,1},{1,0},{2,3},{3,2},{4,5},{5,4},{6,7},{7,6},{8,9},{9,8},{10,11... | collective-permute-start | bytes 196616 | tf_op jit(solution)/shard_map/ppermute | solution.py:590
  68.9 7.0 %collective-permute-start.12 = (bf16[512,512]{1,0:T(8,128)(2,1)S(1)}, bf16[512,512]{1,0:T(8,128)(2,1)S(1)}, u32[]{:S(2)}, u32[]{:S(2)}) collective-permute-start(bf16[512,512]{1,0:T(8,128)(2,1)S(1)} %get-tuple-element.82), channel_id=1, source_target_pairs={{0,1},{1,0},{2,3},{3,2},{4,5},{5,4},{6,7},{7,6},{8,9},{9,8},{10,11... | collective-permute-start | bytes 1572872 | tf_op jit(solution)/shard_map/ppermute | solution.py:590
  69.4 8.1 %collective-permute-start.11 = (bf16[512,512]{1,0:T(8,128)(2,1)S(1)}, bf16[512,512]{1,0:T(8,128)(2,1)S(1)}, u32[]{:S(2)}, u32[]{:S(2)}) collective-permute-start(bf16[512,512]{1,0:T(8,128)(2,1)S(1)} %get-tuple-element.71.refs_6_), channel_id=1, source_target_pairs={{0,1},{1,0},{2,3},{3,2},{4,5},{5,4},{6,7},{7,6},{8,9},{9,8},{10,11... | collective-permute-start | bytes 1572872 | tf_op jit(solution)/shard_map/ppermute | solution.py:590
  73.0 7.4 %collective-permute-start.14 = (bf16[512,512]{1,0:T(8,128)(2,1)S(1)}, bf16[512,512]{1,0:T(8,128)(2,1)S(1)}, u32[]{:S(2)}, u32[]{:S(2)}) collective-permute-start(bf16[512,512]{1,0:T(8,128)(2,1)S(1)} %get-tuple-element.87), channel_id=1, source_target_pairs={{0,1},{1,0},{2,3},{3,2},{4,5},{5,4},{6,7},{7,6},{8,9},{9,8},{10,11... | collective-permute-start | bytes 1572872 | tf_op jit(solution)/shard_map/ppermute | solution.py:590
  73.5 6.9 %collective-permute-start.13 = (bf16[512,512]{1,0:T(8,128)(2,1)S(1)}, bf16[512,512]{1,0:T(8,128)(2,1)S(1)}, u32[]{:S(2)}, u32[]{:S(2)}) collective-permute-start(bf16[512,512]{1,0:T(8,128)(2,1)S(1)} %get-tuple-element.79.refs_7_), channel_id=1, source_target_pairs={{0,1},{1,0},{2,3},{3,2},{4,5},{5,4},{6,7},{7,6},{8,9},{9,8},{10,11... | collective-permute-start | bytes 1572872 | tf_op jit(solution)/shard_map/ppermute | solution.py:590
  75.9 7.5 %collective-permute-start.16 = (bf16[16,2048]{1,0:T(8,128)(2,1)S(1)}, bf16[16,2048]{1,0:T(8,128)(2,1)S(1)}, u32[]{:S(2)}, u32[]{:S(2)}) collective-permute-start(bf16[16,2048]{1,0:T(8,128)(2,1)S(1)} %get-tuple-element.83.refs_6_), channel_id=1, source_target_pairs={{0,2},{1,3},{2,0},{3,1},{4,6},{5,7},{6,4},{7,5},{8,10},{9,11},{10,... | collective-permute-start | bytes 196616 | tf_op jit(solution)/shard_map/ppermute | solution.py:594
  80.4 2.9 %copy-start.2 = (bf16[256,1024]{1,0:T(8,128)(2,1)S(1)}, bf16[256,1024]{1,0:T(8,128)(2,1)}, u32[]{:S(2)}) copy-start(bf16[256,1024]{1,0:T(8,128)(2,1)} %copy-done.1) | copy-start | bytes 1572868
  80.4 2.9 %copy-start.4 = (bf16[256,1024]{1,0:T(8,128)(2,1)S(1)}, bf16[256,1024]{1,0:T(8,128)(2,1)}, u32[]{:S(2)}) copy-start(bf16[256,1024]{1,0:T(8,128)(2,1)} %copy-done.3) | copy-start | bytes 1572868

commit v17 on v16

--- a/solution.py
+++ b/solution.py
@@ -364,14 +364,13 @@
     arrived_hbm, rows_ref, got_ref, keep_ref, sems, *, sizes
 ):
     z = sizes
-    ready()
     inst = lax.axis_index("inst")
-    requests = row_plan(dest_ref, inst, z.cap)
-    known = [jnp.maximum(request, 0) for request in requests]
     extent = z.mig_blocks * z.block
     reads = [
-        pltpu.make_async_copy(got_hbm.at[known[a] // z.mig_per], got_ref.at[a], sems.at[0, a])
-        for a in range(z.cap)
+        pltpu.make_async_copy(
+            got_hbm.at[lax.rem(inst + k, z.insts)], got_ref.at[k - 1], sems.at[0, k - 1]
+        )
+        for k in range(1, z.insts)
     ]
     writes = [
         pltpu.make_async_copy(keep_ref.at[a], arrived_hbm.at[0, a], sems.at[1, a])
@@ -379,6 +378,11 @@
     ]
     for read in reads:
         read.start()
+    ready()
+    requests = row_plan(dest_ref, inst, z.cap)
+    known = [jnp.maximum(request, 0) for request in requests]
+    for read in reads:
+        read.wait()
     launch()
     new_kv = kv_ref[...].reshape(z.tail_kv, 2 * z.width)
     code = fresh_code(z.per, z.tail_kv, z)
@@ -391,13 +395,14 @@
     rows_ref[: z.per, :] = jnp.zeros((z.per, z.width), jnp.float32)
     for a in range(z.cap):
         length = jnp.where(requests[a] >= 0, len_ref[known[a]], 0)
-        reads[a].wait()
-
-        def one(b, carry, a=a, length=length):
+        ahead = lax.rem(known[a] // z.mig_per - inst + z.insts, z.insts)
+        at_hand = jnp.maximum(ahead - 1, 0)
+
+        def one(b, carry, a=a, length=length, at_hand=at_hand):
             inside = place + b * z.block < length
             at = pl.ds(pl.multiple_of(b * z.block, z.block), z.block)
             for s in range(z.slots):
-                value = got_ref[a, s, b].astype(jnp.float32)
+                value = got_ref[at_hand, s, b].astype(jnp.float32)
                 keep_ref[a, s, at, :] = jnp.where(inside, value, 0.0).astype(jnp.bfloat16)
             return carry
 

time: 87.3 us -> 87.1 us (level)
  no operation moved by 1% of the time
where the time goes in v17:
time: 87.1 us; the launch traced here: 86.6 us
  Pallas kernels  58.6 us (67%)
  starting transfers between devices  15 us (17%)
  waiting for transfers between devices  10.2 us (12%)
  local copies, waits for them, and re-layouts  1.64 us (2%)
  between operations  1.08 us (1%)
    pallas_call x17, Pallas kernels, run(): pl.pallas_call(call, grid_spec=pltpu.PrefetchScalarGridSpec(num_scalar_pr...  58.6 us
    ppermute x4, waiting for transfers between devices, across(): return lax.ppermute(x, 'tp', [(i, (i + shift) % tps) for i in range(tps)])  6.88 us
    all_to_all x1, starting transfers between devices, shards(): lax.all_to_all(sends, 'inst', split_axis=0, concat_axis=0, tiled=True)  6.33 us
    ppermute x4, starting transfers between devices, across(): return lax.ppermute(x, 'tp', [(i, (i + shift) % tps) for i in range(tps)])  5.33 us
    ppermute x13, starting transfers between devices, mate_of(): return lax.ppermute(x, 'tp', to_mate)  3.38 us
    all_to_all x1, waiting for transfers between devices, shards(): lax.all_to_all(sends, 'inst', split_axis=0, concat_axis=0, tiled=True)  1.89 us
  transfers between devices with their start and end apart: 18, of which 5 were waited for; matrix products, arithmetic and copies ran while one was open for 0% of the time, Pallas kernels for 61%

profile of v17, /device:TPU:0, one launch (start us, length us, event | category | flops | bytes accessed | tf_op | source)
XLA Modules:
  0.0 86.6 jit_solution(7593722446595023373)
XLA Ops:
  0.6 2.3 %pack.1.refs_6_ = bf16[4,2,32,16,256]{4,3,2,1,0:T(8,128)(2,1)} custom-call(s32[1,2,32]{2,1,0:T(2,128)} %refs_0_.2, s32[8]{0:T(128)} %refs_0_.3, bf16[1,2,64,16,256]{4,3,2,1,0:T(8,128)(2,1)} %refs_2_.1), custom_call_target="tpu_custom_call" | custom-call | bytes 1024 | tf_op jit(solution)/shard_map/pack/pallas_call | solution.py:135
  2.9 6.3 %all-to-all-start = ((bf16[4,2,32,16,256]{4,3,2,1,0:T(8,128)(2,1)}), bf16[4,2,32,16,256]{4,3,2,1,0:T(8,128)(2,1)}, u32[]{:S(2)}, u32[]{:S(2)}) async-start(bf16[4,2,32,16,256]{4,3,2,1,0:T(8,128)(2,1)} %pack.1.refs_6_), calls=%async_computation | async-start | bytes 4194304 | tf_op jit(solution)/shard_map/all_to_all | solution.py:646
  9.2 1.6 %copy-done = bf16[4,2,32,16,256]{4,3,2,1,0:T(8,128)(2,1)S(1)} copy-done((bf16[4,2,32,16,256]{4,3,2,1,0:T(8,128)(2,1)S(1)}, bf16[4,2,32,16,256]{4,3,2,1,0:T(8,128)(2,1)}, u32[]{:S(2)}) %copy-start) | copy-done | bytes 2097176
  10.9 7.8 %attend.2 = (bf16[512,2048]{1,0:T(8,128)(2,1)S(1)}, bf16[2048,512]{1,0:T(8,128)(2,1)S(1)}, bf16[2048,512]{1,0:T(8,128)(2,1)S(1)}, bf16[2048,512]{1,0:T(8,128)(2,...) custom-call(s32[8,125]{1,0:T(8,128)} %bitcast.7, ...), custom_call_target="tpu_custom_call" | custom-call | bytes 1024 | tf_op jit(solution)/shard_map/attend/pallas_call | solution.py:135
  18.7 2.3 %give.3 = (bf16[256,512]{1,0:T(8,128)(2,1)S(1)}, bf16[256,512]{1,0:T(8,128)(2,1)S(1)}, bf16[2048,512]{1,0:T(8,128)(2,1)S(1)}, bf16[2048,512]{1,0:T(8,128)(2,1)S(1)}) custom-call(bf16[512,2048]{1,0:T(8,128)(2,1)S(1)} %get-tuple-element.45.refs_0_.refs_5_, bf16[2048,512]{1,0:T(8,128)(2,1)S(1)} %get-tuple-element.46.refs_1_, ...), custom_call_target="tpu_custom_call" | custom-call | bytes 1024 | tf_op jit(solution)/shard_map/give/pallas_call | solution.py:135
  21.1 0.5 collective-permute-start.2
  21.6 1.8 %give.4 = (bf16[256,512]{1,0:T(8,128)(2,1)S(1)}, bf16[256,512]{1,0:T(8,128)(2,1)S(1)}) custom-call(bf16[512,2048]{1,0:T(8,128)(2,1)S(1)} %get-tuple-element.45.refs_0_.refs_5_, bf16[2048,512]{1,0:T(8,128)(2,1)S(1)} %get-tuple-element.50.refs_1_.refs_3_, bf16[2048,512]{1,0:T(8,128)(2,1)S(1)} %get-tuple-element.51.refs_2_.refs_4_, ...), custom_call_target="tpu_custom_call" | custom-call | bytes 1024 | tf_op jit(solution)/shard_map/give/pallas_call | solution.py:135
  23.4 1.8 %keep.3.refs_5_ = bf16[256,1024]{1,0:T(8,128)(2,1)S(1)} custom-call(bf16[512,2048]{1,0:T(8,128)(2,1)S(1)} %get-tuple-element.45.refs_0_.refs_5_, bf16[2048,512]{1,0:T(8,128)(2,1)S(1)} %get-tuple-element.55.refs_1_, bf16[2048,512]{1,0:T(8,128)(2,1)S(1)} %get-tuple-element.56.refs_2_, bf16[256,512]{1,0:T(8,128)(2,1)S(1)} %collective-permute-done.2.refs_3_, ...), custom_call_target="tpu_custom_call" | custom-call | bytes 1024 | tf_op jit(solution)/shard_map/keep/pallas_call | solution.py:135
  25.2 1.6 %collective-permute-start.4 = (bf16[256,1024]{1,0:T(8,128)(2,1)S(1)}, bf16[256,1024]{1,0:T(8,128)(2,1)S(1)}, u32[]{:S(2)}, u32[]{:S(2)}) collective-permute-start(bf16[256,1024]{1,0:T(8,128)(2,1)S(1)} %keep.3.refs_5_), channel_id=1, source_target_pairs={{0,2},{1,3},{2,0},{3,1},{4,6},{5,7},{6,4},{7,5},{8,10},{9,11},{10,... | collective-permute-start | bytes 1572872 | tf_op jit(solution)/shard_map/ppermute | solution.py:599
  26.8 0.5 collective-permute-start
  27.3 1.0 %collective-permute-done.1.refs_4_ = bf16[256,512]{1,0:T(8,128)(2,1)S(1)} collective-permute-done((bf16[256,512]{1,0:T(8,128)(2,1)S(1)}, bf16[256,512]{1,0:T(8,128)(2,1)S(1)}, u32[]{:S(2)}, u32[]{:S(2)}) %collective-permute-start.1) | collective-permute-done | bytes 262176 | tf_op jit(solution)/shard_map/ppermute | solution.py:595
  28.7 1.8 %keep.4.refs_6_ = bf16[256,1024]{1,0:T(8,128)(2,1)S(1)} custom-call(bf16[512,2048]{1,0:T(8,128)(2,1)S(1)} %get-tuple-element.45.refs_0_.refs_5_, bf16[2048,512]{1,0:T(8,128)(2,1)S(1)} %get-tuple-element.48.refs_1_.refs_3_, bf16[2048,512]{1,0:T(8,128)(2,1)S(1)} %get-tuple-element.49.refs_2_.refs_4_, bf16[256,512]{1,0:T(8,128)(2,1)S(1)} %collective-permute-done.refs_3_, ...), custom_call_target="tpu_custom_call" | custom-call | bytes 1024 | tf_op jit(solution)/shard_map/keep/pallas_call | solution.py:135
  30.5 0.6 collective-permute-start.9
  31.1 7.7 %attend.3.refs_0_.refs_5_ = bf16[512,2048]{1,0:T(8,128)(2,1)S(1)} custom-call(s32[8,125]{1,0:T(8,128)} %bitcast.8, s32[1,125]{1,0:T(1,128)} %refs_1_.6, bf16[8192,128]{1,0:T(8,128)(2,1)} %bitcast.5, bf16[128,4,2,256]{3,2,1,0:T(2,128)(2,1)} %refs_4_.5, bf16[1,2,64,16,256]{4,3,2,1,0:T(8,128)(2,1)} %refs_4_.4, ...), custom_call_target="tpu_custom_call", output_to_operand_aliasing={{}: (5, {})} | custom-call | bytes 1024 | tf_op jit(solution)/shard_map/attend/pallas_call | solution.py:135
  38.8 1.2 %collective-permute-done.4.refs_5_.refs_2_ = bf16[256,1024]{1,0:T(8,128)(2,1)S(1)} collective-permute-done((bf16[256,1024]{1,0:T(8,128)(2,1)S(1)}, bf16[256,1024]{1,0:T(8,128)(2,1)S(1)}, u32[]{:S(2)}, u32[]{:S(2)}) %collective-permute-start.4) | collective-permute-done | bytes 524320 | tf_op jit(solution)/shard_map/ppermute | solution.py:599
  40.1 3.6 %give.5 = (bf16[256,512]{1,0:T(8,128)(2,1)S(1)}, bf16[256,512]{1,0:T(8,128)(2,1)S(1)}, bf16[256,512]{1,0:T(8,128)(2,1)S(1)}, bf16[256,512]{1,0:T(8,128)(2,1)S(1)}) custom-call(bf16[512,2048]{1,0:T(8,128)(2,1)S(1)} %attend.3.refs_0_.refs_5_, bf16[2048,512]{1,0:T(8,128)(2,1)S(1)} %get-tuple-element.46.refs_1_, ...), custom_call_target="tpu_custom_call" | custom-call | bytes 1024 | tf_op jit(solution)/shard_map/give/pallas_call | solution.py:135
  43.8 0.5 collective-permute-start.7
  44.8 5.6 %collective-permute-done.9.refs_10_.refs_3_ = bf16[256,1024]{1,0:T(8,128)(2,1)S(1)} collective-permute-done((bf16[256,1024]{1,0:T(8,128)(2,1)S(1)}, bf16[256,1024]{1,0:T(8,128)(2,1)S(1)}, u32[]{:S(2)}, u32[]{:S(2)}) %collective-permute-start.9) | collective-permute-done | bytes 524320 | tf_op jit(solution)/shard_map/ppermute | solution.py:599
  50.4 3.6 %keep.5.refs_7_ = bf16[256,2048]{1,0:T(8,128)(2,1)S(1)} custom-call(bf16[512,2048]{1,0:T(8,128)(2,1)S(1)} %attend.3.refs_0_.refs_5_, bf16[2048,512]{1,0:T(8,128)(2,1)S(1)} %get-tuple-element.55.refs_1_, bf16[2048,512]{1,0:T(8,128)(2,1)S(1)} %get-tuple-element.56.refs_2_, bf16[2048,512]{1,0:T(8,128)(2,1)S(1)} %get-tuple-element.48.refs_1_.refs_3_, ...), custom_call_target="tpu_custom_call" | custom-call | bytes 1024 | tf_op jit(solution)/shard_map/keep/pallas_call | solution.py:135
  54.1 1.6 %collective-permute-start.15 = (bf16[256,2048]{1,0:T(8,128)(2,1)S(1)}, bf16[256,2048]{1,0:T(8,128)(2,1)}, u32[]{:S(2)}, u32[]{:S(2)}) collective-permute-start(bf16[256,2048]{1,0:T(8,128)(2,1)S(1)} %keep.5.refs_7_), channel_id=1, source_target_pairs={{0,2},{1,3},{2,0},{3,1},{4,6},{5,7},{6,4},{7,5},{8,10},{9,11},{10,... | collective-permute-start | bytes 3145736 | tf_op jit(solution)/shard_map/ppermute | solution.py:599
  55.7 1.9 %all-to-all-done.refs_2_ = bf16[4,2,32,16,256]{4,3,2,1,0:T(8,128)(2,1)} async-done(((bf16[4,2,32,16,256]{4,3,2,1,0:T(8,128)(2,1)}), bf16[4,2,32,16,256]{4,3,2,1,0:T(8,128)(2,1)}, u32[]{:S(2)}, u32[]{:S(2)}) %all-to-all-start) | async-done | bytes 2097184 | tf_op jit(solution)/shard_map/all_to_all | solution.py:646
  57.5 5.8 %settle.1 = (bf16[512,2048]{1,0:T(8,128)(2,1)S(1)}, bf16[16,2048]{1,0:T(8,128)(2,1)S(1)}, bf16[1,3,2,512,256]{4,3,2,1,0:T(8,128)(2,1)}, bf16[2048,512]{1,0:T(8,1...) custom-call(s32[8]{0:T(128)} %refs_0_.3, s32[8]{0:T(128)} %refs_1_.7, ...), custom_call_target="tpu_custom_call", output_to_operand_aliasing={{0}: (5, {})} | custom-call | bytes 1024 | tf_op jit(solution)/shard_map/settle/pallas_call | solution.py:135
  63.3 3.0 %give_own.2 = (bf16[512,512]{1,0:T(8,128)(2,1)S(1)}, bf16[512,512]{1,0:T(8,128)(2,1)S(1)}, bf16[2048,512]{1,0:T(8,128)(2,1)S(1)}, bf16[2048,512]{1,0:T(8,128)(2,1)S(1)}, bf16[2048,512]{1,0:T(8,128)(2,1)S(1)}) custom-call(bf16[512,2048]{1,0:T(8,128)(2,1)S(1)} %get-tuple-element.63.refs_0_, bf16[2048,512]{1,0:T(8,128)(2,1)S(1)} %get-tuple-element.66.refs_1_, ...), custom_call_target="tpu_custom_call" | custom-call | bytes 1024 | tf_op jit(solution)/shard_map/give_own/pallas_call | solution.py:135
  66.3 2.3 %give_last.1 = (bf16[16,2048]{1,0:T(8,128)(2,1)S(1)}, bf16[2048,512]{1,0:T(8,128)(2,1)S(1)}, bf16[2048,512]{1,0:T(8,128)(2,1)S(1)}) custom-call(bf16[16,2048]{1,0:T(8,128)(2,1)S(1)} %get-tuple-element.64.refs_0_, bf16[2048,512]{1,0:T(8,128)(2,1)S(1)} %get-tuple-element.65.refs_1_, bf16[2048,512]{1,0:T(8,128)(2,1)S(1)} %get-tuple-element.68.refs_2_, ...), custom_call_target="tpu_custom_call" | custom-call | bytes 1024 | tf_op jit(solution)/shard_map/give_last/pallas_call | solution.py:135
  68.6 0.5 collective-permute-start.12
  69.2 3.5 %give_own.3 = (bf16[512,512]{1,0:T(8,128)(2,1)S(1)}, bf16[512,512]{1,0:T(8,128)(2,1)S(1)}, bf16[2048,512]{1,0:T(8,128)(2,1)S(1)}, bf16[2048,512]{1,0:T(8,128)(2,...) custom-call(bf16[512,2048]{1,0:T(8,128)(2,1)S(1)} %get-tuple-element.63.refs_0_, ...), custom_call_target="tpu_custom_call" | custom-call | bytes 1024 | tf_op jit(solution)/shard_map/give_own/pallas_call | solution.py:135
  72.8 0.5 collective-permute-start.14
  73.4 2.3 %keep_last.1 = (bf16[16,2048]{1,0:T(8,128)(2,1)S(1)}, bf16[2048,512]{1,0:T(8,128)(2,1)S(1)}, bf16[2048,512]{1,0:T(8,128)(2,1)S(1)}) custom-call(bf16[16,2048]{1,0:T(8,128)(2,1)S(1)} %get-tuple-element.64.refs_0_, bf16[2048,512]{1,0:T(8,128)(2,1)S(1)} %get-tuple-element.75.refs_1_, bf16[2048,512]{1,0:T(8,128)(2,1)S(1)} %get-tuple-element.76.refs_2_, ...), custom_call_target="tpu_custom_call" | custom-call | bytes 1024 | tf_op jit(solution)/shard_map/keep_last/pallas_call | solution.py:135
  75.6 1.6 %collective-permute-start.16 = (bf16[16,2048]{1,0:T(8,128)(2,1)S(1)}, bf16[16,2048]{1,0:T(8,128)(2,1)S(1)}, u32[]{:S(2)}, u32[]{:S(2)}) collective-permute-start(bf16[16,2048]{1,0:T(8,128)(2,1)S(1)} %get-tuple-element.83.refs_6_), channel_id=1, source_target_pairs={{0,2},{1,3},{2,0},{3,1},{4,6},{5,7},{6,4},{7,5},{8,10},{9,11},{10,... | collective-permute-start | bytes 196616 | tf_op jit(solution)/shard_map/ppermute | solution.py:599
  77.2 2.9 %keep_own.2 = (f32[512,1024]{1,0:T(8,128)S(1)}, bf16[2048,512]{1,0:T(8,128)(2,1)S(1)}, bf16[2048,512]{1,0:T(8,128)(2,1)S(1)}) custom-call(bf16[512,2048]{1,0:T(8,128)(2,1)S(1)} %get-tuple-element.63.refs_0_, bf16[2048,512]{1,0:T(8,128)(2,1)S(1)} %get-tuple-element.80.refs_1_, bf16[2048,512]{1,0:T(8,128)(2,1)S(1)} %get-tuple-element.81.refs_2_, ...), custom_call_target="tpu_custom_call" | custom-call | bytes 1024 | tf_op jit(solution)/shard_map/keep_own/pallas_call | solution.py:135
  80.2 2.9 %keep_own.3.refs_1_ = f32[512,1024]{1,0:T(8,128)S(1)} custom-call(bf16[512,2048]{1,0:T(8,128)(2,1)S(1)} %get-tuple-element.63.refs_0_, bf16[2048,512]{1,0:T(8,128)(2,1)S(1)} %get-tuple-element.85.refs_1_, bf16[2048,512]{1,0:T(8,128)(2,1)S(1)} %get-tuple-element.86.refs_2_, bf16[512,512]{1,0:T(8,128)(2,1)S(1)} %collective-permute-done.13.refs_3_, ...), custom_call_target="tpu_custom_call" | custom-call | bytes 1024 | tf_op jit(solution)/shard_map/keep_own/pallas_call | solution.py:135
  83.1 3.3 %finish.1 = bf16[2048,512]{1,0:T(8,128)(2,1)} custom-call(f32[512,1024]{1,0:T(8,128)S(1)} %get-tuple-element.84.refs_5_.refs_0_, f32[512,1024]{1,0:T(8,128)S(1)} %keep_own.3.refs_1_, bf16[256,1024]{1,0:T(8,128)(2,1)S(1)} %copy-done.4, bf16[256,1024]{1,0:T(8,128)(2,1)S(1)} %copy-done.2, bf16[256,2048]{1,0:T(8,128)(2,1)} %collective-permute-done.15.refs_4_, ...), custom_call_target="tpu_custom_call" | custom-call | bytes 1024 | tf_op jit(solution)/shard_map/finish/pallas_call | solution.py:135
  (31 shorter events, 1.3 us)
Async XLA Ops:
  2.9 54.6 %all-to-all-start = ((bf16[4,2,32,16,256]{4,3,2,1,0:T(8,128)(2,1)}), bf16[4,2,32,16,256]{4,3,2,1,0:T(8,128)(2,1)}, u32[]{:S(2)}, u32[]{:S(2)}) async-start(bf16[4,2,32,16,256]{4,3,2,1,0:T(8,128)(2,1)} %pack.1.refs_6_), calls=%async_computation | async-start | bytes 4194304 | tf_op jit(solution)/shard_map/all_to_all | solution.py:646
  9.2 1.6 %copy-start = (bf16[4,2,32,16,256]{4,3,2,1,0:T(8,128)(2,1)S(1)}, bf16[4,2,32,16,256]{4,3,2,1,0:T(8,128)(2,1)}, u32[]{:S(2)}) copy-start(bf16[4,2,32,16,256]{4,3,2,1,0:T(8,128)(2,1)} %pack.1.refs_6_) | copy-start | bytes 6291460
  21.0 2.4 %collective-permute-start.3 = (bf16[256,512]{1,0:T(8,128)(2,1)S(1)}, bf16[256,512]{1,0:T(8,128)(2,1)S(1)}, u32[]{:S(2)}, u32[]{:S(2)}) collective-permute-start(bf16[256,512]{1,0:T(8,128)(2,1)S(1)} %get-tuple-element.57), channel_id=1, source_target_pairs={{0,1},{1,0},{2,3},{3,2},{4,5},{5,4},{6,7},{7,6},{8,9},{9,8},{10,11... | collective-permute-start | bytes 786440 | tf_op jit(solution)/shard_map/ppermute | solution.py:595
  21.1 2.3 %collective-permute-start.2 = (bf16[256,512]{1,0:T(8,128)(2,1)S(1)}, bf16[256,512]{1,0:T(8,128)(2,1)S(1)}, u32[]{:S(2)}, u32[]{:S(2)}) collective-permute-start(bf16[256,512]{1,0:T(8,128)(2,1)S(1)} %get-tuple-element.52.refs_3_), channel_id=1, source_target_pairs={{0,1},{1,0},{2,3},{3,2},{4,5},{5,4},{6,7},{7,6},{8,9},{9,8},{10,11... | collective-permute-start | bytes 786440 | tf_op jit(solution)/shard_map/ppermute | solution.py:595
  25.2 14.8 %collective-permute-start.4 = (bf16[256,1024]{1,0:T(8,128)(2,1)S(1)}, bf16[256,1024]{1,0:T(8,128)(2,1)S(1)}, u32[]{:S(2)}, u32[]{:S(2)}) collective-permute-start(bf16[256,1024]{1,0:T(8,128)(2,1)S(1)} %keep.3.refs_5_), channel_id=1, source_target_pairs={{0,2},{1,3},{2,0},{3,1},{4,6},{5,7},{6,4},{7,5},{8,10},{9,11},{10,... | collective-permute-start | bytes 1572872 | tf_op jit(solution)/shard_map/ppermute | solution.py:599
  26.8 1.5 %collective-permute-start.1 = (bf16[256,512]{1,0:T(8,128)(2,1)S(1)}, bf16[256,512]{1,0:T(8,128)(2,1)S(1)}, u32[]{:S(2)}, u32[]{:S(2)}) collective-permute-start(bf16[256,512]{1,0:T(8,128)(2,1)S(1)} %get-tuple-element.54), channel_id=1, source_target_pairs={{0,1},{1,0},{2,3},{3,2},{4,5},{5,4},{6,7},{7,6},{8,9},{9,8},{10,11... | collective-permute-start | bytes 786440 | tf_op jit(solution)/shard_map/ppermute | solution.py:595
  26.8 1.9 %collective-permute-start = (bf16[256,512]{1,0:T(8,128)(2,1)S(1)}, bf16[256,512]{1,0:T(8,128)(2,1)S(1)}, u32[]{:S(2)}, u32[]{:S(2)}) collective-permute-start(bf16[256,512]{1,0:T(8,128)(2,1)S(1)} %get-tuple-element.53.refs_5_), channel_id=1, source_target_pairs={{0,1},{1,0},{2,3},{3,2},{4,5},{5,4},{6,7},{7,6},{8,9},{9,8},{10,11... | collective-permute-start | bytes 786440 | tf_op jit(solution)/shard_map/ppermute | solution.py:595
  30.5 19.9 %collective-permute-start.9 = (bf16[256,1024]{1,0:T(8,128)(2,1)S(1)}, bf16[256,1024]{1,0:T(8,128)(2,1)S(1)}, u32[]{:S(2)}, u32[]{:S(2)}) collective-permute-start(bf16[256,1024]{1,0:T(8,128)(2,1)S(1)} %keep.4.refs_6_), channel_id=1, source_target_pairs={{0,2},{1,3},{2,0},{3,1},{4,6},{5,7},{6,4},{7,5},{8,10},{9,11},{10,... | collective-permute-start | bytes 1572872 | tf_op jit(solution)/shard_map/ppermute | solution.py:599
  40.1 3.6 %copy-start.3 = (bf16[256,1024]{1,0:T(8,128)(2,1)}, bf16[256,1024]{1,0:T(8,128)(2,1)S(1)}, u32[]{:S(2)}) copy-start(bf16[256,1024]{1,0:T(8,128)(2,1)S(1)} %collective-permute-done.4.refs_5_.refs_2_) | copy-start | bytes 1572868
  43.7 6.7 %collective-permute-start.6 = (bf16[256,512]{1,0:T(8,128)(2,1)S(1)}, bf16[256,512]{1,0:T(8,128)(2,1)S(1)}, u32[]{:S(2)}, u32[]{:S(2)}) collective-permute-start(bf16[256,512]{1,0:T(8,128)(2,1)S(1)} %get-tuple-element.59), channel_id=1, source_target_pairs={{0,1},{1,0},{2,3},{3,2},{4,5},{5,4},{6,7},{7,6},{8,9},{9,8},{10,11... | collective-permute-start | bytes 786440 | tf_op jit(solution)/shard_map/ppermute | solution.py:595
  43.8 6.7 %collective-permute-start.7 = (bf16[256,512]{1,0:T(8,128)(2,1)S(1)}, bf16[256,512]{1,0:T(8,128)(2,1)S(1)}, u32[]{:S(2)}, u32[]{:S(2)}) collective-permute-start(bf16[256,512]{1,0:T(8,128)(2,1)S(1)} %get-tuple-element.60), channel_id=1, source_target_pairs={{0,1},{1,0},{2,3},{3,2},{4,5},{5,4},{6,7},{7,6},{8,9},{9,8},{10,11... | collective-permute-start | bytes 786440 | tf_op jit(solution)/shard_map/ppermute | solution.py:595
  44.3 6.2 %collective-permute-start.8 = (bf16[256,512]{1,0:T(8,128)(2,1)S(1)}, bf16[256,512]{1,0:T(8,128)(2,1)S(1)}, u32[]{:S(2)}, u32[]{:S(2)}) collective-permute-start(bf16[256,512]{1,0:T(8,128)(2,1)S(1)} %get-tuple-element.61), channel_id=1, source_target_pairs={{0,1},{1,0},{2,3},{3,2},{4,5},{5,4},{6,7},{7,6},{8,9},{9,8},{10,11... | collective-permute-start | bytes 786440 | tf_op jit(solution)/shard_map/ppermute | solution.py:595
  44.3 6.1 %collective-permute-start.5 = (bf16[256,512]{1,0:T(8,128)(2,1)S(1)}, bf16[256,512]{1,0:T(8,128)(2,1)S(1)}, u32[]{:S(2)}, u32[]{:S(2)}) collective-permute-start(bf16[256,512]{1,0:T(8,128)(2,1)S(1)} %get-tuple-element.58.refs_9_), channel_id=1, source_target_pairs={{0,1},{1,0},{2,3},{3,2},{4,5},{5,4},{6,7},{7,6},{8,9},{9,8},{10,11... | collective-permute-start | bytes 786440 | tf_op jit(solution)/shard_map/ppermute | solution.py:595
  50.4 3.6 %copy-start.1 = (bf16[256,1024]{1,0:T(8,128)(2,1)}, bf16[256,1024]{1,0:T(8,128)(2,1)S(1)}, u32[]{:S(2)}) copy-start(bf16[256,1024]{1,0:T(8,128)(2,1)S(1)} %collective-permute-done.9.refs_10_.refs_3_) | copy-start | bytes 1572868
  54.1 29.0 %collective-permute-start.15 = (bf16[256,2048]{1,0:T(8,128)(2,1)S(1)}, bf16[256,2048]{1,0:T(8,128)(2,1)}, u32[]{:S(2)}, u32[]{:S(2)}) collective-permute-start(bf16[256,2048]{1,0:T(8,128)(2,1)S(1)} %keep.5.refs_7_), channel_id=1, source_target_pairs={{0,2},{1,3},{2,0},{3,1},{4,6},{5,7},{6,4},{7,5},{8,10},{9,11},{10,... | collective-permute-start | bytes 3145736 | tf_op jit(solution)/shard_map/ppermute | solution.py:599
  68.6 4.7 %collective-permute-start.10 = (bf16[16,2048]{1,0:T(8,128)(2,1)S(1)}, bf16[16,2048]{1,0:T(8,128)(2,1)S(1)}, u32[]{:S(2)}, u32[]{:S(2)}) collective-permute-start(bf16[16,2048]{1,0:T(8,128)(2,1)S(1)} %get-tuple-element.74.refs_4_), channel_id=1, source_target_pairs={{0,1},{1,0},{2,3},{3,2},{4,5},{5,4},{6,7},{7,6},{8,9},{9,8},{10,11... | collective-permute-start | bytes 196616 | tf_op jit(solution)/shard_map/ppermute | solution.py:595
  68.6 7.0 %collective-permute-start.12 = (bf16[512,512]{1,0:T(8,128)(2,1)S(1)}, bf16[512,512]{1,0:T(8,128)(2,1)S(1)}, u32[]{:S(2)}, u32[]{:S(2)}) collective-permute-start(bf16[512,512]{1,0:T(8,128)(2,1)S(1)} %get-tuple-element.82), channel_id=1, source_target_pairs={{0,1},{1,0},{2,3},{3,2},{4,5},{5,4},{6,7},{7,6},{8,9},{9,8},{10,11... | collective-permute-start | bytes 1572872 | tf_op jit(solution)/shard_map/ppermute | solution.py:595
  69.1 8.1 %collective-permute-start.11 = (bf16[512,512]{1,0:T(8,128)(2,1)S(1)}, bf16[512,512]{1,0:T(8,128)(2,1)S(1)}, u32[]{:S(2)}, u32[]{:S(2)}) collective-permute-start(bf16[512,512]{1,0:T(8,128)(2,1)S(1)} %get-tuple-element.71.refs_6_), channel_id=1, source_target_pairs={{0,1},{1,0},{2,3},{3,2},{4,5},{5,4},{6,7},{7,6},{8,9},{9,8},{10,11... | collective-permute-start | bytes 1572872 | tf_op jit(solution)/shard_map/ppermute | solution.py:595
  72.8 7.4 %collective-permute-start.14 = (bf16[512,512]{1,0:T(8,128)(2,1)S(1)}, bf16[512,512]{1,0:T(8,128)(2,1)S(1)}, u32[]{:S(2)}, u32[]{:S(2)}) collective-permute-start(bf16[512,512]{1,0:T(8,128)(2,1)S(1)} %get-tuple-element.87), channel_id=1, source_target_pairs={{0,1},{1,0},{2,3},{3,2},{4,5},{5,4},{6,7},{7,6},{8,9},{9,8},{10,11... | collective-permute-start | bytes 1572872 | tf_op jit(solution)/shard_map/ppermute | solution.py:595
  73.3 6.9 %collective-permute-start.13 = (bf16[512,512]{1,0:T(8,128)(2,1)S(1)}, bf16[512,512]{1,0:T(8,128)(2,1)S(1)}, u32[]{:S(2)}, u32[]{:S(2)}) collective-permute-start(bf16[512,512]{1,0:T(8,128)(2,1)S(1)} %get-tuple-element.79.refs_7_), channel_id=1, source_target_pairs={{0,1},{1,0},{2,3},{3,2},{4,5},{5,4},{6,7},{7,6},{8,9},{9,8},{10,11... | collective-permute-start | bytes 1572872 | tf_op jit(solution)/shard_map/ppermute | solution.py:595
  75.6 7.5 %collective-permute-start.16 = (bf16[16,2048]{1,0:T(8,128)(2,1)S(1)}, bf16[16,2048]{1,0:T(8,128)(2,1)S(1)}, u32[]{:S(2)}, u32[]{:S(2)}) collective-permute-start(bf16[16,2048]{1,0:T(8,128)(2,1)S(1)} %get-tuple-element.83.refs_6_), channel_id=1, source_target_pairs={{0,2},{1,3},{2,0},{3,1},{4,6},{5,7},{6,4},{7,5},{8,10},{9,11},{10,... | collective-permute-start | bytes 196616 | tf_op jit(solution)/shard_map/ppermute | solution.py:599
  80.2 2.9 %copy-start.2 = (bf16[256,1024]{1,0:T(8,128)(2,1)S(1)}, bf16[256,1024]{1,0:T(8,128)(2,1)}, u32[]{:S(2)}) copy-start(bf16[256,1024]{1,0:T(8,128)(2,1)} %copy-done.1) | copy-start | bytes 1572868
  80.2 2.9 %copy-start.4 = (bf16[256,1024]{1,0:T(8,128)(2,1)S(1)}, bf16[256,1024]{1,0:T(8,128)(2,1)}, u32[]{:S(2)}) copy-start(bf16[256,1024]{1,0:T(8,128)(2,1)} %copy-done.3) | copy-start | bytes 1572868
